TPU v7x, 128 devices: a whole 4x4x4 slice. The times are simulated.
128 devices in a mesh: img: 16 (over z, x_lo, core), txt: 8 (over x_hi, y).
Axes of the slice: x: 4 (x_hi: 2, x_lo: 2; x = x_hi * 2 + x_lo), y: 4, z: 4, core: 2. Of those that a mesh axis runs over, the one named last changes fastest.
Arguments:
- images: bfloat16 [16384, 1152], P(('img', 'txt')), may hold values from -4 to 4
- texts: bfloat16 [16384, 1152], P(('txt', 'img')), may hold values from -4 to 4
- logit_scale: float32 [1], replicated, may hold values from 1.6 to 2.5
- bias: float32 [1], replicated, may hold values from -8 to -3
Outputs:
- loss: float32 [1], replicated
- image_grad: float32 [16384, 1152], P(('img', 'txt'))
- text_grad: float32 [16384, 1152], P(('txt', 'img'))
All inputs are finite; a program needn't handle non-finite values.
Results may differ from a plain program's by a relative error of at most 0.0013.
The roundings to bfloat16 on the way count: a program that leaves them out, or rounds other values in their place, can miss the bound.
Values may be sent and summed in bfloat16 or wider, within the bound.
No kernel may reach another device: no remote copies, remote signals or barrier semaphores. Data moves between devices by JAX's collectives and lax.ppermute only.
A program may use at most 64 MiB of HBM per device.

v0:
```python
import jax
import jax.numpy as jnp
from jax import lax
from jax.sharding import PartitionSpec as P


def unit_rows(raw):
    wide = raw.astype(jnp.float32)
    inverse = lax.rsqrt(jnp.sum(wide * wide, axis=1, keepdims=True) + 1e-06)
    return (inverse, wide * inverse)


def back_norm(inverse, unit_wide, grad):
    return inverse * (grad - unit_wide * jnp.sum(unit_wide * grad, axis=1, keepdims=True))


def block_width():
    return 512


def coeff_of(image_all, block, number, width, row_base, col_base, temper, shift):
    height = image_all.shape[0]
    logits = (
        temper
        * lax.dot_general(
            image_all, block, (((1,), (1,)), ((), ())), preferred_element_type=jnp.float32
        )
        + shift
    )
    rows = row_base + lax.broadcasted_iota(jnp.int32, (height, width), 0)
    cols = col_base + number * width + lax.broadcasted_iota(jnp.int32, (height, width), 1)
    sign = jnp.where(rows == cols, 1.0, -1.0).astype(jnp.float32)
    loss_add = -jnp.sum(jax.nn.log_sigmoid(sign * logits))
    coeff = (-sign * jax.nn.sigmoid(-sign * logits) * temper).astype(jnp.bfloat16)
    return (loss_add, coeff)


def pair_terms(image_all, piece, row_base, col_base, temper, shift):
    count = piece.shape[0]
    width = block_width()
    number_blocks = count // width
    blocks = piece.reshape(number_blocks, width, piece.shape[1])
    numbers = jnp.arange(number_blocks, dtype=jnp.int32)

    def visit(carry, item):
        loss_sum, image_part = carry
        block, number = item
        loss_add, coeff = coeff_of(
            image_all, block, number, width, row_base, col_base, temper, shift
        )
        image_part = image_part + jnp.dot(coeff, block, preferred_element_type=jnp.float32)
        text_block = lax.dot_general(
            coeff, image_all, (((0,), (0,)), ((), ())), preferred_element_type=jnp.float32
        )
        return ((loss_sum + loss_add, image_part), text_block)

    start = (
        jnp.zeros((), jnp.float32),
        jnp.zeros((image_all.shape[0], piece.shape[1]), jnp.float32),
    )
    (loss_sum, image_part), text_blocks = lax.scan(visit, start, (blocks, numbers))
    return (loss_sum, image_part, text_blocks.reshape(count, piece.shape[1]))


def shards(images, texts, logit_scale, bias):
    temper = jnp.exp(logit_scale[0])
    shift = bias[0]
    image_inv, image_wide = unit_rows(images)
    text_inv, text_wide = unit_rows(texts)
    image_unit = image_wide.astype(jnp.bfloat16)
    text_unit = text_wide.astype(jnp.bfloat16)
    image_all = lax.all_gather(image_unit, "txt", axis=0, tiled=True)
    image_count = image_all.shape[0]
    text_count = texts.shape[0] * lax.axis_size("img")
    row_base = lax.axis_index("img") * image_count
    col_base = lax.axis_index("txt") * text_count
    text_all = lax.all_gather(text_unit, "img", axis=0, tiled=True)
    loss_part, image_part, text_part = pair_terms(
        image_all, text_all, row_base, col_base, temper, shift
    )
    unit_image_grad = lax.psum_scatter(image_part, "txt", scatter_dimension=0, tiled=True)
    unit_text_grad = lax.psum_scatter(text_part, "img", scatter_dimension=0, tiled=True)
    total = lax.psum(loss_part, ("img", "txt"))
    loss = (total / (image_count * lax.axis_size("img"))).reshape(1)
    image_grad = back_norm(image_inv, image_wide, unit_image_grad)
    text_grad = back_norm(text_inv, text_wide, unit_text_grad)
    return (loss, image_grad, text_grad)


def solution(mesh):
    placed = (P(("img", "txt"), None), P(("txt", "img"), None), P(), P())
    return jax.shard_map(
        shards,
        mesh=mesh,
        in_specs=placed,
        out_specs=(P(), P(("img", "txt"), None), P(("txt", "img"), None)),
        check_vma=False,
    )
```

profile of v0, /device:TPU:0, one launch (start us, length us, event | category | flops | bytes accessed | tf_op | source)
XLA Modules:
  0.0 396.5 jit_solution(4465870561564433479)
XLA Ops:
  7.2 0.0 all-gather.5.cloned.1.call-start
  7.2 1.1 fusion.33
  8.3 1.8 fusion.22
  10.1 0.0 all-gather.5.cloned.1.call-update
  10.1 0.0 all-gather.3.cloned.1.call-start
  10.2 1.1 fusion.29
  11.3 1.8 fusion.25
  13.1 0.0 all-gather.3.cloned.1.call-update
  13.1 0.0 reduce-scatter.3.cloned.1.call-start
  13.9 55.4 %all-gather.5.cloned.1.call-done = bf16[1024,1152]{1,0:T(8,128)(2,1)} async-done(((bf16[128,1152]{1,0:T(8,128)(2,1)}), bf16[1024,1152]{1,0:T(8,128)(2,1)}) %all-gather.5.cloned.1.call-update) | async-done | bytes 2359312 | tf_op jit(solution)/shard_map/all_gather | solution.py:72
  69.3 38.9 %all-gather.3.cloned.1.call-done = bf16[2048,1152]{1,0:T(8,128)(2,1)} async-done(((bf16[128,1152]{1,0:T(8,128)(2,1)}), bf16[2048,1152]{1,0:T(8,128)(2,1)}) %all-gather.3.cloned.1.call-update) | async-done | bytes 4718608 | tf_op jit(solution)/shard_map/all_gather | solution.py:77
  108.2 78.7 %while.15 = (s32[]{:T(128)}, f32[]{:T(128)}, f32[1024,1152]{1,0:T(8,128)}, f32[4,512,1152]{2,1,0:T(8,128)}, s32[]{:T(128)}, /*index=5*/s32[4]{0:T(128)S(1)}, s32...) while((s32[]{:T(128)}, f32[]{:T(128)}, ...), condition=%wide.region_4.5_spmd.clone, body=%wide.region_2.4_spmd.clone.sunk | while | flops 3645638144 | bytes 34631928 | solution.py:61
  108.2 0.6 dynamic_slice.25
  109.4 6.1 %fusion.48 = (f32[]{:T(128)}, f32[512,1024]{1,0:T(8,128)S(1)}) fusion(f32[]{:T(128)} %get-tuple-element.234, f32[]{:T(128)} %get-tuple-element.231, s32[1024]{0:T(1024)S(1)} %iota_add_fusion.4, s32[512]{0:T(512)S(1)} %iota_add_fusion.5, bf16[1024,1152]{1,0:T(8,128)(2,1)} %get-tuple-element.233, bf16[4,512,1152]{2,1,0:T(8,128)(2,1)} %get-tuple-element.232, ...), kind=kOutput, calls=%fused_computation.14.clone.1 | convolution fusion | flops 1214775296 | bytes 5643272 | tf_op jit(solution)/shard_map/while/body/eval_jaxpr/dot_general | solution.py:25
  116.2 0.0 copy-start.2
  116.2 6.3 %convolution_add_fusion.2 = f32[1024,1152]{1,0:T(8,128)} fusion(f32[1024,1152]{1,0:T(8,128)} %get-tuple-element.212, pred[]{:T(512)S(6)} %compare.3, bf16[4,512,1152]{2,1,0:T(8,128)(2,1)} %get-tuple-element.232, s32[]{:T(128)S(6)} %copy.12, f32[512,1024]{1,0:T(8,128)S(1)} %get-tuple-element.195, f32[]{:T(128)} %get-tuple-element.231, ...), kind=kOutput, calls=%fused_computation.1.clone.1 | convolution fusion | flops 1216610304 | bytes 12721669 | tf_op jit(solution)/shard_map/while/body/eval_jaxpr/dot_general | solution.py:51
  122.5 0.0 copy-done.2
  122.5 4.3 %fusion.49 = f32[4,512,1152]{2,1,0:T(8,128)} fusion(f32[4,512,1152]{2,1,0:T(8,128)} %get-tuple-element.213, s32[]{:T(128)S(6)} %copy.12, bf16[1024,1152]{1,0:T(8,128)(2,1)S(1)} %copy-done.2, f32[512,1024]{1,0:T(8,128)S(1)} %get-tuple-element.195, f32[]{:T(128)} %get-tuple-element.231, f32[]{:T(128)} %get-tuple-element.234, ...), kind=kOutput, calls=%fused_computation.3.clone.1 | convolution fusion | flops 1214251008 | bytes 6823428 | tf_op jit(solution)/shard_map/while/body/eval_jaxpr/dot_general | solution.py:52
  126.8 0.6 dynamic_slice.25
  128.0 6.1 %fusion.48 = (f32[]{:T(128)}, f32[512,1024]{1,0:T(8,128)S(1)}) fusion(f32[]{:T(128)} %get-tuple-element.234, f32[]{:T(128)} %get-tuple-element.231, s32[1024]{0:T(1024)S(1)} %iota_add_fusion.4, s32[512]{0:T(512)S(1)} %iota_add_fusion.5, bf16[1024,1152]{1,0:T(8,128)(2,1)} %get-tuple-element.233, bf16[4,512,1152]{2,1,0:T(8,128)(2,1)} %get-tuple-element.232, ...), kind=kOutput, calls=%fused_computation.14.clone.1 | convolution fusion | flops 1214775296 | bytes 5643272 | tf_op jit(solution)/shard_map/while/body/eval_jaxpr/dot_general | solution.py:25
  134.8 0.0 copy-start.2
  134.8 7.7 %convolution_add_fusion.2 = f32[1024,1152]{1,0:T(8,128)} fusion(f32[1024,1152]{1,0:T(8,128)} %get-tuple-element.212, pred[]{:T(512)S(6)} %compare.3, bf16[4,512,1152]{2,1,0:T(8,128)(2,1)} %get-tuple-element.232, s32[]{:T(128)S(6)} %copy.12, f32[512,1024]{1,0:T(8,128)S(1)} %get-tuple-element.195, f32[]{:T(128)} %get-tuple-element.231, ...), kind=kOutput, calls=%fused_computation.1.clone.1 | convolution fusion | flops 1216610304 | bytes 12721669 | tf_op jit(solution)/shard_map/while/body/eval_jaxpr/dot_general | solution.py:51
  142.5 0.0 copy-done.2
  142.5 4.2 %fusion.49 = f32[4,512,1152]{2,1,0:T(8,128)} fusion(f32[4,512,1152]{2,1,0:T(8,128)} %get-tuple-element.213, s32[]{:T(128)S(6)} %copy.12, bf16[1024,1152]{1,0:T(8,128)(2,1)S(1)} %copy-done.2, f32[512,1024]{1,0:T(8,128)S(1)} %get-tuple-element.195, f32[]{:T(128)} %get-tuple-element.231, f32[]{:T(128)} %get-tuple-element.234, ...), kind=kOutput, calls=%fused_computation.3.clone.1 | convolution fusion | flops 1214251008 | bytes 6823428 | tf_op jit(solution)/shard_map/while/body/eval_jaxpr/dot_general | solution.py:52
  146.7 0.6 dynamic_slice.25
  148.0 6.1 %fusion.48 = (f32[]{:T(128)}, f32[512,1024]{1,0:T(8,128)S(1)}) fusion(f32[]{:T(128)} %get-tuple-element.234, f32[]{:T(128)} %get-tuple-element.231, s32[1024]{0:T(1024)S(1)} %iota_add_fusion.4, s32[512]{0:T(512)S(1)} %iota_add_fusion.5, bf16[1024,1152]{1,0:T(8,128)(2,1)} %get-tuple-element.233, bf16[4,512,1152]{2,1,0:T(8,128)(2,1)} %get-tuple-element.232, ...), kind=kOutput, calls=%fused_computation.14.clone.1 | convolution fusion | flops 1214775296 | bytes 5643272 | tf_op jit(solution)/shard_map/while/body/eval_jaxpr/dot_general | solution.py:25
  154.8 0.0 copy-start.2
  154.8 7.7 %convolution_add_fusion.2 = f32[1024,1152]{1,0:T(8,128)} fusion(f32[1024,1152]{1,0:T(8,128)} %get-tuple-element.212, pred[]{:T(512)S(6)} %compare.3, bf16[4,512,1152]{2,1,0:T(8,128)(2,1)} %get-tuple-element.232, s32[]{:T(128)S(6)} %copy.12, f32[512,1024]{1,0:T(8,128)S(1)} %get-tuple-element.195, f32[]{:T(128)} %get-tuple-element.231, ...), kind=kOutput, calls=%fused_computation.1.clone.1 | convolution fusion | flops 1216610304 | bytes 12721669 | tf_op jit(solution)/shard_map/while/body/eval_jaxpr/dot_general | solution.py:51
  162.5 0.0 copy-done.2
  162.5 4.3 %fusion.49 = f32[4,512,1152]{2,1,0:T(8,128)} fusion(f32[4,512,1152]{2,1,0:T(8,128)} %get-tuple-element.213, s32[]{:T(128)S(6)} %copy.12, bf16[1024,1152]{1,0:T(8,128)(2,1)S(1)} %copy-done.2, f32[512,1024]{1,0:T(8,128)S(1)} %get-tuple-element.195, f32[]{:T(128)} %get-tuple-element.231, f32[]{:T(128)} %get-tuple-element.234, ...), kind=kOutput, calls=%fused_computation.3.clone.1 | convolution fusion | flops 1214251008 | bytes 6823428 | tf_op jit(solution)/shard_map/while/body/eval_jaxpr/dot_general | solution.py:52
  166.8 0.6 dynamic_slice.25
  168.1 6.1 %fusion.48 = (f32[]{:T(128)}, f32[512,1024]{1,0:T(8,128)S(1)}) fusion(f32[]{:T(128)} %get-tuple-element.234, f32[]{:T(128)} %get-tuple-element.231, s32[1024]{0:T(1024)S(1)} %iota_add_fusion.4, s32[512]{0:T(512)S(1)} %iota_add_fusion.5, bf16[1024,1152]{1,0:T(8,128)(2,1)} %get-tuple-element.233, bf16[4,512,1152]{2,1,0:T(8,128)(2,1)} %get-tuple-element.232, ...), kind=kOutput, calls=%fused_computation.14.clone.1 | convolution fusion | flops 1214775296 | bytes 5643272 | tf_op jit(solution)/shard_map/while/body/eval_jaxpr/dot_general | solution.py:25
  174.8 0.0 copy-start.2
  174.8 7.7 %convolution_add_fusion.2 = f32[1024,1152]{1,0:T(8,128)} fusion(f32[1024,1152]{1,0:T(8,128)} %get-tuple-element.212, pred[]{:T(512)S(6)} %compare.3, bf16[4,512,1152]{2,1,0:T(8,128)(2,1)} %get-tuple-element.232, s32[]{:T(128)S(6)} %copy.12, f32[512,1024]{1,0:T(8,128)S(1)} %get-tuple-element.195, f32[]{:T(128)} %get-tuple-element.231, ...), kind=kOutput, calls=%fused_computation.1.clone.1 | convolution fusion | flops 1216610304 | bytes 12721669 | tf_op jit(solution)/shard_map/while/body/eval_jaxpr/dot_general | solution.py:51
  182.5 0.0 copy-done.2
  182.5 4.3 %fusion.49 = f32[4,512,1152]{2,1,0:T(8,128)} fusion(f32[4,512,1152]{2,1,0:T(8,128)} %get-tuple-element.213, s32[]{:T(128)S(6)} %copy.12, bf16[1024,1152]{1,0:T(8,128)(2,1)S(1)} %copy-done.2, f32[512,1024]{1,0:T(8,128)S(1)} %get-tuple-element.195, f32[]{:T(128)} %get-tuple-element.231, f32[]{:T(128)} %get-tuple-element.234, ...), kind=kOutput, calls=%fused_computation.3.clone.1 | convolution fusion | flops 1214251008 | bytes 6823428 | tf_op jit(solution)/shard_map/while/body/eval_jaxpr/dot_general | solution.py:52
  186.9 0.0 reduce-scatter.3.cloned.1.call-update
  186.9 0.0 reduce-scatter.5.cloned.1.call-start
  186.9 0.0 copy-start
  186.9 0.5 reduce-scatter.5.cloned.1.call-update
  187.5 0.0 copy-start.1
  187.5 72.1 %psum.7 = f32[]{:T(128)} all-reduce(f32[]{:T(128)} %get-tuple-element.62), channel_id=1, replica_groups=mesh['img'=16,'txt'=8] {'img','txt'}, use_global_device_ids=true, to_apply=%region_5.6 | all-reduce | flops 1 | bytes 8 | tf_op jit(solution)/shard_map/psum | solution.py:83
  260.2 15.5 %reduce-scatter.3.cloned.1.call-done = f32[128,1152]{1,0:T(8,128)} async-done(((f32[1024,1152]{1,0:T(8,128)}), f32[128,1152]{1,0:T(8,128)}) %reduce-scatter.3.cloned.1.call-update) | async-done | bytes 589840 | tf_op jit(solution)/shard_map/reduce_scatter | solution.py:81
  275.7 0.0 copy-done
  275.7 1.3 fusion.30
  277.0 2.1 fusion.32
  279.1 106.4 %reduce-scatter.5.cloned.1.call-done = f32[128,1152]{1,0:T(8,128)} async-done(((f32[2048,1152]{1,0:T(8,128)}), f32[128,1152]{1,0:T(8,128)}) %reduce-scatter.5.cloned.1.call-update) | async-done | bytes 589840 | tf_op jit(solution)/shard_map/reduce_scatter | solution.py:82
  385.5 0.0 copy-done.1
  385.5 1.3 fusion.26
  386.7 2.1 fusion.28
  (13 shorter events, 0.1 us)
Async XLA Ops:
  7.2 62.1 %all-gather.5.cloned.1.call-start = ((), (), s32[]{:S(2)}) async-start(), calls=%async_computation.3 | async-start | bytes 2654208 | tf_op jit(solution)/shard_map/all_gather | solution.py:72
  10.1 98.0 %all-gather.3.cloned.1.call-start = ((), (), s32[]{:S(2)}) async-start(), calls=%async_computation.2 | async-start | bytes 5013504 | tf_op jit(solution)/shard_map/all_gather | solution.py:77
  13.1 262.5 %reduce-scatter.3.cloned.1.call-start = ((), (), s32[]{:S(2)}) async-start(), calls=%async_computation.4 | async-start | bytes 5308416 | tf_op jit(solution)/shard_map/reduce_scatter | solution.py:81
  116.2 6.3 %copy-start.2 = (bf16[1024,1152]{1,0:T(8,128)(2,1)S(1)}, bf16[1024,1152]{1,0:T(8,128)(2,1)}, u32[]{:S(2)}) copy-start(bf16[1024,1152]{1,0:T(8,128)(2,1)} %get-tuple-element.233) | copy-start | bytes 7077892 | tf_op jit(solution)/shard_map/while
  134.8 7.7 %copy-start.2 = (bf16[1024,1152]{1,0:T(8,128)(2,1)S(1)}, bf16[1024,1152]{1,0:T(8,128)(2,1)}, u32[]{:S(2)}) copy-start(bf16[1024,1152]{1,0:T(8,128)(2,1)} %get-tuple-element.233) | copy-start | bytes 7077892 | tf_op jit(solution)/shard_map/while
  154.8 7.7 %copy-start.2 = (bf16[1024,1152]{1,0:T(8,128)(2,1)S(1)}, bf16[1024,1152]{1,0:T(8,128)(2,1)}, u32[]{:S(2)}) copy-start(bf16[1024,1152]{1,0:T(8,128)(2,1)} %get-tuple-element.233) | copy-start | bytes 7077892 | tf_op jit(solution)/shard_map/while
  174.8 7.7 %copy-start.2 = (bf16[1024,1152]{1,0:T(8,128)(2,1)S(1)}, bf16[1024,1152]{1,0:T(8,128)(2,1)}, u32[]{:S(2)}) copy-start(bf16[1024,1152]{1,0:T(8,128)(2,1)} %get-tuple-element.233) | copy-start | bytes 7077892 | tf_op jit(solution)/shard_map/while
  186.9 198.6 %reduce-scatter.5.cloned.1.call-start = ((), (), s32[]{:S(2)}) async-start(), calls=%async_computation.5 | async-start | bytes 10027008 | tf_op jit(solution)/shard_map/reduce_scatter | solution.py:82
  186.9 88.7 %copy-start = (bf16[128,1152]{1,0:T(8,128)(2,1)S(1)}, bf16[128,1152]{1,0:T(8,128)(2,1)}, u32[]{:S(2)}) copy-start(bf16[128,1152]{1,0:T(8,128)(2,1)} %param.6) | copy-start | bytes 884740
  187.5 198.0 %copy-start.1 = (bf16[128,1152]{1,0:T(8,128)(2,1)S(1)}, bf16[128,1152]{1,0:T(8,128)(2,1)}, u32[]{:S(2)}) copy-start(bf16[128,1152]{1,0:T(8,128)(2,1)} %param.7) | copy-start | bytes 884740
Sparse Core Ops, SparseCore 0:
  10.9 58.3 all-gather.4
  71.6 36.5 all-gather.2
  187.0 88.6 reduce-scatter.2
  277.9 107.4 reduce-scatter.4
where the time goes:
time: 397 us; the launch traced here: 396 us
  waiting for transfers between devices  217 us (55%)
  blocking collectives  72.1 us (18%)
  matrix products  71 us (18%)
  between operations  16.3 us (4%)
  other arithmetic  12.6 us (3%)
  loops' own time  5.33 us (1%)
    reduce_scatter x1, waiting for transfers between devices, shards(): lax.psum_scatter(text_part, 'img', scatter_dimension=0, tiled=True)  106 us
    psum x1, blocking collectives, shards(): total = lax.psum(loss_part, ('img', 'txt'))  72.1 us
    all_gather x1, waiting for transfers between devices, shards(): image_all = lax.all_gather(image_unit, 'txt', axis=0, tiled=True)  55.4 us
    all_gather x1, waiting for transfers between devices, shards(): text_all = lax.all_gather(text_unit, 'img', axis=0, tiled=True)  38.9 us
    dot_general x4, matrix products, visit(): jnp.dot(coeff, block, preferred_element_type=jnp.float32)  29.4 us
    dot_general x4, matrix products, coeff_of(): lax.dot_general(image_all, block, (((1,), (1,)), ((), ())), preferred_ele...  24.4 us
    dot_general x4, matrix products, visit(): lax.dot_general(coeff, image_all, (((0,), (0,)), ((), ())), preferred_ele...  17.1 us
    reduce_scatter x1, waiting for transfers between devices, shards(): lax.psum_scatter(image_part, 'txt', scatter_dimension=0, tiled=True)  15.5 us
  transfers between devices with their start and end apart: 4, of which 4 were waited for; matrix products, arithmetic and copies ran while one was open for 2% of the time, Pallas kernels for 0%

commit v1 on v0

v1 whole, which is shorter than its diff:
```python
import functools

import jax
import jax.numpy as jnp
from jax import lax
from jax.experimental import pallas as pl
from jax.experimental.pallas import tpu as pltpu
from jax.sharding import PartitionSpec as P

IMAGE_PAIRS = {"x": 2 << 3, "y": 1, "z": 4 << 3}
TEXT_PAIRS = {"x": (2 << 3) + 4, "y": 3, "z": 12 << 3}
CORE = 1 << 3
PIECE = 128
ROWS = ("", "y", "x", "xz", "z", "yz", "xy", "xyz")
PAIR_VMEM = 28 * 2**20
SMALL_VMEM = 16 * 2**20
LOG2E = 1.4426950408889634
LN2 = 0.6931471805599453
NT = (((1,), (1,)), ((), ()))
NN = (((1,), (0,)), ((), ()))
TN = (((0,), (0,)), ((), ()))
HBM = pl.BlockSpec(memory_space=pl.ANY)
SMEM = pl.BlockSpec(memory_space=pltpu.SMEM)
VMEM = pl.BlockSpec(memory_space=pltpu.VMEM)


def shape_of(rows, depth, dtype):
    return jax.ShapeDtypeStruct((rows, depth), dtype)


def swap(value, mask):
    axes = ("img", "txt")
    return lax.ppermute(value, axes, [(k ^ mask, k) for k in range(lax.axis_size(axes))])


def encode(value):
    square = value * value
    return ((square * value) * (square * square)).astype(jnp.bfloat16)


def decode(code):
    wide = code.astype(jnp.float32)
    root = jnp.exp2(jnp.log2(jnp.abs(wide)) * (1.0 / 7.0))
    return jnp.where(wide < 0.0, -root, root)


def unit_kernel(images_ref, texts_ref, image_out, text_out, raw, sems):
    loads = [pltpu.make_async_copy(ref, raw.at[k], sems.at[k]) for k, ref in enumerate((images_ref, texts_ref))]
    for load in loads:
        load.start()
    for k, out in enumerate((image_out, text_out)):
        loads[k].wait()
        wide = raw[k].astype(jnp.float32)
        inverse = lax.rsqrt(jnp.sum(wide * wide, axis=1, keepdims=True) + 1e-06)
        out[...] = (wide * inverse).astype(jnp.bfloat16)


def unit_rows(images, texts):
    out = shape_of(*images.shape, jnp.bfloat16)
    return pl.pallas_call(
        unit_kernel,
        out_shape=[out, out],
        in_specs=[HBM, HBM],
        out_specs=[VMEM, VMEM],
        scratch_shapes=[pltpu.VMEM((2, *images.shape), jnp.bfloat16), pltpu.SemaphoreType.DMA((2,))],
        compiler_params=pltpu.CompilerParams(vmem_limit_bytes=60 * 2**20),
        name="unit_rows",
    )(images, texts)


def row_masks(pairs):
    return [sum(pairs[axis] for axis in axes) for axes in ROWS]


def logit_kernel(place_ref, scale_ref, bias_ref, *refs):
    image_refs, text_refs = refs[:4], refs[4:12]
    coeff_refs, other_refs, loss_ref = refs[12:14], refs[14:16], refs[16]
    rows = image_refs[0].shape[0]
    pieces = rows // PIECE

    place = place_ref[0]
    image_base = [lax.bitwise_xor(place, mask) * PIECE for mask in row_masks(IMAGE_PAIRS)]
    text_base = []
    for core in (0, CORE):
        for mask in row_masks(TEXT_PAIRS):
            flat = lax.bitwise_xor(place, mask ^ core)
            text_base.append((lax.rem(flat, 8) * 16 + lax.div(flat, 8)) * PIECE)

    temper = jnp.exp(jnp.full((1, PIECE), scale_ref[0], jnp.float32))
    slope = temper * LOG2E
    shift = jnp.full((1, PIECE), bias_ref[0] * LOG2E, jnp.float32)
    apart = lax.broadcasted_iota(jnp.int32, (PIECE, PIECE), 0) - lax.broadcasted_iota(
        jnp.int32, (PIECE, PIECE), 1
    )
    quarter = PIECE // 4
    loss_sum = jnp.zeros((8, PIECE), jnp.float32)
    own_sum = jnp.zeros((8, PIECE), jnp.float32)
    for t in (4, 5, 6, 7, 0, 1, 2, 3):
        coeff_ref, left = coeff_refs[t // 4], t % 4 * rows
        for r, image_ref in enumerate(image_refs):
            dots = lax.dot_general(image_ref[...], text_refs[t][...], NT, preferred_element_type=jnp.float32)
            for a in range(pieces):
                top = r * rows + a * PIECE
                for b in range(pieces):
                    power = dots[a * PIECE : (a + 1) * PIECE, b * PIECE : (b + 1) * PIECE] * slope + shift
                    grown = jnp.exp2(power)
                    match = apart == text_base[t * pieces + b] - image_base[r * pieces + a]
                    weight = jnp.where(match, -1.0, grown) * pl.reciprocal(1.0 + grown) * temper
                    column = left + b * PIECE
                    coeff_ref[top : top + PIECE, column : column + PIECE] = weight.astype(jnp.bfloat16)
                    g = [grown[k * quarter : (k + 1) * quarter] for k in range(4)]
                    low = g[0] + g[1] + g[0] * g[1]
                    high = g[2] + g[3] + g[2] * g[3]
                    terms = jnp.log(1.0 + (low + high + low * high))
                    chosen = jnp.where(match, power, 0.0)
                    for k in range(quarter // 8):
                        loss_sum = loss_sum + terms[k * 8 : (k + 1) * 8]
                    for k in range(PIECE // 8):
                        own_sum = own_sum + chosen[k * 8 : (k + 1) * 8]
        if t >= 4:
            part = text_shares(coeff_ref, left, image_refs)
            other_refs[t % 4 // 2][t % 2 * rows : (t % 2 + 1) * rows, :] = encode(part)
    loss = loss_sum - LN2 * own_sum
    loss_ref[...] = jnp.broadcast_to(jnp.sum(loss, keepdims=True), loss_ref.shape)


def text_shares(coeff_ref, left, image_refs):
    rows = image_refs[0].shape[0]
    part = None
    for r, image_ref in enumerate(image_refs):
        more = lax.dot_general(
            coeff_ref[r * rows : (r + 1) * rows, left : left + rows],
            image_ref[...],
            TN,
            preferred_element_type=jnp.float32,
        )
        part = more if part is None else part + more
    return part


def logit_terms(place, logit_scale, bias, images, texts):
    rows, depth = images[0].shape
    height, count = len(images) * rows, len(texts) * rows
    coeff = shape_of(height, count // 2, jnp.bfloat16)
    outs = pl.pallas_call(
        logit_kernel,
        out_shape=[coeff, coeff]
        + [shape_of(2 * rows, depth, jnp.bfloat16)] * 2
        + [shape_of(8, PIECE, jnp.float32)],
        in_specs=[SMEM, SMEM, SMEM] + [VMEM] * 12,
        out_specs=[VMEM] * 5,
        compiler_params=pltpu.CompilerParams(vmem_limit_bytes=PAIR_VMEM),
        cost_estimate=cost(3 * height * count * depth // 2),
        name="logit_terms",
    )(place, logit_scale, bias, *images, *texts)
    return outs[:2], outs[2:4], outs[4]


def cost(multiplies):
    return pl.CostEstimate(flops=2 * multiplies, bytes_accessed=8 * 2**20, transcendentals=0)


def text_kernel(coeff_ref, *refs):
    image_refs, outs = refs[:4], refs[4:8]
    for t in (2, 3, 0, 1):
        outs[t][...] = text_shares(coeff_ref, t * outs[t].shape[0], image_refs)


def text_terms(coeff, images):
    rows, depth = images[0].shape
    height, count = coeff.shape
    return pl.pallas_call(
        text_kernel,
        out_shape=[shape_of(rows, depth, jnp.float32)] * 4,
        in_specs=[VMEM] * 5,
        out_specs=[VMEM] * 4,
        compiler_params=pltpu.CompilerParams(vmem_limit_bytes=PAIR_VMEM),
        cost_estimate=cost(height * count * depth),
        name="text_terms",
    )(coeff, *images)


def image_kernel(first, own_ref, other_ref, *refs):
    text_refs, outs = refs[:8], refs[8:10]
    rows = outs[0].shape[0]
    for k, out in enumerate(outs):
        top = first + k * rows
        total = None
        for t, text_ref in enumerate(text_refs):
            coeff_ref, left = (own_ref, other_ref)[t // 4], t % 4 * rows
            more = jnp.dot(
                coeff_ref[top : top + rows, left : left + rows], text_ref[...], preferred_element_type=jnp.float32
            )
            total = more if total is None else total + more
        out[...] = total if out.dtype == jnp.float32 else encode(total)


def image_terms(first, dtype, coeffs, texts):
    rows, depth = texts[0].shape
    return pl.pallas_call(
        functools.partial(image_kernel, first),
        out_shape=[shape_of(rows, depth, dtype)] * 2,
        in_specs=[VMEM] * 10,
        out_specs=[VMEM] * 2,
        compiler_params=pltpu.CompilerParams(vmem_limit_bytes=PAIR_VMEM),
        cost_estimate=cost(4 * rows * coeffs[0].shape[1] * depth),
        name="image_terms",
    )(*coeffs, *texts)


def small_call(kernel, name, out_shape, operands):
    return pl.pallas_call(
        kernel,
        out_shape=out_shape,
        in_specs=[VMEM] * len(operands),
        out_specs=[VMEM] * len(out_shape),
        compiler_params=pltpu.CompilerParams(vmem_limit_bytes=SMALL_VMEM),
        name=name,
    )(*operands)


def join_kernel(near_ref, far_ref, came_ref, near_out, far_out, own, came, code, load_sem, store_sem):
    rows = near_ref.shape[0]
    parts = ((1, far_ref, far_out), (0, near_ref, near_out))
    loads, stores = [], []
    for k, own_ref, out in parts:
        place = pl.ds(k * rows, rows)
        loads.append(pltpu.make_async_copy(came_ref.at[place, :], came.at[place, :], load_sem.at[2 * k]))
        loads.append(pltpu.make_async_copy(own_ref, own.at[place, :], load_sem.at[2 * k + 1]))
        stores.append(pltpu.make_async_copy(code.at[place, :], out, store_sem.at[k]))
    for load in loads:
        load.start()
    for n, (k, _, _) in enumerate(parts):
        loads[2 * n].wait()
        loads[2 * n + 1].wait()
        place = pl.ds(k * rows, rows)
        code[place, :] = encode(own[place, :] + decode(came[place, :]))
        stores[n].start()
    for store in stores:
        store.wait()


def join_cores(near, far, came):
    code = shape_of(*near.shape, jnp.bfloat16)
    return pl.pallas_call(
        join_kernel,
        out_shape=[code, code],
        in_specs=[HBM] * 3,
        out_specs=[HBM] * 2,
        scratch_shapes=[
            pltpu.VMEM(came.shape, jnp.float32),
            pltpu.VMEM(came.shape, jnp.bfloat16),
            pltpu.VMEM(came.shape, jnp.bfloat16),
            pltpu.SemaphoreType.DMA((4,)),
            pltpu.SemaphoreType.DMA((2,)),
        ],
        compiler_params=pltpu.CompilerParams(vmem_limit_bytes=PAIR_VMEM),
        name="join_cores",
    )(near, far, came)


def fold_kernel(rows, own_ref, came_ref, *refs):
    core_ref, (kept, sent) = refs[0] if len(refs) == 3 else None, refs[-2:]
    for first, out in ((PIECE, sent), (0, kept)):
        value = own_ref[first : first + PIECE, :] + decode(came_ref[first : first + PIECE, :])
        if core_ref is not None:
            value = value + decode(core_ref[rows + first : rows + first + PIECE, :])
        out[...] = value if out.dtype == jnp.float32 else encode(value)


def fold(own, came, core=None, core_rows=0):
    depth = own.shape[1]
    return small_call(
        functools.partial(fold_kernel, core_rows),
        "fold",
        [shape_of(PIECE, depth, jnp.float32), shape_of(PIECE, depth, jnp.bfloat16)],
        (own, came) if core is None else (own, came, core),
    )


def add_kernel(own_ref, came_ref, out_ref):
    out_ref[...] = encode(own_ref[...] + decode(came_ref[...]))


def add_codes(own, came):
    return small_call(add_kernel, "add_codes", [shape_of(*own.shape, jnp.bfloat16)], (own, came))[0]


def finish_kernel(raw_ref, own_ref, ring_ref, far_ref, out_ref):
    grad = own_ref[...] + decode(ring_ref[...]) + decode(far_ref[...])
    wide = raw_ref[...].astype(jnp.float32)
    inverse = lax.rsqrt(jnp.sum(wide * wide, axis=1, keepdims=True) + 1e-06)
    unit = wide * inverse
    out_ref[...] = inverse * (grad - unit * jnp.sum(unit * grad, axis=1, keepdims=True))


def finish(raw, own, ring, far):
    return small_call(finish_kernel, "finish", [shape_of(*raw.shape, jnp.float32)], (raw, own, ring, far))[0]


def gather(image, text):
    groups = ((image, IMAGE_PAIRS), (text, TEXT_PAIRS))
    far = [swap(unit, pairs["x"]) for unit, pairs in groups]
    *far, image, text = lax.optimization_barrier((*far, image, text))
    groups = ((image, IMAGE_PAIRS), (text, TEXT_PAIRS))
    far = [jnp.concatenate([part, swap(part, pairs["z"])], axis=0) for part, (_, pairs) in zip(far, groups)]
    near = [jnp.concatenate([unit, swap(unit, pairs["y"])], axis=0) for unit, pairs in groups]
    *far, near[0], near[1] = lax.optimization_barrier((*far, *near))
    far_late = [swap(part, pairs["y"]) for part, (_, pairs) in zip(far, groups)]
    near_late = [swap(part, pairs["z"]) for part, (_, pairs) in zip(near, groups)]
    images, texts = ([near[k], far[k], near_late[k], far_late[k]] for k in range(2))
    late_core = [after(far[1], *near_late, *far_late), *texts[2:]]
    return images, texts + [swap(part, CORE) for part in (near[1], *late_core)]


def after(value, *others):
    return lax.optimization_barrier((value, *others))[0]


def shards(images, texts, logit_scale, bias):
    place = (lax.axis_index("img") * lax.axis_size("txt") + lax.axis_index("txt")).astype(jnp.int32)
    image_all, text_all = gather(*unit_rows(images, texts))
    coeffs, other, loss = logit_terms(place.reshape(1), logit_scale, bias, image_all, text_all)

    other_late = swap(other[1], CORE)
    loss = loss + swap(loss, CORE)
    near_late, far_late = image_terms(4 * PIECE, jnp.bfloat16, coeffs, text_all)
    image_far = swap(far_late, IMAGE_PAIRS["y"])
    image_near = swap(near_late, IMAGE_PAIRS["z"])
    own = text_terms(after(coeffs[0], loss, near_late), image_all)
    loss = loss + swap(loss, IMAGE_PAIRS["x"])
    text_near, text_far = join_cores(own[2], own[3], other_late)
    text_far = swap(text_far, TEXT_PAIRS["y"])
    text_near = swap(text_near, TEXT_PAIRS["z"])
    near_early, far_early = image_terms(0, jnp.float32, (after(coeffs[0], loss), coeffs[1]), text_all)
    loss = loss + swap(loss, TEXT_PAIRS["x"])
    other_early = swap(other[0], CORE)

    image_kept, image_sent = fold(far_early, after(image_far, loss))
    image_far = swap(image_sent, IMAGE_PAIRS["z"])
    text_kept, text_sent = fold(own[1], text_far, other_early, 2 * PIECE)
    text_far = swap(text_sent, TEXT_PAIRS["z"])
    loss = loss + swap(loss, IMAGE_PAIRS["y"])
    image_own, image_sent = fold(near_early, image_near)
    image_near = swap(image_sent, IMAGE_PAIRS["y"])
    text_own, text_sent = fold(own[0], text_near, other_early, 0)
    text_near = swap(text_sent, TEXT_PAIRS["y"])

    loss = loss + swap(loss, TEXT_PAIRS["y"])
    image_sent = add_codes(image_kept, after(image_far, loss))
    text_sent = add_codes(text_kept, text_far)
    loss = loss + swap(loss, IMAGE_PAIRS["z"])
    loss = loss + swap(loss, TEXT_PAIRS["z"])
    count = images.shape[0] * lax.axis_size("img") * lax.axis_size("txt")
    loss = loss[0, :1] / count
    image_grad = finish(images, image_own, after(image_near, loss), swap(image_sent, IMAGE_PAIRS["x"]))
    text_grad = finish(texts, text_own, text_near, swap(text_sent, TEXT_PAIRS["x"]))
    return loss, image_grad, text_grad


def solution(mesh):
    placed = (P(("img", "txt"), None), P(("txt", "img"), None), P(), P())
    return jax.shard_map(
        shards,
        mesh=mesh,
        in_specs=placed,
        out_specs=(P(), P(("img", "txt"), None), P(("txt", "img"), None)),
        check_vma=False,
    )
```

time: 397 us -> 122 us (0.31)
  waiting for transfers between devices: 217 us -> 42.4 us
  blocking collectives: 72.1 us -> 0 us
  matrix products: 71 us -> 0 us
  starting transfers between devices: 0.16 us -> 35.4 us
  Pallas kernels: 0 us -> 34.9 us
  other arithmetic: 12.6 us -> 0.21 us
  between operations: 16.3 us -> 3.95 us
  loops' own time: 5.33 us -> 0 us
    reduce_scatter x2 -> x0, waiting for transfers between devices: 122 us -> none  [the longest x1 106 us: shards(): lax.psum_scatter(text_part, 'img', scatter_dimension=0, tiled=True)]
    all_gather x2 -> x0, waiting for transfers between devices: 94.3 us -> none  [the longest x1 55.4 us: shards(): image_all = lax.all_gather(image_unit, 'txt', axis=0, tiled=True)]
    psum x1 -> x0, blocking collectives: 72.1 us -> none  [shards(): total = lax.psum(loss_part, ('img', 'txt'))]
    dot_general x12 -> x0, matrix products: 71 us -> none  [the longest x4 29.4 us: visit(): jnp.dot(coeff, block, preferred_element_type=jnp.float32)]
    ppermute x0 -> x33, waiting for transfers between devices: none -> 42.4 us  [swap(): lax.ppermute(value, axes, [(k ^ mask, k) for k in range(lax.axis_size(axe...]
    ppermute x0 -> x33, starting transfers between devices: none -> 35.4 us  [swap(): lax.ppermute(value, axes, [(k ^ mask, k) for k in range(lax.axis_size(axe...]
    pallas_call x0 -> x14, Pallas kernels: none -> 34.9 us  [the longest x1 13.1 us: logit_terms(): pl.pallas_call(logit_kernel, out_shape=[coeff, coeff] + [shape_of(2 * row...]
    another operation x1 -> x0, loops' own time: 5.33 us -> none  [pair_terms(): lax.scan(visit, start, (blocks, numbers))]
  transfers between devices with their start and end apart: 4 -> 33, of which waited for: 4 -> 17; matrix products, arithmetic and copies ran while one was open for 2% -> 1% of each run, Pallas kernels for 0% -> 15%
where the time goes in v1:
time: 122 us; the launch traced here: 121 us
  waiting for transfers between devices  42.4 us (35%)
  starting transfers between devices  35.4 us (29%)
  Pallas kernels  34.9 us (29%)
  local copies, waits for them, and re-layouts  4.29 us (4%)
  between operations  3.95 us (3%)
    ppermute x33, waiting for transfers between devices, swap(): lax.ppermute(value, axes, [(k ^ mask, k) for k in range(lax.axis_size(axe...  42.4 us
    ppermute x33, starting transfers between devices, swap(): lax.ppermute(value, axes, [(k ^ mask, k) for k in range(lax.axis_size(axe...  35.4 us
    pallas_call x1, Pallas kernels, logit_terms(): pl.pallas_call(logit_kernel, out_shape=[coeff, coeff] + [shape_of(2 * row...  13.1 us
    pallas_call x2, Pallas kernels, image_terms(): pl.pallas_call(functools.partial(image_kernel, first), out_shape=[shape_o...  9.01 us
    pallas_call x8, Pallas kernels, small_call(): pl.pallas_call(kernel, out_shape=out_shape, in_specs=[VMEM] * len(operand...  5.81 us
    unnamed x16, local copies, waits for them, and re-layouts  3.78 us
    pallas_call x1, Pallas kernels, text_terms(): pl.pallas_call(text_kernel, out_shape=[shape_of(rows, depth, jnp.float32)...  2.93 us
  transfers between devices with their start and end apart: 33, of which 17 were waited for; matrix products, arithmetic and copies ran while one was open for 1% of the time, Pallas kernels for 15%

profile of v1, /device:TPU:0, one launch (start us, length us, event | category | flops | bytes accessed | tf_op | source)
XLA Modules:
  0.0 121.2 jit_solution(8033155504016467426)
XLA Ops:
  0.6 2.0 %unit_rows.1 = (bf16[128,1152]{1,0:T(8,128)(2,1)}, bf16[128,1152]{1,0:T(8,128)(2,1)}) custom-call(bf16[128,1152]{1,0:T(8,128)(2,1)} %raw_ref.2, bf16[128,1152]{1,0:T(8,128)(2,1)} %raw_ref.3), custom_call_target="tpu_custom_call" | custom-call | tf_op jit(solution)/shard_map/unit_rows/pallas_call | solution.py:60
  2.6 1.7 %collective-permute-start = (bf16[128,1152]{1,0:T(8,128)(2,1)}, bf16[128,1152]{1,0:T(8,128)(2,1)S(1)}, u32[]{:S(2)}, u32[]{:S(2)}) collective-permute-start(bf16[128,1152]{1,0:T(8,128)(2,1)} %get-tuple-element.46), channel_id=1, source_target_pairs={{16,0},{17,1},{18,2},{19,3},{20,4},{21,5},{22,6},{23,7},{24,8},{25... | collective-permute-start | bytes 884744 | tf_op jit(solution)/shard_map/ppermute | solution.py:33
  4.3 2.1 %collective-permute-start.1 = (bf16[128,1152]{1,0:T(8,128)(2,1)}, bf16[128,1152]{1,0:T(8,128)(2,1)S(1)}, u32[]{:S(2)}, u32[]{:S(2)}) collective-permute-start(bf16[128,1152]{1,0:T(8,128)(2,1)} %get-tuple-element.47), channel_id=1, source_target_pairs={{20,0},{21,1},{22,2},{23,3},{16,4},{17,5},{18,6},{19,7},{28,8},{29... | collective-permute-start | bytes 884744 | tf_op jit(solution)/shard_map/ppermute | solution.py:33
  6.4 5.1 %collective-permute-done = bf16[128,1152]{1,0:T(8,128)(2,1)S(1)} collective-permute-done((bf16[128,1152]{1,0:T(8,128)(2,1)}, bf16[128,1152]{1,0:T(8,128)(2,1)S(1)}, u32[]{:S(2)}, u32[]{:S(2)}) %collective-permute-start) | collective-permute-done | bytes 294944 | tf_op jit(solution)/shard_map/ppermute | solution.py:33
  11.5 2.7 %collective-permute-done.1 = bf16[128,1152]{1,0:T(8,128)(2,1)S(1)} collective-permute-done((bf16[128,1152]{1,0:T(8,128)(2,1)}, bf16[128,1152]{1,0:T(8,128)(2,1)S(1)}, u32[]{:S(2)}, u32[]{:S(2)}) %collective-permute-start.1) | collective-permute-done | bytes 294944 | tf_op jit(solution)/shard_map/ppermute | solution.py:33
  14.2 1.9 %collective-permute-start.2 = (bf16[128,1152]{1,0:T(8,128)(2,1)S(1)}, bf16[128,1152]{1,0:T(8,128)(2,1)S(1)}, u32[]{:S(2)}, u32[]{:S(2)}) collective-permute-start(bf16[128,1152]{1,0:T(8,128)(2,1)S(1)} %collective-permute-done), channel_id=1, source_target_pairs={{32,0},{33,1},{34,2},{35,3},{36,4},{37,5},{38,6},{39,7},{40,8},{41... | collective-permute-start | bytes 884744 | tf_op jit(solution)/shard_map/ppermute | solution.py:33
  16.1 2.5 %collective-permute-start.3 = (bf16[128,1152]{1,0:T(8,128)(2,1)S(1)}, bf16[128,1152]{1,0:T(8,128)(2,1)S(1)}, u32[]{:S(2)}, u32[]{:S(2)}) collective-permute-start(bf16[128,1152]{1,0:T(8,128)(2,1)S(1)} %collective-permute-done.1), channel_id=1, source_target_pairs={{96,0},{97,1},{98,2},{99,3},{100,4},{101,5},{102,6},{103,7},{104,8... | collective-permute-start | bytes 884744 | tf_op jit(solution)/shard_map/ppermute | solution.py:33
  18.6 1.6 %collective-permute-start.4 = (bf16[128,1152]{1,0:T(8,128)(2,1)}, bf16[128,1152]{1,0:T(8,128)(2,1)S(1)}, u32[]{:S(2)}, u32[]{:S(2)}) collective-permute-start(bf16[128,1152]{1,0:T(8,128)(2,1)} %get-tuple-element.46), channel_id=1, source_target_pairs={{1,0},{0,1},{3,2},{2,3},{5,4},{4,5},{7,6},{6,7},{9,8},{8,9},{11,10... | collective-permute-start | bytes 884744 | tf_op jit(solution)/shard_map/ppermute | solution.py:33
  20.2 2.2 %collective-permute-start.5 = (bf16[128,1152]{1,0:T(8,128)(2,1)}, bf16[128,1152]{1,0:T(8,128)(2,1)S(1)}, u32[]{:S(2)}, u32[]{:S(2)}) collective-permute-start(bf16[128,1152]{1,0:T(8,128)(2,1)} %get-tuple-element.47), channel_id=1, source_target_pairs={{3,0},{2,1},{1,2},{0,3},{7,4},{6,5},{5,6},{4,7},{11,8},{10,9},{9,1... | collective-permute-start | bytes 884744 | tf_op jit(solution)/shard_map/ppermute | solution.py:33
  22.4 2.1 %collective-permute-done.3 = bf16[128,1152]{1,0:T(8,128)(2,1)S(1)} collective-permute-done((bf16[128,1152]{1,0:T(8,128)(2,1)S(1)}, bf16[128,1152]{1,0:T(8,128)(2,1)S(1)}, u32[]{:S(2)}, u32[]{:S(2)}) %collective-permute-start.3) | collective-permute-done | bytes 294944 | tf_op jit(solution)/shard_map/ppermute | solution.py:33
  24.6 1.2 collective-permute-done.4
  25.9 2.5 %collective-permute-done.5 = bf16[128,1152]{1,0:T(8,128)(2,1)S(1)} collective-permute-done((bf16[128,1152]{1,0:T(8,128)(2,1)}, bf16[128,1152]{1,0:T(8,128)(2,1)S(1)}, u32[]{:S(2)}, u32[]{:S(2)}) %collective-permute-start.5) | collective-permute-done | bytes 294944 | tf_op jit(solution)/shard_map/ppermute | solution.py:33
  28.4 1.1 collective-permute-start.6
  29.5 0.9 collective-permute-start.8
  30.4 2.3 %collective-permute-start.9 = (bf16[256,1152]{1,0:T(8,128)(2,1)S(1)}, bf16[256,1152]{1,0:T(8,128)(2,1)S(1)}, u32[]{:S(2)}, u32[]{:S(2)}) collective-permute-start(bf16[256,1152]{1,0:T(8,128)(2,1)S(1)} %pad_maximum_fusion.1.refs_5_.refs_1_), channel_id=1, source_target_pairs={{3,0},{2,1},{1,2},{0,3},{7,4},{6,5},{5,6},{4,7},{11,8},{10,9},{9,1... | collective-permute-start | bytes 1769480 | tf_op jit(solution)/shard_map/ppermute | solution.py:33
  32.6 7.7 %collective-permute-done.6.refs_2_ = bf16[256,1152]{1,0:T(8,128)(2,1)S(1)} collective-permute-done((bf16[256,1152]{1,0:T(8,128)(2,1)S(1)}, bf16[256,1152]{1,0:T(8,128)(2,1)S(1)}, u32[]{:S(2)}, u32[]{:S(2)}) %collective-permute-start.6) | collective-permute-done | bytes 589856 | tf_op jit(solution)/shard_map/ppermute | solution.py:33
  40.4 0.8 copy-done.2
  41.2 0.8 copy-done.4
  42.0 0.4 collective-permute-done.8.refs_6_.refs_2_
  42.4 1.0 collective-permute-done.9.refs_7_.refs_3_
  43.4 0.5 collective-permute-start.11
  45.2 0.3 collective-permute-done.12.refs_10_.refs_6_
  45.6 0.8 collective-permute-done.11.refs_9_.refs_5_
  46.4 0.8 collective-permute-done.13.refs_11_.refs_7_
  47.2 1.1 copy-done.3
  48.3 1.1 copy-done.5
  49.4 13.1 %logit_terms.1 = (bf16[1024,1024]{1,0:T(8,128)(2,1)S(1)}, bf16[1024,1024]{1,0:T(8,128)(2,1)S(1)}, bf16[512,1152]{1,0:T(8,128)(2,1)S(1)}, bf16[512,1152]{1,0:T(8,128)(2,1)S(1)}, f32[8,128]{1,0:T(8,128)S(1)}) custom-call(s32[1]{0:T(128)} %bitcast.place_ref, f32[1]{0:T(128)S(6)} %copy.7.scale_ref, f32[1]{0:T(128)S(6)} %copy.8.bias_ref, ...), custom_call_target="tpu_custom_call" | custom-call | flops 7247757312 | bytes 8388608 | tf_op jit(solution)/shard_map/logit_terms/pallas_call | solution.py:145
  62.4 0.2 collective-permute-start.26
  62.7 0.4 collective-permute-start.28
  63.0 0.1 collective-permute-start.14
  63.2 4.5 %image_terms.3 = (bf16[256,1152]{1,0:T(8,128)(2,1)S(1)}, bf16[256,1152]{1,0:T(8,128)(2,1)S(1)}) custom-call(bf16[1024,1024]{1,0:T(8,128)(2,1)S(1)} %get-tuple-element.68.own_ref.coeff_ref, bf16[1024,1024]{1,0:T(8,128)(2,1)S(1)} %get-tuple-element.56.other_ref, bf16[256,1152]{1,0:T(8,128)(2,1)S(1)} %pad_maximum_fusion.3.refs_4_.refs_0_, ...), custom_call_target="tpu_custom_call" | custom-call | flops 2415919104 | bytes 8388608 | tf_op jit(solution)/shard_map/image_terms/pallas_call | solution.py:200
  67.7 0.7 collective-permute-start.23
  68.4 2.9 %text_terms.1 = (f32[256,1152]{1,0:T(8,128)S(1)}, f32[256,1152]{1,0:T(8,128)S(1)}, f32[256,1152]{1,0:T(8,128)S(1)}, f32[256,1152]{1,0:T(8,128)S(1)}) custom-call(bf16[1024,1024]{1,0:T(8,128)(2,1)S(1)} %get-tuple-element.68.own_ref.coeff_ref, bf16[256,1152]{1,0:T(8,128)(2,1)S(1)} %pad_maximum_fusion.2.refs_0_, bf16[256,1152]{1,0:T(8,128)(2,1)S(1)} %pad_maximum_fusion.refs_1_, ...), custom_call_target="tpu_custom_call" | custom-call | flops 2415919104 | bytes 8388608 | tf_op jit(solution)/shard_map/text_terms/pallas_call | solution.py:172
  71.4 2.1 %join_cores.1 = (bf16[256,1152]{1,0:T(8,128)(2,1)S(1)}, bf16[256,1152]{1,0:T(8,128)(2,1)S(1)}) custom-call(f32[256,1152]{1,0:T(8,128)S(1)} %get-tuple-element.70.near_ref, f32[256,1152]{1,0:T(8,128)S(1)} %get-tuple-element.71.far_ref, bf16[512,1152]{1,0:T(8,128)(2,1)S(1)} %collective-permute-done.26.came_ref), custom_call_target="tpu_custom_call" | custom-call | tf_op jit(solution)/shard_map/join_cores/pallas_call | solution.py:245
  73.5 2.3 %collective-permute-start.30 = (bf16[256,1152]{1,0:T(8,128)(2,1)S(1)}, bf16[256,1152]{1,0:T(8,128)(2,1)S(1)}, u32[]{:S(2)}, u32[]{:S(2)}) collective-permute-start(bf16[256,1152]{1,0:T(8,128)(2,1)S(1)} %get-tuple-element.78), channel_id=1, source_target_pairs={{3,0},{2,1},{1,2},{0,3},{7,4},{6,5},{5,6},{4,7},{11,8},{10,9},{9,1... | collective-permute-start | bytes 1769480 | tf_op jit(solution)/shard_map/ppermute | solution.py:33
  75.7 0.6 collective-permute-start.15
  76.3 3.0 %collective-permute-done.15 = f32[8,128]{1,0:T(8,128)S(1)} collective-permute-done((f32[8,128]{1,0:T(8,128)S(1)}, f32[8,128]{1,0:T(8,128)S(1)}, u32[]{:S(2)}, u32[]{:S(2)}) %collective-permute-start.15) | collective-permute-done | bytes 4128 | tf_op jit(solution)/shard_map/ppermute | solution.py:33
  79.3 2.1 %collective-permute-start.16 = (f32[8,128]{1,0:T(8,128)S(1)}, f32[8,128]{1,0:T(8,128)S(1)}, u32[]{:S(2)}, u32[]{:S(2)}) collective-permute-start(f32[8,128]{1,0:T(8,128)S(1)} %add.26), channel_id=1, source_target_pairs={{20,0},{21,1},{22,2},{23,3},{16,4},{17,5},{18,6},{19,7},{28,8},{29... | collective-permute-start | bytes 12296 | tf_op jit(solution)/shard_map/ppermute | solution.py:33
  81.4 0.1 collective-permute-start.21
  81.5 2.6 %collective-permute-done.16 = f32[8,128]{1,0:T(8,128)S(1)} collective-permute-done((f32[8,128]{1,0:T(8,128)S(1)}, f32[8,128]{1,0:T(8,128)S(1)}, u32[]{:S(2)}, u32[]{:S(2)}) %collective-permute-start.16) | collective-permute-done | bytes 4128 | tf_op jit(solution)/shard_map/ppermute | solution.py:33
  84.2 1.7 %collective-permute-start.27 = (bf16[256,1152]{1,0:T(8,128)(2,1)S(1)}, bf16[256,1152]{1,0:T(8,128)(2,1)S(1)}, u32[]{:S(2)}, u32[]{:S(2)}) collective-permute-start(bf16[256,1152]{1,0:T(8,128)(2,1)S(1)} %get-tuple-element.73), channel_id=1, source_target_pairs={{96,0},{97,1},{98,2},{99,3},{100,4},{101,5},{102,6},{103,7},{104,8... | collective-permute-start | bytes 1769480 | tf_op jit(solution)/shard_map/ppermute | solution.py:33
  85.9 4.5 %image_terms.2 = (f32[256,1152]{1,0:T(8,128)S(1)}, f32[256,1152]{1,0:T(8,128)S(1)}) custom-call(bf16[1024,1024]{1,0:T(8,128)(2,1)S(1)} %get-tuple-element.68.own_ref.coeff_ref, bf16[1024,1024]{1,0:T(8,128)(2,1)S(1)} %get-tuple-element.56.other_ref, bf16[256,1152]{1,0:T(8,128)(2,1)S(1)} %pad_maximum_fusion.3.refs_4_.refs_0_, ...), custom_call_target="tpu_custom_call" | custom-call | flops 2415919104 | bytes 8388608 | tf_op jit(solution)/shard_map/image_terms/pallas_call | solution.py:200
  90.4 0.4 fold.5
  90.9 0.2 collective-permute-start.24
  91.0 0.8 fold.7
  91.8 1.5 %collective-permute-start.31 = (bf16[128,1152]{1,0:T(8,128)(2,1)S(1)}, bf16[128,1152]{1,0:T(8,128)(2,1)S(1)}, u32[]{:S(2)}, u32[]{:S(2)}) collective-permute-start(bf16[128,1152]{1,0:T(8,128)(2,1)S(1)} %get-tuple-element.80), channel_id=1, source_target_pairs={{96,0},{97,1},{98,2},{99,3},{100,4},{101,5},{102,6},{103,7},{104,8... | collective-permute-start | bytes 884744 | tf_op jit(solution)/shard_map/ppermute | solution.py:33
  93.3 0.8 collective-permute-start.17
  94.1 2.8 %collective-permute-done.17 = f32[8,128]{1,0:T(8,128)S(1)} collective-permute-done((f32[8,128]{1,0:T(8,128)S(1)}, f32[8,128]{1,0:T(8,128)S(1)}, u32[]{:S(2)}, u32[]{:S(2)}) %collective-permute-start.17) | collective-permute-done | bytes 4128 | tf_op jit(solution)/shard_map/ppermute | solution.py:33
  97.0 1.5 %collective-permute-start.18 = (f32[8,128]{1,0:T(8,128)S(1)}, f32[8,128]{1,0:T(8,128)S(1)}, u32[]{:S(2)}, u32[]{:S(2)}) collective-permute-start(f32[8,128]{1,0:T(8,128)S(1)} %add.28), channel_id=1, source_target_pairs={{3,0},{2,1},{1,2},{0,3},{7,4},{6,5},{5,6},{4,7},{11,8},{10,9},{9,1... | collective-permute-start | bytes 12296 | tf_op jit(solution)/shard_map/ppermute | solution.py:33
  98.5 3.3 %collective-permute-done.18 = f32[8,128]{1,0:T(8,128)S(1)} collective-permute-done((f32[8,128]{1,0:T(8,128)S(1)}, f32[8,128]{1,0:T(8,128)S(1)}, u32[]{:S(2)}, u32[]{:S(2)}) %collective-permute-start.18) | collective-permute-done | bytes 4128 | tf_op jit(solution)/shard_map/ppermute | solution.py:33
  101.8 0.4 fold.4
  102.2 0.1 collective-permute-start.22
  102.3 0.3 add_codes.2
  102.7 0.8 fold.6
  103.5 2.2 %collective-permute-start.29 = (bf16[128,1152]{1,0:T(8,128)(2,1)S(1)}, bf16[128,1152]{1,0:T(8,128)(2,1)S(1)}, u32[]{:S(2)}, u32[]{:S(2)}) collective-permute-start(bf16[128,1152]{1,0:T(8,128)(2,1)S(1)} %get-tuple-element.76), channel_id=1, source_target_pairs={{3,0},{2,1},{1,2},{0,3},{7,4},{6,5},{5,6},{4,7},{11,8},{10,9},{9,1... | collective-permute-start | bytes 884744 | tf_op jit(solution)/shard_map/ppermute | solution.py:33
  105.7 0.3 add_codes.3
  106.0 1.6 %collective-permute-start.32 = (bf16[128,1152]{1,0:T(8,128)(2,1)S(1)}, bf16[128,1152]{1,0:T(8,128)(2,1)S(1)}, u32[]{:S(2)}, u32[]{:S(2)}) collective-permute-start(bf16[128,1152]{1,0:T(8,128)(2,1)S(1)} %add_codes.3), channel_id=1, source_target_pairs={{20,0},{21,1},{22,2},{23,3},{16,4},{17,5},{18,6},{19,7},{28,8},{29... | collective-permute-start | bytes 884744 | tf_op jit(solution)/shard_map/ppermute | solution.py:33
  107.6 0.9 collective-permute-start.19
  108.5 2.7 %collective-permute-done.19 = f32[8,128]{1,0:T(8,128)S(1)} collective-permute-done((f32[8,128]{1,0:T(8,128)S(1)}, f32[8,128]{1,0:T(8,128)S(1)}, u32[]{:S(2)}, u32[]{:S(2)}) %collective-permute-start.19) | collective-permute-done | bytes 4128 | tf_op jit(solution)/shard_map/ppermute | solution.py:33
  111.2 1.6 %collective-permute-start.20 = (f32[8,128]{1,0:T(8,128)S(1)}, f32[8,128]{1,0:T(8,128)S(1)}, u32[]{:S(2)}, u32[]{:S(2)}) collective-permute-start(f32[8,128]{1,0:T(8,128)S(1)} %add.30), channel_id=1, source_target_pairs={{96,0},{97,1},{98,2},{99,3},{100,4},{101,5},{102,6},{103,7},{104,8... | collective-permute-start | bytes 12296 | tf_op jit(solution)/shard_map/ppermute | solution.py:33
  112.8 3.2 %collective-permute-done.20 = f32[8,128]{1,0:T(8,128)S(1)} collective-permute-done((f32[8,128]{1,0:T(8,128)S(1)}, f32[8,128]{1,0:T(8,128)S(1)}, u32[]{:S(2)}, u32[]{:S(2)}) %collective-permute-start.20) | collective-permute-done | bytes 4128 | tf_op jit(solution)/shard_map/ppermute | solution.py:33
  116.0 0.5 slice.3
  117.2 1.4 %finish.2 = f32[128,1152]{1,0:T(8,128)} custom-call(bf16[128,1152]{1,0:T(8,128)(2,1)S(1)} %copy-done, f32[128,1152]{1,0:T(8,128)S(1)} %get-tuple-element.59.own_ref, bf16[128,1152]{1,0:T(8,128)(2,1)S(1)} %collective-permute-done.22.ring_ref, bf16[128,1152]{1,0:T(8,128)(2,1)S(1)} %collective-permute-done.25.far_ref), custom_call_target="tpu_custom_call" | custom-call | tf_op jit(solution)/shard_map/finish/pallas_call | solution.py:212
  118.6 1.4 %finish.3 = f32[128,1152]{1,0:T(8,128)} custom-call(bf16[128,1152]{1,0:T(8,128)(2,1)S(1)} %copy-done.1, f32[128,1152]{1,0:T(8,128)S(1)} %get-tuple-element.75.own_ref, bf16[128,1152]{1,0:T(8,128)(2,1)S(1)} %collective-permute-done.29.ring_ref, bf16[128,1152]{1,0:T(8,128)(2,1)S(1)} %collective-permute-done.32.far_ref), custom_call_target="tpu_custom_call" | custom-call | tf_op jit(solution)/shard_map/finish/pallas_call | solution.py:212
  (44 shorter events, 0.4 us)
Async XLA Ops:
  2.6 8.9 %collective-permute-start = (bf16[128,1152]{1,0:T(8,128)(2,1)}, bf16[128,1152]{1,0:T(8,128)(2,1)S(1)}, u32[]{:S(2)}, u32[]{:S(2)}) collective-permute-start(bf16[128,1152]{1,0:T(8,128)(2,1)} %get-tuple-element.46), channel_id=1, source_target_pairs={{16,0},{17,1},{18,2},{19,3},{20,4},{21,5},{22,6},{23,7},{24,8},{25... | collective-permute-start | bytes 884744 | tf_op jit(solution)/shard_map/ppermute | solution.py:33
  4.3 21.5 %copy-start.7 = (bf16[128,1152]{1,0:T(8,128)(2,1)S(1)}, bf16[128,1152]{1,0:T(8,128)(2,1)}, u32[]{:S(2)}) copy-start(bf16[128,1152]{1,0:T(8,128)(2,1)} %get-tuple-element.46) | copy-start | bytes 884740
  4.3 9.9 %collective-permute-start.1 = (bf16[128,1152]{1,0:T(8,128)(2,1)}, bf16[128,1152]{1,0:T(8,128)(2,1)S(1)}, u32[]{:S(2)}, u32[]{:S(2)}) collective-permute-start(bf16[128,1152]{1,0:T(8,128)(2,1)} %get-tuple-element.47), channel_id=1, source_target_pairs={{20,0},{21,1},{22,2},{23,3},{16,4},{17,5},{18,6},{19,7},{28,8},{29... | collective-permute-start | bytes 884744 | tf_op jit(solution)/shard_map/ppermute | solution.py:33
  14.2 8.2 %collective-permute-start.2 = (bf16[128,1152]{1,0:T(8,128)(2,1)S(1)}, bf16[128,1152]{1,0:T(8,128)(2,1)S(1)}, u32[]{:S(2)}, u32[]{:S(2)}) collective-permute-start(bf16[128,1152]{1,0:T(8,128)(2,1)S(1)} %collective-permute-done), channel_id=1, source_target_pairs={{32,0},{33,1},{34,2},{35,3},{36,4},{37,5},{38,6},{39,7},{40,8},{41... | collective-permute-start | bytes 884744 | tf_op jit(solution)/shard_map/ppermute | solution.py:33
  16.1 8.5 %collective-permute-start.3 = (bf16[128,1152]{1,0:T(8,128)(2,1)S(1)}, bf16[128,1152]{1,0:T(8,128)(2,1)S(1)}, u32[]{:S(2)}, u32[]{:S(2)}) collective-permute-start(bf16[128,1152]{1,0:T(8,128)(2,1)S(1)} %collective-permute-done.1), channel_id=1, source_target_pairs={{96,0},{97,1},{98,2},{99,3},{100,4},{101,5},{102,6},{103,7},{104,8... | collective-permute-start | bytes 884744 | tf_op jit(solution)/shard_map/ppermute | solution.py:33
  18.6 7.2 %collective-permute-start.4 = (bf16[128,1152]{1,0:T(8,128)(2,1)}, bf16[128,1152]{1,0:T(8,128)(2,1)S(1)}, u32[]{:S(2)}, u32[]{:S(2)}) collective-permute-start(bf16[128,1152]{1,0:T(8,128)(2,1)} %get-tuple-element.46), channel_id=1, source_target_pairs={{1,0},{0,1},{3,2},{2,3},{5,4},{4,5},{7,6},{6,7},{9,8},{8,9},{11,10... | collective-permute-start | bytes 884744 | tf_op jit(solution)/shard_map/ppermute | solution.py:33
  20.2 8.1 %collective-permute-start.5 = (bf16[128,1152]{1,0:T(8,128)(2,1)}, bf16[128,1152]{1,0:T(8,128)(2,1)S(1)}, u32[]{:S(2)}, u32[]{:S(2)}) collective-permute-start(bf16[128,1152]{1,0:T(8,128)(2,1)} %get-tuple-element.47), channel_id=1, source_target_pairs={{3,0},{2,1},{1,2},{0,3},{7,4},{6,5},{5,6},{4,7},{11,8},{10,9},{9,1... | collective-permute-start | bytes 884744 | tf_op jit(solution)/shard_map/ppermute | solution.py:33
  22.4 5.9 %copy-start.6 = (bf16[128,1152]{1,0:T(8,128)(2,1)S(1)}, bf16[128,1152]{1,0:T(8,128)(2,1)}, u32[]{:S(2)}) copy-start(bf16[128,1152]{1,0:T(8,128)(2,1)} %get-tuple-element.47) | copy-start | bytes 884740
  28.4 12.0 %collective-permute-start.6 = (bf16[256,1152]{1,0:T(8,128)(2,1)S(1)}, bf16[256,1152]{1,0:T(8,128)(2,1)S(1)}, u32[]{:S(2)}, u32[]{:S(2)}) collective-permute-start(bf16[256,1152]{1,0:T(8,128)(2,1)S(1)} %pad_maximum_fusion.2.refs_0_), channel_id=1, source_target_pairs={{32,0},{33,1},{34,2},{35,3},{36,4},{37,5},{38,6},{39,7},{40,8},{41... | collective-permute-start | bytes 1769480 | tf_op jit(solution)/shard_map/ppermute | solution.py:33
  29.5 11.7 %collective-permute-start.7 = (bf16[256,1152]{1,0:T(8,128)(2,1)S(1)}, bf16[256,1152]{1,0:T(8,128)(2,1)S(1)}, u32[]{:S(2)}, u32[]{:S(2)}) collective-permute-start(bf16[256,1152]{1,0:T(8,128)(2,1)S(1)} %pad_maximum_fusion.refs_1_), channel_id=1, source_target_pairs={{1,0},{0,1},{3,2},{2,3},{5,4},{4,5},{7,6},{6,7},{9,8},{8,9},{11,10... | collective-permute-start | bytes 1769480 | tf_op jit(solution)/shard_map/ppermute | solution.py:33
  29.5 12.9 %collective-permute-start.8 = (bf16[256,1152]{1,0:T(8,128)(2,1)S(1)}, bf16[256,1152]{1,0:T(8,128)(2,1)S(1)}, u32[]{:S(2)}, u32[]{:S(2)}) collective-permute-start(bf16[256,1152]{1,0:T(8,128)(2,1)S(1)} %pad_maximum_fusion.3.refs_4_.refs_0_), channel_id=1, source_target_pairs={{96,0},{97,1},{98,2},{99,3},{100,4},{101,5},{102,6},{103,7},{104,8... | collective-permute-start | bytes 1769480 | tf_op jit(solution)/shard_map/ppermute | solution.py:33
  30.4 13.0 %collective-permute-start.9 = (bf16[256,1152]{1,0:T(8,128)(2,1)S(1)}, bf16[256,1152]{1,0:T(8,128)(2,1)S(1)}, u32[]{:S(2)}, u32[]{:S(2)}) collective-permute-start(bf16[256,1152]{1,0:T(8,128)(2,1)S(1)} %pad_maximum_fusion.1.refs_5_.refs_1_), channel_id=1, source_target_pairs={{3,0},{2,1},{1,2},{0,3},{7,4},{6,5},{5,6},{4,7},{11,8},{10,9},{9,1... | collective-permute-start | bytes 1769480 | tf_op jit(solution)/shard_map/ppermute | solution.py:33
  32.6 12.6 %collective-permute-start.10 = (bf16[256,1152]{1,0:T(8,128)(2,1)S(1)}, bf16[256,1152]{1,0:T(8,128)(2,1)}, u32[]{:S(2)}, u32[]{:S(2)}) collective-permute-start(bf16[256,1152]{1,0:T(8,128)(2,1)S(1)} %pad_maximum_fusion.3.refs_4_.refs_0_), channel_id=1, source_target_pairs={{8,0},{9,1},{10,2},{11,3},{12,4},{13,5},{14,6},{15,7},{0,8},{1,9},... | collective-permute-start | bytes 1769480 | tf_op jit(solution)/shard_map/ppermute | solution.py:33
  40.4 0.8 copy-start.2
  41.2 0.8 copy-start.4
  43.4 2.1 %collective-permute-start.12 = (bf16[256,1152]{1,0:T(8,128)(2,1)S(1)}, bf16[256,1152]{1,0:T(8,128)(2,1)}, u32[]{:S(2)}, u32[]{:S(2)}) collective-permute-start(bf16[256,1152]{1,0:T(8,128)(2,1)S(1)} %collective-permute-done.8.refs_6_.refs_2_), channel_id=1, source_target_pairs={{8,0},{9,1},{10,2},{11,3},{12,4},{13,5},{14,6},{15,7},{0,8},{1,9},... | collective-permute-start | bytes 1769480 | tf_op jit(solution)/shard_map/ppermute | solution.py:33
  43.4 3.0 %collective-permute-start.11 = (bf16[256,1152]{1,0:T(8,128)(2,1)S(1)}, bf16[256,1152]{1,0:T(8,128)(2,1)}, u32[]{:S(2)}, u32[]{:S(2)}) collective-permute-start(bf16[256,1152]{1,0:T(8,128)(2,1)S(1)} %pad_maximum_fusion.1.refs_5_.refs_1_), channel_id=1, source_target_pairs={{8,0},{9,1},{10,2},{11,3},{12,4},{13,5},{14,6},{15,7},{0,8},{1,9},... | collective-permute-start | bytes 1769480 | tf_op jit(solution)/shard_map/ppermute | solution.py:33
  43.9 3.3 %collective-permute-start.13 = (bf16[256,1152]{1,0:T(8,128)(2,1)S(1)}, bf16[256,1152]{1,0:T(8,128)(2,1)}, u32[]{:S(2)}, u32[]{:S(2)}) collective-permute-start(bf16[256,1152]{1,0:T(8,128)(2,1)S(1)} %collective-permute-done.9.refs_7_.refs_3_), channel_id=1, source_target_pairs={{8,0},{9,1},{10,2},{11,3},{12,4},{13,5},{14,6},{15,7},{0,8},{1,9},... | collective-permute-start | bytes 1769480 | tf_op jit(solution)/shard_map/ppermute | solution.py:33
  47.2 1.1 copy-start.3
  48.3 1.1 copy-start.5
  62.4 8.9 %collective-permute-start.26 = (bf16[512,1152]{1,0:T(8,128)(2,1)S(1)}, bf16[512,1152]{1,0:T(8,128)(2,1)S(1)}, u32[]{:S(2)}, u32[]{:S(2)}) collective-permute-start(bf16[512,1152]{1,0:T(8,128)(2,1)S(1)} %get-tuple-element.72), channel_id=1, source_target_pairs={{8,0},{9,1},{10,2},{11,3},{12,4},{13,5},{14,6},{15,7},{0,8},{1,9},... | collective-permute-start | bytes 3538952 | tf_op jit(solution)/shard_map/ppermute | solution.py:33
  62.7 28.4 %collective-permute-start.28 = (bf16[512,1152]{1,0:T(8,128)(2,1)S(1)}, bf16[512,1152]{1,0:T(8,128)(2,1)S(1)}, u32[]{:S(2)}, u32[]{:S(2)}) collective-permute-start(bf16[512,1152]{1,0:T(8,128)(2,1)S(1)} %get-tuple-element.74), channel_id=1, source_target_pairs={{8,0},{9,1},{10,2},{11,3},{12,4},{13,5},{14,6},{15,7},{0,8},{1,9},... | collective-permute-start | bytes 3538952 | tf_op jit(solution)/shard_map/ppermute | solution.py:33
  63.0 5.4 %collective-permute-start.14 = (f32[8,128]{1,0:T(8,128)S(1)}, f32[8,128]{1,0:T(8,128)S(1)}, u32[]{:S(2)}, u32[]{:S(2)}) collective-permute-start(f32[8,128]{1,0:T(8,128)S(1)} %get-tuple-element.53), channel_id=1, source_target_pairs={{8,0},{9,1},{10,2},{11,3},{12,4},{13,5},{14,6},{15,7},{0,8},{1,9},... | collective-permute-start | bytes 12296 | tf_op jit(solution)/shard_map/ppermute | solution.py:33
  67.7 22.7 %collective-permute-start.23 = (bf16[256,1152]{1,0:T(8,128)(2,1)S(1)}, bf16[256,1152]{1,0:T(8,128)(2,1)S(1)}, u32[]{:S(2)}, u32[]{:S(2)}) collective-permute-start(bf16[256,1152]{1,0:T(8,128)(2,1)S(1)} %get-tuple-element.63), channel_id=1, source_target_pairs={{1,0},{0,1},{3,2},{2,3},{5,4},{4,5},{7,6},{6,7},{9,8},{8,9},{11,10... | collective-permute-start | bytes 1769480 | tf_op jit(solution)/shard_map/ppermute | solution.py:33
  73.5 17.6 %collective-permute-start.30 = (bf16[256,1152]{1,0:T(8,128)(2,1)S(1)}, bf16[256,1152]{1,0:T(8,128)(2,1)S(1)}, u32[]{:S(2)}, u32[]{:S(2)}) collective-permute-start(bf16[256,1152]{1,0:T(8,128)(2,1)S(1)} %get-tuple-element.78), channel_id=1, source_target_pairs={{3,0},{2,1},{1,2},{0,3},{7,4},{6,5},{5,6},{4,7},{11,8},{10,9},{9,1... | collective-permute-start | bytes 1769480 | tf_op jit(solution)/shard_map/ppermute | solution.py:33
  75.7 3.6 %collective-permute-start.15 = (f32[8,128]{1,0:T(8,128)S(1)}, f32[8,128]{1,0:T(8,128)S(1)}, u32[]{:S(2)}, u32[]{:S(2)}) collective-permute-start(f32[8,128]{1,0:T(8,128)S(1)} %add.25), channel_id=1, source_target_pairs={{16,0},{17,1},{18,2},{19,3},{20,4},{21,5},{22,6},{23,7},{24,8},{25... | collective-permute-start | bytes 12296 | tf_op jit(solution)/shard_map/ppermute | solution.py:33
  79.3 4.8 %collective-permute-start.16 = (f32[8,128]{1,0:T(8,128)S(1)}, f32[8,128]{1,0:T(8,128)S(1)}, u32[]{:S(2)}, u32[]{:S(2)}) collective-permute-start(f32[8,128]{1,0:T(8,128)S(1)} %add.26), channel_id=1, source_target_pairs={{20,0},{21,1},{22,2},{23,3},{16,4},{17,5},{18,6},{19,7},{28,8},{29... | collective-permute-start | bytes 12296 | tf_op jit(solution)/shard_map/ppermute | solution.py:33
  81.4 20.3 %collective-permute-start.21 = (bf16[256,1152]{1,0:T(8,128)(2,1)S(1)}, bf16[256,1152]{1,0:T(8,128)(2,1)S(1)}, u32[]{:S(2)}, u32[]{:S(2)}) collective-permute-start(bf16[256,1152]{1,0:T(8,128)(2,1)S(1)} %get-tuple-element.58), channel_id=1, source_target_pairs={{32,0},{33,1},{34,2},{35,3},{36,4},{37,5},{38,6},{39,7},{40,8},{41... | collective-permute-start | bytes 1769480 | tf_op jit(solution)/shard_map/ppermute | solution.py:33
  84.2 18.5 %collective-permute-start.27 = (bf16[256,1152]{1,0:T(8,128)(2,1)S(1)}, bf16[256,1152]{1,0:T(8,128)(2,1)S(1)}, u32[]{:S(2)}, u32[]{:S(2)}) collective-permute-start(bf16[256,1152]{1,0:T(8,128)(2,1)S(1)} %get-tuple-element.73), channel_id=1, source_target_pairs={{96,0},{97,1},{98,2},{99,3},{100,4},{101,5},{102,6},{103,7},{104,8... | collective-permute-start | bytes 1769480 | tf_op jit(solution)/shard_map/ppermute | solution.py:33
  90.9 11.5 %collective-permute-start.24 = (bf16[128,1152]{1,0:T(8,128)(2,1)S(1)}, bf16[128,1152]{1,0:T(8,128)(2,1)S(1)}, u32[]{:S(2)}, u32[]{:S(2)}) collective-permute-start(bf16[128,1152]{1,0:T(8,128)(2,1)S(1)} %get-tuple-element.66), channel_id=1, source_target_pairs={{32,0},{33,1},{34,2},{35,3},{36,4},{37,5},{38,6},{39,7},{40,8},{41... | collective-permute-start | bytes 884744 | tf_op jit(solution)/shard_map/ppermute | solution.py:33
  91.8 13.8 %collective-permute-start.31 = (bf16[128,1152]{1,0:T(8,128)(2,1)S(1)}, bf16[128,1152]{1,0:T(8,128)(2,1)S(1)}, u32[]{:S(2)}, u32[]{:S(2)}) collective-permute-start(bf16[128,1152]{1,0:T(8,128)(2,1)S(1)} %get-tuple-element.80), channel_id=1, source_target_pairs={{96,0},{97,1},{98,2},{99,3},{100,4},{101,5},{102,6},{103,7},{104,8... | collective-permute-start | bytes 884744 | tf_op jit(solution)/shard_map/ppermute | solution.py:33
  93.3 3.6 %collective-permute-start.17 = (f32[8,128]{1,0:T(8,128)S(1)}, f32[8,128]{1,0:T(8,128)S(1)}, u32[]{:S(2)}, u32[]{:S(2)}) collective-permute-start(f32[8,128]{1,0:T(8,128)S(1)} %add.27), channel_id=1, source_target_pairs={{1,0},{0,1},{3,2},{2,3},{5,4},{4,5},{7,6},{6,7},{9,8},{8,9},{11,10... | collective-permute-start | bytes 12296 | tf_op jit(solution)/shard_map/ppermute | solution.py:33
  97.0 4.8 %collective-permute-start.18 = (f32[8,128]{1,0:T(8,128)S(1)}, f32[8,128]{1,0:T(8,128)S(1)}, u32[]{:S(2)}, u32[]{:S(2)}) collective-permute-start(f32[8,128]{1,0:T(8,128)S(1)} %add.28), channel_id=1, source_target_pairs={{3,0},{2,1},{1,2},{0,3},{7,4},{6,5},{5,6},{4,7},{11,8},{10,9},{9,1... | collective-permute-start | bytes 12296 | tf_op jit(solution)/shard_map/ppermute | solution.py:33
  102.2 15.0 %collective-permute-start.22 = (bf16[128,1152]{1,0:T(8,128)(2,1)S(1)}, bf16[128,1152]{1,0:T(8,128)(2,1)S(1)}, u32[]{:S(2)}, u32[]{:S(2)}) collective-permute-start(bf16[128,1152]{1,0:T(8,128)(2,1)S(1)} %get-tuple-element.60), channel_id=1, source_target_pairs={{1,0},{0,1},{3,2},{2,3},{5,4},{4,5},{7,6},{6,7},{9,8},{8,9},{11,10... | collective-permute-start | bytes 884744 | tf_op jit(solution)/shard_map/ppermute | solution.py:33
  102.6 14.6 %collective-permute-start.25 = (bf16[128,1152]{1,0:T(8,128)(2,1)S(1)}, bf16[128,1152]{1,0:T(8,128)(2,1)S(1)}, u32[]{:S(2)}, u32[]{:S(2)}) collective-permute-start(bf16[128,1152]{1,0:T(8,128)(2,1)S(1)} %add_codes.2), channel_id=1, source_target_pairs={{16,0},{17,1},{18,2},{19,3},{20,4},{21,5},{22,6},{23,7},{24,8},{25... | collective-permute-start | bytes 884744 | tf_op jit(solution)/shard_map/ppermute | solution.py:33
  103.5 13.7 %copy-start = (bf16[128,1152]{1,0:T(8,128)(2,1)S(1)}, bf16[128,1152]{1,0:T(8,128)(2,1)}, u32[]{:S(2)}) copy-start(bf16[128,1152]{1,0:T(8,128)(2,1)} %raw_ref.2) | copy-start | bytes 884740
  103.5 15.1 %collective-permute-start.29 = (bf16[128,1152]{1,0:T(8,128)(2,1)S(1)}, bf16[128,1152]{1,0:T(8,128)(2,1)S(1)}, u32[]{:S(2)}, u32[]{:S(2)}) collective-permute-start(bf16[128,1152]{1,0:T(8,128)(2,1)S(1)} %get-tuple-element.76), channel_id=1, source_target_pairs={{3,0},{2,1},{1,2},{0,3},{7,4},{6,5},{5,6},{4,7},{11,8},{10,9},{9,1... | collective-permute-start | bytes 884744 | tf_op jit(solution)/shard_map/ppermute | solution.py:33
  106.0 12.7 %copy-start.1 = (bf16[128,1152]{1,0:T(8,128)(2,1)S(1)}, bf16[128,1152]{1,0:T(8,128)(2,1)}, u32[]{:S(2)}) copy-start(bf16[128,1152]{1,0:T(8,128)(2,1)} %raw_ref.3) | copy-start | bytes 884740
  106.0 12.7 %collective-permute-start.32 = (bf16[128,1152]{1,0:T(8,128)(2,1)S(1)}, bf16[128,1152]{1,0:T(8,128)(2,1)S(1)}, u32[]{:S(2)}, u32[]{:S(2)}) collective-permute-start(bf16[128,1152]{1,0:T(8,128)(2,1)S(1)} %add_codes.3), channel_id=1, source_target_pairs={{20,0},{21,1},{22,2},{23,3},{16,4},{17,5},{18,6},{19,7},{28,8},{29... | collective-permute-start | bytes 884744 | tf_op jit(solution)/shard_map/ppermute | solution.py:33
  107.6 3.6 %collective-permute-start.19 = (f32[8,128]{1,0:T(8,128)S(1)}, f32[8,128]{1,0:T(8,128)S(1)}, u32[]{:S(2)}, u32[]{:S(2)}) collective-permute-start(f32[8,128]{1,0:T(8,128)S(1)} %add.29), channel_id=1, source_target_pairs={{32,0},{33,1},{34,2},{35,3},{36,4},{37,5},{38,6},{39,7},{40,8},{41... | collective-permute-start | bytes 12296 | tf_op jit(solution)/shard_map/ppermute | solution.py:33
  111.2 4.8 %collective-permute-start.20 = (f32[8,128]{1,0:T(8,128)S(1)}, f32[8,128]{1,0:T(8,128)S(1)}, u32[]{:S(2)}, u32[]{:S(2)}) collective-permute-start(f32[8,128]{1,0:T(8,128)S(1)} %add.30), channel_id=1, source_target_pairs={{96,0},{97,1},{98,2},{99,3},{100,4},{101,5},{102,6},{103,7},{104,8... | collective-permute-start | bytes 12296 | tf_op jit(solution)/shard_map/ppermute | solution.py:33

commit v2 on v1

v2 whole, which is shorter than its diff:
```python
import functools

import jax
import jax.numpy as jnp
from jax import lax
from jax.experimental import pallas as pl
from jax.experimental.pallas import tpu as pltpu
from jax.sharding import PartitionSpec as P

IMAGE_PAIRS = {"x": 2 << 3, "y": 1, "z": 4 << 3}
TEXT_PAIRS = {"x": (2 << 3) + 4, "y": 3, "z": 12 << 3}
CORE = 1 << 3
PIECE = 128
ROWS = ("", "y", "x", "xz", "z", "yz", "xy", "xyz")
PAIR_VMEM = 12 * 2**20
SMALL_VMEM = 8 * 2**20
LOG2E = 1.4426950408889634
LN2 = 0.6931471805599453
NT = (((1,), (1,)), ((), ()))
NN = (((1,), (0,)), ((), ()))
TN = (((0,), (0,)), ((), ()))
HBM = pl.BlockSpec(memory_space=pl.ANY)
SMEM = pl.BlockSpec(memory_space=pltpu.SMEM)
VMEM = pl.BlockSpec(memory_space=pltpu.VMEM)


def shape_of(rows, depth, dtype):
    return jax.ShapeDtypeStruct((rows, depth), dtype)


def swap(value, mask):
    axes = ("img", "txt")
    return lax.ppermute(value, axes, [(k ^ mask, k) for k in range(lax.axis_size(axes))])


def encode(value):
    square = value * value
    return ((square * value) * (square * square)).astype(jnp.bfloat16)


def decode(code):
    wide = code.astype(jnp.float32)
    root = jnp.exp2(jnp.log2(jnp.abs(wide)) * (1.0 / 7.0))
    return jnp.where(wide < 0.0, -root, root)


def unit_kernel(images_ref, texts_ref, image_out, text_out, raw, sems):
    loads = [pltpu.make_async_copy(ref, raw.at[k], sems.at[k]) for k, ref in enumerate((images_ref, texts_ref))]
    for load in loads:
        load.start()
    for k, out in enumerate((image_out, text_out)):
        loads[k].wait()
        wide = raw[k].astype(jnp.float32)
        inverse = lax.rsqrt(jnp.sum(wide * wide, axis=1, keepdims=True) + 1e-06)
        out[...] = (wide * inverse).astype(jnp.bfloat16)


def unit_rows(images, texts):
    out = shape_of(*images.shape, jnp.bfloat16)
    return pl.pallas_call(
        unit_kernel,
        out_shape=[out, out],
        in_specs=[HBM, HBM],
        out_specs=[VMEM, VMEM],
        scratch_shapes=[pltpu.VMEM((2, *images.shape), jnp.bfloat16), pltpu.SemaphoreType.DMA((2,))],
        compiler_params=pltpu.CompilerParams(vmem_limit_bytes=60 * 2**20),
        name="unit_rows",
    )(images, texts)


def row_masks(pairs):
    return [sum(pairs[axis] for axis in axes) for axes in ROWS]


def logit_kernel(core, loss_scale, place_ref, scale_ref, bias_ref, *refs):
    image_refs, text_refs = refs[:4], refs[4:8]
    if core:
        loss_in, coeff_ref, other_refs, loss_ref = refs[8], refs[9], refs[10:12], refs[12]
    else:
        coeff_ref, loss_ref = refs[8:]
    rows = image_refs[0].shape[0]
    pieces = rows // PIECE

    place = place_ref[0]
    image_base = [lax.bitwise_xor(place, mask) * PIECE for mask in row_masks(IMAGE_PAIRS)]
    text_base = []
    for mask in row_masks(TEXT_PAIRS):
        flat = lax.bitwise_xor(place, mask ^ core)
        text_base.append((lax.rem(flat, 8) * 16 + lax.div(flat, 8)) * PIECE)

    temper = jnp.exp(jnp.full((1, PIECE), scale_ref[0], jnp.float32))
    slope = temper * LOG2E
    shift = jnp.full((1, PIECE), bias_ref[0] * LOG2E, jnp.float32)
    apart = lax.broadcasted_iota(jnp.int32, (PIECE, PIECE), 0) - lax.broadcasted_iota(
        jnp.int32, (PIECE, PIECE), 1
    )
    quarter = PIECE // 4
    loss_sum = jnp.zeros((8, PIECE), jnp.float32)
    own_sum = jnp.zeros((8, PIECE), jnp.float32)
    for t in (2, 3, 0, 1):
        left = t * rows
        for r, image_ref in enumerate(image_refs):
            dots = lax.dot_general(image_ref[...], text_refs[t][...], NT, preferred_element_type=jnp.float32)
            for a in range(pieces):
                top = r * rows + a * PIECE
                for b in range(pieces):
                    power = dots[a * PIECE : (a + 1) * PIECE, b * PIECE : (b + 1) * PIECE] * slope + shift
                    grown = jnp.exp2(power)
                    match = apart == text_base[t * pieces + b] - image_base[r * pieces + a]
                    weight = jnp.where(match, -1.0, grown) * pl.reciprocal(1.0 + grown) * temper
                    column = left + b * PIECE
                    coeff_ref[top : top + PIECE, column : column + PIECE] = weight.astype(jnp.bfloat16)
                    g = [grown[k * quarter : (k + 1) * quarter] for k in range(4)]
                    low = g[0] + g[1] + g[0] * g[1]
                    high = g[2] + g[3] + g[2] * g[3]
                    terms = jnp.log(1.0 + (low + high + low * high))
                    chosen = jnp.where(match, power, 0.0)
                    for k in range(quarter // 8):
                        loss_sum = loss_sum + terms[k * 8 : (k + 1) * 8]
                    for k in range(PIECE // 8):
                        own_sum = own_sum + chosen[k * 8 : (k + 1) * 8]
        if core:
            other_refs[t // 2][t % 2 * rows : (t % 2 + 1) * rows, :] = encode(
                text_shares(coeff_ref, left, image_refs)
            )
    loss = loss_sum - LN2 * own_sum
    if core:
        total = jnp.sum(loss + loss_in[...], keepdims=True) * loss_scale
        loss_ref[...] = jnp.broadcast_to(total, loss_ref.shape)
    else:
        loss_ref[...] = loss


def text_shares(coeff_ref, left, image_refs):
    rows = image_refs[0].shape[0]
    part = None
    for r, image_ref in enumerate(image_refs):
        more = lax.dot_general(
            coeff_ref[r * rows : (r + 1) * rows, left : left + rows],
            image_ref[...],
            TN,
            preferred_element_type=jnp.float32,
        )
        part = more if part is None else part + more
    return part


def logit_terms(place, logit_scale, bias, images, texts, core=0, loss=None, loss_scale=None):
    rows, depth = images[0].shape
    height, count = len(images) * rows, len(texts) * rows
    coeff, loss_tile = shape_of(height, count, jnp.bfloat16), shape_of(8, PIECE, jnp.float32)
    shares = [shape_of(2 * rows, depth, jnp.bfloat16)] * 2 if core else []
    operands = (place, logit_scale, bias, *images, *texts) + ((loss,) if core else ())
    out_shape = [coeff, *shares, loss_tile]
    outs = pl.pallas_call(
        functools.partial(logit_kernel, core, loss_scale),
        out_shape=out_shape,
        in_specs=[SMEM, SMEM, SMEM] + [VMEM] * (len(operands) - 3),
        out_specs=[VMEM] * len(out_shape),
        compiler_params=pltpu.CompilerParams(vmem_limit_bytes=PAIR_VMEM),
        cost_estimate=cost((2 if core else 1) * height * count * depth),
        name="other_logits" if core else "own_logits",
    )(*operands)
    return outs[0], outs[1:-1], outs[-1]


def cost(multiplies):
    return pl.CostEstimate(flops=2 * multiplies, bytes_accessed=8 * 2**20, transcendentals=0)


def text_kernel(first, coeff_ref, came_ref, *refs):
    image_refs, outs = refs[:4], refs[4:]
    rows = outs[0].shape[0]
    for k in (1, 0):
        total = text_shares(coeff_ref, first + k * rows, image_refs) + decode(came_ref[k * rows : (k + 1) * rows, :])
        outs[k][...] = total if outs[k].dtype == jnp.float32 else encode(total)


def text_terms(first, dtype, coeff, came, images):
    rows, depth = images[0].shape
    return pl.pallas_call(
        functools.partial(text_kernel, first),
        out_shape=[shape_of(rows, depth, dtype)] * 2,
        in_specs=[VMEM] * 6,
        out_specs=[VMEM] * 2,
        compiler_params=pltpu.CompilerParams(vmem_limit_bytes=PAIR_VMEM),
        cost_estimate=cost(2 * rows * coeff.shape[0] * depth),
        name="text_terms",
    )(coeff, came, *images)


def image_kernel(first, own_ref, other_ref, *refs):
    text_refs, outs = refs[:8], refs[8:]
    rows = outs[0].shape[0]
    for k, out in enumerate(outs):
        top = first + k * rows
        total = None
        for t, text_ref in enumerate(text_refs):
            coeff_ref, left = (own_ref, other_ref)[t // 4], t % 4 * rows
            more = jnp.dot(
                coeff_ref[top : top + rows, left : left + rows], text_ref[...], preferred_element_type=jnp.float32
            )
            total = more if total is None else total + more
        out[...] = total if out.dtype == jnp.float32 else encode(total)


def image_terms(first, count, dtype, coeffs, texts):
    rows, depth = texts[0].shape
    return pl.pallas_call(
        functools.partial(image_kernel, first),
        out_shape=[shape_of(rows, depth, dtype)] * count,
        in_specs=[VMEM] * 10,
        out_specs=[VMEM] * count,
        compiler_params=pltpu.CompilerParams(vmem_limit_bytes=PAIR_VMEM),
        cost_estimate=cost(2 * count * rows * coeffs[0].shape[1] * depth),
        name="image_terms",
    )(*coeffs, *texts)


def small_call(kernel, name, out_shape, operands):
    return pl.pallas_call(
        kernel,
        out_shape=out_shape,
        in_specs=[VMEM] * len(operands),
        out_specs=[VMEM] * len(out_shape),
        compiler_params=pltpu.CompilerParams(vmem_limit_bytes=SMALL_VMEM),
        name=name,
    )(*operands)


def fold_kernel(own_ref, came_ref, kept, sent):
    sent[...] = encode(own_ref[PIECE:, :] + decode(came_ref[PIECE:, :]))
    kept[...] = own_ref[:PIECE, :] + decode(came_ref[:PIECE, :])


def fold(own, came):
    depth = own.shape[1]
    out_shape = [shape_of(PIECE, depth, jnp.float32), shape_of(PIECE, depth, jnp.bfloat16)]
    return small_call(fold_kernel, "fold", out_shape, (own, came))


def add_kernel(own_ref, came_ref, out_ref):
    out_ref[...] = encode(own_ref[...] + decode(came_ref[...]))


def add_codes(own, came):
    return small_call(add_kernel, "add_codes", [shape_of(*own.shape, jnp.bfloat16)], (own, came))[0]


def finish_kernel(raw_ref, own_ref, ring_ref, far_ref, loss_ref, loss_in, out_ref, loss_out):
    loss_out[0] = jnp.max(loss_ref[...] + loss_in[...])
    grad = own_ref[...] + decode(ring_ref[...]) + decode(far_ref[...])
    wide = raw_ref[...].astype(jnp.float32)
    inverse = lax.rsqrt(jnp.sum(wide * wide, axis=1, keepdims=True) + 1e-06)
    unit = wide * inverse
    out_ref[...] = inverse * (grad - unit * jnp.sum(unit * grad, axis=1, keepdims=True))


def finish(raw, own, ring, far, loss, loss_in):
    return pl.pallas_call(
        finish_kernel,
        out_shape=[shape_of(*raw.shape, jnp.float32), jax.ShapeDtypeStruct((1,), jnp.float32)],
        in_specs=[VMEM] * 6,
        out_specs=[VMEM, SMEM],
        compiler_params=pltpu.CompilerParams(vmem_limit_bytes=SMALL_VMEM),
        name="finish",
    )(raw, own, ring, far, loss, loss_in)


def gather(image, text):
    groups = ((image, IMAGE_PAIRS), (text, TEXT_PAIRS))
    far = [swap(unit, pairs["x"]) for unit, pairs in groups]
    *far, image, text = lax.optimization_barrier((*far, image, text))
    groups = ((image, IMAGE_PAIRS), (text, TEXT_PAIRS))
    far = [jnp.concatenate([part, swap(part, pairs["z"])], axis=0) for part, (_, pairs) in zip(far, groups)]
    near = [jnp.concatenate([unit, swap(unit, pairs["y"])], axis=0) for unit, pairs in groups]
    *far, near[0], near[1] = lax.optimization_barrier((*far, *near))
    far_late = [swap(part, pairs["y"]) for part, (_, pairs) in zip(far, groups)]
    near_late = [swap(part, pairs["z"]) for part, (_, pairs) in zip(near, groups)]
    images, texts = ([near[k], far[k], near_late[k], far_late[k]] for k in range(2))
    late_core = [after(far[1], *near_late, *far_late), *texts[2:]]
    return images, texts + [swap(part, CORE) for part in (near[1], *late_core)]


def after(value, *others):
    return lax.optimization_barrier((value, *others))[0]


def shards(images, texts, logit_scale, bias):
    place = (lax.axis_index("img") * lax.axis_size("txt") + lax.axis_index("txt")).astype(jnp.int32).reshape(1)
    image_all, text_all = gather(*unit_rows(images, texts))
    count = images.shape[0] * lax.axis_size("img") * lax.axis_size("txt")
    own_coeff, _, loss = logit_terms(place, logit_scale, bias, image_all, text_all[:4])
    other_coeff, other, loss = logit_terms(
        place, logit_scale, bias, image_all, text_all[4:], CORE, loss, 1.0 / count
    )
    coeffs = (own_coeff, other_coeff)

    other_late = swap(other[1], CORE)
    loss = loss + swap(loss, CORE)
    near_late, far_late = image_terms(4 * PIECE, 2, jnp.bfloat16, coeffs, text_all)
    image_far = swap(far_late, IMAGE_PAIRS["y"])
    image_near = swap(near_late, IMAGE_PAIRS["z"])
    text_near, text_far = text_terms(
        4 * PIECE, jnp.bfloat16, after(own_coeff, loss, near_late), other_late, image_all
    )
    text_far = swap(text_far, TEXT_PAIRS["y"])
    text_near = swap(text_near, TEXT_PAIRS["z"])
    other_early = swap(other[0], CORE)
    near_early, far_early = image_terms(0, 2, jnp.float32, (after(own_coeff, far_late), other_coeff), text_all)
    text_early = text_terms(0, jnp.float32, after(own_coeff, near_early), other_early, image_all)

    image_kept, image_sent = fold(far_early, image_far)
    image_far = swap(image_sent, IMAGE_PAIRS["z"])
    loss = after(loss, text_early[0])
    loss = loss + swap(loss, IMAGE_PAIRS["y"])
    text_kept, text_sent = fold(text_early[1], after(text_far, loss))
    text_far = swap(text_sent, TEXT_PAIRS["z"])
    image_own, image_sent = fold(near_early, image_near)
    image_near = swap(image_sent, IMAGE_PAIRS["y"])
    text_own, text_sent = fold(text_early[0], text_near)
    text_near = swap(text_sent, TEXT_PAIRS["y"])

    loss = after(loss, text_kept, image_own, text_own)
    loss = loss + swap(loss, IMAGE_PAIRS["x"])
    image_sent = add_codes(image_kept, after(image_far, loss))
    loss = loss + swap(loss, TEXT_PAIRS["x"])
    text_sent = add_codes(text_kept, after(text_far, loss))
    loss = after(loss, text_sent)
    for mask in (IMAGE_PAIRS["z"], TEXT_PAIRS["y"]):
        loss = loss + swap(loss, mask)
    last = swap(loss, TEXT_PAIRS["z"])
    image_grad, _ = finish(images, image_own, image_near, swap(image_sent, IMAGE_PAIRS["x"]), loss, loss)
    text_grad, loss = finish(texts, text_own, text_near, swap(text_sent, TEXT_PAIRS["x"]), loss, last)
    return loss, image_grad, text_grad


def solution(mesh):
    placed = (P(("img", "txt"), None), P(("txt", "img"), None), P(), P())
    return jax.shard_map(
        shards,
        mesh=mesh,
        in_specs=placed,
        out_specs=(P(), P(("img", "txt"), None), P(("txt", "img"), None)),
        check_vma=False,
    )
```

time: 122 us -> 114 us (0.934)
  local copies, waits for them, and re-layouts: 4.29 us -> 0.02 us
  waiting for transfers between devices: 42.4 us -> 38.3 us
  starting transfers between devices: 35.4 us -> 38.1 us
  between operations: 3.95 us -> 2.36 us
    ppermute x33, waiting for transfers between devices: 42.4 us -> 38.3 us  [swap(): lax.ppermute(value, axes, [(k ^ mask, k) for k in range(lax.axis_size(axe...]
    unnamed x16 -> x8, local copies, waits for them, and re-layouts: 3.78 us -> 0.02 us
    pallas_call x8 -> x6, Pallas kernels: 5.81 us -> 2.31 us  [small_call(): pl.pallas_call(kernel, out_shape=out_shape, in_specs=[VMEM] * len(operand...]
    pallas_call x3 -> x6, Pallas kernels: 18.1 us -> 21.1 us  [the longest x2 14.2 us: logit_terms(): pl.pallas_call(functools.partial(logit_kernel, core, loss_scale), out_sha...]
    ppermute x33, starting transfers between devices: 35.4 us -> 38.1 us  [swap(): lax.ppermute(value, axes, [(k ^ mask, k) for k in range(lax.axis_size(axe...]
  transfers between devices with their start and end apart: 33 -> 33, of which waited for: 17 -> 16; matrix products, arithmetic and copies ran while one was open for 1% -> 0% of each run, Pallas kernels for 15% -> 20%
where the time goes in v2:
time: 114 us
  waiting for transfers between devices  38.3 us (34%)
  starting transfers between devices  38.1 us (33%)
  Pallas kernels  35.2 us (31%)
  between operations  2.36 us (2%)
    ppermute x33, waiting for transfers between devices, swap(): lax.ppermute(value, axes, [(k ^ mask, k) for k in range(lax.axis_size(axe...  38.3 us
    ppermute x33, starting transfers between devices, swap(): lax.ppermute(value, axes, [(k ^ mask, k) for k in range(lax.axis_size(axe...  38.1 us
    pallas_call x2, Pallas kernels, logit_terms(): pl.pallas_call(functools.partial(logit_kernel, core, loss_scale), out_sha...  14.2 us
    pallas_call x2, Pallas kernels, image_terms(): pl.pallas_call(functools.partial(image_kernel, first), out_shape=[shape_o...  9.72 us
    pallas_call x2, Pallas kernels, text_terms(): pl.pallas_call(functools.partial(text_kernel, first), out_shape=[shape_of...  4.06 us
    pallas_call x2, Pallas kernels, finish(): pl.pallas_call(finish_kernel, out_shape=[shape_of(*raw.shape, jnp.float32...  2.85 us
    pallas_call x6, Pallas kernels, small_call(): pl.pallas_call(kernel, out_shape=out_shape, in_specs=[VMEM] * len(operand...  2.31 us
  transfers between devices with their start and end apart: 33, of which 16 were waited for; matrix products, arithmetic and copies ran while one was open for 0% of the time, Pallas kernels for 20%

profile of v2, /device:TPU:0, one launch (start us, length us, event | category | flops | bytes accessed | tf_op | source)
XLA Modules:
  0.0 114.2 jit_solution(13526033877876096100)
XLA Ops:
  0.6 2.0 %unit_rows.1 = (bf16[128,1152]{1,0:T(8,128)(2,1)}, bf16[128,1152]{1,0:T(8,128)(2,1)}) custom-call(bf16[128,1152]{1,0:T(8,128)(2,1)} %raw_ref.3, bf16[128,1152]{1,0:T(8,128)(2,1)} %raw_ref.2), custom_call_target="tpu_custom_call" | custom-call | tf_op jit(solution)/shard_map/unit_rows/pallas_call | solution.py:60
  2.6 1.7 %collective-permute-start = (bf16[128,1152]{1,0:T(8,128)(2,1)}, bf16[128,1152]{1,0:T(8,128)(2,1)S(1)}, u32[]{:S(2)}, u32[]{:S(2)}) collective-permute-start(bf16[128,1152]{1,0:T(8,128)(2,1)} %get-tuple-element.52), channel_id=1, source_target_pairs={{16,0},{17,1},{18,2},{19,3},{20,4},{21,5},{22,6},{23,7},{24,8},{25... | collective-permute-start | bytes 884744 | tf_op jit(solution)/shard_map/ppermute | solution.py:33
  4.3 2.1 %collective-permute-start.1 = (bf16[128,1152]{1,0:T(8,128)(2,1)}, bf16[128,1152]{1,0:T(8,128)(2,1)S(1)}, u32[]{:S(2)}, u32[]{:S(2)}) collective-permute-start(bf16[128,1152]{1,0:T(8,128)(2,1)} %get-tuple-element.53), channel_id=1, source_target_pairs={{20,0},{21,1},{22,2},{23,3},{16,4},{17,5},{18,6},{19,7},{28,8},{29... | collective-permute-start | bytes 884744 | tf_op jit(solution)/shard_map/ppermute | solution.py:33
  6.4 5.1 %collective-permute-done = bf16[128,1152]{1,0:T(8,128)(2,1)S(1)} collective-permute-done((bf16[128,1152]{1,0:T(8,128)(2,1)}, bf16[128,1152]{1,0:T(8,128)(2,1)S(1)}, u32[]{:S(2)}, u32[]{:S(2)}) %collective-permute-start) | collective-permute-done | bytes 294944 | tf_op jit(solution)/shard_map/ppermute | solution.py:33
  11.5 2.7 %collective-permute-done.1 = bf16[128,1152]{1,0:T(8,128)(2,1)S(1)} collective-permute-done((bf16[128,1152]{1,0:T(8,128)(2,1)}, bf16[128,1152]{1,0:T(8,128)(2,1)S(1)}, u32[]{:S(2)}, u32[]{:S(2)}) %collective-permute-start.1) | collective-permute-done | bytes 294944 | tf_op jit(solution)/shard_map/ppermute | solution.py:33
  14.2 1.9 %collective-permute-start.2 = (bf16[128,1152]{1,0:T(8,128)(2,1)S(1)}, bf16[128,1152]{1,0:T(8,128)(2,1)S(1)}, u32[]{:S(2)}, u32[]{:S(2)}) collective-permute-start(bf16[128,1152]{1,0:T(8,128)(2,1)S(1)} %collective-permute-done), channel_id=1, source_target_pairs={{32,0},{33,1},{34,2},{35,3},{36,4},{37,5},{38,6},{39,7},{40,8},{41... | collective-permute-start | bytes 884744 | tf_op jit(solution)/shard_map/ppermute | solution.py:33
  16.1 2.5 %collective-permute-start.3 = (bf16[128,1152]{1,0:T(8,128)(2,1)S(1)}, bf16[128,1152]{1,0:T(8,128)(2,1)S(1)}, u32[]{:S(2)}, u32[]{:S(2)}) collective-permute-start(bf16[128,1152]{1,0:T(8,128)(2,1)S(1)} %collective-permute-done.1), channel_id=1, source_target_pairs={{96,0},{97,1},{98,2},{99,3},{100,4},{101,5},{102,6},{103,7},{104,8... | collective-permute-start | bytes 884744 | tf_op jit(solution)/shard_map/ppermute | solution.py:33
  18.6 1.6 %collective-permute-start.4 = (bf16[128,1152]{1,0:T(8,128)(2,1)}, bf16[128,1152]{1,0:T(8,128)(2,1)S(1)}, u32[]{:S(2)}, u32[]{:S(2)}) collective-permute-start(bf16[128,1152]{1,0:T(8,128)(2,1)} %get-tuple-element.52), channel_id=1, source_target_pairs={{1,0},{0,1},{3,2},{2,3},{5,4},{4,5},{7,6},{6,7},{9,8},{8,9},{11,10... | collective-permute-start | bytes 884744 | tf_op jit(solution)/shard_map/ppermute | solution.py:33
  20.2 2.2 %collective-permute-start.5 = (bf16[128,1152]{1,0:T(8,128)(2,1)}, bf16[128,1152]{1,0:T(8,128)(2,1)S(1)}, u32[]{:S(2)}, u32[]{:S(2)}) collective-permute-start(bf16[128,1152]{1,0:T(8,128)(2,1)} %get-tuple-element.53), channel_id=1, source_target_pairs={{3,0},{2,1},{1,2},{0,3},{7,4},{6,5},{5,6},{4,7},{11,8},{10,9},{9,1... | collective-permute-start | bytes 884744 | tf_op jit(solution)/shard_map/ppermute | solution.py:33
  22.4 0.0 copy-start.2
  22.4 2.1 %collective-permute-done.3 = bf16[128,1152]{1,0:T(8,128)(2,1)S(1)} collective-permute-done((bf16[128,1152]{1,0:T(8,128)(2,1)S(1)}, bf16[128,1152]{1,0:T(8,128)(2,1)S(1)}, u32[]{:S(2)}, u32[]{:S(2)}) %collective-permute-start.3) | collective-permute-done | bytes 294944 | tf_op jit(solution)/shard_map/ppermute | solution.py:33
  24.6 1.2 %collective-permute-done.4 = bf16[128,1152]{1,0:T(8,128)(2,1)S(1)} collective-permute-done((bf16[128,1152]{1,0:T(8,128)(2,1)}, bf16[128,1152]{1,0:T(8,128)(2,1)S(1)}, u32[]{:S(2)}, u32[]{:S(2)}) %collective-permute-start.4) | collective-permute-done | bytes 294944 | tf_op jit(solution)/shard_map/ppermute | solution.py:33
  25.9 2.5 %collective-permute-done.5 = bf16[128,1152]{1,0:T(8,128)(2,1)S(1)} collective-permute-done((bf16[128,1152]{1,0:T(8,128)(2,1)}, bf16[128,1152]{1,0:T(8,128)(2,1)S(1)}, u32[]{:S(2)}, u32[]{:S(2)}) %collective-permute-start.5) | collective-permute-done | bytes 294944 | tf_op jit(solution)/shard_map/ppermute | solution.py:33
  28.4 1.1 collective-permute-start.6
  29.5 0.0 collective-permute-start.7
  29.5 0.9 collective-permute-start.8
  30.4 2.3 %collective-permute-start.9 = (bf16[256,1152]{1,0:T(8,128)(2,1)S(1)}, bf16[256,1152]{1,0:T(8,128)(2,1)}, u32[]{:S(2)}, u32[]{:S(2)}) collective-permute-start(bf16[256,1152]{1,0:T(8,128)(2,1)S(1)} %pad_maximum_fusion.1.refs_5_.refs_1_), channel_id=1, source_target_pairs={{3,0},{2,1},{1,2},{0,3},{7,4},{6,5},{5,6},{4,7},{11,8},{10,9},{9,1... | collective-permute-start | bytes 1769480 | tf_op jit(solution)/shard_map/ppermute | solution.py:33
  32.6 7.7 %collective-permute-done.6.refs_2_ = bf16[256,1152]{1,0:T(8,128)(2,1)S(1)} collective-permute-done((bf16[256,1152]{1,0:T(8,128)(2,1)S(1)}, bf16[256,1152]{1,0:T(8,128)(2,1)S(1)}, u32[]{:S(2)}, u32[]{:S(2)}) %collective-permute-start.6) | collective-permute-done | bytes 589856 | tf_op jit(solution)/shard_map/ppermute | solution.py:33
  40.4 0.7 collective-permute-done.7.refs_3_
  41.1 1.4 %collective-permute-done.8.refs_6_.refs_2_ = bf16[256,1152]{1,0:T(8,128)(2,1)} collective-permute-done((bf16[256,1152]{1,0:T(8,128)(2,1)S(1)}, bf16[256,1152]{1,0:T(8,128)(2,1)}, u32[]{:S(2)}, u32[]{:S(2)}) %collective-permute-start.8) | collective-permute-done | bytes 589856 | tf_op jit(solution)/shard_map/ppermute | solution.py:33
  42.5 1.0 collective-permute-done.9.refs_7_.refs_3_
  43.5 0.0 collective-permute-start.12
  43.5 0.5 collective-permute-start.11
  44.0 0.0 collective-permute-start.13
  45.3 5.4 %own_logits.1 = (bf16[1024,1024]{1,0:T(8,128)(2,1)S(1)}, f32[8,128]{1,0:T(8,128)S(1)}) custom-call(s32[1]{0:T(128)} %bitcast.place_ref, f32[1]{0:T(128)S(6)} %copy.7.scale_ref, f32[1]{0:T(128)S(6)} %copy.8.bias_ref, bf16[256,1152]{1,0:T(8,128)(2,1)S(1)} %pad_maximum_fusion.2.refs_0_, bf16[256,1152]{1,0:T(8,128)(2,1)S(1)} %pad_maximum_fusion.refs_1_, ...), custom_call_target="tpu_custom_call" | custom-call | flops 2415919104 | bytes 8388608 | tf_op jit(solution)/shard_map/own_logits/pallas_call | solution.py:155
  50.8 8.9 %other_logits.1 = (bf16[1024,1024]{1,0:T(8,128)(2,1)S(1)}, bf16[512,1152]{1,0:T(8,128)(2,1)S(1)}, bf16[512,1152]{1,0:T(8,128)(2,1)S(1)}, f32[8,128]{1,0:T(8,128)S(1)}) custom-call(s32[1]{0:T(128)} %bitcast.place_ref, f32[1]{0:T(128)S(6)} %copy.7.scale_ref, f32[1]{0:T(128)S(6)} %copy.8.bias_ref, bf16[256,1152]{1,0:T(8,128)(2,1)S(1)} %pad_maximum_fusion.2.refs_0_, ...), custom_call_target="tpu_custom_call" | custom-call | flops 4831838208 | bytes 8388608 | tf_op jit(solution)/shard_map/other_logits/pallas_call | solution.py:155
  59.6 0.6 collective-permute-start.16
  60.2 0.1 collective-permute-start.14
  60.3 0.4 collective-permute-start.15
  60.7 4.9 %image_terms.2 = (bf16[256,1152]{1,0:T(8,128)(2,1)S(1)}, bf16[256,1152]{1,0:T(8,128)(2,1)S(1)}) custom-call(bf16[1024,1024]{1,0:T(8,128)(2,1)S(1)} %get-tuple-element.70.own_ref.coeff_ref, bf16[1024,1024]{1,0:T(8,128)(2,1)S(1)} %get-tuple-element.61.other_ref, bf16[256,1152]{1,0:T(8,128)(2,1)S(1)} %pad_maximum_fusion.3.refs_4_.refs_0_, ...), custom_call_target="tpu_custom_call" | custom-call | flops 2415919104 | bytes 8388608 | tf_op jit(solution)/shard_map/image_terms/pallas_call | solution.py:209
  65.6 0.7 collective-permute-start.30
  66.3 2.2 %text_terms.3 = (bf16[256,1152]{1,0:T(8,128)(2,1)S(1)}, bf16[256,1152]{1,0:T(8,128)(2,1)S(1)}) custom-call(bf16[1024,1024]{1,0:T(8,128)(2,1)S(1)} %get-tuple-element.70.own_ref.coeff_ref, bf16[512,1152]{1,0:T(8,128)(2,1)S(1)} %collective-permute-done.16.came_ref, bf16[256,1152]{1,0:T(8,128)(2,1)S(1)} %pad_maximum_fusion.2.refs_0_, ...), custom_call_target="tpu_custom_call" | custom-call | flops 1207959552 | bytes 8388608 | tf_op jit(solution)/shard_map/text_terms/pallas_call | solution.py:181
  68.6 2.3 %collective-permute-start.19 = (bf16[256,1152]{1,0:T(8,128)(2,1)S(1)}, bf16[256,1152]{1,0:T(8,128)(2,1)S(1)}, u32[]{:S(2)}, u32[]{:S(2)}) collective-permute-start(bf16[256,1152]{1,0:T(8,128)(2,1)S(1)} %get-tuple-element.76), channel_id=1, source_target_pairs={{3,0},{2,1},{1,2},{0,3},{7,4},{6,5},{5,6},{4,7},{11,8},{10,9},{9,1... | collective-permute-start | bytes 1769480 | tf_op jit(solution)/shard_map/ppermute | solution.py:33
  70.8 0.1 collective-permute-start.22
  70.9 2.4 %collective-permute-start.17 = (bf16[256,1152]{1,0:T(8,128)(2,1)S(1)}, bf16[256,1152]{1,0:T(8,128)(2,1)S(1)}, u32[]{:S(2)}, u32[]{:S(2)}) collective-permute-start(bf16[256,1152]{1,0:T(8,128)(2,1)S(1)} %get-tuple-element.72), channel_id=1, source_target_pairs={{96,0},{97,1},{98,2},{99,3},{100,4},{101,5},{102,6},{103,7},{104,8... | collective-permute-start | bytes 1769480 | tf_op jit(solution)/shard_map/ppermute | solution.py:33
  73.3 4.8 %image_terms.3 = (f32[256,1152]{1,0:T(8,128)S(1)}, f32[256,1152]{1,0:T(8,128)S(1)}) custom-call(bf16[1024,1024]{1,0:T(8,128)(2,1)S(1)} %get-tuple-element.70.own_ref.coeff_ref, bf16[1024,1024]{1,0:T(8,128)(2,1)S(1)} %get-tuple-element.61.other_ref, bf16[256,1152]{1,0:T(8,128)(2,1)S(1)} %pad_maximum_fusion.3.refs_4_.refs_0_, ...), custom_call_target="tpu_custom_call" | custom-call | flops 2415919104 | bytes 8388608 | tf_op jit(solution)/shard_map/image_terms/pallas_call | solution.py:209
  78.1 1.8 %text_terms.2 = (f32[256,1152]{1,0:T(8,128)S(1)}, f32[256,1152]{1,0:T(8,128)S(1)}) custom-call(bf16[1024,1024]{1,0:T(8,128)(2,1)S(1)} %get-tuple-element.70.own_ref.coeff_ref, bf16[512,1152]{1,0:T(8,128)(2,1)S(1)} %collective-permute-done.14.came_ref, bf16[256,1152]{1,0:T(8,128)(2,1)S(1)} %pad_maximum_fusion.2.refs_0_, ...), custom_call_target="tpu_custom_call" | custom-call | flops 1207959552 | bytes 8388608 | tf_op jit(solution)/shard_map/text_terms/pallas_call | solution.py:181
  80.0 1.0 collective-permute-start.20
  80.9 0.1 collective-permute-done.30.came_ref
  81.0 0.4 fold.7
  81.5 0.8 collective-permute-start.31
  82.3 1.4 %collective-permute-done.20 = f32[8,128]{1,0:T(8,128)S(1)} collective-permute-done((f32[8,128]{1,0:T(8,128)S(1)}, f32[8,128]{1,0:T(8,128)S(1)}, u32[]{:S(2)}, u32[]{:S(2)}) %collective-permute-start.20) | collective-permute-done | bytes 4128 | tf_op jit(solution)/shard_map/ppermute | solution.py:33
  83.7 1.2 %collective-permute-done.19.came_ref = bf16[256,1152]{1,0:T(8,128)(2,1)S(1)} collective-permute-done((bf16[256,1152]{1,0:T(8,128)(2,1)S(1)}, bf16[256,1152]{1,0:T(8,128)(2,1)S(1)}, u32[]{:S(2)}, u32[]{:S(2)}) %collective-permute-start.19) | collective-permute-done | bytes 589856 | tf_op jit(solution)/shard_map/ppermute | solution.py:33
  84.9 0.4 fold.5
  85.3 2.1 %collective-permute-start.21 = (bf16[128,1152]{1,0:T(8,128)(2,1)S(1)}, bf16[128,1152]{1,0:T(8,128)(2,1)S(1)}, u32[]{:S(2)}, u32[]{:S(2)}) collective-permute-start(bf16[128,1152]{1,0:T(8,128)(2,1)S(1)} %get-tuple-element.80), channel_id=1, source_target_pairs={{96,0},{97,1},{98,2},{99,3},{100,4},{101,5},{102,6},{103,7},{104,8... | collective-permute-start | bytes 884744 | tf_op jit(solution)/shard_map/ppermute | solution.py:33
  87.4 0.4 fold.6
  87.9 0.4 fold.4
  88.3 0.7 collective-permute-start.23
  89.0 3.0 %collective-permute-done.23 = f32[8,128]{1,0:T(8,128)S(1)} collective-permute-done((f32[8,128]{1,0:T(8,128)S(1)}, f32[8,128]{1,0:T(8,128)S(1)}, u32[]{:S(2)}, u32[]{:S(2)}) %collective-permute-start.23) | collective-permute-done | bytes 4128 | tf_op jit(solution)/shard_map/ppermute | solution.py:33
  92.0 2.1 %collective-permute-start.24 = (f32[8,128]{1,0:T(8,128)S(1)}, f32[8,128]{1,0:T(8,128)S(1)}, u32[]{:S(2)}, u32[]{:S(2)}) collective-permute-start(f32[8,128]{1,0:T(8,128)S(1)} %add.24), channel_id=1, source_target_pairs={{20,0},{21,1},{22,2},{23,3},{16,4},{17,5},{18,6},{19,7},{28,8},{29... | collective-permute-start | bytes 12296 | tf_op jit(solution)/shard_map/ppermute | solution.py:33
  94.1 0.4 collective-permute-start.29
  94.5 2.1 %collective-permute-start.18 = (bf16[128,1152]{1,0:T(8,128)(2,1)S(1)}, bf16[128,1152]{1,0:T(8,128)(2,1)S(1)}, u32[]{:S(2)}, u32[]{:S(2)}) collective-permute-start(bf16[128,1152]{1,0:T(8,128)(2,1)S(1)} %get-tuple-element.74), channel_id=1, source_target_pairs={{3,0},{2,1},{1,2},{0,3},{7,4},{6,5},{5,6},{4,7},{11,8},{10,9},{9,1... | collective-permute-start | bytes 884744 | tf_op jit(solution)/shard_map/ppermute | solution.py:33
  96.7 0.3 add_codes.3
  96.9 0.1 collective-permute-start.32
  97.1 0.0 copy-start.1
  97.1 0.3 add_codes.2
  97.4 1.9 %collective-permute-start.25 = (bf16[128,1152]{1,0:T(8,128)(2,1)S(1)}, bf16[128,1152]{1,0:T(8,128)(2,1)S(1)}, u32[]{:S(2)}, u32[]{:S(2)}) collective-permute-start(bf16[128,1152]{1,0:T(8,128)(2,1)S(1)} %add_codes.2), channel_id=1, source_target_pairs={{20,0},{21,1},{22,2},{23,3},{16,4},{17,5},{18,6},{19,7},{28,8},{29... | collective-permute-start | bytes 884744 | tf_op jit(solution)/shard_map/ppermute | solution.py:33
  99.3 3.6 %collective-permute-done.26 = f32[8,128]{1,0:T(8,128)S(1)} collective-permute-done((f32[8,128]{1,0:T(8,128)S(1)}, f32[8,128]{1,0:T(8,128)S(1)}, u32[]{:S(2)}, u32[]{:S(2)}) %collective-permute-start.26) | collective-permute-done | bytes 4128 | tf_op jit(solution)/shard_map/ppermute | solution.py:33
  102.9 2.2 %collective-permute-start.27 = (f32[8,128]{1,0:T(8,128)S(1)}, f32[8,128]{1,0:T(8,128)S(1)}, u32[]{:S(2)}, u32[]{:S(2)}) collective-permute-start(f32[8,128]{1,0:T(8,128)S(1)} %add.26), channel_id=1, source_target_pairs={{3,0},{2,1},{1,2},{0,3},{7,4},{6,5},{5,6},{4,7},{11,8},{10,9},{9,1... | collective-permute-start | bytes 12296 | tf_op jit(solution)/shard_map/ppermute | solution.py:33
  105.1 2.6 %collective-permute-done.27 = f32[8,128]{1,0:T(8,128)S(1)} collective-permute-done((f32[8,128]{1,0:T(8,128)S(1)}, f32[8,128]{1,0:T(8,128)S(1)}, u32[]{:S(2)}, u32[]{:S(2)}) %collective-permute-start.27) | collective-permute-done | bytes 4128 | tf_op jit(solution)/shard_map/ppermute | solution.py:33
  107.7 1.5 %collective-permute-start.28 = (f32[8,128]{1,0:T(8,128)S(1)}, f32[8,128]{1,0:T(8,128)S(1)}, u32[]{:S(2)}, u32[]{:S(2)}) collective-permute-start(f32[8,128]{1,0:T(8,128)S(1)} %add.27.loss_ref.loss_in), channel_id=1, source_target_pairs={{96,0},{97,1},{98,2},{99,3},{100,4},{101,5},{102,6},{103,7},{104,8... | collective-permute-start | bytes 12296 | tf_op jit(solution)/shard_map/ppermute | solution.py:33
  109.2 1.4 %finish.3 = (f32[128,1152]{1,0:T(8,128)}, f32[1]{0:T(128)}) custom-call(bf16[128,1152]{1,0:T(8,128)(2,1)S(1)} %copy-done, f32[128,1152]{1,0:T(8,128)S(1)} %get-tuple-element.81.own_ref, bf16[128,1152]{1,0:T(8,128)(2,1)S(1)} %collective-permute-done.29.ring_ref, bf16[128,1152]{1,0:T(8,128)(2,1)S(1)} %collective-permute-done.32.far_ref, ...), custom_call_target="tpu_custom_call" | custom-call | tf_op jit(solution)/shard_map/finish/pallas_call | solution.py:260
  110.7 1.9 %collective-permute-done.28.loss_in = f32[8,128]{1,0:T(8,128)S(1)} collective-permute-done((f32[8,128]{1,0:T(8,128)S(1)}, f32[8,128]{1,0:T(8,128)S(1)}, u32[]{:S(2)}, u32[]{:S(2)}) %collective-permute-start.28) | collective-permute-done | bytes 4128 | tf_op jit(solution)/shard_map/ppermute | solution.py:33
  112.6 1.4 %finish.2 = (f32[128,1152]{1,0:T(8,128)}, f32[1]{0:T(128)}) custom-call(bf16[128,1152]{1,0:T(8,128)(2,1)S(1)} %copy-done.1, f32[128,1152]{1,0:T(8,128)S(1)} %get-tuple-element.73.own_ref, bf16[128,1152]{1,0:T(8,128)(2,1)S(1)} %collective-permute-done.18.ring_ref, bf16[128,1152]{1,0:T(8,128)(2,1)S(1)} %collective-permute-done.25.far_ref, ...), custom_call_target="tpu_custom_call" | custom-call | tf_op jit(solution)/shard_map/finish/pallas_call | solution.py:260
  (35 shorter events, 0.3 us)
Async XLA Ops:
  2.6 8.9 %collective-permute-start = (bf16[128,1152]{1,0:T(8,128)(2,1)}, bf16[128,1152]{1,0:T(8,128)(2,1)S(1)}, u32[]{:S(2)}, u32[]{:S(2)}) collective-permute-start(bf16[128,1152]{1,0:T(8,128)(2,1)} %get-tuple-element.52), channel_id=1, source_target_pairs={{16,0},{17,1},{18,2},{19,3},{20,4},{21,5},{22,6},{23,7},{24,8},{25... | collective-permute-start | bytes 884744 | tf_op jit(solution)/shard_map/ppermute | solution.py:33
  4.3 21.5 %copy-start.3 = (bf16[128,1152]{1,0:T(8,128)(2,1)S(1)}, bf16[128,1152]{1,0:T(8,128)(2,1)}, u32[]{:S(2)}) copy-start(bf16[128,1152]{1,0:T(8,128)(2,1)} %get-tuple-element.52) | copy-start | bytes 884740
  4.3 9.9 %collective-permute-start.1 = (bf16[128,1152]{1,0:T(8,128)(2,1)}, bf16[128,1152]{1,0:T(8,128)(2,1)S(1)}, u32[]{:S(2)}, u32[]{:S(2)}) collective-permute-start(bf16[128,1152]{1,0:T(8,128)(2,1)} %get-tuple-element.53), channel_id=1, source_target_pairs={{20,0},{21,1},{22,2},{23,3},{16,4},{17,5},{18,6},{19,7},{28,8},{29... | collective-permute-start | bytes 884744 | tf_op jit(solution)/shard_map/ppermute | solution.py:33
  14.2 8.2 %collective-permute-start.2 = (bf16[128,1152]{1,0:T(8,128)(2,1)S(1)}, bf16[128,1152]{1,0:T(8,128)(2,1)S(1)}, u32[]{:S(2)}, u32[]{:S(2)}) collective-permute-start(bf16[128,1152]{1,0:T(8,128)(2,1)S(1)} %collective-permute-done), channel_id=1, source_target_pairs={{32,0},{33,1},{34,2},{35,3},{36,4},{37,5},{38,6},{39,7},{40,8},{41... | collective-permute-start | bytes 884744 | tf_op jit(solution)/shard_map/ppermute | solution.py:33
  16.1 8.5 %collective-permute-start.3 = (bf16[128,1152]{1,0:T(8,128)(2,1)S(1)}, bf16[128,1152]{1,0:T(8,128)(2,1)S(1)}, u32[]{:S(2)}, u32[]{:S(2)}) collective-permute-start(bf16[128,1152]{1,0:T(8,128)(2,1)S(1)} %collective-permute-done.1), channel_id=1, source_target_pairs={{96,0},{97,1},{98,2},{99,3},{100,4},{101,5},{102,6},{103,7},{104,8... | collective-permute-start | bytes 884744 | tf_op jit(solution)/shard_map/ppermute | solution.py:33
  18.6 7.2 %collective-permute-start.4 = (bf16[128,1152]{1,0:T(8,128)(2,1)}, bf16[128,1152]{1,0:T(8,128)(2,1)S(1)}, u32[]{:S(2)}, u32[]{:S(2)}) collective-permute-start(bf16[128,1152]{1,0:T(8,128)(2,1)} %get-tuple-element.52), channel_id=1, source_target_pairs={{1,0},{0,1},{3,2},{2,3},{5,4},{4,5},{7,6},{6,7},{9,8},{8,9},{11,10... | collective-permute-start | bytes 884744 | tf_op jit(solution)/shard_map/ppermute | solution.py:33
  20.2 8.1 %collective-permute-start.5 = (bf16[128,1152]{1,0:T(8,128)(2,1)}, bf16[128,1152]{1,0:T(8,128)(2,1)S(1)}, u32[]{:S(2)}, u32[]{:S(2)}) collective-permute-start(bf16[128,1152]{1,0:T(8,128)(2,1)} %get-tuple-element.53), channel_id=1, source_target_pairs={{3,0},{2,1},{1,2},{0,3},{7,4},{6,5},{5,6},{4,7},{11,8},{10,9},{9,1... | collective-permute-start | bytes 884744 | tf_op jit(solution)/shard_map/ppermute | solution.py:33
  22.4 5.9 %copy-start.2 = (bf16[128,1152]{1,0:T(8,128)(2,1)S(1)}, bf16[128,1152]{1,0:T(8,128)(2,1)}, u32[]{:S(2)}) copy-start(bf16[128,1152]{1,0:T(8,128)(2,1)} %get-tuple-element.53) | copy-start | bytes 884740
  28.4 12.0 %collective-permute-start.6 = (bf16[256,1152]{1,0:T(8,128)(2,1)S(1)}, bf16[256,1152]{1,0:T(8,128)(2,1)S(1)}, u32[]{:S(2)}, u32[]{:S(2)}) collective-permute-start(bf16[256,1152]{1,0:T(8,128)(2,1)S(1)} %pad_maximum_fusion.2.refs_0_), channel_id=1, source_target_pairs={{32,0},{33,1},{34,2},{35,3},{36,4},{37,5},{38,6},{39,7},{40,8},{41... | collective-permute-start | bytes 1769480 | tf_op jit(solution)/shard_map/ppermute | solution.py:33
  29.5 11.6 %collective-permute-start.7 = (bf16[256,1152]{1,0:T(8,128)(2,1)S(1)}, bf16[256,1152]{1,0:T(8,128)(2,1)S(1)}, u32[]{:S(2)}, u32[]{:S(2)}) collective-permute-start(bf16[256,1152]{1,0:T(8,128)(2,1)S(1)} %pad_maximum_fusion.refs_1_), channel_id=1, source_target_pairs={{1,0},{0,1},{3,2},{2,3},{5,4},{4,5},{7,6},{6,7},{9,8},{8,9},{11,10... | collective-permute-start | bytes 1769480 | tf_op jit(solution)/shard_map/ppermute | solution.py:33
  29.5 13.1 %collective-permute-start.8 = (bf16[256,1152]{1,0:T(8,128)(2,1)S(1)}, bf16[256,1152]{1,0:T(8,128)(2,1)}, u32[]{:S(2)}, u32[]{:S(2)}) collective-permute-start(bf16[256,1152]{1,0:T(8,128)(2,1)S(1)} %pad_maximum_fusion.3.refs_4_.refs_0_), channel_id=1, source_target_pairs={{96,0},{97,1},{98,2},{99,3},{100,4},{101,5},{102,6},{103,7},{104,8... | collective-permute-start | bytes 1769480 | tf_op jit(solution)/shard_map/ppermute | solution.py:33
  30.4 13.2 %collective-permute-start.9 = (bf16[256,1152]{1,0:T(8,128)(2,1)S(1)}, bf16[256,1152]{1,0:T(8,128)(2,1)}, u32[]{:S(2)}, u32[]{:S(2)}) collective-permute-start(bf16[256,1152]{1,0:T(8,128)(2,1)S(1)} %pad_maximum_fusion.1.refs_5_.refs_1_), channel_id=1, source_target_pairs={{3,0},{2,1},{1,2},{0,3},{7,4},{6,5},{5,6},{4,7},{11,8},{10,9},{9,1... | collective-permute-start | bytes 1769480 | tf_op jit(solution)/shard_map/ppermute | solution.py:33
  32.6 18.1 %collective-permute-start.10 = (bf16[256,1152]{1,0:T(8,128)(2,1)S(1)}, bf16[256,1152]{1,0:T(8,128)(2,1)}, u32[]{:S(2)}, u32[]{:S(2)}) collective-permute-start(bf16[256,1152]{1,0:T(8,128)(2,1)S(1)} %pad_maximum_fusion.3.refs_4_.refs_0_), channel_id=1, source_target_pairs={{8,0},{9,1},{10,2},{11,3},{12,4},{13,5},{14,6},{15,7},{0,8},{1,9},... | collective-permute-start | bytes 1769480 | tf_op jit(solution)/shard_map/ppermute | solution.py:33
  43.5 7.2 %collective-permute-start.12 = (bf16[256,1152]{1,0:T(8,128)(2,1)}, bf16[256,1152]{1,0:T(8,128)(2,1)}, u32[]{:S(2)}, u32[]{:S(2)}) collective-permute-start(bf16[256,1152]{1,0:T(8,128)(2,1)} %collective-permute-done.8.refs_6_.refs_2_), channel_id=1, source_target_pairs={{8,0},{9,1},{10,2},{11,3},{12,4},{13,5},{14,6},{15,7},{0,8},{1,9},... | collective-permute-start | bytes 1769480 | tf_op jit(solution)/shard_map/ppermute | solution.py:33
  43.5 7.2 %collective-permute-start.11 = (bf16[256,1152]{1,0:T(8,128)(2,1)S(1)}, bf16[256,1152]{1,0:T(8,128)(2,1)}, u32[]{:S(2)}, u32[]{:S(2)}) collective-permute-start(bf16[256,1152]{1,0:T(8,128)(2,1)S(1)} %pad_maximum_fusion.1.refs_5_.refs_1_), channel_id=1, source_target_pairs={{8,0},{9,1},{10,2},{11,3},{12,4},{13,5},{14,6},{15,7},{0,8},{1,9},... | collective-permute-start | bytes 1769480 | tf_op jit(solution)/shard_map/ppermute | solution.py:33
  44.0 6.7 %collective-permute-start.13 = (bf16[256,1152]{1,0:T(8,128)(2,1)}, bf16[256,1152]{1,0:T(8,128)(2,1)}, u32[]{:S(2)}, u32[]{:S(2)}) collective-permute-start(bf16[256,1152]{1,0:T(8,128)(2,1)} %collective-permute-done.9.refs_7_.refs_3_), channel_id=1, source_target_pairs={{8,0},{9,1},{10,2},{11,3},{12,4},{13,5},{14,6},{15,7},{0,8},{1,9},... | collective-permute-start | bytes 1769480 | tf_op jit(solution)/shard_map/ppermute | solution.py:33
  59.6 6.7 %collective-permute-start.16 = (bf16[512,1152]{1,0:T(8,128)(2,1)S(1)}, bf16[512,1152]{1,0:T(8,128)(2,1)S(1)}, u32[]{:S(2)}, u32[]{:S(2)}) collective-permute-start(bf16[512,1152]{1,0:T(8,128)(2,1)S(1)} %get-tuple-element.71), channel_id=1, source_target_pairs={{8,0},{9,1},{10,2},{11,3},{12,4},{13,5},{14,6},{15,7},{0,8},{1,9},... | collective-permute-start | bytes 3538952 | tf_op jit(solution)/shard_map/ppermute | solution.py:33
  60.2 17.9 %collective-permute-start.14 = (bf16[512,1152]{1,0:T(8,128)(2,1)S(1)}, bf16[512,1152]{1,0:T(8,128)(2,1)S(1)}, u32[]{:S(2)}, u32[]{:S(2)}) collective-permute-start(bf16[512,1152]{1,0:T(8,128)(2,1)S(1)} %get-tuple-element.66), channel_id=1, source_target_pairs={{8,0},{9,1},{10,2},{11,3},{12,4},{13,5},{14,6},{15,7},{0,8},{1,9},... | collective-permute-start | bytes 3538952 | tf_op jit(solution)/shard_map/ppermute | solution.py:33
  60.3 6.0 %collective-permute-start.15 = (f32[8,128]{1,0:T(8,128)S(1)}, f32[8,128]{1,0:T(8,128)S(1)}, u32[]{:S(2)}, u32[]{:S(2)}) collective-permute-start(f32[8,128]{1,0:T(8,128)S(1)} %get-tuple-element.68), channel_id=1, source_target_pairs={{8,0},{9,1},{10,2},{11,3},{12,4},{13,5},{14,6},{15,7},{0,8},{1,9},... | collective-permute-start | bytes 12296 | tf_op jit(solution)/shard_map/ppermute | solution.py:33
  65.6 15.4 %collective-permute-start.30 = (bf16[256,1152]{1,0:T(8,128)(2,1)S(1)}, bf16[256,1152]{1,0:T(8,128)(2,1)S(1)}, u32[]{:S(2)}, u32[]{:S(2)}) collective-permute-start(bf16[256,1152]{1,0:T(8,128)(2,1)S(1)} %get-tuple-element.62), channel_id=1, source_target_pairs={{1,0},{0,1},{3,2},{2,3},{5,4},{4,5},{7,6},{6,7},{9,8},{8,9},{11,10... | collective-permute-start | bytes 1769480 | tf_op jit(solution)/shard_map/ppermute | solution.py:33
  68.6 16.3 %collective-permute-start.19 = (bf16[256,1152]{1,0:T(8,128)(2,1)S(1)}, bf16[256,1152]{1,0:T(8,128)(2,1)S(1)}, u32[]{:S(2)}, u32[]{:S(2)}) collective-permute-start(bf16[256,1152]{1,0:T(8,128)(2,1)S(1)} %get-tuple-element.76), channel_id=1, source_target_pairs={{3,0},{2,1},{1,2},{0,3},{7,4},{6,5},{5,6},{4,7},{11,8},{10,9},{9,1... | collective-permute-start | bytes 1769480 | tf_op jit(solution)/shard_map/ppermute | solution.py:33
  70.8 16.6 %collective-permute-start.22 = (bf16[256,1152]{1,0:T(8,128)(2,1)S(1)}, bf16[256,1152]{1,0:T(8,128)(2,1)S(1)}, u32[]{:S(2)}, u32[]{:S(2)}) collective-permute-start(bf16[256,1152]{1,0:T(8,128)(2,1)S(1)} %get-tuple-element.69), channel_id=1, source_target_pairs={{32,0},{33,1},{34,2},{35,3},{36,4},{37,5},{38,6},{39,7},{40,8},{41... | collective-permute-start | bytes 1769480 | tf_op jit(solution)/shard_map/ppermute | solution.py:33
  70.9 17.0 %collective-permute-start.17 = (bf16[256,1152]{1,0:T(8,128)(2,1)S(1)}, bf16[256,1152]{1,0:T(8,128)(2,1)S(1)}, u32[]{:S(2)}, u32[]{:S(2)}) collective-permute-start(bf16[256,1152]{1,0:T(8,128)(2,1)S(1)} %get-tuple-element.72), channel_id=1, source_target_pairs={{96,0},{97,1},{98,2},{99,3},{100,4},{101,5},{102,6},{103,7},{104,8... | collective-permute-start | bytes 1769480 | tf_op jit(solution)/shard_map/ppermute | solution.py:33
  80.0 3.7 %collective-permute-start.20 = (f32[8,128]{1,0:T(8,128)S(1)}, f32[8,128]{1,0:T(8,128)S(1)}, u32[]{:S(2)}, u32[]{:S(2)}) collective-permute-start(f32[8,128]{1,0:T(8,128)S(1)} %add.22), channel_id=1, source_target_pairs={{1,0},{0,1},{3,2},{2,3},{5,4},{4,5},{7,6},{6,7},{9,8},{8,9},{11,10... | collective-permute-start | bytes 12296 | tf_op jit(solution)/shard_map/ppermute | solution.py:33
  81.5 15.2 %collective-permute-start.31 = (bf16[128,1152]{1,0:T(8,128)(2,1)S(1)}, bf16[128,1152]{1,0:T(8,128)(2,1)S(1)}, u32[]{:S(2)}, u32[]{:S(2)}) collective-permute-start(bf16[128,1152]{1,0:T(8,128)(2,1)S(1)} %get-tuple-element.89), channel_id=1, source_target_pairs={{32,0},{33,1},{34,2},{35,3},{36,4},{37,5},{38,6},{39,7},{40,8},{41... | collective-permute-start | bytes 884744 | tf_op jit(solution)/shard_map/ppermute | solution.py:33
  85.3 11.7 %collective-permute-start.21 = (bf16[128,1152]{1,0:T(8,128)(2,1)S(1)}, bf16[128,1152]{1,0:T(8,128)(2,1)S(1)}, u32[]{:S(2)}, u32[]{:S(2)}) collective-permute-start(bf16[128,1152]{1,0:T(8,128)(2,1)S(1)} %get-tuple-element.80), channel_id=1, source_target_pairs={{96,0},{97,1},{98,2},{99,3},{100,4},{101,5},{102,6},{103,7},{104,8... | collective-permute-start | bytes 884744 | tf_op jit(solution)/shard_map/ppermute | solution.py:33
  88.3 3.7 %collective-permute-start.23 = (f32[8,128]{1,0:T(8,128)S(1)}, f32[8,128]{1,0:T(8,128)S(1)}, u32[]{:S(2)}, u32[]{:S(2)}) collective-permute-start(f32[8,128]{1,0:T(8,128)S(1)} %add.23), channel_id=1, source_target_pairs={{16,0},{17,1},{18,2},{19,3},{20,4},{21,5},{22,6},{23,7},{24,8},{25... | collective-permute-start | bytes 12296 | tf_op jit(solution)/shard_map/ppermute | solution.py:33
  92.0 5.0 %collective-permute-start.24 = (f32[8,128]{1,0:T(8,128)S(1)}, f32[8,128]{1,0:T(8,128)S(1)}, u32[]{:S(2)}, u32[]{:S(2)}) collective-permute-start(f32[8,128]{1,0:T(8,128)S(1)} %add.24), channel_id=1, source_target_pairs={{20,0},{21,1},{22,2},{23,3},{16,4},{17,5},{18,6},{19,7},{28,8},{29... | collective-permute-start | bytes 12296 | tf_op jit(solution)/shard_map/ppermute | solution.py:33
  94.1 15.1 %collective-permute-start.29 = (bf16[128,1152]{1,0:T(8,128)(2,1)S(1)}, bf16[128,1152]{1,0:T(8,128)(2,1)S(1)}, u32[]{:S(2)}, u32[]{:S(2)}) collective-permute-start(bf16[128,1152]{1,0:T(8,128)(2,1)S(1)} %get-tuple-element.86), channel_id=1, source_target_pairs={{1,0},{0,1},{3,2},{2,3},{5,4},{4,5},{7,6},{6,7},{9,8},{8,9},{11,10... | collective-permute-start | bytes 884744 | tf_op jit(solution)/shard_map/ppermute | solution.py:33
  94.5 16.1 %collective-permute-start.18 = (bf16[128,1152]{1,0:T(8,128)(2,1)S(1)}, bf16[128,1152]{1,0:T(8,128)(2,1)S(1)}, u32[]{:S(2)}, u32[]{:S(2)}) collective-permute-start(bf16[128,1152]{1,0:T(8,128)(2,1)S(1)} %get-tuple-element.74), channel_id=1, source_target_pairs={{3,0},{2,1},{1,2},{0,3},{7,4},{6,5},{5,6},{4,7},{11,8},{10,9},{9,1... | collective-permute-start | bytes 884744 | tf_op jit(solution)/shard_map/ppermute | solution.py:33
  96.7 12.6 %copy-start = (bf16[128,1152]{1,0:T(8,128)(2,1)S(1)}, bf16[128,1152]{1,0:T(8,128)(2,1)}, u32[]{:S(2)}) copy-start(bf16[128,1152]{1,0:T(8,128)(2,1)} %raw_ref.3) | copy-start | bytes 884740
  96.9 12.3 %collective-permute-start.32 = (bf16[128,1152]{1,0:T(8,128)(2,1)S(1)}, bf16[128,1152]{1,0:T(8,128)(2,1)S(1)}, u32[]{:S(2)}, u32[]{:S(2)}) collective-permute-start(bf16[128,1152]{1,0:T(8,128)(2,1)S(1)} %add_codes.3), channel_id=1, source_target_pairs={{16,0},{17,1},{18,2},{19,3},{20,4},{21,5},{22,6},{23,7},{24,8},{25... | collective-permute-start | bytes 884744 | tf_op jit(solution)/shard_map/ppermute | solution.py:33
  97.1 15.5 %copy-start.1 = (bf16[128,1152]{1,0:T(8,128)(2,1)S(1)}, bf16[128,1152]{1,0:T(8,128)(2,1)}, u32[]{:S(2)}) copy-start(bf16[128,1152]{1,0:T(8,128)(2,1)} %raw_ref.2) | copy-start | bytes 884740
  97.4 15.2 %collective-permute-start.25 = (bf16[128,1152]{1,0:T(8,128)(2,1)S(1)}, bf16[128,1152]{1,0:T(8,128)(2,1)S(1)}, u32[]{:S(2)}, u32[]{:S(2)}) collective-permute-start(bf16[128,1152]{1,0:T(8,128)(2,1)S(1)} %add_codes.2), channel_id=1, source_target_pairs={{20,0},{21,1},{22,2},{23,3},{16,4},{17,5},{18,6},{19,7},{28,8},{29... | collective-permute-start | bytes 884744 | tf_op jit(solution)/shard_map/ppermute | solution.py:33
  99.3 3.6 %collective-permute-start.26 = (f32[8,128]{1,0:T(8,128)S(1)}, f32[8,128]{1,0:T(8,128)S(1)}, u32[]{:S(2)}, u32[]{:S(2)}) collective-permute-start(f32[8,128]{1,0:T(8,128)S(1)} %add.25), channel_id=1, source_target_pairs={{32,0},{33,1},{34,2},{35,3},{36,4},{37,5},{38,6},{39,7},{40,8},{41... | collective-permute-start | bytes 12296 | tf_op jit(solution)/shard_map/ppermute | solution.py:33
  102.9 4.8 %collective-permute-start.27 = (f32[8,128]{1,0:T(8,128)S(1)}, f32[8,128]{1,0:T(8,128)S(1)}, u32[]{:S(2)}, u32[]{:S(2)}) collective-permute-start(f32[8,128]{1,0:T(8,128)S(1)} %add.26), channel_id=1, source_target_pairs={{3,0},{2,1},{1,2},{0,3},{7,4},{6,5},{5,6},{4,7},{11,8},{10,9},{9,1... | collective-permute-start | bytes 12296 | tf_op jit(solution)/shard_map/ppermute | solution.py:33
  107.7 4.8 %collective-permute-start.28 = (f32[8,128]{1,0:T(8,128)S(1)}, f32[8,128]{1,0:T(8,128)S(1)}, u32[]{:S(2)}, u32[]{:S(2)}) collective-permute-start(f32[8,128]{1,0:T(8,128)S(1)} %add.27.loss_ref.loss_in), channel_id=1, source_target_pairs={{96,0},{97,1},{98,2},{99,3},{100,4},{101,5},{102,6},{103,7},{104,8... | collective-permute-start | bytes 12296 | tf_op jit(solution)/shard_map/ppermute | solution.py:33

commit v3 on v2

--- a/solution.py
+++ b/solution.py
@@ -72,7 +72,10 @@
     return [sum(pairs[axis] for axis in axes) for axes in ROWS]
 
 
-def logit_kernel(core, loss_scale, place_ref, scale_ref, bias_ref, *refs):
+ORDER = (2, 3, 0, 1)
+
+
+def logit_kernel(core, loss_scale, place_ref, temper_ref, shift_ref, *refs):
     image_refs, text_refs = refs[:4], refs[4:8]
     if core:
         loss_in, coeff_ref, other_refs, loss_ref = refs[8], refs[9], refs[10:12], refs[12]
@@ -88,16 +91,21 @@
         flat = lax.bitwise_xor(place, mask ^ core)
         text_base.append((lax.rem(flat, 8) * 16 + lax.div(flat, 8)) * PIECE)
 
-    temper = jnp.exp(jnp.full((1, PIECE), scale_ref[0], jnp.float32))
+    temper = jnp.broadcast_to(temper_ref[...], (1, PIECE))
     slope = temper * LOG2E
-    shift = jnp.full((1, PIECE), bias_ref[0] * LOG2E, jnp.float32)
+    shift = jnp.broadcast_to(shift_ref[...], (1, PIECE))
     apart = lax.broadcasted_iota(jnp.int32, (PIECE, PIECE), 0) - lax.broadcasted_iota(
         jnp.int32, (PIECE, PIECE), 1
     )
     quarter = PIECE // 4
     loss_sum = jnp.zeros((8, PIECE), jnp.float32)
     own_sum = jnp.zeros((8, PIECE), jnp.float32)
-    for t in (2, 3, 0, 1):
+    def put_shares(t):
+        other_refs[t // 2][t % 2 * rows : (t % 2 + 1) * rows, :] = encode(
+            text_shares(coeff_ref, t * rows, image_refs)
+        )
+
+    for n, t in enumerate(ORDER):
         left = t * rows
         for r, image_ref in enumerate(image_refs):
             dots = lax.dot_general(image_ref[...], text_refs[t][...], NT, preferred_element_type=jnp.float32)
@@ -119,10 +127,10 @@
                         loss_sum = loss_sum + terms[k * 8 : (k + 1) * 8]
                     for k in range(PIECE // 8):
                         own_sum = own_sum + chosen[k * 8 : (k + 1) * 8]
-        if core:
-            other_refs[t // 2][t % 2 * rows : (t % 2 + 1) * rows, :] = encode(
-                text_shares(coeff_ref, left, image_refs)
-            )
+        if core and n:
+            put_shares(ORDER[n - 1])
+    if core:
+        put_shares(ORDER[-1])
     loss = loss_sum - LN2 * own_sum
     if core:
         total = jnp.sum(loss + loss_in[...], keepdims=True) * loss_scale
@@ -145,17 +153,17 @@
     return part
 
 
-def logit_terms(place, logit_scale, bias, images, texts, core=0, loss=None, loss_scale=None):
+def logit_terms(scalars, images, texts, core=0, loss=None, loss_scale=None):
     rows, depth = images[0].shape
     height, count = len(images) * rows, len(texts) * rows
     coeff, loss_tile = shape_of(height, count, jnp.bfloat16), shape_of(8, PIECE, jnp.float32)
     shares = [shape_of(2 * rows, depth, jnp.bfloat16)] * 2 if core else []
-    operands = (place, logit_scale, bias, *images, *texts) + ((loss,) if core else ())
+    operands = (*scalars, *images, *texts) + ((loss,) if core else ())
     out_shape = [coeff, *shares, loss_tile]
     outs = pl.pallas_call(
         functools.partial(logit_kernel, core, loss_scale),
         out_shape=out_shape,
-        in_specs=[SMEM, SMEM, SMEM] + [VMEM] * (len(operands) - 3),
+        in_specs=[SMEM] + [VMEM] * (len(operands) - 1),
         out_specs=[VMEM] * len(out_shape),
         compiler_params=pltpu.CompilerParams(vmem_limit_bytes=PAIR_VMEM),
         cost_estimate=cost((2 if core else 1) * height * count * depth),
@@ -267,10 +275,10 @@
     )(raw, own, ring, far, loss, loss_in)
 
 
-def gather(image, text):
+def gather(image, text, scalars):
     groups = ((image, IMAGE_PAIRS), (text, TEXT_PAIRS))
     far = [swap(unit, pairs["x"]) for unit, pairs in groups]
-    *far, image, text = lax.optimization_barrier((*far, image, text))
+    *far, image, text, scalars = lax.optimization_barrier((*far, image, text, scalars))
     groups = ((image, IMAGE_PAIRS), (text, TEXT_PAIRS))
     far = [jnp.concatenate([part, swap(part, pairs["z"])], axis=0) for part, (_, pairs) in zip(far, groups)]
     near = [jnp.concatenate([unit, swap(unit, pairs["y"])], axis=0) for unit, pairs in groups]
@@ -279,7 +287,7 @@
     near_late = [swap(part, pairs["z"]) for part, (_, pairs) in zip(near, groups)]
     images, texts = ([near[k], far[k], near_late[k], far_late[k]] for k in range(2))
     late_core = [after(far[1], *near_late, *far_late), *texts[2:]]
-    return images, texts + [swap(part, CORE) for part in (near[1], *late_core)]
+    return images, texts + [swap(part, CORE) for part in (near[1], *late_core)], scalars
 
 
 def after(value, *others):
@@ -288,31 +296,31 @@
 
 def shards(images, texts, logit_scale, bias):
     place = (lax.axis_index("img") * lax.axis_size("txt") + lax.axis_index("txt")).astype(jnp.int32).reshape(1)
-    image_all, text_all = gather(*unit_rows(images, texts))
+    scalars = (place, jnp.exp(logit_scale).reshape(1, 1), (bias * LOG2E).reshape(1, 1))
+    image_all, text_all, scalars = gather(*unit_rows(images, texts), scalars)
     count = images.shape[0] * lax.axis_size("img") * lax.axis_size("txt")
-    own_coeff, _, loss = logit_terms(place, logit_scale, bias, image_all, text_all[:4])
-    other_coeff, other, loss = logit_terms(
-        place, logit_scale, bias, image_all, text_all[4:], CORE, loss, 1.0 / count
-    )
+    own_coeff, _, loss = logit_terms(scalars, image_all, text_all[:4])
+    other_coeff, other, loss = logit_terms(scalars, image_all, text_all[4:], CORE, loss, 1.0 / count)
     coeffs = (own_coeff, other_coeff)
 
     other_late = swap(other[1], CORE)
+    other_early = swap(other[0], CORE)
     loss = loss + swap(loss, CORE)
     near_late, far_late = image_terms(4 * PIECE, 2, jnp.bfloat16, coeffs, text_all)
     image_far = swap(far_late, IMAGE_PAIRS["y"])
     image_near = swap(near_late, IMAGE_PAIRS["z"])
     text_near, text_far = text_terms(
-        4 * PIECE, jnp.bfloat16, after(own_coeff, loss, near_late), other_late, image_all
+        4 * PIECE, jnp.bfloat16, after(own_coeff, loss, near_late, other_early), other_late, image_all
     )
     text_far = swap(text_far, TEXT_PAIRS["y"])
     text_near = swap(text_near, TEXT_PAIRS["z"])
-    other_early = swap(other[0], CORE)
+    tiles = swap(jnp.broadcast_to(loss[None], (64, *loss.shape)), IMAGE_PAIRS["x"])
     near_early, far_early = image_terms(0, 2, jnp.float32, (after(own_coeff, far_late), other_coeff), text_all)
     text_early = text_terms(0, jnp.float32, after(own_coeff, near_early), other_early, image_all)
 
     image_kept, image_sent = fold(far_early, image_far)
     image_far = swap(image_sent, IMAGE_PAIRS["z"])
-    loss = after(loss, text_early[0])
+    loss = after(loss, text_early[0]) + tiles[0]
     loss = loss + swap(loss, IMAGE_PAIRS["y"])
     text_kept, text_sent = fold(text_early[1], after(text_far, loss))
     text_far = swap(text_sent, TEXT_PAIRS["z"])
@@ -321,14 +329,12 @@
     text_own, text_sent = fold(text_early[0], text_near)
     text_near = swap(text_sent, TEXT_PAIRS["y"])
 
-    loss = after(loss, text_kept, image_own, text_own)
-    loss = loss + swap(loss, IMAGE_PAIRS["x"])
-    image_sent = add_codes(image_kept, after(image_far, loss))
+    loss = after(loss, text_kept)
     loss = loss + swap(loss, TEXT_PAIRS["x"])
+    image_sent = add_codes(image_kept, image_far)
+    loss = loss + swap(loss, IMAGE_PAIRS["z"])
     text_sent = add_codes(text_kept, after(text_far, loss))
-    loss = after(loss, text_sent)
-    for mask in (IMAGE_PAIRS["z"], TEXT_PAIRS["y"]):
-        loss = loss + swap(loss, mask)
+    loss = loss + swap(after(loss, text_sent), TEXT_PAIRS["y"])
     last = swap(loss, TEXT_PAIRS["z"])
     image_grad, _ = finish(images, image_own, image_near, swap(image_sent, IMAGE_PAIRS["x"]), loss, loss)
     text_grad, loss = finish(texts, text_own, text_near, swap(text_sent, TEXT_PAIRS["x"]), loss, last)

time: 114 us -> 105 us (0.921)
  Pallas kernels: 35.2 us -> 28.3 us
  starting transfers between devices: 38.1 us -> 33 us
  waiting for transfers between devices: 38.3 us -> 39.8 us
    ppermute x33, starting transfers between devices: 38.1 us -> 33 us  [swap(): lax.ppermute(value, axes, [(k ^ mask, k) for k in range(lax.axis_size(axe...]
    pallas_call x2, Pallas kernels: 9.72 us -> 5.81 us  [image_terms(): pl.pallas_call(functools.partial(image_kernel, first), out_shape=[shape_o...]
    pallas_call x2, Pallas kernels: 14.2 us -> 11.2 us  [logit_terms(): pl.pallas_call(functools.partial(logit_kernel, core, loss_scale), out_sha...]
    ppermute x33, waiting for transfers between devices: 38.3 us -> 39.8 us  [swap(): lax.ppermute(value, axes, [(k ^ mask, k) for k in range(lax.axis_size(axe...]
  transfers between devices with their start and end apart: 33 -> 33, of which waited for: 16 -> 17; matrix products, arithmetic and copies ran while one was open for 0% -> 1% of each run, Pallas kernels for 20% -> 17%
where the time goes in v3:
time: 105 us
  waiting for transfers between devices  39.8 us (38%)
  starting transfers between devices  33 us (31%)
  Pallas kernels  28.3 us (27%)
  between operations  2.39 us (2%)
  other arithmetic  1.16 us (1%)
    ppermute x33, waiting for transfers between devices, swap(): lax.ppermute(value, axes, [(k ^ mask, k) for k in range(lax.axis_size(axe...  39.8 us
    ppermute x33, starting transfers between devices, swap(): lax.ppermute(value, axes, [(k ^ mask, k) for k in range(lax.axis_size(axe...  33 us
    pallas_call x2, Pallas kernels, logit_terms(): pl.pallas_call(functools.partial(logit_kernel, core, loss_scale), out_sha...  11.2 us
    pallas_call x2, Pallas kernels, image_terms(): pl.pallas_call(functools.partial(image_kernel, first), out_shape=[shape_o...  5.81 us
    pallas_call x2, Pallas kernels, text_terms(): pl.pallas_call(functools.partial(text_kernel, first), out_shape=[shape_of...  4.06 us
    pallas_call x2, Pallas kernels, finish(): pl.pallas_call(finish_kernel, out_shape=[shape_of(*raw.shape, jnp.float32...  2.86 us
    pallas_call x6, Pallas kernels, small_call(): pl.pallas_call(kernel, out_shape=out_shape, in_specs=[VMEM] * len(operand...  2.31 us
  transfers between devices with their start and end apart: 33, of which 17 were waited for; matrix products, arithmetic and copies ran while one was open for 1% of the time, Pallas kernels for 17%

profile of v3, /device:TPU:0, one launch (start us, length us, event | category | flops | bytes accessed | tf_op | source)
XLA Modules:
  0.0 104.7 jit_solution(17402891369879312408)
XLA Ops:
  0.6 2.0 %unit_rows.1 = (bf16[128,1152]{1,0:T(8,128)(2,1)}, bf16[128,1152]{1,0:T(8,128)(2,1)}) custom-call(bf16[128,1152]{1,0:T(8,128)(2,1)} %raw_ref.3, bf16[128,1152]{1,0:T(8,128)(2,1)} %raw_ref.2), custom_call_target="tpu_custom_call" | custom-call | tf_op jit(solution)/shard_map/unit_rows/pallas_call | solution.py:60
  2.6 0.0 copy-start.2
  2.6 1.7 %collective-permute-start = (bf16[128,1152]{1,0:T(8,128)(2,1)}, bf16[128,1152]{1,0:T(8,128)(2,1)S(1)}, u32[]{:S(2)}, u32[]{:S(2)}) collective-permute-start(bf16[128,1152]{1,0:T(8,128)(2,1)} %get-tuple-element.57), channel_id=1, source_target_pairs={{16,0},{17,1},{18,2},{19,3},{20,4},{21,5},{22,6},{23,7},{24,8},{25... | collective-permute-start | bytes 884744 | tf_op jit(solution)/shard_map/ppermute | solution.py:33
  4.3 2.1 %collective-permute-start.1 = (bf16[128,1152]{1,0:T(8,128)(2,1)}, bf16[128,1152]{1,0:T(8,128)(2,1)S(1)}, u32[]{:S(2)}, u32[]{:S(2)}) collective-permute-start(bf16[128,1152]{1,0:T(8,128)(2,1)} %get-tuple-element.58), channel_id=1, source_target_pairs={{20,0},{21,1},{22,2},{23,3},{16,4},{17,5},{18,6},{19,7},{28,8},{29... | collective-permute-start | bytes 884744 | tf_op jit(solution)/shard_map/ppermute | solution.py:33
  7.7 3.8 %collective-permute-done = bf16[128,1152]{1,0:T(8,128)(2,1)S(1)} collective-permute-done((bf16[128,1152]{1,0:T(8,128)(2,1)}, bf16[128,1152]{1,0:T(8,128)(2,1)S(1)}, u32[]{:S(2)}, u32[]{:S(2)}) %collective-permute-start) | collective-permute-done | bytes 294944 | tf_op jit(solution)/shard_map/ppermute | solution.py:33
  11.5 2.7 %collective-permute-done.1 = bf16[128,1152]{1,0:T(8,128)(2,1)S(1)} collective-permute-done((bf16[128,1152]{1,0:T(8,128)(2,1)}, bf16[128,1152]{1,0:T(8,128)(2,1)S(1)}, u32[]{:S(2)}, u32[]{:S(2)}) %collective-permute-start.1) | collective-permute-done | bytes 294944 | tf_op jit(solution)/shard_map/ppermute | solution.py:33
  14.2 1.6 %collective-permute-start.4 = (bf16[128,1152]{1,0:T(8,128)(2,1)}, bf16[128,1152]{1,0:T(8,128)(2,1)S(1)}, u32[]{:S(2)}, u32[]{:S(2)}) collective-permute-start(bf16[128,1152]{1,0:T(8,128)(2,1)} %get-tuple-element.57), channel_id=1, source_target_pairs={{1,0},{0,1},{3,2},{2,3},{5,4},{4,5},{7,6},{6,7},{9,8},{8,9},{11,10... | collective-permute-start | bytes 884744 | tf_op jit(solution)/shard_map/ppermute | solution.py:33
  15.8 2.2 %collective-permute-start.5 = (bf16[128,1152]{1,0:T(8,128)(2,1)}, bf16[128,1152]{1,0:T(8,128)(2,1)S(1)}, u32[]{:S(2)}, u32[]{:S(2)}) collective-permute-start(bf16[128,1152]{1,0:T(8,128)(2,1)} %get-tuple-element.58), channel_id=1, source_target_pairs={{3,0},{2,1},{1,2},{0,3},{7,4},{6,5},{5,6},{4,7},{11,8},{10,9},{9,1... | collective-permute-start | bytes 884744 | tf_op jit(solution)/shard_map/ppermute | solution.py:33
  17.9 4.0 %collective-permute-start.3 = (bf16[128,1152]{1,0:T(8,128)(2,1)S(1)}, bf16[128,1152]{1,0:T(8,128)(2,1)S(1)}, u32[]{:S(2)}, u32[]{:S(2)}) collective-permute-start(bf16[128,1152]{1,0:T(8,128)(2,1)S(1)} %collective-permute-done.1), channel_id=1, source_target_pairs={{96,0},{97,1},{98,2},{99,3},{100,4},{101,5},{102,6},{103,7},{104,8... | collective-permute-start | bytes 884744 | tf_op jit(solution)/shard_map/ppermute | solution.py:33
  22.0 1.0 pad_maximum_fusion.2.refs_0_
  23.0 1.5 %collective-permute-done.5 = bf16[128,1152]{1,0:T(8,128)(2,1)S(1)} collective-permute-done((bf16[128,1152]{1,0:T(8,128)(2,1)}, bf16[128,1152]{1,0:T(8,128)(2,1)S(1)}, u32[]{:S(2)}, u32[]{:S(2)}) %collective-permute-start.5) | collective-permute-done | bytes 294944 | tf_op jit(solution)/shard_map/ppermute | solution.py:33
  24.5 2.7 %collective-permute-done.3 = bf16[128,1152]{1,0:T(8,128)(2,1)S(1)} collective-permute-done((bf16[128,1152]{1,0:T(8,128)(2,1)S(1)}, bf16[128,1152]{1,0:T(8,128)(2,1)S(1)}, u32[]{:S(2)}, u32[]{:S(2)}) %collective-permute-start.3) | collective-permute-done | bytes 294944 | tf_op jit(solution)/shard_map/ppermute | solution.py:33
  27.3 1.7 %collective-permute-done.2 = bf16[128,1152]{1,0:T(8,128)(2,1)S(1)} collective-permute-done((bf16[128,1152]{1,0:T(8,128)(2,1)S(1)}, bf16[128,1152]{1,0:T(8,128)(2,1)S(1)}, u32[]{:S(2)}, u32[]{:S(2)}) %collective-permute-start.2) | collective-permute-done | bytes 294944 | tf_op jit(solution)/shard_map/ppermute | solution.py:33
  29.0 0.1 collective-permute-start.6
  29.2 0.7 collective-permute-start.7
  29.9 1.3 %collective-permute-start.8 = (bf16[256,1152]{1,0:T(8,128)(2,1)S(1)}, bf16[256,1152]{1,0:T(8,128)(2,1)S(1)}, u32[]{:S(2)}, u32[]{:S(2)}) collective-permute-start(bf16[256,1152]{1,0:T(8,128)(2,1)S(1)} %pad_maximum_fusion.3.refs_4_.refs_0_), channel_id=1, source_target_pairs={{96,0},{97,1},{98,2},{99,3},{100,4},{101,5},{102,6},{103,7},{104,8... | collective-permute-start | bytes 1769480 | tf_op jit(solution)/shard_map/ppermute | solution.py:33
  31.2 0.9 collective-permute-start.9
  32.0 9.3 %collective-permute-done.6.refs_2_ = bf16[256,1152]{1,0:T(8,128)(2,1)S(1)} collective-permute-done((bf16[256,1152]{1,0:T(8,128)(2,1)S(1)}, bf16[256,1152]{1,0:T(8,128)(2,1)S(1)}, u32[]{:S(2)}, u32[]{:S(2)}) %collective-permute-start.6) | collective-permute-done | bytes 589856 | tf_op jit(solution)/shard_map/ppermute | solution.py:33
  41.3 1.5 %collective-permute-done.8.refs_6_.refs_2_ = bf16[256,1152]{1,0:T(8,128)(2,1)S(1)} collective-permute-done((bf16[256,1152]{1,0:T(8,128)(2,1)S(1)}, bf16[256,1152]{1,0:T(8,128)(2,1)S(1)}, u32[]{:S(2)}, u32[]{:S(2)}) %collective-permute-start.8) | collective-permute-done | bytes 589856 | tf_op jit(solution)/shard_map/ppermute | solution.py:33
  42.8 1.4 %collective-permute-done.9.refs_7_.refs_3_ = bf16[256,1152]{1,0:T(8,128)(2,1)S(1)} collective-permute-done((bf16[256,1152]{1,0:T(8,128)(2,1)S(1)}, bf16[256,1152]{1,0:T(8,128)(2,1)S(1)}, u32[]{:S(2)}, u32[]{:S(2)}) %collective-permute-start.9) | collective-permute-done | bytes 589856 | tf_op jit(solution)/shard_map/ppermute | solution.py:33
  44.2 0.5 collective-permute-start.12
  44.7 4.1 %own_logits.1 = (bf16[1024,1024]{1,0:T(8,128)(2,1)S(1)}, f32[8,128]{1,0:T(8,128)S(1)}) custom-call(s32[1]{0:T(128)} %bitcast.place_ref, f32[1,1]{1,0:T(1,128)} %bitcast.1.temper_ref, f32[1,1]{1,0:T(1,128)} %bitcast.2.shift_ref, bf16[256,1152]{1,0:T(8,128)(2,1)S(1)} %pad_maximum_fusion.2.refs_0_, bf16[256,1152]{1,0:T(8,128)(2,1)S(1)} %pad_maximum_fusion.refs_1_, ...), custom_call_target="tpu_custom_call" | custom-call | flops 2415919104 | bytes 8388608 | tf_op jit(solution)/shard_map/own_logits/pallas_call | solution.py:163
  48.9 7.1 %other_logits.1 = (bf16[1024,1024]{1,0:T(8,128)(2,1)S(1)}, bf16[512,1152]{1,0:T(8,128)(2,1)S(1)}, bf16[512,1152]{1,0:T(8,128)(2,1)S(1)}, f32[8,128]{1,0:T(8,128)S(1)}) custom-call(s32[1]{0:T(128)} %bitcast.place_ref, f32[1,1]{1,0:T(1,128)} %bitcast.1.temper_ref, f32[1,1]{1,0:T(1,128)} %bitcast.2.shift_ref, bf16[256,1152]{1,0:T(8,128)(2,1)S(1)} %pad_maximum_fusion.2.refs_0_, ...), custom_call_target="tpu_custom_call" | custom-call | flops 4831838208 | bytes 8388608 | tf_op jit(solution)/shard_map/other_logits/pallas_call | solution.py:163
  56.0 0.6 collective-permute-start.14
  56.6 0.1 collective-permute-start.16
  56.7 0.4 collective-permute-start.15
  57.1 2.9 %image_terms.2 = (bf16[256,1152]{1,0:T(8,128)(2,1)S(1)}, bf16[256,1152]{1,0:T(8,128)(2,1)S(1)}) custom-call(bf16[1024,1024]{1,0:T(8,128)(2,1)S(1)} %get-tuple-element.75.own_ref.coeff_ref, bf16[1024,1024]{1,0:T(8,128)(2,1)S(1)} %get-tuple-element.66.other_ref, bf16[256,1152]{1,0:T(8,128)(2,1)S(1)} %pad_maximum_fusion.3.refs_4_.refs_0_, ...), custom_call_target="tpu_custom_call" | custom-call | flops 2415919104 | bytes 8388608 | tf_op jit(solution)/shard_map/image_terms/pallas_call | solution.py:217
  60.0 0.2 collective-permute-start.30
  60.3 0.5 collective-permute-done.15
  60.8 2.2 %text_terms.3 = (bf16[256,1152]{1,0:T(8,128)(2,1)S(1)}, bf16[256,1152]{1,0:T(8,128)(2,1)S(1)}) custom-call(bf16[1024,1024]{1,0:T(8,128)(2,1)S(1)} %get-tuple-element.75.own_ref.coeff_ref, bf16[512,1152]{1,0:T(8,128)(2,1)S(1)} %collective-permute-done.16.came_ref, bf16[256,1152]{1,0:T(8,128)(2,1)S(1)} %pad_maximum_fusion.2.refs_0_, ...), custom_call_target="tpu_custom_call" | custom-call | flops 1207959552 | bytes 8388608 | tf_op jit(solution)/shard_map/text_terms/pallas_call | solution.py:189
  63.0 1.3 %collective-permute-start.19 = (bf16[256,1152]{1,0:T(8,128)(2,1)S(1)}, bf16[256,1152]{1,0:T(8,128)(2,1)S(1)}, u32[]{:S(2)}, u32[]{:S(2)}) collective-permute-start(bf16[256,1152]{1,0:T(8,128)(2,1)S(1)} %get-tuple-element.81), channel_id=1, source_target_pairs={{3,0},{2,1},{1,2},{0,3},{7,4},{6,5},{5,6},{4,7},{11,8},{10,9},{9,1... | collective-permute-start | bytes 1769480 | tf_op jit(solution)/shard_map/ppermute | solution.py:33
  64.3 1.0 collective-permute-start.28
  65.3 0.4 collective-permute-start.20
  65.7 2.9 %image_terms.3 = (f32[256,1152]{1,0:T(8,128)S(1)}, f32[256,1152]{1,0:T(8,128)S(1)}) custom-call(bf16[1024,1024]{1,0:T(8,128)(2,1)S(1)} %get-tuple-element.75.own_ref.coeff_ref, bf16[1024,1024]{1,0:T(8,128)(2,1)S(1)} %get-tuple-element.66.other_ref, bf16[256,1152]{1,0:T(8,128)(2,1)S(1)} %pad_maximum_fusion.3.refs_4_.refs_0_, ...), custom_call_target="tpu_custom_call" | custom-call | flops 2415919104 | bytes 8388608 | tf_op jit(solution)/shard_map/image_terms/pallas_call | solution.py:217
  68.6 1.5 %collective-permute-start.17 = (bf16[256,1152]{1,0:T(8,128)(2,1)S(1)}, bf16[256,1152]{1,0:T(8,128)(2,1)S(1)}, u32[]{:S(2)}, u32[]{:S(2)}) collective-permute-start(bf16[256,1152]{1,0:T(8,128)(2,1)S(1)} %get-tuple-element.77), channel_id=1, source_target_pairs={{96,0},{97,1},{98,2},{99,3},{100,4},{101,5},{102,6},{103,7},{104,8... | collective-permute-start | bytes 1769480 | tf_op jit(solution)/shard_map/ppermute | solution.py:33
  70.1 1.8 %text_terms.2 = (f32[256,1152]{1,0:T(8,128)S(1)}, f32[256,1152]{1,0:T(8,128)S(1)}) custom-call(bf16[1024,1024]{1,0:T(8,128)(2,1)S(1)} %get-tuple-element.75.own_ref.coeff_ref, bf16[512,1152]{1,0:T(8,128)(2,1)S(1)} %collective-permute-done.14.came_ref, bf16[256,1152]{1,0:T(8,128)(2,1)S(1)} %pad_maximum_fusion.2.refs_0_, ...), custom_call_target="tpu_custom_call" | custom-call | flops 1207959552 | bytes 8388608 | tf_op jit(solution)/shard_map/text_terms/pallas_call | solution.py:189
  72.0 1.4 %collective-permute-done.20 = f32[64,8,128]{2,1,0:T(8,128)S(1)} collective-permute-done((f32[64,8,128]{2,1,0:T(8,128)S(1)}, f32[64,8,128]{2,1,0:T(8,128)S(1)}, u32[]{:S(2)}, u32[]{:S(2)}) %collective-permute-start.20) | collective-permute-done | bytes 262176 | tf_op jit(solution)/shard_map/ppermute | solution.py:33
  73.4 0.2 collective-permute-start.21
  73.6 1.9 %collective-permute-done.30.came_ref = bf16[256,1152]{1,0:T(8,128)(2,1)S(1)} collective-permute-done((bf16[256,1152]{1,0:T(8,128)(2,1)S(1)}, bf16[256,1152]{1,0:T(8,128)(2,1)S(1)}, u32[]{:S(2)}, u32[]{:S(2)}) %collective-permute-start.30) | collective-permute-done | bytes 589856 | tf_op jit(solution)/shard_map/ppermute | solution.py:33
  75.5 0.4 fold.7
  75.9 1.1 %collective-permute-start.31 = (bf16[128,1152]{1,0:T(8,128)(2,1)S(1)}, bf16[128,1152]{1,0:T(8,128)(2,1)S(1)}, u32[]{:S(2)}, u32[]{:S(2)}) collective-permute-start(bf16[128,1152]{1,0:T(8,128)(2,1)S(1)} %get-tuple-element.94), channel_id=1, source_target_pairs={{32,0},{33,1},{34,2},{35,3},{36,4},{37,5},{38,6},{39,7},{40,8},{41... | collective-permute-start | bytes 884744 | tf_op jit(solution)/shard_map/ppermute | solution.py:33
  77.1 2.8 %collective-permute-done.19.came_ref = bf16[256,1152]{1,0:T(8,128)(2,1)S(1)} collective-permute-done((bf16[256,1152]{1,0:T(8,128)(2,1)S(1)}, bf16[256,1152]{1,0:T(8,128)(2,1)S(1)}, u32[]{:S(2)}, u32[]{:S(2)}) %collective-permute-start.19) | collective-permute-done | bytes 589856 | tf_op jit(solution)/shard_map/ppermute | solution.py:33
  79.9 0.4 fold.5
  80.3 1.7 %collective-permute-start.22 = (bf16[128,1152]{1,0:T(8,128)(2,1)S(1)}, bf16[128,1152]{1,0:T(8,128)(2,1)S(1)}, u32[]{:S(2)}, u32[]{:S(2)}) collective-permute-start(bf16[128,1152]{1,0:T(8,128)(2,1)S(1)} %get-tuple-element.85), channel_id=1, source_target_pairs={{96,0},{97,1},{98,2},{99,3},{100,4},{101,5},{102,6},{103,7},{104,8... | collective-permute-start | bytes 884744 | tf_op jit(solution)/shard_map/ppermute | solution.py:33
  82.0 2.1 %collective-permute-start.23 = (f32[8,128]{1,0:T(8,128)S(1)}, f32[8,128]{1,0:T(8,128)S(1)}, u32[]{:S(2)}, u32[]{:S(2)}) collective-permute-start(f32[8,128]{1,0:T(8,128)S(1)} %add.24), channel_id=1, source_target_pairs={{20,0},{21,1},{22,2},{23,3},{16,4},{17,5},{18,6},{19,7},{28,8},{29... | collective-permute-start | bytes 12296 | tf_op jit(solution)/shard_map/ppermute | solution.py:33
  84.1 2.7 %collective-permute-done.23 = f32[8,128]{1,0:T(8,128)S(1)} collective-permute-done((f32[8,128]{1,0:T(8,128)S(1)}, f32[8,128]{1,0:T(8,128)S(1)}, u32[]{:S(2)}, u32[]{:S(2)}) %collective-permute-start.23) | collective-permute-done | bytes 4128 | tf_op jit(solution)/shard_map/ppermute | solution.py:33
  86.8 0.3 collective-permute-start.24
  87.1 0.4 fold.6
  87.6 0.1 collective-permute-start.29
  87.7 0.3 add_codes.3
  88.0 0.0 copy-start
  88.0 0.1 collective-permute-start.32
  88.1 0.4 fold.4
  88.5 1.2 %collective-permute-start.18 = (bf16[128,1152]{1,0:T(8,128)(2,1)S(1)}, bf16[128,1152]{1,0:T(8,128)(2,1)S(1)}, u32[]{:S(2)}, u32[]{:S(2)}) collective-permute-start(bf16[128,1152]{1,0:T(8,128)(2,1)S(1)} %get-tuple-element.79), channel_id=1, source_target_pairs={{3,0},{2,1},{1,2},{0,3},{7,4},{6,5},{5,6},{4,7},{11,8},{10,9},{9,1... | collective-permute-start | bytes 884744 | tf_op jit(solution)/shard_map/ppermute | solution.py:33
  89.7 0.7 collective-permute-done.24
  90.4 0.6 collective-permute-done.22.came_ref
  91.0 0.3 add_codes.2
  91.3 2.1 %collective-permute-start.25 = (bf16[128,1152]{1,0:T(8,128)(2,1)S(1)}, bf16[128,1152]{1,0:T(8,128)(2,1)S(1)}, u32[]{:S(2)}, u32[]{:S(2)}) collective-permute-start(bf16[128,1152]{1,0:T(8,128)(2,1)S(1)} %add_codes.2), channel_id=1, source_target_pairs={{20,0},{21,1},{22,2},{23,3},{16,4},{17,5},{18,6},{19,7},{28,8},{29... | collective-permute-start | bytes 884744 | tf_op jit(solution)/shard_map/ppermute | solution.py:33
  93.4 2.1 %collective-permute-start.26 = (f32[8,128]{1,0:T(8,128)S(1)}, f32[8,128]{1,0:T(8,128)S(1)}, u32[]{:S(2)}, u32[]{:S(2)}) collective-permute-start(f32[8,128]{1,0:T(8,128)S(1)} %add.26), channel_id=1, source_target_pairs={{3,0},{2,1},{1,2},{0,3},{7,4},{6,5},{5,6},{4,7},{11,8},{10,9},{9,1... | collective-permute-start | bytes 12296 | tf_op jit(solution)/shard_map/ppermute | solution.py:33
  95.5 2.7 %collective-permute-done.26 = f32[8,128]{1,0:T(8,128)S(1)} collective-permute-done((f32[8,128]{1,0:T(8,128)S(1)}, f32[8,128]{1,0:T(8,128)S(1)}, u32[]{:S(2)}, u32[]{:S(2)}) %collective-permute-start.26) | collective-permute-done | bytes 4128 | tf_op jit(solution)/shard_map/ppermute | solution.py:33
  98.2 1.4 %collective-permute-start.27 = (f32[8,128]{1,0:T(8,128)S(1)}, f32[8,128]{1,0:T(8,128)S(1)}, u32[]{:S(2)}, u32[]{:S(2)}) collective-permute-start(f32[8,128]{1,0:T(8,128)S(1)} %add.27.loss_ref.loss_in), channel_id=1, source_target_pairs={{96,0},{97,1},{98,2},{99,3},{100,4},{101,5},{102,6},{103,7},{104,8... | collective-permute-start | bytes 12296 | tf_op jit(solution)/shard_map/ppermute | solution.py:33
  99.6 1.4 %finish.3 = (f32[128,1152]{1,0:T(8,128)}, f32[1]{0:T(128)}) custom-call(bf16[128,1152]{1,0:T(8,128)(2,1)S(1)} %copy-done, f32[128,1152]{1,0:T(8,128)S(1)} %get-tuple-element.90.own_ref, bf16[128,1152]{1,0:T(8,128)(2,1)S(1)} %collective-permute-done.29.ring_ref, bf16[128,1152]{1,0:T(8,128)(2,1)S(1)} %collective-permute-done.32.far_ref, ...), custom_call_target="tpu_custom_call" | custom-call | tf_op jit(solution)/shard_map/finish/pallas_call | solution.py:268
  101.1 2.0 %collective-permute-done.27.loss_in = f32[8,128]{1,0:T(8,128)S(1)} collective-permute-done((f32[8,128]{1,0:T(8,128)S(1)}, f32[8,128]{1,0:T(8,128)S(1)}, u32[]{:S(2)}, u32[]{:S(2)}) %collective-permute-start.27) | collective-permute-done | bytes 4128 | tf_op jit(solution)/shard_map/ppermute | solution.py:33
  103.0 1.4 %finish.2 = (f32[128,1152]{1,0:T(8,128)}, f32[1]{0:T(128)}) custom-call(bf16[128,1152]{1,0:T(8,128)(2,1)S(1)} %copy-done.1, f32[128,1152]{1,0:T(8,128)S(1)} %get-tuple-element.78.own_ref, bf16[128,1152]{1,0:T(8,128)(2,1)S(1)} %collective-permute-done.18.ring_ref, bf16[128,1152]{1,0:T(8,128)(2,1)S(1)} %collective-permute-done.25.far_ref, ...), custom_call_target="tpu_custom_call" | custom-call | tf_op jit(solution)/shard_map/finish/pallas_call | solution.py:268
  (34 shorter events, 0.2 us)
Async XLA Ops:
  2.6 21.8 %copy-start.2 = (bf16[128,1152]{1,0:T(8,128)(2,1)S(1)}, bf16[128,1152]{1,0:T(8,128)(2,1)}, u32[]{:S(2)}) copy-start(bf16[128,1152]{1,0:T(8,128)(2,1)} %get-tuple-element.58) | copy-start | bytes 884740
  2.6 8.9 %collective-permute-start = (bf16[128,1152]{1,0:T(8,128)(2,1)}, bf16[128,1152]{1,0:T(8,128)(2,1)S(1)}, u32[]{:S(2)}, u32[]{:S(2)}) collective-permute-start(bf16[128,1152]{1,0:T(8,128)(2,1)} %get-tuple-element.57), channel_id=1, source_target_pairs={{16,0},{17,1},{18,2},{19,3},{20,4},{21,5},{22,6},{23,7},{24,8},{25... | collective-permute-start | bytes 884744 | tf_op jit(solution)/shard_map/ppermute | solution.py:33
  4.3 9.9 %collective-permute-start.1 = (bf16[128,1152]{1,0:T(8,128)(2,1)}, bf16[128,1152]{1,0:T(8,128)(2,1)S(1)}, u32[]{:S(2)}, u32[]{:S(2)}) collective-permute-start(bf16[128,1152]{1,0:T(8,128)(2,1)} %get-tuple-element.58), channel_id=1, source_target_pairs={{20,0},{21,1},{22,2},{23,3},{16,4},{17,5},{18,6},{19,7},{28,8},{29... | collective-permute-start | bytes 884744 | tf_op jit(solution)/shard_map/ppermute | solution.py:33
  14.2 7.8 %collective-permute-start.4 = (bf16[128,1152]{1,0:T(8,128)(2,1)}, bf16[128,1152]{1,0:T(8,128)(2,1)S(1)}, u32[]{:S(2)}, u32[]{:S(2)}) collective-permute-start(bf16[128,1152]{1,0:T(8,128)(2,1)} %get-tuple-element.57), channel_id=1, source_target_pairs={{1,0},{0,1},{3,2},{2,3},{5,4},{4,5},{7,6},{6,7},{9,8},{8,9},{11,10... | collective-permute-start | bytes 884744 | tf_op jit(solution)/shard_map/ppermute | solution.py:33
  15.8 8.7 %collective-permute-start.5 = (bf16[128,1152]{1,0:T(8,128)(2,1)}, bf16[128,1152]{1,0:T(8,128)(2,1)S(1)}, u32[]{:S(2)}, u32[]{:S(2)}) collective-permute-start(bf16[128,1152]{1,0:T(8,128)(2,1)} %get-tuple-element.58), channel_id=1, source_target_pairs={{3,0},{2,1},{1,2},{0,3},{7,4},{6,5},{5,6},{4,7},{11,8},{10,9},{9,1... | collective-permute-start | bytes 884744 | tf_op jit(solution)/shard_map/ppermute | solution.py:33
  17.9 9.3 %collective-permute-start.3 = (bf16[128,1152]{1,0:T(8,128)(2,1)S(1)}, bf16[128,1152]{1,0:T(8,128)(2,1)S(1)}, u32[]{:S(2)}, u32[]{:S(2)}) collective-permute-start(bf16[128,1152]{1,0:T(8,128)(2,1)S(1)} %collective-permute-done.1), channel_id=1, source_target_pairs={{96,0},{97,1},{98,2},{99,3},{100,4},{101,5},{102,6},{103,7},{104,8... | collective-permute-start | bytes 884744 | tf_op jit(solution)/shard_map/ppermute | solution.py:33
  22.0 7.0 %collective-permute-start.2 = (bf16[128,1152]{1,0:T(8,128)(2,1)S(1)}, bf16[128,1152]{1,0:T(8,128)(2,1)S(1)}, u32[]{:S(2)}, u32[]{:S(2)}) collective-permute-start(bf16[128,1152]{1,0:T(8,128)(2,1)S(1)} %collective-permute-done), channel_id=1, source_target_pairs={{32,0},{33,1},{34,2},{35,3},{36,4},{37,5},{38,6},{39,7},{40,8},{41... | collective-permute-start | bytes 884744 | tf_op jit(solution)/shard_map/ppermute | solution.py:33
  29.0 12.3 %collective-permute-start.6 = (bf16[256,1152]{1,0:T(8,128)(2,1)S(1)}, bf16[256,1152]{1,0:T(8,128)(2,1)S(1)}, u32[]{:S(2)}, u32[]{:S(2)}) collective-permute-start(bf16[256,1152]{1,0:T(8,128)(2,1)S(1)} %pad_maximum_fusion.2.refs_0_), channel_id=1, source_target_pairs={{32,0},{33,1},{34,2},{35,3},{36,4},{37,5},{38,6},{39,7},{40,8},{41... | collective-permute-start | bytes 1769480 | tf_op jit(solution)/shard_map/ppermute | solution.py:33
  29.2 12.2 %collective-permute-start.7 = (bf16[256,1152]{1,0:T(8,128)(2,1)S(1)}, bf16[256,1152]{1,0:T(8,128)(2,1)S(1)}, u32[]{:S(2)}, u32[]{:S(2)}) collective-permute-start(bf16[256,1152]{1,0:T(8,128)(2,1)S(1)} %pad_maximum_fusion.refs_1_), channel_id=1, source_target_pairs={{1,0},{0,1},{3,2},{2,3},{5,4},{4,5},{7,6},{6,7},{9,8},{8,9},{11,10... | collective-permute-start | bytes 1769480 | tf_op jit(solution)/shard_map/ppermute | solution.py:33
  29.9 13.0 %collective-permute-start.8 = (bf16[256,1152]{1,0:T(8,128)(2,1)S(1)}, bf16[256,1152]{1,0:T(8,128)(2,1)S(1)}, u32[]{:S(2)}, u32[]{:S(2)}) collective-permute-start(bf16[256,1152]{1,0:T(8,128)(2,1)S(1)} %pad_maximum_fusion.3.refs_4_.refs_0_), channel_id=1, source_target_pairs={{96,0},{97,1},{98,2},{99,3},{100,4},{101,5},{102,6},{103,7},{104,8... | collective-permute-start | bytes 1769480 | tf_op jit(solution)/shard_map/ppermute | solution.py:33
  31.2 13.0 %collective-permute-start.9 = (bf16[256,1152]{1,0:T(8,128)(2,1)S(1)}, bf16[256,1152]{1,0:T(8,128)(2,1)S(1)}, u32[]{:S(2)}, u32[]{:S(2)}) collective-permute-start(bf16[256,1152]{1,0:T(8,128)(2,1)S(1)} %pad_maximum_fusion.1.refs_5_.refs_1_), channel_id=1, source_target_pairs={{3,0},{2,1},{1,2},{0,3},{7,4},{6,5},{5,6},{4,7},{11,8},{10,9},{9,1... | collective-permute-start | bytes 1769480 | tf_op jit(solution)/shard_map/ppermute | solution.py:33
  32.0 16.8 %collective-permute-start.10 = (bf16[256,1152]{1,0:T(8,128)(2,1)S(1)}, bf16[256,1152]{1,0:T(8,128)(2,1)S(1)}, u32[]{:S(2)}, u32[]{:S(2)}) collective-permute-start(bf16[256,1152]{1,0:T(8,128)(2,1)S(1)} %pad_maximum_fusion.3.refs_4_.refs_0_), channel_id=1, source_target_pairs={{8,0},{9,1},{10,2},{11,3},{12,4},{13,5},{14,6},{15,7},{0,8},{1,9},... | collective-permute-start | bytes 1769480 | tf_op jit(solution)/shard_map/ppermute | solution.py:33
  44.2 4.6 %collective-permute-start.11 = (bf16[256,1152]{1,0:T(8,128)(2,1)S(1)}, bf16[256,1152]{1,0:T(8,128)(2,1)S(1)}, u32[]{:S(2)}, u32[]{:S(2)}) collective-permute-start(bf16[256,1152]{1,0:T(8,128)(2,1)S(1)} %pad_maximum_fusion.1.refs_5_.refs_1_), channel_id=1, source_target_pairs={{8,0},{9,1},{10,2},{11,3},{12,4},{13,5},{14,6},{15,7},{0,8},{1,9},... | collective-permute-start | bytes 1769480 | tf_op jit(solution)/shard_map/ppermute | solution.py:33
  44.2 4.6 %collective-permute-start.12 = (bf16[256,1152]{1,0:T(8,128)(2,1)S(1)}, bf16[256,1152]{1,0:T(8,128)(2,1)S(1)}, u32[]{:S(2)}, u32[]{:S(2)}) collective-permute-start(bf16[256,1152]{1,0:T(8,128)(2,1)S(1)} %collective-permute-done.8.refs_6_.refs_2_), channel_id=1, source_target_pairs={{8,0},{9,1},{10,2},{11,3},{12,4},{13,5},{14,6},{15,7},{0,8},{1,9},... | collective-permute-start | bytes 1769480 | tf_op jit(solution)/shard_map/ppermute | solution.py:33
  44.7 4.1 %collective-permute-start.13 = (bf16[256,1152]{1,0:T(8,128)(2,1)S(1)}, bf16[256,1152]{1,0:T(8,128)(2,1)S(1)}, u32[]{:S(2)}, u32[]{:S(2)}) collective-permute-start(bf16[256,1152]{1,0:T(8,128)(2,1)S(1)} %collective-permute-done.9.refs_7_.refs_3_), channel_id=1, source_target_pairs={{8,0},{9,1},{10,2},{11,3},{12,4},{13,5},{14,6},{15,7},{0,8},{1,9},... | collective-permute-start | bytes 1769480 | tf_op jit(solution)/shard_map/ppermute | solution.py:33
  56.0 4.7 %collective-permute-start.14 = (bf16[512,1152]{1,0:T(8,128)(2,1)S(1)}, bf16[512,1152]{1,0:T(8,128)(2,1)S(1)}, u32[]{:S(2)}, u32[]{:S(2)}) collective-permute-start(bf16[512,1152]{1,0:T(8,128)(2,1)S(1)} %get-tuple-element.71), channel_id=1, source_target_pairs={{8,0},{9,1},{10,2},{11,3},{12,4},{13,5},{14,6},{15,7},{0,8},{1,9},... | collective-permute-start | bytes 3538952 | tf_op jit(solution)/shard_map/ppermute | solution.py:33
  56.6 4.2 %collective-permute-start.16 = (bf16[512,1152]{1,0:T(8,128)(2,1)S(1)}, bf16[512,1152]{1,0:T(8,128)(2,1)S(1)}, u32[]{:S(2)}, u32[]{:S(2)}) collective-permute-start(bf16[512,1152]{1,0:T(8,128)(2,1)S(1)} %get-tuple-element.76), channel_id=1, source_target_pairs={{8,0},{9,1},{10,2},{11,3},{12,4},{13,5},{14,6},{15,7},{0,8},{1,9},... | collective-permute-start | bytes 3538952 | tf_op jit(solution)/shard_map/ppermute | solution.py:33
  56.7 4.1 %collective-permute-start.15 = (f32[8,128]{1,0:T(8,128)S(1)}, f32[8,128]{1,0:T(8,128)S(1)}, u32[]{:S(2)}, u32[]{:S(2)}) collective-permute-start(f32[8,128]{1,0:T(8,128)S(1)} %get-tuple-element.73), channel_id=1, source_target_pairs={{8,0},{9,1},{10,2},{11,3},{12,4},{13,5},{14,6},{15,7},{0,8},{1,9},... | collective-permute-start | bytes 12296 | tf_op jit(solution)/shard_map/ppermute | solution.py:33
  60.0 15.5 %collective-permute-start.30 = (bf16[256,1152]{1,0:T(8,128)(2,1)S(1)}, bf16[256,1152]{1,0:T(8,128)(2,1)S(1)}, u32[]{:S(2)}, u32[]{:S(2)}) collective-permute-start(bf16[256,1152]{1,0:T(8,128)(2,1)S(1)} %get-tuple-element.67), channel_id=1, source_target_pairs={{1,0},{0,1},{3,2},{2,3},{5,4},{4,5},{7,6},{6,7},{9,8},{8,9},{11,10... | collective-permute-start | bytes 1769480 | tf_op jit(solution)/shard_map/ppermute | solution.py:33
  63.0 16.9 %collective-permute-start.19 = (bf16[256,1152]{1,0:T(8,128)(2,1)S(1)}, bf16[256,1152]{1,0:T(8,128)(2,1)S(1)}, u32[]{:S(2)}, u32[]{:S(2)}) collective-permute-start(bf16[256,1152]{1,0:T(8,128)(2,1)S(1)} %get-tuple-element.81), channel_id=1, source_target_pairs={{3,0},{2,1},{1,2},{0,3},{7,4},{6,5},{5,6},{4,7},{11,8},{10,9},{9,1... | collective-permute-start | bytes 1769480 | tf_op jit(solution)/shard_map/ppermute | solution.py:33
  64.3 22.9 %collective-permute-start.28 = (bf16[256,1152]{1,0:T(8,128)(2,1)S(1)}, bf16[256,1152]{1,0:T(8,128)(2,1)S(1)}, u32[]{:S(2)}, u32[]{:S(2)}) collective-permute-start(bf16[256,1152]{1,0:T(8,128)(2,1)S(1)} %get-tuple-element.74), channel_id=1, source_target_pairs={{32,0},{33,1},{34,2},{35,3},{36,4},{37,5},{38,6},{39,7},{40,8},{41... | collective-permute-start | bytes 1769480 | tf_op jit(solution)/shard_map/ppermute | solution.py:33
  65.3 8.1 %collective-permute-start.20 = (f32[64,8,128]{2,1,0:T(8,128)S(1)}, f32[64,8,128]{2,1,0:T(8,128)S(1)}, u32[]{:S(2)}, u32[]{:S(2)}) collective-permute-start(f32[64,8,128]{2,1,0:T(8,128)S(1)} %broadcast_in_dim.2), channel_id=1, source_target_pairs={{16,0},{17,1},{18,2},{19,3},{20,4},{21,5},{22,6},{23,7},{24,8},{25... | collective-permute-start | bytes 786440 | tf_op jit(solution)/shard_map/ppermute | solution.py:33
  68.6 19.4 %collective-permute-start.17 = (bf16[256,1152]{1,0:T(8,128)(2,1)S(1)}, bf16[256,1152]{1,0:T(8,128)(2,1)S(1)}, u32[]{:S(2)}, u32[]{:S(2)}) collective-permute-start(bf16[256,1152]{1,0:T(8,128)(2,1)S(1)} %get-tuple-element.77), channel_id=1, source_target_pairs={{96,0},{97,1},{98,2},{99,3},{100,4},{101,5},{102,6},{103,7},{104,8... | collective-permute-start | bytes 1769480 | tf_op jit(solution)/shard_map/ppermute | solution.py:33
  73.4 3.7 %collective-permute-start.21 = (f32[8,128]{1,0:T(8,128)S(1)}, f32[8,128]{1,0:T(8,128)S(1)}, u32[]{:S(2)}, u32[]{:S(2)}) collective-permute-start(f32[8,128]{1,0:T(8,128)S(1)} %fusion), channel_id=1, source_target_pairs={{1,0},{0,1},{3,2},{2,3},{5,4},{4,5},{7,6},{6,7},{9,8},{8,9},{11,10... | collective-permute-start | bytes 12296 | tf_op jit(solution)/shard_map/ppermute | solution.py:33
  75.9 11.7 %collective-permute-start.31 = (bf16[128,1152]{1,0:T(8,128)(2,1)S(1)}, bf16[128,1152]{1,0:T(8,128)(2,1)S(1)}, u32[]{:S(2)}, u32[]{:S(2)}) collective-permute-start(bf16[128,1152]{1,0:T(8,128)(2,1)S(1)} %get-tuple-element.94), channel_id=1, source_target_pairs={{32,0},{33,1},{34,2},{35,3},{36,4},{37,5},{38,6},{39,7},{40,8},{41... | collective-permute-start | bytes 884744 | tf_op jit(solution)/shard_map/ppermute | solution.py:33
  80.3 10.7 %collective-permute-start.22 = (bf16[128,1152]{1,0:T(8,128)(2,1)S(1)}, bf16[128,1152]{1,0:T(8,128)(2,1)S(1)}, u32[]{:S(2)}, u32[]{:S(2)}) collective-permute-start(bf16[128,1152]{1,0:T(8,128)(2,1)S(1)} %get-tuple-element.85), channel_id=1, source_target_pairs={{96,0},{97,1},{98,2},{99,3},{100,4},{101,5},{102,6},{103,7},{104,8... | collective-permute-start | bytes 884744 | tf_op jit(solution)/shard_map/ppermute | solution.py:33
  82.0 4.8 %collective-permute-start.23 = (f32[8,128]{1,0:T(8,128)S(1)}, f32[8,128]{1,0:T(8,128)S(1)}, u32[]{:S(2)}, u32[]{:S(2)}) collective-permute-start(f32[8,128]{1,0:T(8,128)S(1)} %add.24), channel_id=1, source_target_pairs={{20,0},{21,1},{22,2},{23,3},{16,4},{17,5},{18,6},{19,7},{28,8},{29... | collective-permute-start | bytes 12296 | tf_op jit(solution)/shard_map/ppermute | solution.py:33
  86.8 3.6 %collective-permute-start.24 = (f32[8,128]{1,0:T(8,128)S(1)}, f32[8,128]{1,0:T(8,128)S(1)}, u32[]{:S(2)}, u32[]{:S(2)}) collective-permute-start(f32[8,128]{1,0:T(8,128)S(1)} %add.25), channel_id=1, source_target_pairs={{32,0},{33,1},{34,2},{35,3},{36,4},{37,5},{38,6},{39,7},{40,8},{41... | collective-permute-start | bytes 12296 | tf_op jit(solution)/shard_map/ppermute | solution.py:33
  87.6 12.0 %collective-permute-start.29 = (bf16[128,1152]{1,0:T(8,128)(2,1)S(1)}, bf16[128,1152]{1,0:T(8,128)(2,1)S(1)}, u32[]{:S(2)}, u32[]{:S(2)}) collective-permute-start(bf16[128,1152]{1,0:T(8,128)(2,1)S(1)} %get-tuple-element.91), channel_id=1, source_target_pairs={{1,0},{0,1},{3,2},{2,3},{5,4},{4,5},{7,6},{6,7},{9,8},{8,9},{11,10... | collective-permute-start | bytes 884744 | tf_op jit(solution)/shard_map/ppermute | solution.py:33
  88.0 11.7 %copy-start = (bf16[128,1152]{1,0:T(8,128)(2,1)S(1)}, bf16[128,1152]{1,0:T(8,128)(2,1)}, u32[]{:S(2)}) copy-start(bf16[128,1152]{1,0:T(8,128)(2,1)} %raw_ref.3) | copy-start | bytes 884740
  88.0 11.6 %collective-permute-start.32 = (bf16[128,1152]{1,0:T(8,128)(2,1)S(1)}, bf16[128,1152]{1,0:T(8,128)(2,1)S(1)}, u32[]{:S(2)}, u32[]{:S(2)}) collective-permute-start(bf16[128,1152]{1,0:T(8,128)(2,1)S(1)} %add_codes.3), channel_id=1, source_target_pairs={{16,0},{17,1},{18,2},{19,3},{20,4},{21,5},{22,6},{23,7},{24,8},{25... | collective-permute-start | bytes 884744 | tf_op jit(solution)/shard_map/ppermute | solution.py:33
  88.5 12.5 %collective-permute-start.18 = (bf16[128,1152]{1,0:T(8,128)(2,1)S(1)}, bf16[128,1152]{1,0:T(8,128)(2,1)S(1)}, u32[]{:S(2)}, u32[]{:S(2)}) collective-permute-start(bf16[128,1152]{1,0:T(8,128)(2,1)S(1)} %get-tuple-element.79), channel_id=1, source_target_pairs={{3,0},{2,1},{1,2},{0,3},{7,4},{6,5},{5,6},{4,7},{11,8},{10,9},{9,1... | collective-permute-start | bytes 884744 | tf_op jit(solution)/shard_map/ppermute | solution.py:33
  90.4 12.6 %copy-start.1 = (bf16[128,1152]{1,0:T(8,128)(2,1)S(1)}, bf16[128,1152]{1,0:T(8,128)(2,1)}, u32[]{:S(2)}) copy-start(bf16[128,1152]{1,0:T(8,128)(2,1)} %raw_ref.2) | copy-start | bytes 884740
  91.3 11.7 %collective-permute-start.25 = (bf16[128,1152]{1,0:T(8,128)(2,1)S(1)}, bf16[128,1152]{1,0:T(8,128)(2,1)S(1)}, u32[]{:S(2)}, u32[]{:S(2)}) collective-permute-start(bf16[128,1152]{1,0:T(8,128)(2,1)S(1)} %add_codes.2), channel_id=1, source_target_pairs={{20,0},{21,1},{22,2},{23,3},{16,4},{17,5},{18,6},{19,7},{28,8},{29... | collective-permute-start | bytes 884744 | tf_op jit(solution)/shard_map/ppermute | solution.py:33
  93.4 4.8 %collective-permute-start.26 = (f32[8,128]{1,0:T(8,128)S(1)}, f32[8,128]{1,0:T(8,128)S(1)}, u32[]{:S(2)}, u32[]{:S(2)}) collective-permute-start(f32[8,128]{1,0:T(8,128)S(1)} %add.26), channel_id=1, source_target_pairs={{3,0},{2,1},{1,2},{0,3},{7,4},{6,5},{5,6},{4,7},{11,8},{10,9},{9,1... | collective-permute-start | bytes 12296 | tf_op jit(solution)/shard_map/ppermute | solution.py:33
  98.2 4.8 %collective-permute-start.27 = (f32[8,128]{1,0:T(8,128)S(1)}, f32[8,128]{1,0:T(8,128)S(1)}, u32[]{:S(2)}, u32[]{:S(2)}) collective-permute-start(f32[8,128]{1,0:T(8,128)S(1)} %add.27.loss_ref.loss_in), channel_id=1, source_target_pairs={{96,0},{97,1},{98,2},{99,3},{100,4},{101,5},{102,6},{103,7},{104,8... | collective-permute-start | bytes 12296 | tf_op jit(solution)/shard_map/ppermute | solution.py:33

commit v4 on v3

--- a/solution.py
+++ b/solution.py
@@ -66,6 +66,13 @@
         compiler_params=pltpu.CompilerParams(vmem_limit_bytes=60 * 2**20),
         name="unit_rows",
     )(images, texts)
+
+
+def far_kernel(images_ref, texts_ref, *out_refs):
+    for raw_ref, out_ref in zip((images_ref, texts_ref), out_refs):
+        wide = raw_ref[...].astype(jnp.float32)
+        inverse = lax.rsqrt(jnp.sum(wide * wide, axis=1, keepdims=True) + 1e-06)
+        out_ref[...] = (wide * inverse).astype(jnp.bfloat16)
 
 
 def row_masks(pairs):
@@ -277,8 +284,10 @@
 
 def gather(image, text, scalars):
     groups = ((image, IMAGE_PAIRS), (text, TEXT_PAIRS))
-    far = [swap(unit, pairs["x"]) for unit, pairs in groups]
+    far = [swap(raw, pairs["x"]) for raw, pairs in groups]
+    image, text = unit_rows(image, text)
     *far, image, text, scalars = lax.optimization_barrier((*far, image, text, scalars))
+    far = small_call(far_kernel, "far_units", [shape_of(*part.shape, part.dtype) for part in far], far)
     groups = ((image, IMAGE_PAIRS), (text, TEXT_PAIRS))
     far = [jnp.concatenate([part, swap(part, pairs["z"])], axis=0) for part, (_, pairs) in zip(far, groups)]
     near = [jnp.concatenate([unit, swap(unit, pairs["y"])], axis=0) for unit, pairs in groups]
@@ -297,7 +306,7 @@
 def shards(images, texts, logit_scale, bias):
     place = (lax.axis_index("img") * lax.axis_size("txt") + lax.axis_index("txt")).astype(jnp.int32).reshape(1)
     scalars = (place, jnp.exp(logit_scale).reshape(1, 1), (bias * LOG2E).reshape(1, 1))
-    image_all, text_all, scalars = gather(*unit_rows(images, texts), scalars)
+    image_all, text_all, scalars = gather(images, texts, scalars)
     count = images.shape[0] * lax.axis_size("img") * lax.axis_size("txt")
     own_coeff, _, loss = logit_terms(scalars, image_all, text_all[:4])
     other_coeff, other, loss = logit_terms(scalars, image_all, text_all[4:], CORE, loss, 1.0 / count)
@@ -314,8 +323,11 @@
     )
     text_far = swap(text_far, TEXT_PAIRS["y"])
     text_near = swap(text_near, TEXT_PAIRS["z"])
-    tiles = swap(jnp.broadcast_to(loss[None], (64, *loss.shape)), IMAGE_PAIRS["x"])
-    near_early, far_early = image_terms(0, 2, jnp.float32, (after(own_coeff, far_late), other_coeff), text_all)
+    loss = after(loss, near_late)
+    tiles = swap(jnp.broadcast_to(loss[None], (32, *loss.shape)), IMAGE_PAIRS["x"])
+    loss = loss + tiles[0]
+    near_early, far_early = image_terms(0, 2, jnp.float32, (after(own_coeff, far_late, loss), other_coeff), text_all)
+    tiles = swap(jnp.broadcast_to(loss[None], (32, *loss.shape)), TEXT_PAIRS["x"])
     text_early = text_terms(0, jnp.float32, after(own_coeff, near_early), other_early, image_all)
 
     image_kept, image_sent = fold(far_early, image_far)
@@ -329,12 +341,11 @@
     text_own, text_sent = fold(text_early[0], text_near)
     text_near = swap(text_sent, TEXT_PAIRS["y"])
 
+    image_sent = add_codes(image_kept, image_far)
     loss = after(loss, text_kept)
-    loss = loss + swap(loss, TEXT_PAIRS["x"])
-    image_sent = add_codes(image_kept, image_far)
     loss = loss + swap(loss, IMAGE_PAIRS["z"])
+    loss = loss + swap(loss, TEXT_PAIRS["y"])
     text_sent = add_codes(text_kept, after(text_far, loss))
-    loss = loss + swap(after(loss, text_sent), TEXT_PAIRS["y"])
     last = swap(loss, TEXT_PAIRS["z"])
     image_grad, _ = finish(images, image_own, image_near, swap(image_sent, IMAGE_PAIRS["x"]), loss, loss)
     text_grad, loss = finish(texts, text_own, text_near, swap(text_sent, TEXT_PAIRS["x"]), loss, last)

time: 105 us -> 102 us (0.971)
  waiting for transfers between devices: 39.8 us -> 31.2 us
  starting transfers between devices: 33 us -> 39.5 us
    ppermute x33, waiting for transfers between devices: 39.8 us -> 31.2 us  [swap(): lax.ppermute(value, axes, [(k ^ mask, k) for k in range(lax.axis_size(axe...]
    ppermute x33, starting transfers between devices: 33 us -> 39.5 us  [swap(): lax.ppermute(value, axes, [(k ^ mask, k) for k in range(lax.axis_size(axe...]
    pallas_call x6 -> x7, Pallas kernels: 2.31 us -> 2.51 us  [small_call(): pl.pallas_call(kernel, out_shape=out_shape, in_specs=[VMEM] * len(operand...]
  transfers between devices with their start and end apart: 33 -> 33, of which waited for: 17 -> 18; matrix products, arithmetic and copies ran while one was open for 1% -> 0% of each run, Pallas kernels for 17% -> 19%
where the time goes in v4:
time: 102 us
  starting transfers between devices  39.5 us (39%)
  waiting for transfers between devices  31.2 us (31%)
  Pallas kernels  28.5 us (28%)
  between operations  2.38 us (2%)
    ppermute x33, starting transfers between devices, swap(): lax.ppermute(value, axes, [(k ^ mask, k) for k in range(lax.axis_size(axe...  39.5 us
    ppermute x33, waiting for transfers between devices, swap(): lax.ppermute(value, axes, [(k ^ mask, k) for k in range(lax.axis_size(axe...  31.2 us
    pallas_call x2, Pallas kernels, logit_terms(): pl.pallas_call(functools.partial(logit_kernel, core, loss_scale), out_sha...  11.2 us
    pallas_call x2, Pallas kernels, image_terms(): pl.pallas_call(functools.partial(image_kernel, first), out_shape=[shape_o...  5.81 us
    pallas_call x2, Pallas kernels, text_terms(): pl.pallas_call(functools.partial(text_kernel, first), out_shape=[shape_of...  4.06 us
    pallas_call x2, Pallas kernels, finish(): pl.pallas_call(finish_kernel, out_shape=[shape_of(*raw.shape, jnp.float32...  2.86 us
    pallas_call x7, Pallas kernels, small_call(): pl.pallas_call(kernel, out_shape=out_shape, in_specs=[VMEM] * len(operand...  2.51 us
  transfers between devices with their start and end apart: 33, of which 18 were waited for; matrix products, arithmetic and copies ran while one was open for 0% of the time, Pallas kernels for 19%

profile of v4, /device:TPU:0, one launch (start us, length us, event | category | flops | bytes accessed | tf_op | source)
XLA Modules:
  0.0 101.8 jit_solution(17954494323227485589)
XLA Ops:
  0.6 1.7 %collective-permute-start = (bf16[128,1152]{1,0:T(8,128)(2,1)}, bf16[128,1152]{1,0:T(8,128)(2,1)S(1)}, u32[]{:S(2)}, u32[]{:S(2)}) collective-permute-start(bf16[128,1152]{1,0:T(8,128)(2,1)} %raw_ref.3), channel_id=1, source_target_pairs={{16,0},{17,1},{18,2},{19,3},{20,4},{21,5},{22,6},{23,7},{24,8},{25... | collective-permute-start | bytes 884744 | tf_op jit(solution)/shard_map/ppermute | solution.py:33
  2.3 2.1 %collective-permute-start.1 = (bf16[128,1152]{1,0:T(8,128)(2,1)}, bf16[128,1152]{1,0:T(8,128)(2,1)S(1)}, u32[]{:S(2)}, u32[]{:S(2)}) collective-permute-start(bf16[128,1152]{1,0:T(8,128)(2,1)} %raw_ref.2), channel_id=1, source_target_pairs={{20,0},{21,1},{22,2},{23,3},{16,4},{17,5},{18,6},{19,7},{28,8},{29... | collective-permute-start | bytes 884744 | tf_op jit(solution)/shard_map/ppermute | solution.py:33
  4.4 2.0 %unit_rows.1 = (bf16[128,1152]{1,0:T(8,128)(2,1)}, bf16[128,1152]{1,0:T(8,128)(2,1)}) custom-call(bf16[128,1152]{1,0:T(8,128)(2,1)} %raw_ref.3, bf16[128,1152]{1,0:T(8,128)(2,1)} %raw_ref.2), custom_call_target="tpu_custom_call" | custom-call | tf_op jit(solution)/shard_map/unit_rows/pallas_call | solution.py:60
  7.7 1.8 %collective-permute-done.images_ref = bf16[128,1152]{1,0:T(8,128)(2,1)S(1)} collective-permute-done((bf16[128,1152]{1,0:T(8,128)(2,1)}, bf16[128,1152]{1,0:T(8,128)(2,1)S(1)}, u32[]{:S(2)}, u32[]{:S(2)}) %collective-permute-start) | collective-permute-done | bytes 294944 | tf_op jit(solution)/shard_map/ppermute | solution.py:33
  9.5 2.7 %collective-permute-done.1.texts_ref = bf16[128,1152]{1,0:T(8,128)(2,1)S(1)} collective-permute-done((bf16[128,1152]{1,0:T(8,128)(2,1)}, bf16[128,1152]{1,0:T(8,128)(2,1)S(1)}, u32[]{:S(2)}, u32[]{:S(2)}) %collective-permute-start.1) | collective-permute-done | bytes 294944 | tf_op jit(solution)/shard_map/ppermute | solution.py:33
  12.2 0.2 far_units.1
  12.4 2.0 %collective-permute-start.2 = (bf16[128,1152]{1,0:T(8,128)(2,1)S(1)}, bf16[128,1152]{1,0:T(8,128)(2,1)S(1)}, u32[]{:S(2)}, u32[]{:S(2)}) collective-permute-start(bf16[128,1152]{1,0:T(8,128)(2,1)S(1)} %get-tuple-element.59), channel_id=1, source_target_pairs={{32,0},{33,1},{34,2},{35,3},{36,4},{37,5},{38,6},{39,7},{40,8},{41... | collective-permute-start | bytes 884744 | tf_op jit(solution)/shard_map/ppermute | solution.py:33
  14.4 2.5 %collective-permute-start.3 = (bf16[128,1152]{1,0:T(8,128)(2,1)S(1)}, bf16[128,1152]{1,0:T(8,128)(2,1)S(1)}, u32[]{:S(2)}, u32[]{:S(2)}) collective-permute-start(bf16[128,1152]{1,0:T(8,128)(2,1)S(1)} %get-tuple-element.60), channel_id=1, source_target_pairs={{96,0},{97,1},{98,2},{99,3},{100,4},{101,5},{102,6},{103,7},{104,8... | collective-permute-start | bytes 884744 | tf_op jit(solution)/shard_map/ppermute | solution.py:33
  16.9 1.6 %collective-permute-start.4 = (bf16[128,1152]{1,0:T(8,128)(2,1)}, bf16[128,1152]{1,0:T(8,128)(2,1)S(1)}, u32[]{:S(2)}, u32[]{:S(2)}) collective-permute-start(bf16[128,1152]{1,0:T(8,128)(2,1)} %get-tuple-element.61), channel_id=1, source_target_pairs={{1,0},{0,1},{3,2},{2,3},{5,4},{4,5},{7,6},{6,7},{9,8},{8,9},{11,10... | collective-permute-start | bytes 884744 | tf_op jit(solution)/shard_map/ppermute | solution.py:33
  18.5 2.2 %collective-permute-start.5 = (bf16[128,1152]{1,0:T(8,128)(2,1)}, bf16[128,1152]{1,0:T(8,128)(2,1)S(1)}, u32[]{:S(2)}, u32[]{:S(2)}) collective-permute-start(bf16[128,1152]{1,0:T(8,128)(2,1)} %get-tuple-element.62), channel_id=1, source_target_pairs={{3,0},{2,1},{1,2},{0,3},{7,4},{6,5},{5,6},{4,7},{11,8},{10,9},{9,1... | collective-permute-start | bytes 884744 | tf_op jit(solution)/shard_map/ppermute | solution.py:33
  20.7 0.0 copy-start.2
  20.7 2.1 %collective-permute-done.3 = bf16[128,1152]{1,0:T(8,128)(2,1)S(1)} collective-permute-done((bf16[128,1152]{1,0:T(8,128)(2,1)S(1)}, bf16[128,1152]{1,0:T(8,128)(2,1)S(1)}, u32[]{:S(2)}, u32[]{:S(2)}) %collective-permute-start.3) | collective-permute-done | bytes 294944 | tf_op jit(solution)/shard_map/ppermute | solution.py:33
  22.9 1.2 %collective-permute-done.4 = bf16[128,1152]{1,0:T(8,128)(2,1)S(1)} collective-permute-done((bf16[128,1152]{1,0:T(8,128)(2,1)}, bf16[128,1152]{1,0:T(8,128)(2,1)S(1)}, u32[]{:S(2)}, u32[]{:S(2)}) %collective-permute-start.4) | collective-permute-done | bytes 294944 | tf_op jit(solution)/shard_map/ppermute | solution.py:33
  24.2 2.5 %collective-permute-done.5 = bf16[128,1152]{1,0:T(8,128)(2,1)S(1)} collective-permute-done((bf16[128,1152]{1,0:T(8,128)(2,1)}, bf16[128,1152]{1,0:T(8,128)(2,1)S(1)}, u32[]{:S(2)}, u32[]{:S(2)}) %collective-permute-start.5) | collective-permute-done | bytes 294944 | tf_op jit(solution)/shard_map/ppermute | solution.py:33
  26.7 1.1 %collective-permute-start.6 = (bf16[256,1152]{1,0:T(8,128)(2,1)S(1)}, bf16[256,1152]{1,0:T(8,128)(2,1)S(1)}, u32[]{:S(2)}, u32[]{:S(2)}) collective-permute-start(bf16[256,1152]{1,0:T(8,128)(2,1)S(1)} %pad_maximum_fusion.2.refs_0_), channel_id=1, source_target_pairs={{32,0},{33,1},{34,2},{35,3},{36,4},{37,5},{38,6},{39,7},{40,8},{41... | collective-permute-start | bytes 1769480 | tf_op jit(solution)/shard_map/ppermute | solution.py:33
  27.8 0.9 collective-permute-start.8
  28.7 2.3 %collective-permute-start.9 = (bf16[256,1152]{1,0:T(8,128)(2,1)S(1)}, bf16[256,1152]{1,0:T(8,128)(2,1)S(1)}, u32[]{:S(2)}, u32[]{:S(2)}) collective-permute-start(bf16[256,1152]{1,0:T(8,128)(2,1)S(1)} %pad_maximum_fusion.1.refs_5_.refs_1_), channel_id=1, source_target_pairs={{3,0},{2,1},{1,2},{0,3},{7,4},{6,5},{5,6},{4,7},{11,8},{10,9},{9,1... | collective-permute-start | bytes 1769480 | tf_op jit(solution)/shard_map/ppermute | solution.py:33
  30.9 7.7 %collective-permute-done.6.refs_2_ = bf16[256,1152]{1,0:T(8,128)(2,1)S(1)} collective-permute-done((bf16[256,1152]{1,0:T(8,128)(2,1)S(1)}, bf16[256,1152]{1,0:T(8,128)(2,1)S(1)}, u32[]{:S(2)}, u32[]{:S(2)}) %collective-permute-start.6) | collective-permute-done | bytes 589856 | tf_op jit(solution)/shard_map/ppermute | solution.py:33
  38.6 0.7 collective-permute-done.7.refs_3_
  39.4 1.3 %collective-permute-done.8.refs_6_.refs_2_ = bf16[256,1152]{1,0:T(8,128)(2,1)S(1)} collective-permute-done((bf16[256,1152]{1,0:T(8,128)(2,1)S(1)}, bf16[256,1152]{1,0:T(8,128)(2,1)S(1)}, u32[]{:S(2)}, u32[]{:S(2)}) %collective-permute-start.8) | collective-permute-done | bytes 589856 | tf_op jit(solution)/shard_map/ppermute | solution.py:33
  40.7 1.0 collective-permute-done.9.refs_7_.refs_3_
  41.7 0.5 collective-permute-start.11
  42.2 4.1 %own_logits.1 = (bf16[1024,1024]{1,0:T(8,128)(2,1)S(1)}, f32[8,128]{1,0:T(8,128)S(1)}) custom-call(s32[1]{0:T(128)} %bitcast.place_ref, f32[1,1]{1,0:T(1,128)} %bitcast.1.temper_ref, f32[1,1]{1,0:T(1,128)} %bitcast.2.shift_ref, bf16[256,1152]{1,0:T(8,128)(2,1)S(1)} %pad_maximum_fusion.2.refs_0_, bf16[256,1152]{1,0:T(8,128)(2,1)S(1)} %pad_maximum_fusion.refs_1_, ...), custom_call_target="tpu_custom_call" | custom-call | flops 2415919104 | bytes 8388608 | tf_op jit(solution)/shard_map/own_logits/pallas_call | solution.py:170
  46.4 7.1 %other_logits.1 = (bf16[1024,1024]{1,0:T(8,128)(2,1)S(1)}, bf16[512,1152]{1,0:T(8,128)(2,1)S(1)}, bf16[512,1152]{1,0:T(8,128)(2,1)S(1)}, f32[8,128]{1,0:T(8,128)S(1)}) custom-call(s32[1]{0:T(128)} %bitcast.place_ref, f32[1,1]{1,0:T(1,128)} %bitcast.1.temper_ref, f32[1,1]{1,0:T(1,128)} %bitcast.2.shift_ref, bf16[256,1152]{1,0:T(8,128)(2,1)S(1)} %pad_maximum_fusion.2.refs_0_, ...), custom_call_target="tpu_custom_call" | custom-call | flops 4831838208 | bytes 8388608 | tf_op jit(solution)/shard_map/other_logits/pallas_call | solution.py:170
  53.5 0.6 collective-permute-start.16
  54.1 0.1 collective-permute-start.17
  54.2 0.4 collective-permute-start.14
  54.6 2.9 %image_terms.2 = (bf16[256,1152]{1,0:T(8,128)(2,1)S(1)}, bf16[256,1152]{1,0:T(8,128)(2,1)S(1)}) custom-call(bf16[1024,1024]{1,0:T(8,128)(2,1)S(1)} %get-tuple-element.80.own_ref.coeff_ref, bf16[1024,1024]{1,0:T(8,128)(2,1)S(1)} %get-tuple-element.70.other_ref, bf16[256,1152]{1,0:T(8,128)(2,1)S(1)} %pad_maximum_fusion.3.refs_4_.refs_0_, ...), custom_call_target="tpu_custom_call" | custom-call | flops 2415919104 | bytes 8388608 | tf_op jit(solution)/shard_map/image_terms/pallas_call | solution.py:224
  57.5 0.7 collective-permute-done.14
  58.3 0.5 collective-permute-start.15
  58.7 0.1 collective-permute-start.28
  58.8 0.8 collective-permute-start.30
  59.6 2.2 %text_terms.3 = (bf16[256,1152]{1,0:T(8,128)(2,1)S(1)}, bf16[256,1152]{1,0:T(8,128)(2,1)S(1)}) custom-call(bf16[1024,1024]{1,0:T(8,128)(2,1)S(1)} %get-tuple-element.80.own_ref.coeff_ref, bf16[512,1152]{1,0:T(8,128)(2,1)S(1)} %collective-permute-done.17.came_ref, bf16[256,1152]{1,0:T(8,128)(2,1)S(1)} %pad_maximum_fusion.2.refs_0_, ...), custom_call_target="tpu_custom_call" | custom-call | flops 1207959552 | bytes 8388608 | tf_op jit(solution)/shard_map/text_terms/pallas_call | solution.py:196
  61.8 2.2 %collective-permute-start.20 = (bf16[256,1152]{1,0:T(8,128)(2,1)S(1)}, bf16[256,1152]{1,0:T(8,128)(2,1)S(1)}, u32[]{:S(2)}, u32[]{:S(2)}) collective-permute-start(bf16[256,1152]{1,0:T(8,128)(2,1)S(1)} %get-tuple-element.86), channel_id=1, source_target_pairs={{3,0},{2,1},{1,2},{0,3},{7,4},{6,5},{5,6},{4,7},{11,8},{10,9},{9,1... | collective-permute-start | bytes 1769480 | tf_op jit(solution)/shard_map/ppermute | solution.py:33
  64.1 0.1 collective-permute-done.15
  64.1 2.2 %collective-permute-start.21 = (f32[32,8,128]{2,1,0:T(8,128)S(1)}, f32[32,8,128]{2,1,0:T(8,128)S(1)}, u32[]{:S(2)}, u32[]{:S(2)}) collective-permute-start(f32[32,8,128]{2,1,0:T(8,128)S(1)} %broadcast_in_dim.5), channel_id=1, source_target_pairs={{20,0},{21,1},{22,2},{23,3},{16,4},{17,5},{18,6},{19,7},{28,8},{29... | collective-permute-start | bytes 393224 | tf_op jit(solution)/shard_map/ppermute | solution.py:33
  66.3 2.9 %image_terms.3 = (f32[256,1152]{1,0:T(8,128)S(1)}, f32[256,1152]{1,0:T(8,128)S(1)}) custom-call(bf16[1024,1024]{1,0:T(8,128)(2,1)S(1)} %get-tuple-element.80.own_ref.coeff_ref, bf16[1024,1024]{1,0:T(8,128)(2,1)S(1)} %get-tuple-element.70.other_ref, bf16[256,1152]{1,0:T(8,128)(2,1)S(1)} %pad_maximum_fusion.3.refs_4_.refs_0_, ...), custom_call_target="tpu_custom_call" | custom-call | flops 2415919104 | bytes 8388608 | tf_op jit(solution)/shard_map/image_terms/pallas_call | solution.py:224
  69.2 2.1 %collective-permute-start.18 = (bf16[256,1152]{1,0:T(8,128)(2,1)S(1)}, bf16[256,1152]{1,0:T(8,128)(2,1)S(1)}, u32[]{:S(2)}, u32[]{:S(2)}) collective-permute-start(bf16[256,1152]{1,0:T(8,128)(2,1)S(1)} %get-tuple-element.82), channel_id=1, source_target_pairs={{96,0},{97,1},{98,2},{99,3},{100,4},{101,5},{102,6},{103,7},{104,8... | collective-permute-start | bytes 1769480 | tf_op jit(solution)/shard_map/ppermute | solution.py:33
  71.3 1.8 %text_terms.2 = (f32[256,1152]{1,0:T(8,128)S(1)}, f32[256,1152]{1,0:T(8,128)S(1)}) custom-call(bf16[1024,1024]{1,0:T(8,128)(2,1)S(1)} %get-tuple-element.80.own_ref.coeff_ref, bf16[512,1152]{1,0:T(8,128)(2,1)S(1)} %collective-permute-done.16.came_ref, bf16[256,1152]{1,0:T(8,128)(2,1)S(1)} %pad_maximum_fusion.2.refs_0_, ...), custom_call_target="tpu_custom_call" | custom-call | flops 1207959552 | bytes 8388608 | tf_op jit(solution)/shard_map/text_terms/pallas_call | solution.py:196
  73.1 0.9 collective-permute-start.22
  74.0 0.1 collective-permute-done.30.came_ref
  74.1 0.4 fold.7
  74.6 1.8 %collective-permute-start.31 = (bf16[128,1152]{1,0:T(8,128)(2,1)S(1)}, bf16[128,1152]{1,0:T(8,128)(2,1)S(1)}, u32[]{:S(2)}, u32[]{:S(2)}) collective-permute-start(bf16[128,1152]{1,0:T(8,128)(2,1)S(1)} %get-tuple-element.98), channel_id=1, source_target_pairs={{32,0},{33,1},{34,2},{35,3},{36,4},{37,5},{38,6},{39,7},{40,8},{41... | collective-permute-start | bytes 884744 | tf_op jit(solution)/shard_map/ppermute | solution.py:33
  76.4 0.5 collective-permute-done.22
  76.8 1.3 %collective-permute-done.20.came_ref = bf16[256,1152]{1,0:T(8,128)(2,1)S(1)} collective-permute-done((bf16[256,1152]{1,0:T(8,128)(2,1)S(1)}, bf16[256,1152]{1,0:T(8,128)(2,1)S(1)}, u32[]{:S(2)}, u32[]{:S(2)}) %collective-permute-start.20) | collective-permute-done | bytes 589856 | tf_op jit(solution)/shard_map/ppermute | solution.py:33
  78.2 0.4 fold.5
  78.6 1.9 %collective-permute-start.23 = (bf16[128,1152]{1,0:T(8,128)(2,1)S(1)}, bf16[128,1152]{1,0:T(8,128)(2,1)S(1)}, u32[]{:S(2)}, u32[]{:S(2)}) collective-permute-start(bf16[128,1152]{1,0:T(8,128)(2,1)S(1)} %get-tuple-element.90), channel_id=1, source_target_pairs={{96,0},{97,1},{98,2},{99,3},{100,4},{101,5},{102,6},{103,7},{104,8... | collective-permute-start | bytes 884744 | tf_op jit(solution)/shard_map/ppermute | solution.py:33
  80.5 1.0 %collective-permute-start.24 = (f32[8,128]{1,0:T(8,128)S(1)}, f32[8,128]{1,0:T(8,128)S(1)}, u32[]{:S(2)}, u32[]{:S(2)}) collective-permute-start(f32[8,128]{1,0:T(8,128)S(1)} %add.25), channel_id=1, source_target_pairs={{32,0},{33,1},{34,2},{35,3},{36,4},{37,5},{38,6},{39,7},{40,8},{41... | collective-permute-start | bytes 12296 | tf_op jit(solution)/shard_map/ppermute | solution.py:33
  81.5 2.6 %collective-permute-done.24 = f32[8,128]{1,0:T(8,128)S(1)} collective-permute-done((f32[8,128]{1,0:T(8,128)S(1)}, f32[8,128]{1,0:T(8,128)S(1)}, u32[]{:S(2)}, u32[]{:S(2)}) %collective-permute-start.24) | collective-permute-done | bytes 4128 | tf_op jit(solution)/shard_map/ppermute | solution.py:33
  84.1 2.3 %collective-permute-start.25 = (f32[8,128]{1,0:T(8,128)S(1)}, f32[8,128]{1,0:T(8,128)S(1)}, u32[]{:S(2)}, u32[]{:S(2)}) collective-permute-start(f32[8,128]{1,0:T(8,128)S(1)} %add.26), channel_id=1, source_target_pairs={{3,0},{2,1},{1,2},{0,3},{7,4},{6,5},{5,6},{4,7},{11,8},{10,9},{9,1... | collective-permute-start | bytes 12296 | tf_op jit(solution)/shard_map/ppermute | solution.py:33
  86.4 0.4 fold.6
  86.9 0.1 collective-permute-start.29
  87.0 0.3 add_codes.3
  87.2 1.7 %collective-permute-start.32 = (bf16[128,1152]{1,0:T(8,128)(2,1)S(1)}, bf16[128,1152]{1,0:T(8,128)(2,1)S(1)}, u32[]{:S(2)}, u32[]{:S(2)}) collective-permute-start(bf16[128,1152]{1,0:T(8,128)(2,1)S(1)} %add_codes.3), channel_id=1, source_target_pairs={{16,0},{17,1},{18,2},{19,3},{20,4},{21,5},{22,6},{23,7},{24,8},{25... | collective-permute-start | bytes 884744 | tf_op jit(solution)/shard_map/ppermute | solution.py:33
  89.0 0.4 fold.4
  89.4 0.9 collective-permute-start.19
  90.4 0.9 collective-permute-done.23.came_ref
  91.3 0.3 add_codes.2
  91.6 1.2 %collective-permute-start.26 = (bf16[128,1152]{1,0:T(8,128)(2,1)S(1)}, bf16[128,1152]{1,0:T(8,128)(2,1)S(1)}, u32[]{:S(2)}, u32[]{:S(2)}) collective-permute-start(bf16[128,1152]{1,0:T(8,128)(2,1)S(1)} %add_codes.2), channel_id=1, source_target_pairs={{20,0},{21,1},{22,2},{23,3},{16,4},{17,5},{18,6},{19,7},{28,8},{29... | collective-permute-start | bytes 884744 | tf_op jit(solution)/shard_map/ppermute | solution.py:33
  92.9 1.9 %collective-permute-start.27 = (f32[8,128]{1,0:T(8,128)S(1)}, f32[8,128]{1,0:T(8,128)S(1)}, u32[]{:S(2)}, u32[]{:S(2)}) collective-permute-start(f32[8,128]{1,0:T(8,128)S(1)} %add.27.loss_ref.loss_in), channel_id=1, source_target_pairs={{96,0},{97,1},{98,2},{99,3},{100,4},{101,5},{102,6},{103,7},{104,8... | collective-permute-start | bytes 12296 | tf_op jit(solution)/shard_map/ppermute | solution.py:33
  94.8 1.4 %finish.3 = (f32[128,1152]{1,0:T(8,128)}, f32[1]{0:T(128)}) custom-call(bf16[128,1152]{1,0:T(8,128)(2,1)S(1)} %copy-done, f32[128,1152]{1,0:T(8,128)S(1)} %get-tuple-element.94.own_ref, bf16[128,1152]{1,0:T(8,128)(2,1)S(1)} %collective-permute-done.29.ring_ref, bf16[128,1152]{1,0:T(8,128)(2,1)S(1)} %collective-permute-done.32.far_ref, ...), custom_call_target="tpu_custom_call" | custom-call | tf_op jit(solution)/shard_map/finish/pallas_call | solution.py:275
  96.2 1.4 %collective-permute-done.27.loss_in = f32[8,128]{1,0:T(8,128)S(1)} collective-permute-done((f32[8,128]{1,0:T(8,128)S(1)}, f32[8,128]{1,0:T(8,128)S(1)}, u32[]{:S(2)}, u32[]{:S(2)}) %collective-permute-start.27) | collective-permute-done | bytes 4128 | tf_op jit(solution)/shard_map/ppermute | solution.py:33
  97.7 2.5 %collective-permute-done.26.far_ref = bf16[128,1152]{1,0:T(8,128)(2,1)S(1)} collective-permute-done((bf16[128,1152]{1,0:T(8,128)(2,1)S(1)}, bf16[128,1152]{1,0:T(8,128)(2,1)S(1)}, u32[]{:S(2)}, u32[]{:S(2)}) %collective-permute-start.26) | collective-permute-done | bytes 294944 | tf_op jit(solution)/shard_map/ppermute | solution.py:33
  100.2 1.4 %finish.2 = (f32[128,1152]{1,0:T(8,128)}, f32[1]{0:T(128)}) custom-call(bf16[128,1152]{1,0:T(8,128)(2,1)S(1)} %copy-done.1, f32[128,1152]{1,0:T(8,128)S(1)} %get-tuple-element.83.own_ref, bf16[128,1152]{1,0:T(8,128)(2,1)S(1)} %collective-permute-done.19.ring_ref, bf16[128,1152]{1,0:T(8,128)(2,1)S(1)} %collective-permute-done.26.far_ref, ...), custom_call_target="tpu_custom_call" | custom-call | tf_op jit(solution)/shard_map/finish/pallas_call | solution.py:275
  (38 shorter events, 0.3 us)
Async XLA Ops:
  0.6 8.9 %collective-permute-start = (bf16[128,1152]{1,0:T(8,128)(2,1)}, bf16[128,1152]{1,0:T(8,128)(2,1)S(1)}, u32[]{:S(2)}, u32[]{:S(2)}) collective-permute-start(bf16[128,1152]{1,0:T(8,128)(2,1)} %raw_ref.3), channel_id=1, source_target_pairs={{16,0},{17,1},{18,2},{19,3},{20,4},{21,5},{22,6},{23,7},{24,8},{25... | collective-permute-start | bytes 884744 | tf_op jit(solution)/shard_map/ppermute | solution.py:33
  2.3 9.9 %collective-permute-start.1 = (bf16[128,1152]{1,0:T(8,128)(2,1)}, bf16[128,1152]{1,0:T(8,128)(2,1)S(1)}, u32[]{:S(2)}, u32[]{:S(2)}) collective-permute-start(bf16[128,1152]{1,0:T(8,128)(2,1)} %raw_ref.2), channel_id=1, source_target_pairs={{20,0},{21,1},{22,2},{23,3},{16,4},{17,5},{18,6},{19,7},{28,8},{29... | collective-permute-start | bytes 884744 | tf_op jit(solution)/shard_map/ppermute | solution.py:33
  12.4 8.3 %collective-permute-start.2 = (bf16[128,1152]{1,0:T(8,128)(2,1)S(1)}, bf16[128,1152]{1,0:T(8,128)(2,1)S(1)}, u32[]{:S(2)}, u32[]{:S(2)}) collective-permute-start(bf16[128,1152]{1,0:T(8,128)(2,1)S(1)} %get-tuple-element.59), channel_id=1, source_target_pairs={{32,0},{33,1},{34,2},{35,3},{36,4},{37,5},{38,6},{39,7},{40,8},{41... | collective-permute-start | bytes 884744 | tf_op jit(solution)/shard_map/ppermute | solution.py:33
  14.4 9.7 %copy-start.3 = (bf16[128,1152]{1,0:T(8,128)(2,1)S(1)}, bf16[128,1152]{1,0:T(8,128)(2,1)}, u32[]{:S(2)}) copy-start(bf16[128,1152]{1,0:T(8,128)(2,1)} %get-tuple-element.61) | copy-start | bytes 884740
  14.4 8.5 %collective-permute-start.3 = (bf16[128,1152]{1,0:T(8,128)(2,1)S(1)}, bf16[128,1152]{1,0:T(8,128)(2,1)S(1)}, u32[]{:S(2)}, u32[]{:S(2)}) collective-permute-start(bf16[128,1152]{1,0:T(8,128)(2,1)S(1)} %get-tuple-element.60), channel_id=1, source_target_pairs={{96,0},{97,1},{98,2},{99,3},{100,4},{101,5},{102,6},{103,7},{104,8... | collective-permute-start | bytes 884744 | tf_op jit(solution)/shard_map/ppermute | solution.py:33
  16.9 7.2 %collective-permute-start.4 = (bf16[128,1152]{1,0:T(8,128)(2,1)}, bf16[128,1152]{1,0:T(8,128)(2,1)S(1)}, u32[]{:S(2)}, u32[]{:S(2)}) collective-permute-start(bf16[128,1152]{1,0:T(8,128)(2,1)} %get-tuple-element.61), channel_id=1, source_target_pairs={{1,0},{0,1},{3,2},{2,3},{5,4},{4,5},{7,6},{6,7},{9,8},{8,9},{11,10... | collective-permute-start | bytes 884744 | tf_op jit(solution)/shard_map/ppermute | solution.py:33
  18.5 8.1 %collective-permute-start.5 = (bf16[128,1152]{1,0:T(8,128)(2,1)}, bf16[128,1152]{1,0:T(8,128)(2,1)S(1)}, u32[]{:S(2)}, u32[]{:S(2)}) collective-permute-start(bf16[128,1152]{1,0:T(8,128)(2,1)} %get-tuple-element.62), channel_id=1, source_target_pairs={{3,0},{2,1},{1,2},{0,3},{7,4},{6,5},{5,6},{4,7},{11,8},{10,9},{9,1... | collective-permute-start | bytes 884744 | tf_op jit(solution)/shard_map/ppermute | solution.py:33
  20.7 5.9 %copy-start.2 = (bf16[128,1152]{1,0:T(8,128)(2,1)S(1)}, bf16[128,1152]{1,0:T(8,128)(2,1)}, u32[]{:S(2)}) copy-start(bf16[128,1152]{1,0:T(8,128)(2,1)} %get-tuple-element.62) | copy-start | bytes 884740
  26.7 12.0 %collective-permute-start.6 = (bf16[256,1152]{1,0:T(8,128)(2,1)S(1)}, bf16[256,1152]{1,0:T(8,128)(2,1)S(1)}, u32[]{:S(2)}, u32[]{:S(2)}) collective-permute-start(bf16[256,1152]{1,0:T(8,128)(2,1)S(1)} %pad_maximum_fusion.2.refs_0_), channel_id=1, source_target_pairs={{32,0},{33,1},{34,2},{35,3},{36,4},{37,5},{38,6},{39,7},{40,8},{41... | collective-permute-start | bytes 1769480 | tf_op jit(solution)/shard_map/ppermute | solution.py:33
  27.8 11.6 %collective-permute-start.7 = (bf16[256,1152]{1,0:T(8,128)(2,1)S(1)}, bf16[256,1152]{1,0:T(8,128)(2,1)S(1)}, u32[]{:S(2)}, u32[]{:S(2)}) collective-permute-start(bf16[256,1152]{1,0:T(8,128)(2,1)S(1)} %pad_maximum_fusion.refs_1_), channel_id=1, source_target_pairs={{1,0},{0,1},{3,2},{2,3},{5,4},{4,5},{7,6},{6,7},{9,8},{8,9},{11,10... | collective-permute-start | bytes 1769480 | tf_op jit(solution)/shard_map/ppermute | solution.py:33
  27.8 12.9 %collective-permute-start.8 = (bf16[256,1152]{1,0:T(8,128)(2,1)S(1)}, bf16[256,1152]{1,0:T(8,128)(2,1)S(1)}, u32[]{:S(2)}, u32[]{:S(2)}) collective-permute-start(bf16[256,1152]{1,0:T(8,128)(2,1)S(1)} %pad_maximum_fusion.3.refs_4_.refs_0_), channel_id=1, source_target_pairs={{96,0},{97,1},{98,2},{99,3},{100,4},{101,5},{102,6},{103,7},{104,8... | collective-permute-start | bytes 1769480 | tf_op jit(solution)/shard_map/ppermute | solution.py:33
  28.7 13.0 %collective-permute-start.9 = (bf16[256,1152]{1,0:T(8,128)(2,1)S(1)}, bf16[256,1152]{1,0:T(8,128)(2,1)S(1)}, u32[]{:S(2)}, u32[]{:S(2)}) collective-permute-start(bf16[256,1152]{1,0:T(8,128)(2,1)S(1)} %pad_maximum_fusion.1.refs_5_.refs_1_), channel_id=1, source_target_pairs={{3,0},{2,1},{1,2},{0,3},{7,4},{6,5},{5,6},{4,7},{11,8},{10,9},{9,1... | collective-permute-start | bytes 1769480 | tf_op jit(solution)/shard_map/ppermute | solution.py:33
  30.9 15.4 %collective-permute-start.10 = (bf16[256,1152]{1,0:T(8,128)(2,1)S(1)}, bf16[256,1152]{1,0:T(8,128)(2,1)S(1)}, u32[]{:S(2)}, u32[]{:S(2)}) collective-permute-start(bf16[256,1152]{1,0:T(8,128)(2,1)S(1)} %pad_maximum_fusion.3.refs_4_.refs_0_), channel_id=1, source_target_pairs={{8,0},{9,1},{10,2},{11,3},{12,4},{13,5},{14,6},{15,7},{0,8},{1,9},... | collective-permute-start | bytes 1769480 | tf_op jit(solution)/shard_map/ppermute | solution.py:33
  41.7 4.6 %collective-permute-start.12 = (bf16[256,1152]{1,0:T(8,128)(2,1)S(1)}, bf16[256,1152]{1,0:T(8,128)(2,1)S(1)}, u32[]{:S(2)}, u32[]{:S(2)}) collective-permute-start(bf16[256,1152]{1,0:T(8,128)(2,1)S(1)} %collective-permute-done.8.refs_6_.refs_2_), channel_id=1, source_target_pairs={{8,0},{9,1},{10,2},{11,3},{12,4},{13,5},{14,6},{15,7},{0,8},{1,9},... | collective-permute-start | bytes 1769480 | tf_op jit(solution)/shard_map/ppermute | solution.py:33
  41.7 4.6 %collective-permute-start.11 = (bf16[256,1152]{1,0:T(8,128)(2,1)S(1)}, bf16[256,1152]{1,0:T(8,128)(2,1)S(1)}, u32[]{:S(2)}, u32[]{:S(2)}) collective-permute-start(bf16[256,1152]{1,0:T(8,128)(2,1)S(1)} %pad_maximum_fusion.1.refs_5_.refs_1_), channel_id=1, source_target_pairs={{8,0},{9,1},{10,2},{11,3},{12,4},{13,5},{14,6},{15,7},{0,8},{1,9},... | collective-permute-start | bytes 1769480 | tf_op jit(solution)/shard_map/ppermute | solution.py:33
  42.2 4.1 %collective-permute-start.13 = (bf16[256,1152]{1,0:T(8,128)(2,1)S(1)}, bf16[256,1152]{1,0:T(8,128)(2,1)S(1)}, u32[]{:S(2)}, u32[]{:S(2)}) collective-permute-start(bf16[256,1152]{1,0:T(8,128)(2,1)S(1)} %collective-permute-done.9.refs_7_.refs_3_), channel_id=1, source_target_pairs={{8,0},{9,1},{10,2},{11,3},{12,4},{13,5},{14,6},{15,7},{0,8},{1,9},... | collective-permute-start | bytes 1769480 | tf_op jit(solution)/shard_map/ppermute | solution.py:33
  53.5 6.1 %collective-permute-start.16 = (bf16[512,1152]{1,0:T(8,128)(2,1)S(1)}, bf16[512,1152]{1,0:T(8,128)(2,1)S(1)}, u32[]{:S(2)}, u32[]{:S(2)}) collective-permute-start(bf16[512,1152]{1,0:T(8,128)(2,1)S(1)} %get-tuple-element.78), channel_id=1, source_target_pairs={{8,0},{9,1},{10,2},{11,3},{12,4},{13,5},{14,6},{15,7},{0,8},{1,9},... | collective-permute-start | bytes 3538952 | tf_op jit(solution)/shard_map/ppermute | solution.py:33
  54.1 5.5 %collective-permute-start.17 = (bf16[512,1152]{1,0:T(8,128)(2,1)S(1)}, bf16[512,1152]{1,0:T(8,128)(2,1)S(1)}, u32[]{:S(2)}, u32[]{:S(2)}) collective-permute-start(bf16[512,1152]{1,0:T(8,128)(2,1)S(1)} %get-tuple-element.81), channel_id=1, source_target_pairs={{8,0},{9,1},{10,2},{11,3},{12,4},{13,5},{14,6},{15,7},{0,8},{1,9},... | collective-permute-start | bytes 3538952 | tf_op jit(solution)/shard_map/ppermute | solution.py:33
  54.2 4.1 %collective-permute-start.14 = (f32[8,128]{1,0:T(8,128)S(1)}, f32[8,128]{1,0:T(8,128)S(1)}, u32[]{:S(2)}, u32[]{:S(2)}) collective-permute-start(f32[8,128]{1,0:T(8,128)S(1)} %get-tuple-element.72), channel_id=1, source_target_pairs={{8,0},{9,1},{10,2},{11,3},{12,4},{13,5},{14,6},{15,7},{0,8},{1,9},... | collective-permute-start | bytes 12296 | tf_op jit(solution)/shard_map/ppermute | solution.py:33
  58.3 5.9 %collective-permute-start.15 = (f32[32,8,128]{2,1,0:T(8,128)S(1)}, f32[32,8,128]{2,1,0:T(8,128)S(1)}, u32[]{:S(2)}, u32[]{:S(2)}) collective-permute-start(f32[32,8,128]{2,1,0:T(8,128)S(1)} %broadcast_in_dim.4), channel_id=1, source_target_pairs={{16,0},{17,1},{18,2},{19,3},{20,4},{21,5},{22,6},{23,7},{24,8},{25... | collective-permute-start | bytes 393224 | tf_op jit(solution)/shard_map/ppermute | solution.py:33
  58.7 27.7 %collective-permute-start.28 = (bf16[256,1152]{1,0:T(8,128)(2,1)S(1)}, bf16[256,1152]{1,0:T(8,128)(2,1)S(1)}, u32[]{:S(2)}, u32[]{:S(2)}) collective-permute-start(bf16[256,1152]{1,0:T(8,128)(2,1)S(1)} %get-tuple-element.73), channel_id=1, source_target_pairs={{32,0},{33,1},{34,2},{35,3},{36,4},{37,5},{38,6},{39,7},{40,8},{41... | collective-permute-start | bytes 1769480 | tf_op jit(solution)/shard_map/ppermute | solution.py:33
  58.8 15.3 %collective-permute-start.30 = (bf16[256,1152]{1,0:T(8,128)(2,1)S(1)}, bf16[256,1152]{1,0:T(8,128)(2,1)S(1)}, u32[]{:S(2)}, u32[]{:S(2)}) collective-permute-start(bf16[256,1152]{1,0:T(8,128)(2,1)S(1)} %get-tuple-element.71), channel_id=1, source_target_pairs={{1,0},{0,1},{3,2},{2,3},{5,4},{4,5},{7,6},{6,7},{9,8},{8,9},{11,10... | collective-permute-start | bytes 1769480 | tf_op jit(solution)/shard_map/ppermute | solution.py:33
  61.8 16.3 %collective-permute-start.20 = (bf16[256,1152]{1,0:T(8,128)(2,1)S(1)}, bf16[256,1152]{1,0:T(8,128)(2,1)S(1)}, u32[]{:S(2)}, u32[]{:S(2)}) collective-permute-start(bf16[256,1152]{1,0:T(8,128)(2,1)S(1)} %get-tuple-element.86), channel_id=1, source_target_pairs={{3,0},{2,1},{1,2},{0,3},{7,4},{6,5},{5,6},{4,7},{11,8},{10,9},{9,1... | collective-permute-start | bytes 1769480 | tf_op jit(solution)/shard_map/ppermute | solution.py:33
  64.1 9.0 %collective-permute-start.21 = (f32[32,8,128]{2,1,0:T(8,128)S(1)}, f32[32,8,128]{2,1,0:T(8,128)S(1)}, u32[]{:S(2)}, u32[]{:S(2)}) collective-permute-start(f32[32,8,128]{2,1,0:T(8,128)S(1)} %broadcast_in_dim.5), channel_id=1, source_target_pairs={{20,0},{21,1},{22,2},{23,3},{16,4},{17,5},{18,6},{19,7},{28,8},{29... | collective-permute-start | bytes 393224 | tf_op jit(solution)/shard_map/ppermute | solution.py:33
  69.2 19.8 %collective-permute-start.18 = (bf16[256,1152]{1,0:T(8,128)(2,1)S(1)}, bf16[256,1152]{1,0:T(8,128)(2,1)S(1)}, u32[]{:S(2)}, u32[]{:S(2)}) collective-permute-start(bf16[256,1152]{1,0:T(8,128)(2,1)S(1)} %get-tuple-element.82), channel_id=1, source_target_pairs={{96,0},{97,1},{98,2},{99,3},{100,4},{101,5},{102,6},{103,7},{104,8... | collective-permute-start | bytes 1769480 | tf_op jit(solution)/shard_map/ppermute | solution.py:33
  73.1 3.7 %collective-permute-start.22 = (f32[8,128]{1,0:T(8,128)S(1)}, f32[8,128]{1,0:T(8,128)S(1)}, u32[]{:S(2)}, u32[]{:S(2)}) collective-permute-start(f32[8,128]{1,0:T(8,128)S(1)} %fusion), channel_id=1, source_target_pairs={{1,0},{0,1},{3,2},{2,3},{5,4},{4,5},{7,6},{6,7},{9,8},{8,9},{11,10... | collective-permute-start | bytes 12296 | tf_op jit(solution)/shard_map/ppermute | solution.py:33
  74.6 12.4 %collective-permute-start.31 = (bf16[128,1152]{1,0:T(8,128)(2,1)S(1)}, bf16[128,1152]{1,0:T(8,128)(2,1)S(1)}, u32[]{:S(2)}, u32[]{:S(2)}) collective-permute-start(bf16[128,1152]{1,0:T(8,128)(2,1)S(1)} %get-tuple-element.98), channel_id=1, source_target_pairs={{32,0},{33,1},{34,2},{35,3},{36,4},{37,5},{38,6},{39,7},{40,8},{41... | collective-permute-start | bytes 884744 | tf_op jit(solution)/shard_map/ppermute | solution.py:33
  78.6 12.7 %collective-permute-start.23 = (bf16[128,1152]{1,0:T(8,128)(2,1)S(1)}, bf16[128,1152]{1,0:T(8,128)(2,1)S(1)}, u32[]{:S(2)}, u32[]{:S(2)}) collective-permute-start(bf16[128,1152]{1,0:T(8,128)(2,1)S(1)} %get-tuple-element.90), channel_id=1, source_target_pairs={{96,0},{97,1},{98,2},{99,3},{100,4},{101,5},{102,6},{103,7},{104,8... | collective-permute-start | bytes 884744 | tf_op jit(solution)/shard_map/ppermute | solution.py:33
  80.5 3.6 %collective-permute-start.24 = (f32[8,128]{1,0:T(8,128)S(1)}, f32[8,128]{1,0:T(8,128)S(1)}, u32[]{:S(2)}, u32[]{:S(2)}) collective-permute-start(f32[8,128]{1,0:T(8,128)S(1)} %add.25), channel_id=1, source_target_pairs={{32,0},{33,1},{34,2},{35,3},{36,4},{37,5},{38,6},{39,7},{40,8},{41... | collective-permute-start | bytes 12296 | tf_op jit(solution)/shard_map/ppermute | solution.py:33
  84.1 6.3 %collective-permute-start.25 = (f32[8,128]{1,0:T(8,128)S(1)}, f32[8,128]{1,0:T(8,128)S(1)}, u32[]{:S(2)}, u32[]{:S(2)}) collective-permute-start(f32[8,128]{1,0:T(8,128)S(1)} %add.26), channel_id=1, source_target_pairs={{3,0},{2,1},{1,2},{0,3},{7,4},{6,5},{5,6},{4,7},{11,8},{10,9},{9,1... | collective-permute-start | bytes 12296 | tf_op jit(solution)/shard_map/ppermute | solution.py:33
  86.9 7.9 %collective-permute-start.29 = (bf16[128,1152]{1,0:T(8,128)(2,1)S(1)}, bf16[128,1152]{1,0:T(8,128)(2,1)S(1)}, u32[]{:S(2)}, u32[]{:S(2)}) collective-permute-start(bf16[128,1152]{1,0:T(8,128)(2,1)S(1)} %get-tuple-element.95), channel_id=1, source_target_pairs={{1,0},{0,1},{3,2},{2,3},{5,4},{4,5},{7,6},{6,7},{9,8},{8,9},{11,10... | collective-permute-start | bytes 884744 | tf_op jit(solution)/shard_map/ppermute | solution.py:33
  87.2 7.6 %copy-start = (bf16[128,1152]{1,0:T(8,128)(2,1)S(1)}, bf16[128,1152]{1,0:T(8,128)(2,1)}, u32[]{:S(2)}) copy-start(bf16[128,1152]{1,0:T(8,128)(2,1)} %raw_ref.3) | copy-start | bytes 884740
  87.2 7.6 %collective-permute-start.32 = (bf16[128,1152]{1,0:T(8,128)(2,1)S(1)}, bf16[128,1152]{1,0:T(8,128)(2,1)S(1)}, u32[]{:S(2)}, u32[]{:S(2)}) collective-permute-start(bf16[128,1152]{1,0:T(8,128)(2,1)S(1)} %add_codes.3), channel_id=1, source_target_pairs={{16,0},{17,1},{18,2},{19,3},{20,4},{21,5},{22,6},{23,7},{24,8},{25... | collective-permute-start | bytes 884744 | tf_op jit(solution)/shard_map/ppermute | solution.py:33
  89.4 8.2 %collective-permute-start.19 = (bf16[128,1152]{1,0:T(8,128)(2,1)S(1)}, bf16[128,1152]{1,0:T(8,128)(2,1)S(1)}, u32[]{:S(2)}, u32[]{:S(2)}) collective-permute-start(bf16[128,1152]{1,0:T(8,128)(2,1)S(1)} %get-tuple-element.84), channel_id=1, source_target_pairs={{3,0},{2,1},{1,2},{0,3},{7,4},{6,5},{5,6},{4,7},{11,8},{10,9},{9,1... | collective-permute-start | bytes 884744 | tf_op jit(solution)/shard_map/ppermute | solution.py:33
  90.4 9.8 %copy-start.1 = (bf16[128,1152]{1,0:T(8,128)(2,1)S(1)}, bf16[128,1152]{1,0:T(8,128)(2,1)}, u32[]{:S(2)}) copy-start(bf16[128,1152]{1,0:T(8,128)(2,1)} %raw_ref.2) | copy-start | bytes 884740
  91.6 8.6 %collective-permute-start.26 = (bf16[128,1152]{1,0:T(8,128)(2,1)S(1)}, bf16[128,1152]{1,0:T(8,128)(2,1)S(1)}, u32[]{:S(2)}, u32[]{:S(2)}) collective-permute-start(bf16[128,1152]{1,0:T(8,128)(2,1)S(1)} %add_codes.2), channel_id=1, source_target_pairs={{20,0},{21,1},{22,2},{23,3},{16,4},{17,5},{18,6},{19,7},{28,8},{29... | collective-permute-start | bytes 884744 | tf_op jit(solution)/shard_map/ppermute | solution.py:33
  92.9 4.8 %collective-permute-start.27 = (f32[8,128]{1,0:T(8,128)S(1)}, f32[8,128]{1,0:T(8,128)S(1)}, u32[]{:S(2)}, u32[]{:S(2)}) collective-permute-start(f32[8,128]{1,0:T(8,128)S(1)} %add.27.loss_ref.loss_in), channel_id=1, source_target_pairs={{96,0},{97,1},{98,2},{99,3},{100,4},{101,5},{102,6},{103,7},{104,8... | collective-permute-start | bytes 12296 | tf_op jit(solution)/shard_map/ppermute | solution.py:33

commit v5 on v4

--- a/solution.py
+++ b/solution.py
@@ -282,16 +282,24 @@
     )(raw, own, ring, far, loss, loss_in)
 
 
+def stack_kernel(first_ref, second_ref, out_ref):
+    out_ref[:PIECE, :] = first_ref[...]
+    out_ref[PIECE:, :] = second_ref[...]
+
+
+def stack(first, second):
+    return small_call(stack_kernel, "stack", [shape_of(2 * PIECE, *first.shape[1:], first.dtype)], (first, second))[0]
+
+
 def gather(image, text, scalars):
     groups = ((image, IMAGE_PAIRS), (text, TEXT_PAIRS))
     far = [swap(raw, pairs["x"]) for raw, pairs in groups]
     image, text = unit_rows(image, text)
-    *far, image, text, scalars = lax.optimization_barrier((*far, image, text, scalars))
+    *far, scalars = lax.optimization_barrier((*far, scalars))
     far = small_call(far_kernel, "far_units", [shape_of(*part.shape, part.dtype) for part in far], far)
     groups = ((image, IMAGE_PAIRS), (text, TEXT_PAIRS))
     far = [jnp.concatenate([part, swap(part, pairs["z"])], axis=0) for part, (_, pairs) in zip(far, groups)]
-    near = [jnp.concatenate([unit, swap(unit, pairs["y"])], axis=0) for unit, pairs in groups]
-    *far, near[0], near[1] = lax.optimization_barrier((*far, *near))
+    near = [stack(unit, swap(unit, pairs["y"])) for unit, pairs in groups]
     far_late = [swap(part, pairs["y"]) for part, (_, pairs) in zip(far, groups)]
     near_late = [swap(part, pairs["z"]) for part, (_, pairs) in zip(near, groups)]
     images, texts = ([near[k], far[k], near_late[k], far_late[k]] for k in range(2))

time: 102 us -> 98 us (0.961)
  waiting for transfers between devices: 31.2 us -> 24.4 us
  starting transfers between devices: 39.5 us -> 42.3 us
    ppermute x33, waiting for transfers between devices: 31.2 us -> 24.4 us  [swap(): lax.ppermute(value, axes, [(k ^ mask, k) for k in range(lax.axis_size(axe...]
    ppermute x33, starting transfers between devices: 39.5 us -> 42.3 us  [swap(): lax.ppermute(value, axes, [(k ^ mask, k) for k in range(lax.axis_size(axe...]
    pallas_call x7 -> x9, Pallas kernels: 2.51 us -> 2.59 us  [small_call(): pl.pallas_call(kernel, out_shape=out_shape, in_specs=[VMEM] * len(operand...]
  transfers between devices with their start and end apart: 33 -> 33, of which waited for: 18 -> 15; matrix products, arithmetic and copies ran while one was open for 0% -> 0% of each run, Pallas kernels for 19% -> 20%
where the time goes in v5:
time: 98 us; the launch traced here: 97.9 us
  starting transfers between devices  42.3 us (43%)
  Pallas kernels  28.6 us (29%)
  waiting for transfers between devices  24.4 us (25%)
  between operations  2.41 us (2%)
    ppermute x33, starting transfers between devices, swap(): lax.ppermute(value, axes, [(k ^ mask, k) for k in range(lax.axis_size(axe...  42.3 us
    ppermute x33, waiting for transfers between devices, swap(): lax.ppermute(value, axes, [(k ^ mask, k) for k in range(lax.axis_size(axe...  24.4 us
    pallas_call x2, Pallas kernels, logit_terms(): pl.pallas_call(functools.partial(logit_kernel, core, loss_scale), out_sha...  11.3 us
    pallas_call x2, Pallas kernels, image_terms(): pl.pallas_call(functools.partial(image_kernel, first), out_shape=[shape_o...  5.82 us
    pallas_call x2, Pallas kernels, text_terms(): pl.pallas_call(functools.partial(text_kernel, first), out_shape=[shape_of...  4.06 us
    pallas_call x2, Pallas kernels, finish(): pl.pallas_call(finish_kernel, out_shape=[shape_of(*raw.shape, jnp.float32...  2.86 us
    pallas_call x9, Pallas kernels, small_call(): pl.pallas_call(kernel, out_shape=out_shape, in_specs=[VMEM] * len(operand...  2.59 us
    pallas_call x1, Pallas kernels, unit_rows(): pl.pallas_call(unit_kernel, out_shape=[out, out], in_specs=[HBM, HBM], ou...  1.99 us
  transfers between devices with their start and end apart: 33, of which 15 were waited for; matrix products, arithmetic and copies ran while one was open for 0% of the time, Pallas kernels for 20%

profile of v5, /device:TPU:0, one launch (start us, length us, event | category | flops | bytes accessed | tf_op | source)
XLA Modules:
  0.0 97.9 jit_solution(17341952220445859453)
XLA Ops:
  0.6 1.7 %collective-permute-start = (bf16[128,1152]{1,0:T(8,128)(2,1)}, bf16[128,1152]{1,0:T(8,128)(2,1)S(1)}, u32[]{:S(2)}, u32[]{:S(2)}) collective-permute-start(bf16[128,1152]{1,0:T(8,128)(2,1)} %raw_ref.3), channel_id=1, source_target_pairs={{16,0},{17,1},{18,2},{19,3},{20,4},{21,5},{22,6},{23,7},{24,8},{25... | collective-permute-start | bytes 884744 | tf_op jit(solution)/shard_map/ppermute | solution.py:33
  2.3 2.1 %collective-permute-start.1 = (bf16[128,1152]{1,0:T(8,128)(2,1)}, bf16[128,1152]{1,0:T(8,128)(2,1)S(1)}, u32[]{:S(2)}, u32[]{:S(2)}) collective-permute-start(bf16[128,1152]{1,0:T(8,128)(2,1)} %raw_ref.2), channel_id=1, source_target_pairs={{20,0},{21,1},{22,2},{23,3},{16,4},{17,5},{18,6},{19,7},{28,8},{29... | collective-permute-start | bytes 884744 | tf_op jit(solution)/shard_map/ppermute | solution.py:33
  4.4 2.0 %unit_rows.1 = (bf16[128,1152]{1,0:T(8,128)(2,1)}, bf16[128,1152]{1,0:T(8,128)(2,1)}) custom-call(bf16[128,1152]{1,0:T(8,128)(2,1)} %raw_ref.3, bf16[128,1152]{1,0:T(8,128)(2,1)} %raw_ref.2), custom_call_target="tpu_custom_call" | custom-call | tf_op jit(solution)/shard_map/unit_rows/pallas_call | solution.py:60
  6.4 0.0 copy-start.3
  6.4 1.7 %collective-permute-start.2 = (bf16[128,1152]{1,0:T(8,128)(2,1)}, bf16[128,1152]{1,0:T(8,128)(2,1)S(1)}, u32[]{:S(2)}, u32[]{:S(2)}) collective-permute-start(bf16[128,1152]{1,0:T(8,128)(2,1)} %get-tuple-element.49.first_ref), channel_id=1, source_target_pairs={{1,0},{0,1},{3,2},{2,3},{5,4},{4,5},{7,6},{6,7},{9,8},{8,9},{11,10... | collective-permute-start | bytes 884744 | tf_op jit(solution)/shard_map/ppermute | solution.py:33
  8.0 2.2 %collective-permute-start.6 = (bf16[128,1152]{1,0:T(8,128)(2,1)}, bf16[128,1152]{1,0:T(8,128)(2,1)S(1)}, u32[]{:S(2)}, u32[]{:S(2)}) collective-permute-start(bf16[128,1152]{1,0:T(8,128)(2,1)} %get-tuple-element.53.first_ref), channel_id=1, source_target_pairs={{3,0},{2,1},{1,2},{0,3},{7,4},{6,5},{5,6},{4,7},{11,8},{10,9},{9,1... | collective-permute-start | bytes 884744 | tf_op jit(solution)/shard_map/ppermute | solution.py:33
  11.6 0.0 collective-permute-done.images_ref
  11.6 0.6 collective-permute-done.1.texts_ref
  12.2 0.2 far_units.1
  12.4 2.0 %collective-permute-start.3 = (bf16[128,1152]{1,0:T(8,128)(2,1)S(1)}, bf16[128,1152]{1,0:T(8,128)(2,1)S(1)}, u32[]{:S(2)}, u32[]{:S(2)}) collective-permute-start(bf16[128,1152]{1,0:T(8,128)(2,1)S(1)} %get-tuple-element.52), channel_id=1, source_target_pairs={{32,0},{33,1},{34,2},{35,3},{36,4},{37,5},{38,6},{39,7},{40,8},{41... | collective-permute-start | bytes 884744 | tf_op jit(solution)/shard_map/ppermute | solution.py:33
  14.4 2.5 %collective-permute-start.7 = (bf16[128,1152]{1,0:T(8,128)(2,1)S(1)}, bf16[128,1152]{1,0:T(8,128)(2,1)S(1)}, u32[]{:S(2)}, u32[]{:S(2)}) collective-permute-start(bf16[128,1152]{1,0:T(8,128)(2,1)S(1)} %get-tuple-element.54), channel_id=1, source_target_pairs={{96,0},{97,1},{98,2},{99,3},{100,4},{101,5},{102,6},{103,7},{104,8... | collective-permute-start | bytes 884744 | tf_op jit(solution)/shard_map/ppermute | solution.py:33
  17.0 0.4 collective-permute-done.6.second_ref
  17.4 4.1 %collective-permute-start.8 = (bf16[256,1152]{1,0:T(8,128)(2,1)S(1)}, bf16[256,1152]{1,0:T(8,128)(2,1)S(1)}, u32[]{:S(2)}, u32[]{:S(2)}) collective-permute-start(bf16[256,1152]{1,0:T(8,128)(2,1)S(1)} %stack.3.refs_4_.refs_0_), channel_id=1, source_target_pairs={{96,0},{97,1},{98,2},{99,3},{100,4},{101,5},{102,6},{103,7},{104,8... | collective-permute-start | bytes 1769480 | tf_op jit(solution)/shard_map/ppermute | solution.py:33
  21.6 0.1 collective-permute-start.4
  21.7 3.5 %collective-permute-done.7 = bf16[128,1152]{1,0:T(8,128)(2,1)S(1)} collective-permute-done((bf16[128,1152]{1,0:T(8,128)(2,1)S(1)}, bf16[128,1152]{1,0:T(8,128)(2,1)S(1)}, u32[]{:S(2)}, u32[]{:S(2)}) %collective-permute-start.7) | collective-permute-done | bytes 294944 | tf_op jit(solution)/shard_map/ppermute | solution.py:33
  25.3 3.4 %collective-permute-start.9 = (bf16[256,1152]{1,0:T(8,128)(2,1)S(1)}, bf16[256,1152]{1,0:T(8,128)(2,1)S(1)}, u32[]{:S(2)}, u32[]{:S(2)}) collective-permute-start(bf16[256,1152]{1,0:T(8,128)(2,1)S(1)} %constant_dynamic-update-slice_fusion.2.refs_5_.refs_1_), channel_id=1, source_target_pairs={{3,0},{2,1},{1,2},{0,3},{7,4},{6,5},{5,6},{4,7},{11,8},{10,9},{9,1... | collective-permute-start | bytes 1769480 | tf_op jit(solution)/shard_map/ppermute | solution.py:33
  28.7 0.2 collective-permute-start.5
  28.9 6.6 %collective-permute-done.8.refs_6_.refs_2_ = bf16[256,1152]{1,0:T(8,128)(2,1)S(1)} collective-permute-done((bf16[256,1152]{1,0:T(8,128)(2,1)S(1)}, bf16[256,1152]{1,0:T(8,128)(2,1)S(1)}, u32[]{:S(2)}, u32[]{:S(2)}) %collective-permute-start.8) | collective-permute-done | bytes 589856 | tf_op jit(solution)/shard_map/ppermute | solution.py:33
  35.5 1.4 %collective-permute-done.9.refs_7_.refs_3_ = bf16[256,1152]{1,0:T(8,128)(2,1)S(1)} collective-permute-done((bf16[256,1152]{1,0:T(8,128)(2,1)S(1)}, bf16[256,1152]{1,0:T(8,128)(2,1)S(1)}, u32[]{:S(2)}, u32[]{:S(2)}) %collective-permute-start.9) | collective-permute-done | bytes 589856 | tf_op jit(solution)/shard_map/ppermute | solution.py:33
  36.9 1.7 %collective-permute-done.5.refs_3_ = bf16[256,1152]{1,0:T(8,128)(2,1)S(1)} collective-permute-done((bf16[256,1152]{1,0:T(8,128)(2,1)S(1)}, bf16[256,1152]{1,0:T(8,128)(2,1)S(1)}, u32[]{:S(2)}, u32[]{:S(2)}) %collective-permute-start.5) | collective-permute-done | bytes 589856 | tf_op jit(solution)/shard_map/ppermute | solution.py:33
  38.7 0.5 collective-permute-start.11
  39.2 4.1 %own_logits.1 = (bf16[1024,1024]{1,0:T(8,128)(2,1)S(1)}, f32[8,128]{1,0:T(8,128)S(1)}) custom-call(s32[1]{0:T(128)} %bitcast.place_ref, f32[1,1]{1,0:T(1,128)} %bitcast.1.temper_ref, f32[1,1]{1,0:T(1,128)} %bitcast.2.shift_ref, bf16[256,1152]{1,0:T(8,128)(2,1)S(1)} %stack.2.refs_0_, bf16[256,1152]{1,0:T(8,128)(2,1)S(1)} %constant_dynamic-update-slice_fusion.refs_1_, ...), custom_call_target="tpu_custom_call" | custom-call | flops 2415919104 | bytes 8388608 | tf_op jit(solution)/shard_map/own_logits/pallas_call | solution.py:170
  43.3 7.2 %other_logits.1 = (bf16[1024,1024]{1,0:T(8,128)(2,1)S(1)}, bf16[512,1152]{1,0:T(8,128)(2,1)S(1)}, bf16[512,1152]{1,0:T(8,128)(2,1)S(1)}, f32[8,128]{1,0:T(8,128)S(1)}) custom-call(s32[1]{0:T(128)} %bitcast.place_ref, f32[1,1]{1,0:T(1,128)} %bitcast.1.temper_ref, f32[1,1]{1,0:T(1,128)} %bitcast.2.shift_ref, bf16[256,1152]{1,0:T(8,128)(2,1)S(1)} %stack.2.refs_0_, ...), custom_call_target="tpu_custom_call" | custom-call | flops 4831838208 | bytes 8388608 | tf_op jit(solution)/shard_map/other_logits/pallas_call | solution.py:170
  50.5 0.1 collective-permute-start.16
  50.6 0.5 collective-permute-start.17
  51.1 0.1 collective-permute-start.14
  51.2 2.9 %image_terms.2 = (bf16[256,1152]{1,0:T(8,128)(2,1)S(1)}, bf16[256,1152]{1,0:T(8,128)(2,1)S(1)}) custom-call(bf16[1024,1024]{1,0:T(8,128)(2,1)S(1)} %get-tuple-element.68.own_ref.coeff_ref, bf16[1024,1024]{1,0:T(8,128)(2,1)S(1)} %get-tuple-element.58.other_ref, bf16[256,1152]{1,0:T(8,128)(2,1)S(1)} %stack.3.refs_4_.refs_0_, ...), custom_call_target="tpu_custom_call" | custom-call | flops 2415919104 | bytes 8388608 | tf_op jit(solution)/shard_map/image_terms/pallas_call | solution.py:224
  54.1 1.0 %collective-permute-done.14 = f32[8,128]{1,0:T(8,128)S(1)} collective-permute-done((f32[8,128]{1,0:T(8,128)S(1)}, f32[8,128]{1,0:T(8,128)S(1)}, u32[]{:S(2)}, u32[]{:S(2)}) %collective-permute-start.14) | collective-permute-done | bytes 4128 | tf_op jit(solution)/shard_map/ppermute | solution.py:33
  55.1 0.3 collective-permute-start.15
  55.4 0.9 collective-permute-start.28
  56.3 0.3 collective-permute-start.30
  56.6 2.2 %text_terms.3 = (bf16[256,1152]{1,0:T(8,128)(2,1)S(1)}, bf16[256,1152]{1,0:T(8,128)(2,1)S(1)}) custom-call(bf16[1024,1024]{1,0:T(8,128)(2,1)S(1)} %get-tuple-element.68.own_ref.coeff_ref, bf16[512,1152]{1,0:T(8,128)(2,1)S(1)} %collective-permute-done.17.came_ref, bf16[256,1152]{1,0:T(8,128)(2,1)S(1)} %stack.2.refs_0_, ...), custom_call_target="tpu_custom_call" | custom-call | flops 1207959552 | bytes 8388608 | tf_op jit(solution)/shard_map/text_terms/pallas_call | solution.py:196
  58.8 1.2 %collective-permute-start.20 = (bf16[256,1152]{1,0:T(8,128)(2,1)S(1)}, bf16[256,1152]{1,0:T(8,128)(2,1)S(1)}, u32[]{:S(2)}, u32[]{:S(2)}) collective-permute-start(bf16[256,1152]{1,0:T(8,128)(2,1)S(1)} %get-tuple-element.74), channel_id=1, source_target_pairs={{3,0},{2,1},{1,2},{0,3},{7,4},{6,5},{5,6},{4,7},{11,8},{10,9},{9,1... | collective-permute-start | bytes 1769480 | tf_op jit(solution)/shard_map/ppermute | solution.py:33
  60.0 0.8 collective-permute-done.15
  60.7 2.2 %collective-permute-start.21 = (f32[32,8,128]{2,1,0:T(8,128)S(1)}, f32[32,8,128]{2,1,0:T(8,128)S(1)}, u32[]{:S(2)}, u32[]{:S(2)}) collective-permute-start(f32[32,8,128]{2,1,0:T(8,128)S(1)} %broadcast_in_dim.5), channel_id=1, source_target_pairs={{20,0},{21,1},{22,2},{23,3},{16,4},{17,5},{18,6},{19,7},{28,8},{29... | collective-permute-start | bytes 393224 | tf_op jit(solution)/shard_map/ppermute | solution.py:33
  62.9 2.9 %image_terms.3 = (f32[256,1152]{1,0:T(8,128)S(1)}, f32[256,1152]{1,0:T(8,128)S(1)}) custom-call(bf16[1024,1024]{1,0:T(8,128)(2,1)S(1)} %get-tuple-element.68.own_ref.coeff_ref, bf16[1024,1024]{1,0:T(8,128)(2,1)S(1)} %get-tuple-element.58.other_ref, bf16[256,1152]{1,0:T(8,128)(2,1)S(1)} %stack.3.refs_4_.refs_0_, ...), custom_call_target="tpu_custom_call" | custom-call | flops 2415919104 | bytes 8388608 | tf_op jit(solution)/shard_map/image_terms/pallas_call | solution.py:224
  65.8 2.6 %collective-permute-start.18 = (bf16[256,1152]{1,0:T(8,128)(2,1)S(1)}, bf16[256,1152]{1,0:T(8,128)(2,1)S(1)}, u32[]{:S(2)}, u32[]{:S(2)}) collective-permute-start(bf16[256,1152]{1,0:T(8,128)(2,1)S(1)} %get-tuple-element.70), channel_id=1, source_target_pairs={{96,0},{97,1},{98,2},{99,3},{100,4},{101,5},{102,6},{103,7},{104,8... | collective-permute-start | bytes 1769480 | tf_op jit(solution)/shard_map/ppermute | solution.py:33
  68.4 1.8 %text_terms.2 = (f32[256,1152]{1,0:T(8,128)S(1)}, f32[256,1152]{1,0:T(8,128)S(1)}) custom-call(bf16[1024,1024]{1,0:T(8,128)(2,1)S(1)} %get-tuple-element.68.own_ref.coeff_ref, bf16[512,1152]{1,0:T(8,128)(2,1)S(1)} %collective-permute-done.16.came_ref, bf16[256,1152]{1,0:T(8,128)(2,1)S(1)} %stack.2.refs_0_, ...), custom_call_target="tpu_custom_call" | custom-call | flops 1207959552 | bytes 8388608 | tf_op jit(solution)/shard_map/text_terms/pallas_call | solution.py:196
  70.3 0.2 collective-permute-start.22
  70.5 0.6 collective-permute-done.30.came_ref
  71.1 0.4 fold.7
  71.5 1.4 %collective-permute-start.31 = (bf16[128,1152]{1,0:T(8,128)(2,1)S(1)}, bf16[128,1152]{1,0:T(8,128)(2,1)S(1)}, u32[]{:S(2)}, u32[]{:S(2)}) collective-permute-start(bf16[128,1152]{1,0:T(8,128)(2,1)S(1)} %get-tuple-element.86), channel_id=1, source_target_pairs={{32,0},{33,1},{34,2},{35,3},{36,4},{37,5},{38,6},{39,7},{40,8},{41... | collective-permute-start | bytes 884744 | tf_op jit(solution)/shard_map/ppermute | solution.py:33
  73.0 1.0 %collective-permute-done.22 = f32[8,128]{1,0:T(8,128)S(1)} collective-permute-done((f32[8,128]{1,0:T(8,128)S(1)}, f32[8,128]{1,0:T(8,128)S(1)}, u32[]{:S(2)}, u32[]{:S(2)}) %collective-permute-start.22) | collective-permute-done | bytes 4128 | tf_op jit(solution)/shard_map/ppermute | solution.py:33
  74.0 0.7 collective-permute-done.20.came_ref
  74.6 0.4 fold.5
  75.1 2.3 %collective-permute-start.23 = (bf16[128,1152]{1,0:T(8,128)(2,1)S(1)}, bf16[128,1152]{1,0:T(8,128)(2,1)S(1)}, u32[]{:S(2)}, u32[]{:S(2)}) collective-permute-start(bf16[128,1152]{1,0:T(8,128)(2,1)S(1)} %get-tuple-element.78), channel_id=1, source_target_pairs={{96,0},{97,1},{98,2},{99,3},{100,4},{101,5},{102,6},{103,7},{104,8... | collective-permute-start | bytes 884744 | tf_op jit(solution)/shard_map/ppermute | solution.py:33
  77.3 1.0 %collective-permute-start.24 = (f32[8,128]{1,0:T(8,128)S(1)}, f32[8,128]{1,0:T(8,128)S(1)}, u32[]{:S(2)}, u32[]{:S(2)}) collective-permute-start(f32[8,128]{1,0:T(8,128)S(1)} %add.25), channel_id=1, source_target_pairs={{32,0},{33,1},{34,2},{35,3},{36,4},{37,5},{38,6},{39,7},{40,8},{41... | collective-permute-start | bytes 12296 | tf_op jit(solution)/shard_map/ppermute | solution.py:33
  78.4 2.6 %collective-permute-done.24 = f32[8,128]{1,0:T(8,128)S(1)} collective-permute-done((f32[8,128]{1,0:T(8,128)S(1)}, f32[8,128]{1,0:T(8,128)S(1)}, u32[]{:S(2)}, u32[]{:S(2)}) %collective-permute-start.24) | collective-permute-done | bytes 4128 | tf_op jit(solution)/shard_map/ppermute | solution.py:33
  81.0 1.2 %collective-permute-start.25 = (f32[8,128]{1,0:T(8,128)S(1)}, f32[8,128]{1,0:T(8,128)S(1)}, u32[]{:S(2)}, u32[]{:S(2)}) collective-permute-start(f32[8,128]{1,0:T(8,128)S(1)} %add.26), channel_id=1, source_target_pairs={{3,0},{2,1},{1,2},{0,3},{7,4},{6,5},{5,6},{4,7},{11,8},{10,9},{9,1... | collective-permute-start | bytes 12296 | tf_op jit(solution)/shard_map/ppermute | solution.py:33
  82.2 0.4 fold.6
  82.6 0.1 collective-permute-start.29
  82.7 0.3 add_codes.3
  83.0 0.0 copy-start
  83.0 1.7 %collective-permute-start.32 = (bf16[128,1152]{1,0:T(8,128)(2,1)S(1)}, bf16[128,1152]{1,0:T(8,128)(2,1)S(1)}, u32[]{:S(2)}, u32[]{:S(2)}) collective-permute-start(bf16[128,1152]{1,0:T(8,128)(2,1)S(1)} %add_codes.3), channel_id=1, source_target_pairs={{16,0},{17,1},{18,2},{19,3},{20,4},{21,5},{22,6},{23,7},{24,8},{25... | collective-permute-start | bytes 884744 | tf_op jit(solution)/shard_map/ppermute | solution.py:33
  84.8 0.4 fold.4
  85.2 2.1 %collective-permute-start.19 = (bf16[128,1152]{1,0:T(8,128)(2,1)S(1)}, bf16[128,1152]{1,0:T(8,128)(2,1)S(1)}, u32[]{:S(2)}, u32[]{:S(2)}) collective-permute-start(bf16[128,1152]{1,0:T(8,128)(2,1)S(1)} %get-tuple-element.72), channel_id=1, source_target_pairs={{3,0},{2,1},{1,2},{0,3},{7,4},{6,5},{5,6},{4,7},{11,8},{10,9},{9,1... | collective-permute-start | bytes 884744 | tf_op jit(solution)/shard_map/ppermute | solution.py:33
  87.3 0.4 collective-permute-done.23.came_ref
  87.7 0.3 add_codes.2
  88.0 1.8 %collective-permute-start.26 = (bf16[128,1152]{1,0:T(8,128)(2,1)S(1)}, bf16[128,1152]{1,0:T(8,128)(2,1)S(1)}, u32[]{:S(2)}, u32[]{:S(2)}) collective-permute-start(bf16[128,1152]{1,0:T(8,128)(2,1)S(1)} %add_codes.2), channel_id=1, source_target_pairs={{20,0},{21,1},{22,2},{23,3},{16,4},{17,5},{18,6},{19,7},{28,8},{29... | collective-permute-start | bytes 884744 | tf_op jit(solution)/shard_map/ppermute | solution.py:33
  89.8 1.9 %collective-permute-start.27 = (f32[8,128]{1,0:T(8,128)S(1)}, f32[8,128]{1,0:T(8,128)S(1)}, u32[]{:S(2)}, u32[]{:S(2)}) collective-permute-start(f32[8,128]{1,0:T(8,128)S(1)} %add.27.loss_ref.loss_in), channel_id=1, source_target_pairs={{96,0},{97,1},{98,2},{99,3},{100,4},{101,5},{102,6},{103,7},{104,8... | collective-permute-start | bytes 12296 | tf_op jit(solution)/shard_map/ppermute | solution.py:33
  91.7 1.4 %finish.3 = (f32[128,1152]{1,0:T(8,128)}, f32[1]{0:T(128)}) custom-call(bf16[128,1152]{1,0:T(8,128)(2,1)S(1)} %copy-done, f32[128,1152]{1,0:T(8,128)S(1)} %get-tuple-element.82.own_ref, bf16[128,1152]{1,0:T(8,128)(2,1)S(1)} %collective-permute-done.29.ring_ref, bf16[128,1152]{1,0:T(8,128)(2,1)S(1)} %collective-permute-done.32.far_ref, ...), custom_call_target="tpu_custom_call" | custom-call | tf_op jit(solution)/shard_map/finish/pallas_call | solution.py:275
  93.2 1.4 %collective-permute-done.27.loss_in = f32[8,128]{1,0:T(8,128)S(1)} collective-permute-done((f32[8,128]{1,0:T(8,128)S(1)}, f32[8,128]{1,0:T(8,128)S(1)}, u32[]{:S(2)}, u32[]{:S(2)}) %collective-permute-start.27) | collective-permute-done | bytes 4128 | tf_op jit(solution)/shard_map/ppermute | solution.py:33
  94.6 1.7 %collective-permute-done.26.far_ref = bf16[128,1152]{1,0:T(8,128)(2,1)S(1)} collective-permute-done((bf16[128,1152]{1,0:T(8,128)(2,1)S(1)}, bf16[128,1152]{1,0:T(8,128)(2,1)S(1)}, u32[]{:S(2)}, u32[]{:S(2)}) %collective-permute-start.26) | collective-permute-done | bytes 294944 | tf_op jit(solution)/shard_map/ppermute | solution.py:33
  96.3 1.4 %finish.2 = (f32[128,1152]{1,0:T(8,128)}, f32[1]{0:T(128)}) custom-call(bf16[128,1152]{1,0:T(8,128)(2,1)S(1)} %copy-done.1, f32[128,1152]{1,0:T(8,128)S(1)} %get-tuple-element.71.own_ref, bf16[128,1152]{1,0:T(8,128)(2,1)S(1)} %collective-permute-done.19.ring_ref, bf16[128,1152]{1,0:T(8,128)(2,1)S(1)} %collective-permute-done.26.far_ref, ...), custom_call_target="tpu_custom_call" | custom-call | tf_op jit(solution)/shard_map/finish/pallas_call | solution.py:275
  (40 shorter events, 0.3 us)
Async XLA Ops:
  0.6 10.9 %collective-permute-start = (bf16[128,1152]{1,0:T(8,128)(2,1)}, bf16[128,1152]{1,0:T(8,128)(2,1)S(1)}, u32[]{:S(2)}, u32[]{:S(2)}) collective-permute-start(bf16[128,1152]{1,0:T(8,128)(2,1)} %raw_ref.3), channel_id=1, source_target_pairs={{16,0},{17,1},{18,2},{19,3},{20,4},{21,5},{22,6},{23,7},{24,8},{25... | collective-permute-start | bytes 884744 | tf_op jit(solution)/shard_map/ppermute | solution.py:33
  2.3 9.9 %collective-permute-start.1 = (bf16[128,1152]{1,0:T(8,128)(2,1)}, bf16[128,1152]{1,0:T(8,128)(2,1)S(1)}, u32[]{:S(2)}, u32[]{:S(2)}) collective-permute-start(bf16[128,1152]{1,0:T(8,128)(2,1)} %raw_ref.2), channel_id=1, source_target_pairs={{20,0},{21,1},{22,2},{23,3},{16,4},{17,5},{18,6},{19,7},{28,8},{29... | collective-permute-start | bytes 884744 | tf_op jit(solution)/shard_map/ppermute | solution.py:33
  6.4 11.0 %copy-start.3 = (bf16[128,1152]{1,0:T(8,128)(2,1)S(1)}, bf16[128,1152]{1,0:T(8,128)(2,1)}, u32[]{:S(2)}) copy-start(bf16[128,1152]{1,0:T(8,128)(2,1)} %get-tuple-element.53.first_ref) | copy-start | bytes 884740
  6.4 15.2 %collective-permute-start.2 = (bf16[128,1152]{1,0:T(8,128)(2,1)}, bf16[128,1152]{1,0:T(8,128)(2,1)S(1)}, u32[]{:S(2)}, u32[]{:S(2)}) collective-permute-start(bf16[128,1152]{1,0:T(8,128)(2,1)} %get-tuple-element.49.first_ref), channel_id=1, source_target_pairs={{1,0},{0,1},{3,2},{2,3},{5,4},{4,5},{7,6},{6,7},{9,8},{8,9},{11,10... | collective-permute-start | bytes 884744 | tf_op jit(solution)/shard_map/ppermute | solution.py:33
  8.0 9.3 %collective-permute-start.6 = (bf16[128,1152]{1,0:T(8,128)(2,1)}, bf16[128,1152]{1,0:T(8,128)(2,1)S(1)}, u32[]{:S(2)}, u32[]{:S(2)}) collective-permute-start(bf16[128,1152]{1,0:T(8,128)(2,1)} %get-tuple-element.53.first_ref), channel_id=1, source_target_pairs={{3,0},{2,1},{1,2},{0,3},{7,4},{6,5},{5,6},{4,7},{11,8},{10,9},{9,1... | collective-permute-start | bytes 884744 | tf_op jit(solution)/shard_map/ppermute | solution.py:33
  12.4 16.3 %collective-permute-start.3 = (bf16[128,1152]{1,0:T(8,128)(2,1)S(1)}, bf16[128,1152]{1,0:T(8,128)(2,1)S(1)}, u32[]{:S(2)}, u32[]{:S(2)}) collective-permute-start(bf16[128,1152]{1,0:T(8,128)(2,1)S(1)} %get-tuple-element.52), channel_id=1, source_target_pairs={{32,0},{33,1},{34,2},{35,3},{36,4},{37,5},{38,6},{39,7},{40,8},{41... | collective-permute-start | bytes 884744 | tf_op jit(solution)/shard_map/ppermute | solution.py:33
  14.4 7.2 %copy-start.2 = (bf16[128,1152]{1,0:T(8,128)(2,1)S(1)}, bf16[128,1152]{1,0:T(8,128)(2,1)}, u32[]{:S(2)}) copy-start(bf16[128,1152]{1,0:T(8,128)(2,1)} %get-tuple-element.49.first_ref) | copy-start | bytes 884740
  14.4 10.9 %collective-permute-start.7 = (bf16[128,1152]{1,0:T(8,128)(2,1)S(1)}, bf16[128,1152]{1,0:T(8,128)(2,1)S(1)}, u32[]{:S(2)}, u32[]{:S(2)}) collective-permute-start(bf16[128,1152]{1,0:T(8,128)(2,1)S(1)} %get-tuple-element.54), channel_id=1, source_target_pairs={{96,0},{97,1},{98,2},{99,3},{100,4},{101,5},{102,6},{103,7},{104,8... | collective-permute-start | bytes 884744 | tf_op jit(solution)/shard_map/ppermute | solution.py:33
  17.4 18.1 %collective-permute-start.8 = (bf16[256,1152]{1,0:T(8,128)(2,1)S(1)}, bf16[256,1152]{1,0:T(8,128)(2,1)S(1)}, u32[]{:S(2)}, u32[]{:S(2)}) collective-permute-start(bf16[256,1152]{1,0:T(8,128)(2,1)S(1)} %stack.3.refs_4_.refs_0_), channel_id=1, source_target_pairs={{96,0},{97,1},{98,2},{99,3},{100,4},{101,5},{102,6},{103,7},{104,8... | collective-permute-start | bytes 1769480 | tf_op jit(solution)/shard_map/ppermute | solution.py:33
  21.6 13.9 %collective-permute-start.4 = (bf16[256,1152]{1,0:T(8,128)(2,1)S(1)}, bf16[256,1152]{1,0:T(8,128)(2,1)S(1)}, u32[]{:S(2)}, u32[]{:S(2)}) collective-permute-start(bf16[256,1152]{1,0:T(8,128)(2,1)S(1)} %stack.2.refs_0_), channel_id=1, source_target_pairs={{32,0},{33,1},{34,2},{35,3},{36,4},{37,5},{38,6},{39,7},{40,8},{41... | collective-permute-start | bytes 1769480 | tf_op jit(solution)/shard_map/ppermute | solution.py:33
  25.3 11.7 %collective-permute-start.9 = (bf16[256,1152]{1,0:T(8,128)(2,1)S(1)}, bf16[256,1152]{1,0:T(8,128)(2,1)S(1)}, u32[]{:S(2)}, u32[]{:S(2)}) collective-permute-start(bf16[256,1152]{1,0:T(8,128)(2,1)S(1)} %constant_dynamic-update-slice_fusion.2.refs_5_.refs_1_), channel_id=1, source_target_pairs={{3,0},{2,1},{1,2},{0,3},{7,4},{6,5},{5,6},{4,7},{11,8},{10,9},{9,1... | collective-permute-start | bytes 1769480 | tf_op jit(solution)/shard_map/ppermute | solution.py:33
  28.7 10.0 %collective-permute-start.5 = (bf16[256,1152]{1,0:T(8,128)(2,1)S(1)}, bf16[256,1152]{1,0:T(8,128)(2,1)S(1)}, u32[]{:S(2)}, u32[]{:S(2)}) collective-permute-start(bf16[256,1152]{1,0:T(8,128)(2,1)S(1)} %constant_dynamic-update-slice_fusion.refs_1_), channel_id=1, source_target_pairs={{1,0},{0,1},{3,2},{2,3},{5,4},{4,5},{7,6},{6,7},{9,8},{8,9},{11,10... | collective-permute-start | bytes 1769480 | tf_op jit(solution)/shard_map/ppermute | solution.py:33
  28.9 14.3 %collective-permute-start.10 = (bf16[256,1152]{1,0:T(8,128)(2,1)S(1)}, bf16[256,1152]{1,0:T(8,128)(2,1)S(1)}, u32[]{:S(2)}, u32[]{:S(2)}) collective-permute-start(bf16[256,1152]{1,0:T(8,128)(2,1)S(1)} %stack.3.refs_4_.refs_0_), channel_id=1, source_target_pairs={{8,0},{9,1},{10,2},{11,3},{12,4},{13,5},{14,6},{15,7},{0,8},{1,9},... | collective-permute-start | bytes 1769480 | tf_op jit(solution)/shard_map/ppermute | solution.py:33
  35.5 7.8 %collective-permute-start.12 = (bf16[256,1152]{1,0:T(8,128)(2,1)S(1)}, bf16[256,1152]{1,0:T(8,128)(2,1)S(1)}, u32[]{:S(2)}, u32[]{:S(2)}) collective-permute-start(bf16[256,1152]{1,0:T(8,128)(2,1)S(1)} %collective-permute-done.8.refs_6_.refs_2_), channel_id=1, source_target_pairs={{8,0},{9,1},{10,2},{11,3},{12,4},{13,5},{14,6},{15,7},{0,8},{1,9},... | collective-permute-start | bytes 1769480 | tf_op jit(solution)/shard_map/ppermute | solution.py:33
  38.7 4.6 %collective-permute-start.13 = (bf16[256,1152]{1,0:T(8,128)(2,1)S(1)}, bf16[256,1152]{1,0:T(8,128)(2,1)S(1)}, u32[]{:S(2)}, u32[]{:S(2)}) collective-permute-start(bf16[256,1152]{1,0:T(8,128)(2,1)S(1)} %collective-permute-done.9.refs_7_.refs_3_), channel_id=1, source_target_pairs={{8,0},{9,1},{10,2},{11,3},{12,4},{13,5},{14,6},{15,7},{0,8},{1,9},... | collective-permute-start | bytes 1769480 | tf_op jit(solution)/shard_map/ppermute | solution.py:33
  38.7 4.6 %collective-permute-start.11 = (bf16[256,1152]{1,0:T(8,128)(2,1)S(1)}, bf16[256,1152]{1,0:T(8,128)(2,1)S(1)}, u32[]{:S(2)}, u32[]{:S(2)}) collective-permute-start(bf16[256,1152]{1,0:T(8,128)(2,1)S(1)} %constant_dynamic-update-slice_fusion.2.refs_5_.refs_1_), channel_id=1, source_target_pairs={{8,0},{9,1},{10,2},{11,3},{12,4},{13,5},{14,6},{15,7},{0,8},{1,9},... | collective-permute-start | bytes 1769480 | tf_op jit(solution)/shard_map/ppermute | solution.py:33
  50.5 6.1 %collective-permute-start.16 = (bf16[512,1152]{1,0:T(8,128)(2,1)S(1)}, bf16[512,1152]{1,0:T(8,128)(2,1)S(1)}, u32[]{:S(2)}, u32[]{:S(2)}) collective-permute-start(bf16[512,1152]{1,0:T(8,128)(2,1)S(1)} %get-tuple-element.66), channel_id=1, source_target_pairs={{8,0},{9,1},{10,2},{11,3},{12,4},{13,5},{14,6},{15,7},{0,8},{1,9},... | collective-permute-start | bytes 3538952 | tf_op jit(solution)/shard_map/ppermute | solution.py:33
  50.6 6.0 %collective-permute-start.17 = (bf16[512,1152]{1,0:T(8,128)(2,1)S(1)}, bf16[512,1152]{1,0:T(8,128)(2,1)S(1)}, u32[]{:S(2)}, u32[]{:S(2)}) collective-permute-start(bf16[512,1152]{1,0:T(8,128)(2,1)S(1)} %get-tuple-element.69), channel_id=1, source_target_pairs={{8,0},{9,1},{10,2},{11,3},{12,4},{13,5},{14,6},{15,7},{0,8},{1,9},... | collective-permute-start | bytes 3538952 | tf_op jit(solution)/shard_map/ppermute | solution.py:33
  51.1 4.0 %collective-permute-start.14 = (f32[8,128]{1,0:T(8,128)S(1)}, f32[8,128]{1,0:T(8,128)S(1)}, u32[]{:S(2)}, u32[]{:S(2)}) collective-permute-start(f32[8,128]{1,0:T(8,128)S(1)} %get-tuple-element.60), channel_id=1, source_target_pairs={{8,0},{9,1},{10,2},{11,3},{12,4},{13,5},{14,6},{15,7},{0,8},{1,9},... | collective-permute-start | bytes 12296 | tf_op jit(solution)/shard_map/ppermute | solution.py:33
  55.1 5.6 %collective-permute-start.15 = (f32[32,8,128]{2,1,0:T(8,128)S(1)}, f32[32,8,128]{2,1,0:T(8,128)S(1)}, u32[]{:S(2)}, u32[]{:S(2)}) collective-permute-start(f32[32,8,128]{2,1,0:T(8,128)S(1)} %broadcast_in_dim.4), channel_id=1, source_target_pairs={{16,0},{17,1},{18,2},{19,3},{20,4},{21,5},{22,6},{23,7},{24,8},{25... | collective-permute-start | bytes 393224 | tf_op jit(solution)/shard_map/ppermute | solution.py:33
  55.4 26.8 %collective-permute-start.28 = (bf16[256,1152]{1,0:T(8,128)(2,1)S(1)}, bf16[256,1152]{1,0:T(8,128)(2,1)S(1)}, u32[]{:S(2)}, u32[]{:S(2)}) collective-permute-start(bf16[256,1152]{1,0:T(8,128)(2,1)S(1)} %get-tuple-element.61), channel_id=1, source_target_pairs={{32,0},{33,1},{34,2},{35,3},{36,4},{37,5},{38,6},{39,7},{40,8},{41... | collective-permute-start | bytes 1769480 | tf_op jit(solution)/shard_map/ppermute | solution.py:33
  56.3 14.8 %collective-permute-start.30 = (bf16[256,1152]{1,0:T(8,128)(2,1)S(1)}, bf16[256,1152]{1,0:T(8,128)(2,1)S(1)}, u32[]{:S(2)}, u32[]{:S(2)}) collective-permute-start(bf16[256,1152]{1,0:T(8,128)(2,1)S(1)} %get-tuple-element.59), channel_id=1, source_target_pairs={{1,0},{0,1},{3,2},{2,3},{5,4},{4,5},{7,6},{6,7},{9,8},{8,9},{11,10... | collective-permute-start | bytes 1769480 | tf_op jit(solution)/shard_map/ppermute | solution.py:33
  58.8 15.8 %collective-permute-start.20 = (bf16[256,1152]{1,0:T(8,128)(2,1)S(1)}, bf16[256,1152]{1,0:T(8,128)(2,1)S(1)}, u32[]{:S(2)}, u32[]{:S(2)}) collective-permute-start(bf16[256,1152]{1,0:T(8,128)(2,1)S(1)} %get-tuple-element.74), channel_id=1, source_target_pairs={{3,0},{2,1},{1,2},{0,3},{7,4},{6,5},{5,6},{4,7},{11,8},{10,9},{9,1... | collective-permute-start | bytes 1769480 | tf_op jit(solution)/shard_map/ppermute | solution.py:33
  60.7 9.5 %collective-permute-start.21 = (f32[32,8,128]{2,1,0:T(8,128)S(1)}, f32[32,8,128]{2,1,0:T(8,128)S(1)}, u32[]{:S(2)}, u32[]{:S(2)}) collective-permute-start(f32[32,8,128]{2,1,0:T(8,128)S(1)} %broadcast_in_dim.5), channel_id=1, source_target_pairs={{20,0},{21,1},{22,2},{23,3},{16,4},{17,5},{18,6},{19,7},{28,8},{29... | collective-permute-start | bytes 393224 | tf_op jit(solution)/shard_map/ppermute | solution.py:33
  65.8 19.0 %collective-permute-start.18 = (bf16[256,1152]{1,0:T(8,128)(2,1)S(1)}, bf16[256,1152]{1,0:T(8,128)(2,1)S(1)}, u32[]{:S(2)}, u32[]{:S(2)}) collective-permute-start(bf16[256,1152]{1,0:T(8,128)(2,1)S(1)} %get-tuple-element.70), channel_id=1, source_target_pairs={{96,0},{97,1},{98,2},{99,3},{100,4},{101,5},{102,6},{103,7},{104,8... | collective-permute-start | bytes 1769480 | tf_op jit(solution)/shard_map/ppermute | solution.py:33
  70.3 3.7 %collective-permute-start.22 = (f32[8,128]{1,0:T(8,128)S(1)}, f32[8,128]{1,0:T(8,128)S(1)}, u32[]{:S(2)}, u32[]{:S(2)}) collective-permute-start(f32[8,128]{1,0:T(8,128)S(1)} %fusion), channel_id=1, source_target_pairs={{1,0},{0,1},{3,2},{2,3},{5,4},{4,5},{7,6},{6,7},{9,8},{8,9},{11,10... | collective-permute-start | bytes 12296 | tf_op jit(solution)/shard_map/ppermute | solution.py:33
  71.5 11.2 %collective-permute-start.31 = (bf16[128,1152]{1,0:T(8,128)(2,1)S(1)}, bf16[128,1152]{1,0:T(8,128)(2,1)S(1)}, u32[]{:S(2)}, u32[]{:S(2)}) collective-permute-start(bf16[128,1152]{1,0:T(8,128)(2,1)S(1)} %get-tuple-element.86), channel_id=1, source_target_pairs={{32,0},{33,1},{34,2},{35,3},{36,4},{37,5},{38,6},{39,7},{40,8},{41... | collective-permute-start | bytes 884744 | tf_op jit(solution)/shard_map/ppermute | solution.py:33
  75.1 12.6 %collective-permute-start.23 = (bf16[128,1152]{1,0:T(8,128)(2,1)S(1)}, bf16[128,1152]{1,0:T(8,128)(2,1)S(1)}, u32[]{:S(2)}, u32[]{:S(2)}) collective-permute-start(bf16[128,1152]{1,0:T(8,128)(2,1)S(1)} %get-tuple-element.78), channel_id=1, source_target_pairs={{96,0},{97,1},{98,2},{99,3},{100,4},{101,5},{102,6},{103,7},{104,8... | collective-permute-start | bytes 884744 | tf_op jit(solution)/shard_map/ppermute | solution.py:33
  77.3 3.6 %collective-permute-start.24 = (f32[8,128]{1,0:T(8,128)S(1)}, f32[8,128]{1,0:T(8,128)S(1)}, u32[]{:S(2)}, u32[]{:S(2)}) collective-permute-start(f32[8,128]{1,0:T(8,128)S(1)} %add.25), channel_id=1, source_target_pairs={{32,0},{33,1},{34,2},{35,3},{36,4},{37,5},{38,6},{39,7},{40,8},{41... | collective-permute-start | bytes 12296 | tf_op jit(solution)/shard_map/ppermute | solution.py:33
  81.0 6.3 %collective-permute-start.25 = (f32[8,128]{1,0:T(8,128)S(1)}, f32[8,128]{1,0:T(8,128)S(1)}, u32[]{:S(2)}, u32[]{:S(2)}) collective-permute-start(f32[8,128]{1,0:T(8,128)S(1)} %add.26), channel_id=1, source_target_pairs={{3,0},{2,1},{1,2},{0,3},{7,4},{6,5},{5,6},{4,7},{11,8},{10,9},{9,1... | collective-permute-start | bytes 12296 | tf_op jit(solution)/shard_map/ppermute | solution.py:33
  82.6 9.1 %collective-permute-start.29 = (bf16[128,1152]{1,0:T(8,128)(2,1)S(1)}, bf16[128,1152]{1,0:T(8,128)(2,1)S(1)}, u32[]{:S(2)}, u32[]{:S(2)}) collective-permute-start(bf16[128,1152]{1,0:T(8,128)(2,1)S(1)} %get-tuple-element.83), channel_id=1, source_target_pairs={{1,0},{0,1},{3,2},{2,3},{5,4},{4,5},{7,6},{6,7},{9,8},{8,9},{11,10... | collective-permute-start | bytes 884744 | tf_op jit(solution)/shard_map/ppermute | solution.py:33
  83.0 8.7 %copy-start = (bf16[128,1152]{1,0:T(8,128)(2,1)S(1)}, bf16[128,1152]{1,0:T(8,128)(2,1)}, u32[]{:S(2)}) copy-start(bf16[128,1152]{1,0:T(8,128)(2,1)} %raw_ref.3) | copy-start | bytes 884740
  83.0 8.7 %collective-permute-start.32 = (bf16[128,1152]{1,0:T(8,128)(2,1)S(1)}, bf16[128,1152]{1,0:T(8,128)(2,1)S(1)}, u32[]{:S(2)}, u32[]{:S(2)}) collective-permute-start(bf16[128,1152]{1,0:T(8,128)(2,1)S(1)} %add_codes.3), channel_id=1, source_target_pairs={{16,0},{17,1},{18,2},{19,3},{20,4},{21,5},{22,6},{23,7},{24,8},{25... | collective-permute-start | bytes 884744 | tf_op jit(solution)/shard_map/ppermute | solution.py:33
  85.2 9.4 %collective-permute-start.19 = (bf16[128,1152]{1,0:T(8,128)(2,1)S(1)}, bf16[128,1152]{1,0:T(8,128)(2,1)S(1)}, u32[]{:S(2)}, u32[]{:S(2)}) collective-permute-start(bf16[128,1152]{1,0:T(8,128)(2,1)S(1)} %get-tuple-element.72), channel_id=1, source_target_pairs={{3,0},{2,1},{1,2},{0,3},{7,4},{6,5},{5,6},{4,7},{11,8},{10,9},{9,1... | collective-permute-start | bytes 884744 | tf_op jit(solution)/shard_map/ppermute | solution.py:33
  87.3 9.0 %copy-start.1 = (bf16[128,1152]{1,0:T(8,128)(2,1)S(1)}, bf16[128,1152]{1,0:T(8,128)(2,1)}, u32[]{:S(2)}) copy-start(bf16[128,1152]{1,0:T(8,128)(2,1)} %raw_ref.2) | copy-start | bytes 884740
  88.0 8.3 %collective-permute-start.26 = (bf16[128,1152]{1,0:T(8,128)(2,1)S(1)}, bf16[128,1152]{1,0:T(8,128)(2,1)S(1)}, u32[]{:S(2)}, u32[]{:S(2)}) collective-permute-start(bf16[128,1152]{1,0:T(8,128)(2,1)S(1)} %add_codes.2), channel_id=1, source_target_pairs={{20,0},{21,1},{22,2},{23,3},{16,4},{17,5},{18,6},{19,7},{28,8},{29... | collective-permute-start | bytes 884744 | tf_op jit(solution)/shard_map/ppermute | solution.py:33
  89.8 4.8 %collective-permute-start.27 = (f32[8,128]{1,0:T(8,128)S(1)}, f32[8,128]{1,0:T(8,128)S(1)}, u32[]{:S(2)}, u32[]{:S(2)}) collective-permute-start(f32[8,128]{1,0:T(8,128)S(1)} %add.27.loss_ref.loss_in), channel_id=1, source_target_pairs={{96,0},{97,1},{98,2},{99,3},{100,4},{101,5},{102,6},{103,7},{104,8... | collective-permute-start | bytes 12296 | tf_op jit(solution)/shard_map/ppermute | solution.py:33

commit v6 on v5

--- a/solution.py
+++ b/solution.py
@@ -12,7 +12,7 @@
 CORE = 1 << 3
 PIECE = 128
 ROWS = ("", "y", "x", "xz", "z", "yz", "xy", "xyz")
-PAIR_VMEM = 12 * 2**20
+PAIR_VMEM = 10 * 2**20
 SMALL_VMEM = 8 * 2**20
 LOG2E = 1.4426950408889634
 LN2 = 0.6931471805599453
@@ -332,10 +332,10 @@
     text_far = swap(text_far, TEXT_PAIRS["y"])
     text_near = swap(text_near, TEXT_PAIRS["z"])
     loss = after(loss, near_late)
-    tiles = swap(jnp.broadcast_to(loss[None], (32, *loss.shape)), IMAGE_PAIRS["x"])
+    tiles = swap(jnp.broadcast_to(loss[None], (24, *loss.shape)), IMAGE_PAIRS["x"])
     loss = loss + tiles[0]
     near_early, far_early = image_terms(0, 2, jnp.float32, (after(own_coeff, far_late, loss), other_coeff), text_all)
-    tiles = swap(jnp.broadcast_to(loss[None], (32, *loss.shape)), TEXT_PAIRS["x"])
+    tiles = swap(jnp.broadcast_to(loss[None], (24, *loss.shape)), TEXT_PAIRS["x"])
     text_early = text_terms(0, jnp.float32, after(own_coeff, near_early), other_early, image_all)
 
     image_kept, image_sent = fold(far_early, image_far)

time: 98 us -> 97.2 us (level)
  waiting for transfers between devices: 24.4 us -> 23 us
    ppermute x33, waiting for transfers between devices: 24.4 us -> 23 us  [swap(): lax.ppermute(value, axes, [(k ^ mask, k) for k in range(lax.axis_size(axe...]
  transfers between devices with their start and end apart: 33 -> 33, of which waited for: 15 -> 12; matrix products, arithmetic and copies ran while one was open for 0% -> 0% of each run, Pallas kernels for 20% -> 21%
where the time goes in v6:
time: 97.2 us; the launch traced here: 97.1 us
  starting transfers between devices  42.9 us (44%)
  Pallas kernels  28.5 us (29%)
  waiting for transfers between devices  23 us (24%)
  between operations  2.43 us (2%)
    ppermute x33, starting transfers between devices, swap(): lax.ppermute(value, axes, [(k ^ mask, k) for k in range(lax.axis_size(axe...  42.9 us
    ppermute x33, waiting for transfers between devices, swap(): lax.ppermute(value, axes, [(k ^ mask, k) for k in range(lax.axis_size(axe...  23 us
    pallas_call x2, Pallas kernels, logit_terms(): pl.pallas_call(functools.partial(logit_kernel, core, loss_scale), out_sha...  11.2 us
    pallas_call x2, Pallas kernels, image_terms(): pl.pallas_call(functools.partial(image_kernel, first), out_shape=[shape_o...  5.82 us
    pallas_call x2, Pallas kernels, text_terms(): pl.pallas_call(functools.partial(text_kernel, first), out_shape=[shape_of...  4.06 us
    pallas_call x2, Pallas kernels, finish(): pl.pallas_call(finish_kernel, out_shape=[shape_of(*raw.shape, jnp.float32...  2.85 us
    pallas_call x9, Pallas kernels, small_call(): pl.pallas_call(kernel, out_shape=out_shape, in_specs=[VMEM] * len(operand...  2.6 us
    pallas_call x1, Pallas kernels, unit_rows(): pl.pallas_call(unit_kernel, out_shape=[out, out], in_specs=[HBM, HBM], ou...  1.99 us
  transfers between devices with their start and end apart: 33, of which 12 were waited for; matrix products, arithmetic and copies ran while one was open for 0% of the time, Pallas kernels for 21%

profile of v6, /device:TPU:0, one launch (start us, length us, event | category | flops | bytes accessed | tf_op | source)
XLA Modules:
  0.0 97.1 jit_solution(17103935291021701846)
XLA Ops:
  0.6 1.7 %collective-permute-start = (bf16[128,1152]{1,0:T(8,128)(2,1)}, bf16[128,1152]{1,0:T(8,128)(2,1)S(1)}, u32[]{:S(2)}, u32[]{:S(2)}) collective-permute-start(bf16[128,1152]{1,0:T(8,128)(2,1)} %raw_ref.3), channel_id=1, source_target_pairs={{16,0},{17,1},{18,2},{19,3},{20,4},{21,5},{22,6},{23,7},{24,8},{25... | collective-permute-start | bytes 884744 | tf_op jit(solution)/shard_map/ppermute | solution.py:33
  2.3 2.1 %collective-permute-start.1 = (bf16[128,1152]{1,0:T(8,128)(2,1)}, bf16[128,1152]{1,0:T(8,128)(2,1)S(1)}, u32[]{:S(2)}, u32[]{:S(2)}) collective-permute-start(bf16[128,1152]{1,0:T(8,128)(2,1)} %raw_ref.2), channel_id=1, source_target_pairs={{20,0},{21,1},{22,2},{23,3},{16,4},{17,5},{18,6},{19,7},{28,8},{29... | collective-permute-start | bytes 884744 | tf_op jit(solution)/shard_map/ppermute | solution.py:33
  4.4 2.0 %unit_rows.1 = (bf16[128,1152]{1,0:T(8,128)(2,1)}, bf16[128,1152]{1,0:T(8,128)(2,1)}) custom-call(bf16[128,1152]{1,0:T(8,128)(2,1)} %raw_ref.3, bf16[128,1152]{1,0:T(8,128)(2,1)} %raw_ref.2), custom_call_target="tpu_custom_call" | custom-call | tf_op jit(solution)/shard_map/unit_rows/pallas_call | solution.py:60
  6.4 0.0 copy-start.3
  6.4 1.7 %collective-permute-start.2 = (bf16[128,1152]{1,0:T(8,128)(2,1)}, bf16[128,1152]{1,0:T(8,128)(2,1)S(1)}, u32[]{:S(2)}, u32[]{:S(2)}) collective-permute-start(bf16[128,1152]{1,0:T(8,128)(2,1)} %get-tuple-element.49.first_ref), channel_id=1, source_target_pairs={{1,0},{0,1},{3,2},{2,3},{5,4},{4,5},{7,6},{6,7},{9,8},{8,9},{11,10... | collective-permute-start | bytes 884744 | tf_op jit(solution)/shard_map/ppermute | solution.py:33
  8.0 2.2 %collective-permute-start.6 = (bf16[128,1152]{1,0:T(8,128)(2,1)}, bf16[128,1152]{1,0:T(8,128)(2,1)S(1)}, u32[]{:S(2)}, u32[]{:S(2)}) collective-permute-start(bf16[128,1152]{1,0:T(8,128)(2,1)} %get-tuple-element.53.first_ref), channel_id=1, source_target_pairs={{3,0},{2,1},{1,2},{0,3},{7,4},{6,5},{5,6},{4,7},{11,8},{10,9},{9,1... | collective-permute-start | bytes 884744 | tf_op jit(solution)/shard_map/ppermute | solution.py:33
  11.6 0.6 collective-permute-done.1.texts_ref
  12.2 0.2 far_units.1
  12.4 2.0 %collective-permute-start.3 = (bf16[128,1152]{1,0:T(8,128)(2,1)S(1)}, bf16[128,1152]{1,0:T(8,128)(2,1)S(1)}, u32[]{:S(2)}, u32[]{:S(2)}) collective-permute-start(bf16[128,1152]{1,0:T(8,128)(2,1)S(1)} %get-tuple-element.52), channel_id=1, source_target_pairs={{32,0},{33,1},{34,2},{35,3},{36,4},{37,5},{38,6},{39,7},{40,8},{41... | collective-permute-start | bytes 884744 | tf_op jit(solution)/shard_map/ppermute | solution.py:33
  14.4 2.5 %collective-permute-start.7 = (bf16[128,1152]{1,0:T(8,128)(2,1)S(1)}, bf16[128,1152]{1,0:T(8,128)(2,1)S(1)}, u32[]{:S(2)}, u32[]{:S(2)}) collective-permute-start(bf16[128,1152]{1,0:T(8,128)(2,1)S(1)} %get-tuple-element.54), channel_id=1, source_target_pairs={{96,0},{97,1},{98,2},{99,3},{100,4},{101,5},{102,6},{103,7},{104,8... | collective-permute-start | bytes 884744 | tf_op jit(solution)/shard_map/ppermute | solution.py:33
  17.0 0.4 collective-permute-done.6.second_ref
  17.4 4.1 %collective-permute-start.8 = (bf16[256,1152]{1,0:T(8,128)(2,1)S(1)}, bf16[256,1152]{1,0:T(8,128)(2,1)S(1)}, u32[]{:S(2)}, u32[]{:S(2)}) collective-permute-start(bf16[256,1152]{1,0:T(8,128)(2,1)S(1)} %stack.3.refs_4_.refs_0_), channel_id=1, source_target_pairs={{96,0},{97,1},{98,2},{99,3},{100,4},{101,5},{102,6},{103,7},{104,8... | collective-permute-start | bytes 1769480 | tf_op jit(solution)/shard_map/ppermute | solution.py:33
  21.5 0.0 collective-permute-done.2.second_ref
  21.6 0.1 collective-permute-start.4
  21.7 3.5 %collective-permute-done.7 = bf16[128,1152]{1,0:T(8,128)(2,1)S(1)} collective-permute-done((bf16[128,1152]{1,0:T(8,128)(2,1)S(1)}, bf16[128,1152]{1,0:T(8,128)(2,1)S(1)}, u32[]{:S(2)}, u32[]{:S(2)}) %collective-permute-start.7) | collective-permute-done | bytes 294944 | tf_op jit(solution)/shard_map/ppermute | solution.py:33
  25.3 3.4 %collective-permute-start.9 = (bf16[256,1152]{1,0:T(8,128)(2,1)S(1)}, bf16[256,1152]{1,0:T(8,128)(2,1)S(1)}, u32[]{:S(2)}, u32[]{:S(2)}) collective-permute-start(bf16[256,1152]{1,0:T(8,128)(2,1)S(1)} %constant_dynamic-update-slice_fusion.2.refs_5_.refs_1_), channel_id=1, source_target_pairs={{3,0},{2,1},{1,2},{0,3},{7,4},{6,5},{5,6},{4,7},{11,8},{10,9},{9,1... | collective-permute-start | bytes 1769480 | tf_op jit(solution)/shard_map/ppermute | solution.py:33
  28.7 0.2 collective-permute-start.5
  28.9 6.6 %collective-permute-done.8.refs_6_.refs_2_ = bf16[256,1152]{1,0:T(8,128)(2,1)S(1)} collective-permute-done((bf16[256,1152]{1,0:T(8,128)(2,1)S(1)}, bf16[256,1152]{1,0:T(8,128)(2,1)S(1)}, u32[]{:S(2)}, u32[]{:S(2)}) %collective-permute-start.8) | collective-permute-done | bytes 589856 | tf_op jit(solution)/shard_map/ppermute | solution.py:33
  35.5 1.4 %collective-permute-done.9.refs_7_.refs_3_ = bf16[256,1152]{1,0:T(8,128)(2,1)S(1)} collective-permute-done((bf16[256,1152]{1,0:T(8,128)(2,1)S(1)}, bf16[256,1152]{1,0:T(8,128)(2,1)S(1)}, u32[]{:S(2)}, u32[]{:S(2)}) %collective-permute-start.9) | collective-permute-done | bytes 589856 | tf_op jit(solution)/shard_map/ppermute | solution.py:33
  36.9 1.7 %collective-permute-done.5.refs_3_ = bf16[256,1152]{1,0:T(8,128)(2,1)S(1)} collective-permute-done((bf16[256,1152]{1,0:T(8,128)(2,1)S(1)}, bf16[256,1152]{1,0:T(8,128)(2,1)S(1)}, u32[]{:S(2)}, u32[]{:S(2)}) %collective-permute-start.5) | collective-permute-done | bytes 589856 | tf_op jit(solution)/shard_map/ppermute | solution.py:33
  38.7 0.0 collective-permute-start.13
  38.7 0.5 collective-permute-start.11
  39.2 4.1 %own_logits.1 = (bf16[1024,1024]{1,0:T(8,128)(2,1)S(1)}, f32[8,128]{1,0:T(8,128)S(1)}) custom-call(s32[1]{0:T(128)} %bitcast.place_ref, f32[1,1]{1,0:T(1,128)} %bitcast.1.temper_ref, f32[1,1]{1,0:T(1,128)} %bitcast.2.shift_ref, bf16[256,1152]{1,0:T(8,128)(2,1)S(1)} %stack.2.refs_0_, bf16[256,1152]{1,0:T(8,128)(2,1)S(1)} %constant_dynamic-update-slice_fusion.refs_1_, ...), custom_call_target="tpu_custom_call" | custom-call | flops 2415919104 | bytes 8388608 | tf_op jit(solution)/shard_map/own_logits/pallas_call | solution.py:170
  43.3 0.0 collective-permute-done.13.refs_7_
  43.3 0.0 collective-permute-done.11.refs_5_
  43.3 7.1 %other_logits.1 = (bf16[1024,1024]{1,0:T(8,128)(2,1)S(1)}, bf16[512,1152]{1,0:T(8,128)(2,1)S(1)}, bf16[512,1152]{1,0:T(8,128)(2,1)S(1)}, f32[8,128]{1,0:T(8,128)S(1)}) custom-call(s32[1]{0:T(128)} %bitcast.place_ref, f32[1,1]{1,0:T(1,128)} %bitcast.1.temper_ref, f32[1,1]{1,0:T(1,128)} %bitcast.2.shift_ref, bf16[256,1152]{1,0:T(8,128)(2,1)S(1)} %stack.2.refs_0_, ...), custom_call_target="tpu_custom_call" | custom-call | flops 4831838208 | bytes 8388608 | tf_op jit(solution)/shard_map/other_logits/pallas_call | solution.py:170
  50.5 0.1 collective-permute-start.16
  50.5 0.5 collective-permute-start.17
  51.0 0.1 collective-permute-start.14
  51.1 2.9 %image_terms.2 = (bf16[256,1152]{1,0:T(8,128)(2,1)S(1)}, bf16[256,1152]{1,0:T(8,128)(2,1)S(1)}) custom-call(bf16[1024,1024]{1,0:T(8,128)(2,1)S(1)} %get-tuple-element.68.own_ref.coeff_ref, bf16[1024,1024]{1,0:T(8,128)(2,1)S(1)} %get-tuple-element.58.other_ref, bf16[256,1152]{1,0:T(8,128)(2,1)S(1)} %stack.3.refs_4_.refs_0_, ...), custom_call_target="tpu_custom_call" | custom-call | flops 2415919104 | bytes 8388608 | tf_op jit(solution)/shard_map/image_terms/pallas_call | solution.py:224
  54.1 0.2 collective-permute-start.30
  54.3 0.9 collective-permute-start.28
  55.2 0.5 collective-permute-start.15
  55.6 2.2 %text_terms.3 = (bf16[256,1152]{1,0:T(8,128)(2,1)S(1)}, bf16[256,1152]{1,0:T(8,128)(2,1)S(1)}) custom-call(bf16[1024,1024]{1,0:T(8,128)(2,1)S(1)} %get-tuple-element.68.own_ref.coeff_ref, bf16[512,1152]{1,0:T(8,128)(2,1)S(1)} %collective-permute-done.17.came_ref, bf16[256,1152]{1,0:T(8,128)(2,1)S(1)} %stack.2.refs_0_, ...), custom_call_target="tpu_custom_call" | custom-call | flops 1207959552 | bytes 8388608 | tf_op jit(solution)/shard_map/text_terms/pallas_call | solution.py:196
  57.9 1.2 %collective-permute-start.20 = (bf16[256,1152]{1,0:T(8,128)(2,1)S(1)}, bf16[256,1152]{1,0:T(8,128)(2,1)S(1)}, u32[]{:S(2)}, u32[]{:S(2)}) collective-permute-start(bf16[256,1152]{1,0:T(8,128)(2,1)S(1)} %get-tuple-element.74), channel_id=1, source_target_pairs={{3,0},{2,1},{1,2},{0,3},{7,4},{6,5},{5,6},{4,7},{11,8},{10,9},{9,1... | collective-permute-start | bytes 1769480 | tf_op jit(solution)/shard_map/ppermute | solution.py:33
  59.1 0.9 collective-permute-done.15
  60.0 2.9 %image_terms.3 = (f32[256,1152]{1,0:T(8,128)S(1)}, f32[256,1152]{1,0:T(8,128)S(1)}) custom-call(bf16[1024,1024]{1,0:T(8,128)(2,1)S(1)} %get-tuple-element.68.own_ref.coeff_ref, bf16[1024,1024]{1,0:T(8,128)(2,1)S(1)} %get-tuple-element.58.other_ref, bf16[256,1152]{1,0:T(8,128)(2,1)S(1)} %stack.3.refs_4_.refs_0_, ...), custom_call_target="tpu_custom_call" | custom-call | flops 2415919104 | bytes 8388608 | tf_op jit(solution)/shard_map/image_terms/pallas_call | solution.py:224
  62.9 2.2 %collective-permute-start.21 = (f32[24,8,128]{2,1,0:T(8,128)S(1)}, f32[24,8,128]{2,1,0:T(8,128)S(1)}, u32[]{:S(2)}, u32[]{:S(2)}) collective-permute-start(f32[24,8,128]{2,1,0:T(8,128)S(1)} %broadcast_in_dim.5), channel_id=1, source_target_pairs={{20,0},{21,1},{22,2},{23,3},{16,4},{17,5},{18,6},{19,7},{28,8},{29... | collective-permute-start | bytes 294920 | tf_op jit(solution)/shard_map/ppermute | solution.py:33
  65.1 2.5 %collective-permute-start.18 = (bf16[256,1152]{1,0:T(8,128)(2,1)S(1)}, bf16[256,1152]{1,0:T(8,128)(2,1)S(1)}, u32[]{:S(2)}, u32[]{:S(2)}) collective-permute-start(bf16[256,1152]{1,0:T(8,128)(2,1)S(1)} %get-tuple-element.70), channel_id=1, source_target_pairs={{96,0},{97,1},{98,2},{99,3},{100,4},{101,5},{102,6},{103,7},{104,8... | collective-permute-start | bytes 1769480 | tf_op jit(solution)/shard_map/ppermute | solution.py:33
  67.6 1.8 %text_terms.2 = (f32[256,1152]{1,0:T(8,128)S(1)}, f32[256,1152]{1,0:T(8,128)S(1)}) custom-call(bf16[1024,1024]{1,0:T(8,128)(2,1)S(1)} %get-tuple-element.68.own_ref.coeff_ref, bf16[512,1152]{1,0:T(8,128)(2,1)S(1)} %collective-permute-done.16.came_ref, bf16[256,1152]{1,0:T(8,128)(2,1)S(1)} %stack.2.refs_0_, ...), custom_call_target="tpu_custom_call" | custom-call | flops 1207959552 | bytes 8388608 | tf_op jit(solution)/shard_map/text_terms/pallas_call | solution.py:196
  69.5 1.4 %collective-permute-start.22 = (f32[8,128]{1,0:T(8,128)S(1)}, f32[8,128]{1,0:T(8,128)S(1)}, u32[]{:S(2)}, u32[]{:S(2)}) collective-permute-start(f32[8,128]{1,0:T(8,128)S(1)} %fusion), channel_id=1, source_target_pairs={{1,0},{0,1},{3,2},{2,3},{5,4},{4,5},{7,6},{6,7},{9,8},{8,9},{11,10... | collective-permute-start | bytes 12296 | tf_op jit(solution)/shard_map/ppermute | solution.py:33
  70.9 0.4 fold.7
  71.3 1.1 %collective-permute-start.31 = (bf16[128,1152]{1,0:T(8,128)(2,1)S(1)}, bf16[128,1152]{1,0:T(8,128)(2,1)S(1)}, u32[]{:S(2)}, u32[]{:S(2)}) collective-permute-start(bf16[128,1152]{1,0:T(8,128)(2,1)S(1)} %get-tuple-element.86), channel_id=1, source_target_pairs={{32,0},{33,1},{34,2},{35,3},{36,4},{37,5},{38,6},{39,7},{40,8},{41... | collective-permute-start | bytes 884744 | tf_op jit(solution)/shard_map/ppermute | solution.py:33
  72.4 0.8 collective-permute-done.22
  73.2 0.9 collective-permute-done.20.came_ref
  74.1 0.4 fold.5
  74.5 2.6 %collective-permute-start.23 = (bf16[128,1152]{1,0:T(8,128)(2,1)S(1)}, bf16[128,1152]{1,0:T(8,128)(2,1)S(1)}, u32[]{:S(2)}, u32[]{:S(2)}) collective-permute-start(bf16[128,1152]{1,0:T(8,128)(2,1)S(1)} %get-tuple-element.78), channel_id=1, source_target_pairs={{96,0},{97,1},{98,2},{99,3},{100,4},{101,5},{102,6},{103,7},{104,8... | collective-permute-start | bytes 884744 | tf_op jit(solution)/shard_map/ppermute | solution.py:33
  77.1 0.6 collective-permute-start.24
  77.7 3.0 %collective-permute-done.24 = f32[8,128]{1,0:T(8,128)S(1)} collective-permute-done((f32[8,128]{1,0:T(8,128)S(1)}, f32[8,128]{1,0:T(8,128)S(1)}, u32[]{:S(2)}, u32[]{:S(2)}) %collective-permute-start.24) | collective-permute-done | bytes 4128 | tf_op jit(solution)/shard_map/ppermute | solution.py:33
  80.7 1.3 %collective-permute-start.25 = (f32[8,128]{1,0:T(8,128)S(1)}, f32[8,128]{1,0:T(8,128)S(1)}, u32[]{:S(2)}, u32[]{:S(2)}) collective-permute-start(f32[8,128]{1,0:T(8,128)S(1)} %add.26), channel_id=1, source_target_pairs={{3,0},{2,1},{1,2},{0,3},{7,4},{6,5},{5,6},{4,7},{11,8},{10,9},{9,1... | collective-permute-start | bytes 12296 | tf_op jit(solution)/shard_map/ppermute | solution.py:33
  82.0 0.4 fold.6
  82.5 0.1 collective-permute-start.29
  82.6 0.3 add_codes.3
  82.8 0.0 copy-start
  82.9 1.7 %collective-permute-start.32 = (bf16[128,1152]{1,0:T(8,128)(2,1)S(1)}, bf16[128,1152]{1,0:T(8,128)(2,1)S(1)}, u32[]{:S(2)}, u32[]{:S(2)}) collective-permute-start(bf16[128,1152]{1,0:T(8,128)(2,1)S(1)} %add_codes.3), channel_id=1, source_target_pairs={{16,0},{17,1},{18,2},{19,3},{20,4},{21,5},{22,6},{23,7},{24,8},{25... | collective-permute-start | bytes 884744 | tf_op jit(solution)/shard_map/ppermute | solution.py:33
  84.6 0.4 fold.4
  85.0 2.1 %collective-permute-start.19 = (bf16[128,1152]{1,0:T(8,128)(2,1)S(1)}, bf16[128,1152]{1,0:T(8,128)(2,1)S(1)}, u32[]{:S(2)}, u32[]{:S(2)}) collective-permute-start(bf16[128,1152]{1,0:T(8,128)(2,1)S(1)} %get-tuple-element.72), channel_id=1, source_target_pairs={{3,0},{2,1},{1,2},{0,3},{7,4},{6,5},{5,6},{4,7},{11,8},{10,9},{9,1... | collective-permute-start | bytes 884744 | tf_op jit(solution)/shard_map/ppermute | solution.py:33
  87.2 0.3 add_codes.2
  87.4 2.2 %collective-permute-start.26 = (bf16[128,1152]{1,0:T(8,128)(2,1)S(1)}, bf16[128,1152]{1,0:T(8,128)(2,1)S(1)}, u32[]{:S(2)}, u32[]{:S(2)}) collective-permute-start(bf16[128,1152]{1,0:T(8,128)(2,1)S(1)} %add_codes.2), channel_id=1, source_target_pairs={{20,0},{21,1},{22,2},{23,3},{16,4},{17,5},{18,6},{19,7},{28,8},{29... | collective-permute-start | bytes 884744 | tf_op jit(solution)/shard_map/ppermute | solution.py:33
  89.6 1.3 %collective-permute-start.27 = (f32[8,128]{1,0:T(8,128)S(1)}, f32[8,128]{1,0:T(8,128)S(1)}, u32[]{:S(2)}, u32[]{:S(2)}) collective-permute-start(f32[8,128]{1,0:T(8,128)S(1)} %add.27.loss_ref.loss_in), channel_id=1, source_target_pairs={{96,0},{97,1},{98,2},{99,3},{100,4},{101,5},{102,6},{103,7},{104,8... | collective-permute-start | bytes 12296 | tf_op jit(solution)/shard_map/ppermute | solution.py:33
  90.9 1.4 %finish.3 = (f32[128,1152]{1,0:T(8,128)}, f32[1]{0:T(128)}) custom-call(bf16[128,1152]{1,0:T(8,128)(2,1)S(1)} %copy-done, f32[128,1152]{1,0:T(8,128)S(1)} %get-tuple-element.82.own_ref, bf16[128,1152]{1,0:T(8,128)(2,1)S(1)} %collective-permute-done.29.ring_ref, bf16[128,1152]{1,0:T(8,128)(2,1)S(1)} %collective-permute-done.32.far_ref, ...), custom_call_target="tpu_custom_call" | custom-call | tf_op jit(solution)/shard_map/finish/pallas_call | solution.py:275
  92.4 2.1 %collective-permute-done.27.loss_in = f32[8,128]{1,0:T(8,128)S(1)} collective-permute-done((f32[8,128]{1,0:T(8,128)S(1)}, f32[8,128]{1,0:T(8,128)S(1)}, u32[]{:S(2)}, u32[]{:S(2)}) %collective-permute-start.27) | collective-permute-done | bytes 4128 | tf_op jit(solution)/shard_map/ppermute | solution.py:33
  94.4 1.0 %collective-permute-done.26.far_ref = bf16[128,1152]{1,0:T(8,128)(2,1)S(1)} collective-permute-done((bf16[128,1152]{1,0:T(8,128)(2,1)S(1)}, bf16[128,1152]{1,0:T(8,128)(2,1)S(1)}, u32[]{:S(2)}, u32[]{:S(2)}) %collective-permute-start.26) | collective-permute-done | bytes 294944 | tf_op jit(solution)/shard_map/ppermute | solution.py:33
  95.5 1.4 %finish.2 = (f32[128,1152]{1,0:T(8,128)}, f32[1]{0:T(128)}) custom-call(bf16[128,1152]{1,0:T(8,128)(2,1)S(1)} %copy-done.1, f32[128,1152]{1,0:T(8,128)S(1)} %get-tuple-element.71.own_ref, bf16[128,1152]{1,0:T(8,128)(2,1)S(1)} %collective-permute-done.19.ring_ref, bf16[128,1152]{1,0:T(8,128)(2,1)S(1)} %collective-permute-done.26.far_ref, ...), custom_call_target="tpu_custom_call" | custom-call | tf_op jit(solution)/shard_map/finish/pallas_call | solution.py:275
  (40 shorter events, 0.3 us)
Async XLA Ops:
  0.6 10.9 %collective-permute-start = (bf16[128,1152]{1,0:T(8,128)(2,1)}, bf16[128,1152]{1,0:T(8,128)(2,1)S(1)}, u32[]{:S(2)}, u32[]{:S(2)}) collective-permute-start(bf16[128,1152]{1,0:T(8,128)(2,1)} %raw_ref.3), channel_id=1, source_target_pairs={{16,0},{17,1},{18,2},{19,3},{20,4},{21,5},{22,6},{23,7},{24,8},{25... | collective-permute-start | bytes 884744 | tf_op jit(solution)/shard_map/ppermute | solution.py:33
  2.3 9.9 %collective-permute-start.1 = (bf16[128,1152]{1,0:T(8,128)(2,1)}, bf16[128,1152]{1,0:T(8,128)(2,1)S(1)}, u32[]{:S(2)}, u32[]{:S(2)}) collective-permute-start(bf16[128,1152]{1,0:T(8,128)(2,1)} %raw_ref.2), channel_id=1, source_target_pairs={{20,0},{21,1},{22,2},{23,3},{16,4},{17,5},{18,6},{19,7},{28,8},{29... | collective-permute-start | bytes 884744 | tf_op jit(solution)/shard_map/ppermute | solution.py:33
  6.4 11.0 %copy-start.3 = (bf16[128,1152]{1,0:T(8,128)(2,1)S(1)}, bf16[128,1152]{1,0:T(8,128)(2,1)}, u32[]{:S(2)}) copy-start(bf16[128,1152]{1,0:T(8,128)(2,1)} %get-tuple-element.53.first_ref) | copy-start | bytes 884740
  6.4 15.2 %collective-permute-start.2 = (bf16[128,1152]{1,0:T(8,128)(2,1)}, bf16[128,1152]{1,0:T(8,128)(2,1)S(1)}, u32[]{:S(2)}, u32[]{:S(2)}) collective-permute-start(bf16[128,1152]{1,0:T(8,128)(2,1)} %get-tuple-element.49.first_ref), channel_id=1, source_target_pairs={{1,0},{0,1},{3,2},{2,3},{5,4},{4,5},{7,6},{6,7},{9,8},{8,9},{11,10... | collective-permute-start | bytes 884744 | tf_op jit(solution)/shard_map/ppermute | solution.py:33
  8.0 9.3 %collective-permute-start.6 = (bf16[128,1152]{1,0:T(8,128)(2,1)}, bf16[128,1152]{1,0:T(8,128)(2,1)S(1)}, u32[]{:S(2)}, u32[]{:S(2)}) collective-permute-start(bf16[128,1152]{1,0:T(8,128)(2,1)} %get-tuple-element.53.first_ref), channel_id=1, source_target_pairs={{3,0},{2,1},{1,2},{0,3},{7,4},{6,5},{5,6},{4,7},{11,8},{10,9},{9,1... | collective-permute-start | bytes 884744 | tf_op jit(solution)/shard_map/ppermute | solution.py:33
  12.4 16.3 %collective-permute-start.3 = (bf16[128,1152]{1,0:T(8,128)(2,1)S(1)}, bf16[128,1152]{1,0:T(8,128)(2,1)S(1)}, u32[]{:S(2)}, u32[]{:S(2)}) collective-permute-start(bf16[128,1152]{1,0:T(8,128)(2,1)S(1)} %get-tuple-element.52), channel_id=1, source_target_pairs={{32,0},{33,1},{34,2},{35,3},{36,4},{37,5},{38,6},{39,7},{40,8},{41... | collective-permute-start | bytes 884744 | tf_op jit(solution)/shard_map/ppermute | solution.py:33
  14.4 7.2 %copy-start.2 = (bf16[128,1152]{1,0:T(8,128)(2,1)S(1)}, bf16[128,1152]{1,0:T(8,128)(2,1)}, u32[]{:S(2)}) copy-start(bf16[128,1152]{1,0:T(8,128)(2,1)} %get-tuple-element.49.first_ref) | copy-start | bytes 884740
  14.4 10.9 %collective-permute-start.7 = (bf16[128,1152]{1,0:T(8,128)(2,1)S(1)}, bf16[128,1152]{1,0:T(8,128)(2,1)S(1)}, u32[]{:S(2)}, u32[]{:S(2)}) collective-permute-start(bf16[128,1152]{1,0:T(8,128)(2,1)S(1)} %get-tuple-element.54), channel_id=1, source_target_pairs={{96,0},{97,1},{98,2},{99,3},{100,4},{101,5},{102,6},{103,7},{104,8... | collective-permute-start | bytes 884744 | tf_op jit(solution)/shard_map/ppermute | solution.py:33
  17.4 18.1 %collective-permute-start.8 = (bf16[256,1152]{1,0:T(8,128)(2,1)S(1)}, bf16[256,1152]{1,0:T(8,128)(2,1)S(1)}, u32[]{:S(2)}, u32[]{:S(2)}) collective-permute-start(bf16[256,1152]{1,0:T(8,128)(2,1)S(1)} %stack.3.refs_4_.refs_0_), channel_id=1, source_target_pairs={{96,0},{97,1},{98,2},{99,3},{100,4},{101,5},{102,6},{103,7},{104,8... | collective-permute-start | bytes 1769480 | tf_op jit(solution)/shard_map/ppermute | solution.py:33
  21.6 13.9 %collective-permute-start.4 = (bf16[256,1152]{1,0:T(8,128)(2,1)S(1)}, bf16[256,1152]{1,0:T(8,128)(2,1)S(1)}, u32[]{:S(2)}, u32[]{:S(2)}) collective-permute-start(bf16[256,1152]{1,0:T(8,128)(2,1)S(1)} %stack.2.refs_0_), channel_id=1, source_target_pairs={{32,0},{33,1},{34,2},{35,3},{36,4},{37,5},{38,6},{39,7},{40,8},{41... | collective-permute-start | bytes 1769480 | tf_op jit(solution)/shard_map/ppermute | solution.py:33
  25.3 11.7 %collective-permute-start.9 = (bf16[256,1152]{1,0:T(8,128)(2,1)S(1)}, bf16[256,1152]{1,0:T(8,128)(2,1)S(1)}, u32[]{:S(2)}, u32[]{:S(2)}) collective-permute-start(bf16[256,1152]{1,0:T(8,128)(2,1)S(1)} %constant_dynamic-update-slice_fusion.2.refs_5_.refs_1_), channel_id=1, source_target_pairs={{3,0},{2,1},{1,2},{0,3},{7,4},{6,5},{5,6},{4,7},{11,8},{10,9},{9,1... | collective-permute-start | bytes 1769480 | tf_op jit(solution)/shard_map/ppermute | solution.py:33
  28.7 10.0 %collective-permute-start.5 = (bf16[256,1152]{1,0:T(8,128)(2,1)S(1)}, bf16[256,1152]{1,0:T(8,128)(2,1)S(1)}, u32[]{:S(2)}, u32[]{:S(2)}) collective-permute-start(bf16[256,1152]{1,0:T(8,128)(2,1)S(1)} %constant_dynamic-update-slice_fusion.refs_1_), channel_id=1, source_target_pairs={{1,0},{0,1},{3,2},{2,3},{5,4},{4,5},{7,6},{6,7},{9,8},{8,9},{11,10... | collective-permute-start | bytes 1769480 | tf_op jit(solution)/shard_map/ppermute | solution.py:33
  28.9 14.3 %collective-permute-start.10 = (bf16[256,1152]{1,0:T(8,128)(2,1)S(1)}, bf16[256,1152]{1,0:T(8,128)(2,1)S(1)}, u32[]{:S(2)}, u32[]{:S(2)}) collective-permute-start(bf16[256,1152]{1,0:T(8,128)(2,1)S(1)} %stack.3.refs_4_.refs_0_), channel_id=1, source_target_pairs={{8,0},{9,1},{10,2},{11,3},{12,4},{13,5},{14,6},{15,7},{0,8},{1,9},... | collective-permute-start | bytes 1769480 | tf_op jit(solution)/shard_map/ppermute | solution.py:33
  35.5 7.8 %collective-permute-start.12 = (bf16[256,1152]{1,0:T(8,128)(2,1)S(1)}, bf16[256,1152]{1,0:T(8,128)(2,1)S(1)}, u32[]{:S(2)}, u32[]{:S(2)}) collective-permute-start(bf16[256,1152]{1,0:T(8,128)(2,1)S(1)} %collective-permute-done.8.refs_6_.refs_2_), channel_id=1, source_target_pairs={{8,0},{9,1},{10,2},{11,3},{12,4},{13,5},{14,6},{15,7},{0,8},{1,9},... | collective-permute-start | bytes 1769480 | tf_op jit(solution)/shard_map/ppermute | solution.py:33
  38.7 4.6 %collective-permute-start.13 = (bf16[256,1152]{1,0:T(8,128)(2,1)S(1)}, bf16[256,1152]{1,0:T(8,128)(2,1)S(1)}, u32[]{:S(2)}, u32[]{:S(2)}) collective-permute-start(bf16[256,1152]{1,0:T(8,128)(2,1)S(1)} %collective-permute-done.9.refs_7_.refs_3_), channel_id=1, source_target_pairs={{8,0},{9,1},{10,2},{11,3},{12,4},{13,5},{14,6},{15,7},{0,8},{1,9},... | collective-permute-start | bytes 1769480 | tf_op jit(solution)/shard_map/ppermute | solution.py:33
  38.7 4.6 %collective-permute-start.11 = (bf16[256,1152]{1,0:T(8,128)(2,1)S(1)}, bf16[256,1152]{1,0:T(8,128)(2,1)S(1)}, u32[]{:S(2)}, u32[]{:S(2)}) collective-permute-start(bf16[256,1152]{1,0:T(8,128)(2,1)S(1)} %constant_dynamic-update-slice_fusion.2.refs_5_.refs_1_), channel_id=1, source_target_pairs={{8,0},{9,1},{10,2},{11,3},{12,4},{13,5},{14,6},{15,7},{0,8},{1,9},... | collective-permute-start | bytes 1769480 | tf_op jit(solution)/shard_map/ppermute | solution.py:33
  50.5 5.2 %collective-permute-start.16 = (bf16[512,1152]{1,0:T(8,128)(2,1)S(1)}, bf16[512,1152]{1,0:T(8,128)(2,1)S(1)}, u32[]{:S(2)}, u32[]{:S(2)}) collective-permute-start(bf16[512,1152]{1,0:T(8,128)(2,1)S(1)} %get-tuple-element.66), channel_id=1, source_target_pairs={{8,0},{9,1},{10,2},{11,3},{12,4},{13,5},{14,6},{15,7},{0,8},{1,9},... | collective-permute-start | bytes 3538952 | tf_op jit(solution)/shard_map/ppermute | solution.py:33
  50.5 5.1 %collective-permute-start.17 = (bf16[512,1152]{1,0:T(8,128)(2,1)S(1)}, bf16[512,1152]{1,0:T(8,128)(2,1)S(1)}, u32[]{:S(2)}, u32[]{:S(2)}) collective-permute-start(bf16[512,1152]{1,0:T(8,128)(2,1)S(1)} %get-tuple-element.69), channel_id=1, source_target_pairs={{8,0},{9,1},{10,2},{11,3},{12,4},{13,5},{14,6},{15,7},{0,8},{1,9},... | collective-permute-start | bytes 3538952 | tf_op jit(solution)/shard_map/ppermute | solution.py:33
  51.0 4.1 %collective-permute-start.14 = (f32[8,128]{1,0:T(8,128)S(1)}, f32[8,128]{1,0:T(8,128)S(1)}, u32[]{:S(2)}, u32[]{:S(2)}) collective-permute-start(f32[8,128]{1,0:T(8,128)S(1)} %get-tuple-element.60), channel_id=1, source_target_pairs={{8,0},{9,1},{10,2},{11,3},{12,4},{13,5},{14,6},{15,7},{0,8},{1,9},... | collective-permute-start | bytes 12296 | tf_op jit(solution)/shard_map/ppermute | solution.py:33
  54.1 16.8 %collective-permute-start.30 = (bf16[256,1152]{1,0:T(8,128)(2,1)S(1)}, bf16[256,1152]{1,0:T(8,128)(2,1)S(1)}, u32[]{:S(2)}, u32[]{:S(2)}) collective-permute-start(bf16[256,1152]{1,0:T(8,128)(2,1)S(1)} %get-tuple-element.59), channel_id=1, source_target_pairs={{1,0},{0,1},{3,2},{2,3},{5,4},{4,5},{7,6},{6,7},{9,8},{8,9},{11,10... | collective-permute-start | bytes 1769480 | tf_op jit(solution)/shard_map/ppermute | solution.py:33
  54.3 27.7 %collective-permute-start.28 = (bf16[256,1152]{1,0:T(8,128)(2,1)S(1)}, bf16[256,1152]{1,0:T(8,128)(2,1)S(1)}, u32[]{:S(2)}, u32[]{:S(2)}) collective-permute-start(bf16[256,1152]{1,0:T(8,128)(2,1)S(1)} %get-tuple-element.61), channel_id=1, source_target_pairs={{32,0},{33,1},{34,2},{35,3},{36,4},{37,5},{38,6},{39,7},{40,8},{41... | collective-permute-start | bytes 1769480 | tf_op jit(solution)/shard_map/ppermute | solution.py:33
  55.2 4.8 %collective-permute-start.15 = (f32[24,8,128]{2,1,0:T(8,128)S(1)}, f32[24,8,128]{2,1,0:T(8,128)S(1)}, u32[]{:S(2)}, u32[]{:S(2)}) collective-permute-start(f32[24,8,128]{2,1,0:T(8,128)S(1)} %broadcast_in_dim.4), channel_id=1, source_target_pairs={{16,0},{17,1},{18,2},{19,3},{20,4},{21,5},{22,6},{23,7},{24,8},{25... | collective-permute-start | bytes 294920 | tf_op jit(solution)/shard_map/ppermute | solution.py:33
  57.9 16.2 %collective-permute-start.20 = (bf16[256,1152]{1,0:T(8,128)(2,1)S(1)}, bf16[256,1152]{1,0:T(8,128)(2,1)S(1)}, u32[]{:S(2)}, u32[]{:S(2)}) collective-permute-start(bf16[256,1152]{1,0:T(8,128)(2,1)S(1)} %get-tuple-element.74), channel_id=1, source_target_pairs={{3,0},{2,1},{1,2},{0,3},{7,4},{6,5},{5,6},{4,7},{11,8},{10,9},{9,1... | collective-permute-start | bytes 1769480 | tf_op jit(solution)/shard_map/ppermute | solution.py:33
  62.9 6.5 %collective-permute-start.21 = (f32[24,8,128]{2,1,0:T(8,128)S(1)}, f32[24,8,128]{2,1,0:T(8,128)S(1)}, u32[]{:S(2)}, u32[]{:S(2)}) collective-permute-start(f32[24,8,128]{2,1,0:T(8,128)S(1)} %broadcast_in_dim.5), channel_id=1, source_target_pairs={{20,0},{21,1},{22,2},{23,3},{16,4},{17,5},{18,6},{19,7},{28,8},{29... | collective-permute-start | bytes 294920 | tf_op jit(solution)/shard_map/ppermute | solution.py:33
  65.1 19.5 %collective-permute-start.18 = (bf16[256,1152]{1,0:T(8,128)(2,1)S(1)}, bf16[256,1152]{1,0:T(8,128)(2,1)S(1)}, u32[]{:S(2)}, u32[]{:S(2)}) collective-permute-start(bf16[256,1152]{1,0:T(8,128)(2,1)S(1)} %get-tuple-element.70), channel_id=1, source_target_pairs={{96,0},{97,1},{98,2},{99,3},{100,4},{101,5},{102,6},{103,7},{104,8... | collective-permute-start | bytes 1769480 | tf_op jit(solution)/shard_map/ppermute | solution.py:33
  69.5 3.7 %collective-permute-start.22 = (f32[8,128]{1,0:T(8,128)S(1)}, f32[8,128]{1,0:T(8,128)S(1)}, u32[]{:S(2)}, u32[]{:S(2)}) collective-permute-start(f32[8,128]{1,0:T(8,128)S(1)} %fusion), channel_id=1, source_target_pairs={{1,0},{0,1},{3,2},{2,3},{5,4},{4,5},{7,6},{6,7},{9,8},{8,9},{11,10... | collective-permute-start | bytes 12296 | tf_op jit(solution)/shard_map/ppermute | solution.py:33
  71.3 11.2 %collective-permute-start.31 = (bf16[128,1152]{1,0:T(8,128)(2,1)S(1)}, bf16[128,1152]{1,0:T(8,128)(2,1)S(1)}, u32[]{:S(2)}, u32[]{:S(2)}) collective-permute-start(bf16[128,1152]{1,0:T(8,128)(2,1)S(1)} %get-tuple-element.86), channel_id=1, source_target_pairs={{32,0},{33,1},{34,2},{35,3},{36,4},{37,5},{38,6},{39,7},{40,8},{41... | collective-permute-start | bytes 884744 | tf_op jit(solution)/shard_map/ppermute | solution.py:33
  74.5 12.6 %collective-permute-start.23 = (bf16[128,1152]{1,0:T(8,128)(2,1)S(1)}, bf16[128,1152]{1,0:T(8,128)(2,1)S(1)}, u32[]{:S(2)}, u32[]{:S(2)}) collective-permute-start(bf16[128,1152]{1,0:T(8,128)(2,1)S(1)} %get-tuple-element.78), channel_id=1, source_target_pairs={{96,0},{97,1},{98,2},{99,3},{100,4},{101,5},{102,6},{103,7},{104,8... | collective-permute-start | bytes 884744 | tf_op jit(solution)/shard_map/ppermute | solution.py:33
  77.1 3.6 %collective-permute-start.24 = (f32[8,128]{1,0:T(8,128)S(1)}, f32[8,128]{1,0:T(8,128)S(1)}, u32[]{:S(2)}, u32[]{:S(2)}) collective-permute-start(f32[8,128]{1,0:T(8,128)S(1)} %add.25), channel_id=1, source_target_pairs={{32,0},{33,1},{34,2},{35,3},{36,4},{37,5},{38,6},{39,7},{40,8},{41... | collective-permute-start | bytes 12296 | tf_op jit(solution)/shard_map/ppermute | solution.py:33
  80.7 6.4 %collective-permute-start.25 = (f32[8,128]{1,0:T(8,128)S(1)}, f32[8,128]{1,0:T(8,128)S(1)}, u32[]{:S(2)}, u32[]{:S(2)}) collective-permute-start(f32[8,128]{1,0:T(8,128)S(1)} %add.26), channel_id=1, source_target_pairs={{3,0},{2,1},{1,2},{0,3},{7,4},{6,5},{5,6},{4,7},{11,8},{10,9},{9,1... | collective-permute-start | bytes 12296 | tf_op jit(solution)/shard_map/ppermute | solution.py:33
  82.5 8.4 %collective-permute-start.29 = (bf16[128,1152]{1,0:T(8,128)(2,1)S(1)}, bf16[128,1152]{1,0:T(8,128)(2,1)S(1)}, u32[]{:S(2)}, u32[]{:S(2)}) collective-permute-start(bf16[128,1152]{1,0:T(8,128)(2,1)S(1)} %get-tuple-element.83), channel_id=1, source_target_pairs={{1,0},{0,1},{3,2},{2,3},{5,4},{4,5},{7,6},{6,7},{9,8},{8,9},{11,10... | collective-permute-start | bytes 884744 | tf_op jit(solution)/shard_map/ppermute | solution.py:33
  82.8 8.1 %copy-start = (bf16[128,1152]{1,0:T(8,128)(2,1)S(1)}, bf16[128,1152]{1,0:T(8,128)(2,1)}, u32[]{:S(2)}) copy-start(bf16[128,1152]{1,0:T(8,128)(2,1)} %raw_ref.3) | copy-start | bytes 884740
  82.9 8.1 %collective-permute-start.32 = (bf16[128,1152]{1,0:T(8,128)(2,1)S(1)}, bf16[128,1152]{1,0:T(8,128)(2,1)S(1)}, u32[]{:S(2)}, u32[]{:S(2)}) collective-permute-start(bf16[128,1152]{1,0:T(8,128)(2,1)S(1)} %add_codes.3), channel_id=1, source_target_pairs={{16,0},{17,1},{18,2},{19,3},{20,4},{21,5},{22,6},{23,7},{24,8},{25... | collective-permute-start | bytes 884744 | tf_op jit(solution)/shard_map/ppermute | solution.py:33
  85.0 9.4 %collective-permute-start.19 = (bf16[128,1152]{1,0:T(8,128)(2,1)S(1)}, bf16[128,1152]{1,0:T(8,128)(2,1)S(1)}, u32[]{:S(2)}, u32[]{:S(2)}) collective-permute-start(bf16[128,1152]{1,0:T(8,128)(2,1)S(1)} %get-tuple-element.72), channel_id=1, source_target_pairs={{3,0},{2,1},{1,2},{0,3},{7,4},{6,5},{5,6},{4,7},{11,8},{10,9},{9,1... | collective-permute-start | bytes 884744 | tf_op jit(solution)/shard_map/ppermute | solution.py:33
  87.1 8.3 %copy-start.1 = (bf16[128,1152]{1,0:T(8,128)(2,1)S(1)}, bf16[128,1152]{1,0:T(8,128)(2,1)}, u32[]{:S(2)}) copy-start(bf16[128,1152]{1,0:T(8,128)(2,1)} %raw_ref.2) | copy-start | bytes 884740
  87.4 8.0 %collective-permute-start.26 = (bf16[128,1152]{1,0:T(8,128)(2,1)S(1)}, bf16[128,1152]{1,0:T(8,128)(2,1)S(1)}, u32[]{:S(2)}, u32[]{:S(2)}) collective-permute-start(bf16[128,1152]{1,0:T(8,128)(2,1)S(1)} %add_codes.2), channel_id=1, source_target_pairs={{20,0},{21,1},{22,2},{23,3},{16,4},{17,5},{18,6},{19,7},{28,8},{29... | collective-permute-start | bytes 884744 | tf_op jit(solution)/shard_map/ppermute | solution.py:33
  89.6 4.8 %collective-permute-start.27 = (f32[8,128]{1,0:T(8,128)S(1)}, f32[8,128]{1,0:T(8,128)S(1)}, u32[]{:S(2)}, u32[]{:S(2)}) collective-permute-start(f32[8,128]{1,0:T(8,128)S(1)} %add.27.loss_ref.loss_in), channel_id=1, source_target_pairs={{96,0},{97,1},{98,2},{99,3},{100,4},{101,5},{102,6},{103,7},{104,8... | collective-permute-start | bytes 12296 | tf_op jit(solution)/shard_map/ppermute | solution.py:33

commit v7 on v6

--- a/solution.py
+++ b/solution.py
@@ -332,10 +332,10 @@
     text_far = swap(text_far, TEXT_PAIRS["y"])
     text_near = swap(text_near, TEXT_PAIRS["z"])
     loss = after(loss, near_late)
-    tiles = swap(jnp.broadcast_to(loss[None], (24, *loss.shape)), IMAGE_PAIRS["x"])
+    tiles = swap(jnp.broadcast_to(loss[None], (16, *loss.shape)), IMAGE_PAIRS["x"])
     loss = loss + tiles[0]
     near_early, far_early = image_terms(0, 2, jnp.float32, (after(own_coeff, far_late, loss), other_coeff), text_all)
-    tiles = swap(jnp.broadcast_to(loss[None], (24, *loss.shape)), TEXT_PAIRS["x"])
+    tiles = swap(jnp.broadcast_to(loss[None], (16, *loss.shape)), TEXT_PAIRS["x"])
     text_early = text_terms(0, jnp.float32, after(own_coeff, near_early), other_early, image_all)
 
     image_kept, image_sent = fold(far_early, image_far)

time: 97.2 us -> 97.2 us (level)
  no operation moved by 1% of the time
where the time goes in v7:
time: 97.2 us; the launch traced here: 97.1 us
  starting transfers between devices  42.5 us (44%)
  Pallas kernels  28.5 us (29%)
  waiting for transfers between devices  23.5 us (24%)
  between operations  2.43 us (2%)
    ppermute x33, starting transfers between devices, swap(): lax.ppermute(value, axes, [(k ^ mask, k) for k in range(lax.axis_size(axe...  42.5 us
    ppermute x33, waiting for transfers between devices, swap(): lax.ppermute(value, axes, [(k ^ mask, k) for k in range(lax.axis_size(axe...  23.5 us
    pallas_call x2, Pallas kernels, logit_terms(): pl.pallas_call(functools.partial(logit_kernel, core, loss_scale), out_sha...  11.2 us
    pallas_call x2, Pallas kernels, image_terms(): pl.pallas_call(functools.partial(image_kernel, first), out_shape=[shape_o...  5.82 us
    pallas_call x2, Pallas kernels, text_terms(): pl.pallas_call(functools.partial(text_kernel, first), out_shape=[shape_of...  4.06 us
    pallas_call x2, Pallas kernels, finish(): pl.pallas_call(finish_kernel, out_shape=[shape_of(*raw.shape, jnp.float32...  2.85 us
    pallas_call x9, Pallas kernels, small_call(): pl.pallas_call(kernel, out_shape=out_shape, in_specs=[VMEM] * len(operand...  2.6 us
    pallas_call x1, Pallas kernels, unit_rows(): pl.pallas_call(unit_kernel, out_shape=[out, out], in_specs=[HBM, HBM], ou...  1.99 us
  transfers between devices with their start and end apart: 33, of which 12 were waited for; matrix products, arithmetic and copies ran while one was open for 0% of the time, Pallas kernels for 21%

profile of v7, /device:TPU:0, one launch (start us, length us, event | category | flops | bytes accessed | tf_op | source)
XLA Modules:
  0.0 97.1 jit_solution(1078213728158696166)
XLA Ops:
  0.6 1.7 %collective-permute-start = (bf16[128,1152]{1,0:T(8,128)(2,1)}, bf16[128,1152]{1,0:T(8,128)(2,1)S(1)}, u32[]{:S(2)}, u32[]{:S(2)}) collective-permute-start(bf16[128,1152]{1,0:T(8,128)(2,1)} %raw_ref.3), channel_id=1, source_target_pairs={{16,0},{17,1},{18,2},{19,3},{20,4},{21,5},{22,6},{23,7},{24,8},{25... | collective-permute-start | bytes 884744 | tf_op jit(solution)/shard_map/ppermute | solution.py:33
  2.3 2.1 %collective-permute-start.1 = (bf16[128,1152]{1,0:T(8,128)(2,1)}, bf16[128,1152]{1,0:T(8,128)(2,1)S(1)}, u32[]{:S(2)}, u32[]{:S(2)}) collective-permute-start(bf16[128,1152]{1,0:T(8,128)(2,1)} %raw_ref.2), channel_id=1, source_target_pairs={{20,0},{21,1},{22,2},{23,3},{16,4},{17,5},{18,6},{19,7},{28,8},{29... | collective-permute-start | bytes 884744 | tf_op jit(solution)/shard_map/ppermute | solution.py:33
  4.4 2.0 %unit_rows.1 = (bf16[128,1152]{1,0:T(8,128)(2,1)}, bf16[128,1152]{1,0:T(8,128)(2,1)}) custom-call(bf16[128,1152]{1,0:T(8,128)(2,1)} %raw_ref.3, bf16[128,1152]{1,0:T(8,128)(2,1)} %raw_ref.2), custom_call_target="tpu_custom_call" | custom-call | tf_op jit(solution)/shard_map/unit_rows/pallas_call | solution.py:60
  6.4 0.0 copy-start.3
  6.4 1.7 %collective-permute-start.2 = (bf16[128,1152]{1,0:T(8,128)(2,1)}, bf16[128,1152]{1,0:T(8,128)(2,1)S(1)}, u32[]{:S(2)}, u32[]{:S(2)}) collective-permute-start(bf16[128,1152]{1,0:T(8,128)(2,1)} %get-tuple-element.49.first_ref), channel_id=1, source_target_pairs={{1,0},{0,1},{3,2},{2,3},{5,4},{4,5},{7,6},{6,7},{9,8},{8,9},{11,10... | collective-permute-start | bytes 884744 | tf_op jit(solution)/shard_map/ppermute | solution.py:33
  8.0 2.2 %collective-permute-start.6 = (bf16[128,1152]{1,0:T(8,128)(2,1)}, bf16[128,1152]{1,0:T(8,128)(2,1)S(1)}, u32[]{:S(2)}, u32[]{:S(2)}) collective-permute-start(bf16[128,1152]{1,0:T(8,128)(2,1)} %get-tuple-element.53.first_ref), channel_id=1, source_target_pairs={{3,0},{2,1},{1,2},{0,3},{7,4},{6,5},{5,6},{4,7},{11,8},{10,9},{9,1... | collective-permute-start | bytes 884744 | tf_op jit(solution)/shard_map/ppermute | solution.py:33
  11.6 0.0 collective-permute-done.images_ref
  11.6 0.6 collective-permute-done.1.texts_ref
  12.2 0.2 far_units.1
  12.4 2.0 %collective-permute-start.3 = (bf16[128,1152]{1,0:T(8,128)(2,1)S(1)}, bf16[128,1152]{1,0:T(8,128)(2,1)S(1)}, u32[]{:S(2)}, u32[]{:S(2)}) collective-permute-start(bf16[128,1152]{1,0:T(8,128)(2,1)S(1)} %get-tuple-element.52), channel_id=1, source_target_pairs={{32,0},{33,1},{34,2},{35,3},{36,4},{37,5},{38,6},{39,7},{40,8},{41... | collective-permute-start | bytes 884744 | tf_op jit(solution)/shard_map/ppermute | solution.py:33
  14.4 2.5 %collective-permute-start.7 = (bf16[128,1152]{1,0:T(8,128)(2,1)S(1)}, bf16[128,1152]{1,0:T(8,128)(2,1)S(1)}, u32[]{:S(2)}, u32[]{:S(2)}) collective-permute-start(bf16[128,1152]{1,0:T(8,128)(2,1)S(1)} %get-tuple-element.54), channel_id=1, source_target_pairs={{96,0},{97,1},{98,2},{99,3},{100,4},{101,5},{102,6},{103,7},{104,8... | collective-permute-start | bytes 884744 | tf_op jit(solution)/shard_map/ppermute | solution.py:33
  17.0 0.4 collective-permute-done.6.second_ref
  17.4 4.1 %collective-permute-start.8 = (bf16[256,1152]{1,0:T(8,128)(2,1)S(1)}, bf16[256,1152]{1,0:T(8,128)(2,1)S(1)}, u32[]{:S(2)}, u32[]{:S(2)}) collective-permute-start(bf16[256,1152]{1,0:T(8,128)(2,1)S(1)} %stack.3.refs_4_.refs_0_), channel_id=1, source_target_pairs={{96,0},{97,1},{98,2},{99,3},{100,4},{101,5},{102,6},{103,7},{104,8... | collective-permute-start | bytes 1769480 | tf_op jit(solution)/shard_map/ppermute | solution.py:33
  21.5 0.0 collective-permute-done.2.second_ref
  21.6 0.1 collective-permute-start.4
  21.7 3.5 %collective-permute-done.7 = bf16[128,1152]{1,0:T(8,128)(2,1)S(1)} collective-permute-done((bf16[128,1152]{1,0:T(8,128)(2,1)S(1)}, bf16[128,1152]{1,0:T(8,128)(2,1)S(1)}, u32[]{:S(2)}, u32[]{:S(2)}) %collective-permute-start.7) | collective-permute-done | bytes 294944 | tf_op jit(solution)/shard_map/ppermute | solution.py:33
  25.3 3.4 %collective-permute-start.9 = (bf16[256,1152]{1,0:T(8,128)(2,1)S(1)}, bf16[256,1152]{1,0:T(8,128)(2,1)S(1)}, u32[]{:S(2)}, u32[]{:S(2)}) collective-permute-start(bf16[256,1152]{1,0:T(8,128)(2,1)S(1)} %constant_dynamic-update-slice_fusion.2.refs_5_.refs_1_), channel_id=1, source_target_pairs={{3,0},{2,1},{1,2},{0,3},{7,4},{6,5},{5,6},{4,7},{11,8},{10,9},{9,1... | collective-permute-start | bytes 1769480 | tf_op jit(solution)/shard_map/ppermute | solution.py:33
  28.7 0.0 collective-permute-done.3
  28.7 0.2 collective-permute-start.5
  28.9 6.6 %collective-permute-done.8.refs_6_.refs_2_ = bf16[256,1152]{1,0:T(8,128)(2,1)S(1)} collective-permute-done((bf16[256,1152]{1,0:T(8,128)(2,1)S(1)}, bf16[256,1152]{1,0:T(8,128)(2,1)S(1)}, u32[]{:S(2)}, u32[]{:S(2)}) %collective-permute-start.8) | collective-permute-done | bytes 589856 | tf_op jit(solution)/shard_map/ppermute | solution.py:33
  35.5 0.0 collective-permute-start.12
  35.5 1.4 %collective-permute-done.9.refs_7_.refs_3_ = bf16[256,1152]{1,0:T(8,128)(2,1)S(1)} collective-permute-done((bf16[256,1152]{1,0:T(8,128)(2,1)S(1)}, bf16[256,1152]{1,0:T(8,128)(2,1)S(1)}, u32[]{:S(2)}, u32[]{:S(2)}) %collective-permute-start.9) | collective-permute-done | bytes 589856 | tf_op jit(solution)/shard_map/ppermute | solution.py:33
  36.9 1.7 %collective-permute-done.5.refs_3_ = bf16[256,1152]{1,0:T(8,128)(2,1)S(1)} collective-permute-done((bf16[256,1152]{1,0:T(8,128)(2,1)S(1)}, bf16[256,1152]{1,0:T(8,128)(2,1)S(1)}, u32[]{:S(2)}, u32[]{:S(2)}) %collective-permute-start.5) | collective-permute-done | bytes 589856 | tf_op jit(solution)/shard_map/ppermute | solution.py:33
  38.7 0.5 collective-permute-start.11
  39.2 4.1 %own_logits.1 = (bf16[1024,1024]{1,0:T(8,128)(2,1)S(1)}, f32[8,128]{1,0:T(8,128)S(1)}) custom-call(s32[1]{0:T(128)} %bitcast.place_ref, f32[1,1]{1,0:T(1,128)} %bitcast.1.temper_ref, f32[1,1]{1,0:T(1,128)} %bitcast.2.shift_ref, bf16[256,1152]{1,0:T(8,128)(2,1)S(1)} %stack.2.refs_0_, bf16[256,1152]{1,0:T(8,128)(2,1)S(1)} %constant_dynamic-update-slice_fusion.refs_1_, ...), custom_call_target="tpu_custom_call" | custom-call | flops 2415919104 | bytes 8388608 | tf_op jit(solution)/shard_map/own_logits/pallas_call | solution.py:170
  43.3 7.1 %other_logits.1 = (bf16[1024,1024]{1,0:T(8,128)(2,1)S(1)}, bf16[512,1152]{1,0:T(8,128)(2,1)S(1)}, bf16[512,1152]{1,0:T(8,128)(2,1)S(1)}, f32[8,128]{1,0:T(8,128)S(1)}) custom-call(s32[1]{0:T(128)} %bitcast.place_ref, f32[1,1]{1,0:T(1,128)} %bitcast.1.temper_ref, f32[1,1]{1,0:T(1,128)} %bitcast.2.shift_ref, bf16[256,1152]{1,0:T(8,128)(2,1)S(1)} %stack.2.refs_0_, ...), custom_call_target="tpu_custom_call" | custom-call | flops 4831838208 | bytes 8388608 | tf_op jit(solution)/shard_map/other_logits/pallas_call | solution.py:170
  50.5 0.1 collective-permute-start.16
  50.5 0.5 collective-permute-start.17
  51.0 0.1 collective-permute-start.14
  51.1 2.9 %image_terms.2 = (bf16[256,1152]{1,0:T(8,128)(2,1)S(1)}, bf16[256,1152]{1,0:T(8,128)(2,1)S(1)}) custom-call(bf16[1024,1024]{1,0:T(8,128)(2,1)S(1)} %get-tuple-element.68.own_ref.coeff_ref, bf16[1024,1024]{1,0:T(8,128)(2,1)S(1)} %get-tuple-element.58.other_ref, bf16[256,1152]{1,0:T(8,128)(2,1)S(1)} %stack.3.refs_4_.refs_0_, ...), custom_call_target="tpu_custom_call" | custom-call | flops 2415919104 | bytes 8388608 | tf_op jit(solution)/shard_map/image_terms/pallas_call | solution.py:224
  54.1 0.2 collective-permute-start.30
  54.3 0.9 collective-permute-start.28
  55.2 0.5 collective-permute-start.15
  55.6 2.2 %text_terms.3 = (bf16[256,1152]{1,0:T(8,128)(2,1)S(1)}, bf16[256,1152]{1,0:T(8,128)(2,1)S(1)}) custom-call(bf16[1024,1024]{1,0:T(8,128)(2,1)S(1)} %get-tuple-element.68.own_ref.coeff_ref, bf16[512,1152]{1,0:T(8,128)(2,1)S(1)} %collective-permute-done.17.came_ref, bf16[256,1152]{1,0:T(8,128)(2,1)S(1)} %stack.2.refs_0_, ...), custom_call_target="tpu_custom_call" | custom-call | flops 1207959552 | bytes 8388608 | tf_op jit(solution)/shard_map/text_terms/pallas_call | solution.py:196
  57.9 1.2 %collective-permute-start.20 = (bf16[256,1152]{1,0:T(8,128)(2,1)S(1)}, bf16[256,1152]{1,0:T(8,128)(2,1)S(1)}, u32[]{:S(2)}, u32[]{:S(2)}) collective-permute-start(bf16[256,1152]{1,0:T(8,128)(2,1)S(1)} %get-tuple-element.74), channel_id=1, source_target_pairs={{3,0},{2,1},{1,2},{0,3},{7,4},{6,5},{5,6},{4,7},{11,8},{10,9},{9,1... | collective-permute-start | bytes 1769480 | tf_op jit(solution)/shard_map/ppermute | solution.py:33
  59.1 0.4 collective-permute-done.15
  59.5 2.9 %image_terms.3 = (f32[256,1152]{1,0:T(8,128)S(1)}, f32[256,1152]{1,0:T(8,128)S(1)}) custom-call(bf16[1024,1024]{1,0:T(8,128)(2,1)S(1)} %get-tuple-element.68.own_ref.coeff_ref, bf16[1024,1024]{1,0:T(8,128)(2,1)S(1)} %get-tuple-element.58.other_ref, bf16[256,1152]{1,0:T(8,128)(2,1)S(1)} %stack.3.refs_4_.refs_0_, ...), custom_call_target="tpu_custom_call" | custom-call | flops 2415919104 | bytes 8388608 | tf_op jit(solution)/shard_map/image_terms/pallas_call | solution.py:224
  62.4 2.2 %collective-permute-start.21 = (f32[16,8,128]{2,1,0:T(8,128)S(1)}, f32[16,8,128]{2,1,0:T(8,128)S(1)}, u32[]{:S(2)}, u32[]{:S(2)}) collective-permute-start(f32[16,8,128]{2,1,0:T(8,128)S(1)} %broadcast_in_dim.5), channel_id=1, source_target_pairs={{20,0},{21,1},{22,2},{23,3},{16,4},{17,5},{18,6},{19,7},{28,8},{29... | collective-permute-start | bytes 196616 | tf_op jit(solution)/shard_map/ppermute | solution.py:33
  64.6 2.4 %collective-permute-start.18 = (bf16[256,1152]{1,0:T(8,128)(2,1)S(1)}, bf16[256,1152]{1,0:T(8,128)(2,1)S(1)}, u32[]{:S(2)}, u32[]{:S(2)}) collective-permute-start(bf16[256,1152]{1,0:T(8,128)(2,1)S(1)} %get-tuple-element.70), channel_id=1, source_target_pairs={{96,0},{97,1},{98,2},{99,3},{100,4},{101,5},{102,6},{103,7},{104,8... | collective-permute-start | bytes 1769480 | tf_op jit(solution)/shard_map/ppermute | solution.py:33
  67.0 1.8 %text_terms.2 = (f32[256,1152]{1,0:T(8,128)S(1)}, f32[256,1152]{1,0:T(8,128)S(1)}) custom-call(bf16[1024,1024]{1,0:T(8,128)(2,1)S(1)} %get-tuple-element.68.own_ref.coeff_ref, bf16[512,1152]{1,0:T(8,128)(2,1)S(1)} %collective-permute-done.16.came_ref, bf16[256,1152]{1,0:T(8,128)(2,1)S(1)} %stack.2.refs_0_, ...), custom_call_target="tpu_custom_call" | custom-call | flops 1207959552 | bytes 8388608 | tf_op jit(solution)/shard_map/text_terms/pallas_call | solution.py:196
  68.9 1.6 %collective-permute-start.22 = (f32[8,128]{1,0:T(8,128)S(1)}, f32[8,128]{1,0:T(8,128)S(1)}, u32[]{:S(2)}, u32[]{:S(2)}) collective-permute-start(f32[8,128]{1,0:T(8,128)S(1)} %fusion), channel_id=1, source_target_pairs={{1,0},{0,1},{3,2},{2,3},{5,4},{4,5},{7,6},{6,7},{9,8},{8,9},{11,10... | collective-permute-start | bytes 12296 | tf_op jit(solution)/shard_map/ppermute | solution.py:33
  70.5 0.4 fold.7
  71.0 1.1 %collective-permute-start.31 = (bf16[128,1152]{1,0:T(8,128)(2,1)S(1)}, bf16[128,1152]{1,0:T(8,128)(2,1)S(1)}, u32[]{:S(2)}, u32[]{:S(2)}) collective-permute-start(bf16[128,1152]{1,0:T(8,128)(2,1)S(1)} %get-tuple-element.86), channel_id=1, source_target_pairs={{32,0},{33,1},{34,2},{35,3},{36,4},{37,5},{38,6},{39,7},{40,8},{41... | collective-permute-start | bytes 884744 | tf_op jit(solution)/shard_map/ppermute | solution.py:33
  72.0 0.5 collective-permute-done.22
  72.6 1.5 %collective-permute-done.20.came_ref = bf16[256,1152]{1,0:T(8,128)(2,1)S(1)} collective-permute-done((bf16[256,1152]{1,0:T(8,128)(2,1)S(1)}, bf16[256,1152]{1,0:T(8,128)(2,1)S(1)}, u32[]{:S(2)}, u32[]{:S(2)}) %collective-permute-start.20) | collective-permute-done | bytes 589856 | tf_op jit(solution)/shard_map/ppermute | solution.py:33
  74.1 0.4 fold.5
  74.5 2.6 %collective-permute-start.23 = (bf16[128,1152]{1,0:T(8,128)(2,1)S(1)}, bf16[128,1152]{1,0:T(8,128)(2,1)S(1)}, u32[]{:S(2)}, u32[]{:S(2)}) collective-permute-start(bf16[128,1152]{1,0:T(8,128)(2,1)S(1)} %get-tuple-element.78), channel_id=1, source_target_pairs={{96,0},{97,1},{98,2},{99,3},{100,4},{101,5},{102,6},{103,7},{104,8... | collective-permute-start | bytes 884744 | tf_op jit(solution)/shard_map/ppermute | solution.py:33
  77.1 0.6 collective-permute-start.24
  77.7 3.0 %collective-permute-done.24 = f32[8,128]{1,0:T(8,128)S(1)} collective-permute-done((f32[8,128]{1,0:T(8,128)S(1)}, f32[8,128]{1,0:T(8,128)S(1)}, u32[]{:S(2)}, u32[]{:S(2)}) %collective-permute-start.24) | collective-permute-done | bytes 4128 | tf_op jit(solution)/shard_map/ppermute | solution.py:33
  80.7 1.3 %collective-permute-start.25 = (f32[8,128]{1,0:T(8,128)S(1)}, f32[8,128]{1,0:T(8,128)S(1)}, u32[]{:S(2)}, u32[]{:S(2)}) collective-permute-start(f32[8,128]{1,0:T(8,128)S(1)} %add.26), channel_id=1, source_target_pairs={{3,0},{2,1},{1,2},{0,3},{7,4},{6,5},{5,6},{4,7},{11,8},{10,9},{9,1... | collective-permute-start | bytes 12296 | tf_op jit(solution)/shard_map/ppermute | solution.py:33
  82.0 0.4 fold.6
  82.5 0.1 collective-permute-start.29
  82.6 0.3 add_codes.3
  82.8 0.0 copy-start
  82.8 1.7 %collective-permute-start.32 = (bf16[128,1152]{1,0:T(8,128)(2,1)S(1)}, bf16[128,1152]{1,0:T(8,128)(2,1)S(1)}, u32[]{:S(2)}, u32[]{:S(2)}) collective-permute-start(bf16[128,1152]{1,0:T(8,128)(2,1)S(1)} %add_codes.3), channel_id=1, source_target_pairs={{16,0},{17,1},{18,2},{19,3},{20,4},{21,5},{22,6},{23,7},{24,8},{25... | collective-permute-start | bytes 884744 | tf_op jit(solution)/shard_map/ppermute | solution.py:33
  84.6 0.4 fold.4
  85.0 2.1 %collective-permute-start.19 = (bf16[128,1152]{1,0:T(8,128)(2,1)S(1)}, bf16[128,1152]{1,0:T(8,128)(2,1)S(1)}, u32[]{:S(2)}, u32[]{:S(2)}) collective-permute-start(bf16[128,1152]{1,0:T(8,128)(2,1)S(1)} %get-tuple-element.72), channel_id=1, source_target_pairs={{3,0},{2,1},{1,2},{0,3},{7,4},{6,5},{5,6},{4,7},{11,8},{10,9},{9,1... | collective-permute-start | bytes 884744 | tf_op jit(solution)/shard_map/ppermute | solution.py:33
  87.2 0.3 add_codes.2
  87.4 2.2 %collective-permute-start.26 = (bf16[128,1152]{1,0:T(8,128)(2,1)S(1)}, bf16[128,1152]{1,0:T(8,128)(2,1)S(1)}, u32[]{:S(2)}, u32[]{:S(2)}) collective-permute-start(bf16[128,1152]{1,0:T(8,128)(2,1)S(1)} %add_codes.2), channel_id=1, source_target_pairs={{20,0},{21,1},{22,2},{23,3},{16,4},{17,5},{18,6},{19,7},{28,8},{29... | collective-permute-start | bytes 884744 | tf_op jit(solution)/shard_map/ppermute | solution.py:33
  89.6 0.7 collective-permute-start.27
  90.3 1.4 %finish.3 = (f32[128,1152]{1,0:T(8,128)}, f32[1]{0:T(128)}) custom-call(bf16[128,1152]{1,0:T(8,128)(2,1)S(1)} %copy-done, f32[128,1152]{1,0:T(8,128)S(1)} %get-tuple-element.82.own_ref, bf16[128,1152]{1,0:T(8,128)(2,1)S(1)} %collective-permute-done.29.ring_ref, bf16[128,1152]{1,0:T(8,128)(2,1)S(1)} %collective-permute-done.32.far_ref, ...), custom_call_target="tpu_custom_call" | custom-call | tf_op jit(solution)/shard_map/finish/pallas_call | solution.py:275
  91.8 2.6 %collective-permute-done.27.loss_in = f32[8,128]{1,0:T(8,128)S(1)} collective-permute-done((f32[8,128]{1,0:T(8,128)S(1)}, f32[8,128]{1,0:T(8,128)S(1)}, u32[]{:S(2)}, u32[]{:S(2)}) %collective-permute-start.27) | collective-permute-done | bytes 4128 | tf_op jit(solution)/shard_map/ppermute | solution.py:33
  94.4 1.0 %collective-permute-done.26.far_ref = bf16[128,1152]{1,0:T(8,128)(2,1)S(1)} collective-permute-done((bf16[128,1152]{1,0:T(8,128)(2,1)S(1)}, bf16[128,1152]{1,0:T(8,128)(2,1)S(1)}, u32[]{:S(2)}, u32[]{:S(2)}) %collective-permute-start.26) | collective-permute-done | bytes 294944 | tf_op jit(solution)/shard_map/ppermute | solution.py:33
  95.5 1.4 %finish.2 = (f32[128,1152]{1,0:T(8,128)}, f32[1]{0:T(128)}) custom-call(bf16[128,1152]{1,0:T(8,128)(2,1)S(1)} %copy-done.1, f32[128,1152]{1,0:T(8,128)S(1)} %get-tuple-element.71.own_ref, bf16[128,1152]{1,0:T(8,128)(2,1)S(1)} %collective-permute-done.19.ring_ref, bf16[128,1152]{1,0:T(8,128)(2,1)S(1)} %collective-permute-done.26.far_ref, ...), custom_call_target="tpu_custom_call" | custom-call | tf_op jit(solution)/shard_map/finish/pallas_call | solution.py:275
  (40 shorter events, 0.3 us)
Async XLA Ops:
  0.6 10.9 %collective-permute-start = (bf16[128,1152]{1,0:T(8,128)(2,1)}, bf16[128,1152]{1,0:T(8,128)(2,1)S(1)}, u32[]{:S(2)}, u32[]{:S(2)}) collective-permute-start(bf16[128,1152]{1,0:T(8,128)(2,1)} %raw_ref.3), channel_id=1, source_target_pairs={{16,0},{17,1},{18,2},{19,3},{20,4},{21,5},{22,6},{23,7},{24,8},{25... | collective-permute-start | bytes 884744 | tf_op jit(solution)/shard_map/ppermute | solution.py:33
  2.3 9.9 %collective-permute-start.1 = (bf16[128,1152]{1,0:T(8,128)(2,1)}, bf16[128,1152]{1,0:T(8,128)(2,1)S(1)}, u32[]{:S(2)}, u32[]{:S(2)}) collective-permute-start(bf16[128,1152]{1,0:T(8,128)(2,1)} %raw_ref.2), channel_id=1, source_target_pairs={{20,0},{21,1},{22,2},{23,3},{16,4},{17,5},{18,6},{19,7},{28,8},{29... | collective-permute-start | bytes 884744 | tf_op jit(solution)/shard_map/ppermute | solution.py:33
  6.4 11.0 %copy-start.3 = (bf16[128,1152]{1,0:T(8,128)(2,1)S(1)}, bf16[128,1152]{1,0:T(8,128)(2,1)}, u32[]{:S(2)}) copy-start(bf16[128,1152]{1,0:T(8,128)(2,1)} %get-tuple-element.53.first_ref) | copy-start | bytes 884740
  6.4 15.2 %collective-permute-start.2 = (bf16[128,1152]{1,0:T(8,128)(2,1)}, bf16[128,1152]{1,0:T(8,128)(2,1)S(1)}, u32[]{:S(2)}, u32[]{:S(2)}) collective-permute-start(bf16[128,1152]{1,0:T(8,128)(2,1)} %get-tuple-element.49.first_ref), channel_id=1, source_target_pairs={{1,0},{0,1},{3,2},{2,3},{5,4},{4,5},{7,6},{6,7},{9,8},{8,9},{11,10... | collective-permute-start | bytes 884744 | tf_op jit(solution)/shard_map/ppermute | solution.py:33
  8.0 9.3 %collective-permute-start.6 = (bf16[128,1152]{1,0:T(8,128)(2,1)}, bf16[128,1152]{1,0:T(8,128)(2,1)S(1)}, u32[]{:S(2)}, u32[]{:S(2)}) collective-permute-start(bf16[128,1152]{1,0:T(8,128)(2,1)} %get-tuple-element.53.first_ref), channel_id=1, source_target_pairs={{3,0},{2,1},{1,2},{0,3},{7,4},{6,5},{5,6},{4,7},{11,8},{10,9},{9,1... | collective-permute-start | bytes 884744 | tf_op jit(solution)/shard_map/ppermute | solution.py:33
  12.4 16.3 %collective-permute-start.3 = (bf16[128,1152]{1,0:T(8,128)(2,1)S(1)}, bf16[128,1152]{1,0:T(8,128)(2,1)S(1)}, u32[]{:S(2)}, u32[]{:S(2)}) collective-permute-start(bf16[128,1152]{1,0:T(8,128)(2,1)S(1)} %get-tuple-element.52), channel_id=1, source_target_pairs={{32,0},{33,1},{34,2},{35,3},{36,4},{37,5},{38,6},{39,7},{40,8},{41... | collective-permute-start | bytes 884744 | tf_op jit(solution)/shard_map/ppermute | solution.py:33
  14.4 7.2 %copy-start.2 = (bf16[128,1152]{1,0:T(8,128)(2,1)S(1)}, bf16[128,1152]{1,0:T(8,128)(2,1)}, u32[]{:S(2)}) copy-start(bf16[128,1152]{1,0:T(8,128)(2,1)} %get-tuple-element.49.first_ref) | copy-start | bytes 884740
  14.4 10.9 %collective-permute-start.7 = (bf16[128,1152]{1,0:T(8,128)(2,1)S(1)}, bf16[128,1152]{1,0:T(8,128)(2,1)S(1)}, u32[]{:S(2)}, u32[]{:S(2)}) collective-permute-start(bf16[128,1152]{1,0:T(8,128)(2,1)S(1)} %get-tuple-element.54), channel_id=1, source_target_pairs={{96,0},{97,1},{98,2},{99,3},{100,4},{101,5},{102,6},{103,7},{104,8... | collective-permute-start | bytes 884744 | tf_op jit(solution)/shard_map/ppermute | solution.py:33
  17.4 18.1 %collective-permute-start.8 = (bf16[256,1152]{1,0:T(8,128)(2,1)S(1)}, bf16[256,1152]{1,0:T(8,128)(2,1)S(1)}, u32[]{:S(2)}, u32[]{:S(2)}) collective-permute-start(bf16[256,1152]{1,0:T(8,128)(2,1)S(1)} %stack.3.refs_4_.refs_0_), channel_id=1, source_target_pairs={{96,0},{97,1},{98,2},{99,3},{100,4},{101,5},{102,6},{103,7},{104,8... | collective-permute-start | bytes 1769480 | tf_op jit(solution)/shard_map/ppermute | solution.py:33
  21.6 13.9 %collective-permute-start.4 = (bf16[256,1152]{1,0:T(8,128)(2,1)S(1)}, bf16[256,1152]{1,0:T(8,128)(2,1)S(1)}, u32[]{:S(2)}, u32[]{:S(2)}) collective-permute-start(bf16[256,1152]{1,0:T(8,128)(2,1)S(1)} %stack.2.refs_0_), channel_id=1, source_target_pairs={{32,0},{33,1},{34,2},{35,3},{36,4},{37,5},{38,6},{39,7},{40,8},{41... | collective-permute-start | bytes 1769480 | tf_op jit(solution)/shard_map/ppermute | solution.py:33
  25.3 11.7 %collective-permute-start.9 = (bf16[256,1152]{1,0:T(8,128)(2,1)S(1)}, bf16[256,1152]{1,0:T(8,128)(2,1)S(1)}, u32[]{:S(2)}, u32[]{:S(2)}) collective-permute-start(bf16[256,1152]{1,0:T(8,128)(2,1)S(1)} %constant_dynamic-update-slice_fusion.2.refs_5_.refs_1_), channel_id=1, source_target_pairs={{3,0},{2,1},{1,2},{0,3},{7,4},{6,5},{5,6},{4,7},{11,8},{10,9},{9,1... | collective-permute-start | bytes 1769480 | tf_op jit(solution)/shard_map/ppermute | solution.py:33
  28.7 10.0 %collective-permute-start.5 = (bf16[256,1152]{1,0:T(8,128)(2,1)S(1)}, bf16[256,1152]{1,0:T(8,128)(2,1)S(1)}, u32[]{:S(2)}, u32[]{:S(2)}) collective-permute-start(bf16[256,1152]{1,0:T(8,128)(2,1)S(1)} %constant_dynamic-update-slice_fusion.refs_1_), channel_id=1, source_target_pairs={{1,0},{0,1},{3,2},{2,3},{5,4},{4,5},{7,6},{6,7},{9,8},{8,9},{11,10... | collective-permute-start | bytes 1769480 | tf_op jit(solution)/shard_map/ppermute | solution.py:33
  28.9 14.3 %collective-permute-start.10 = (bf16[256,1152]{1,0:T(8,128)(2,1)S(1)}, bf16[256,1152]{1,0:T(8,128)(2,1)S(1)}, u32[]{:S(2)}, u32[]{:S(2)}) collective-permute-start(bf16[256,1152]{1,0:T(8,128)(2,1)S(1)} %stack.3.refs_4_.refs_0_), channel_id=1, source_target_pairs={{8,0},{9,1},{10,2},{11,3},{12,4},{13,5},{14,6},{15,7},{0,8},{1,9},... | collective-permute-start | bytes 1769480 | tf_op jit(solution)/shard_map/ppermute | solution.py:33
  35.5 7.8 %collective-permute-start.12 = (bf16[256,1152]{1,0:T(8,128)(2,1)S(1)}, bf16[256,1152]{1,0:T(8,128)(2,1)S(1)}, u32[]{:S(2)}, u32[]{:S(2)}) collective-permute-start(bf16[256,1152]{1,0:T(8,128)(2,1)S(1)} %collective-permute-done.8.refs_6_.refs_2_), channel_id=1, source_target_pairs={{8,0},{9,1},{10,2},{11,3},{12,4},{13,5},{14,6},{15,7},{0,8},{1,9},... | collective-permute-start | bytes 1769480 | tf_op jit(solution)/shard_map/ppermute | solution.py:33
  38.7 4.6 %collective-permute-start.13 = (bf16[256,1152]{1,0:T(8,128)(2,1)S(1)}, bf16[256,1152]{1,0:T(8,128)(2,1)S(1)}, u32[]{:S(2)}, u32[]{:S(2)}) collective-permute-start(bf16[256,1152]{1,0:T(8,128)(2,1)S(1)} %collective-permute-done.9.refs_7_.refs_3_), channel_id=1, source_target_pairs={{8,0},{9,1},{10,2},{11,3},{12,4},{13,5},{14,6},{15,7},{0,8},{1,9},... | collective-permute-start | bytes 1769480 | tf_op jit(solution)/shard_map/ppermute | solution.py:33
  38.7 4.6 %collective-permute-start.11 = (bf16[256,1152]{1,0:T(8,128)(2,1)S(1)}, bf16[256,1152]{1,0:T(8,128)(2,1)S(1)}, u32[]{:S(2)}, u32[]{:S(2)}) collective-permute-start(bf16[256,1152]{1,0:T(8,128)(2,1)S(1)} %constant_dynamic-update-slice_fusion.2.refs_5_.refs_1_), channel_id=1, source_target_pairs={{8,0},{9,1},{10,2},{11,3},{12,4},{13,5},{14,6},{15,7},{0,8},{1,9},... | collective-permute-start | bytes 1769480 | tf_op jit(solution)/shard_map/ppermute | solution.py:33
  50.5 5.2 %collective-permute-start.16 = (bf16[512,1152]{1,0:T(8,128)(2,1)S(1)}, bf16[512,1152]{1,0:T(8,128)(2,1)S(1)}, u32[]{:S(2)}, u32[]{:S(2)}) collective-permute-start(bf16[512,1152]{1,0:T(8,128)(2,1)S(1)} %get-tuple-element.66), channel_id=1, source_target_pairs={{8,0},{9,1},{10,2},{11,3},{12,4},{13,5},{14,6},{15,7},{0,8},{1,9},... | collective-permute-start | bytes 3538952 | tf_op jit(solution)/shard_map/ppermute | solution.py:33
  50.5 5.1 %collective-permute-start.17 = (bf16[512,1152]{1,0:T(8,128)(2,1)S(1)}, bf16[512,1152]{1,0:T(8,128)(2,1)S(1)}, u32[]{:S(2)}, u32[]{:S(2)}) collective-permute-start(bf16[512,1152]{1,0:T(8,128)(2,1)S(1)} %get-tuple-element.69), channel_id=1, source_target_pairs={{8,0},{9,1},{10,2},{11,3},{12,4},{13,5},{14,6},{15,7},{0,8},{1,9},... | collective-permute-start | bytes 3538952 | tf_op jit(solution)/shard_map/ppermute | solution.py:33
  51.0 4.1 %collective-permute-start.14 = (f32[8,128]{1,0:T(8,128)S(1)}, f32[8,128]{1,0:T(8,128)S(1)}, u32[]{:S(2)}, u32[]{:S(2)}) collective-permute-start(f32[8,128]{1,0:T(8,128)S(1)} %get-tuple-element.60), channel_id=1, source_target_pairs={{8,0},{9,1},{10,2},{11,3},{12,4},{13,5},{14,6},{15,7},{0,8},{1,9},... | collective-permute-start | bytes 12296 | tf_op jit(solution)/shard_map/ppermute | solution.py:33
  54.1 16.5 %collective-permute-start.30 = (bf16[256,1152]{1,0:T(8,128)(2,1)S(1)}, bf16[256,1152]{1,0:T(8,128)(2,1)S(1)}, u32[]{:S(2)}, u32[]{:S(2)}) collective-permute-start(bf16[256,1152]{1,0:T(8,128)(2,1)S(1)} %get-tuple-element.59), channel_id=1, source_target_pairs={{1,0},{0,1},{3,2},{2,3},{5,4},{4,5},{7,6},{6,7},{9,8},{8,9},{11,10... | collective-permute-start | bytes 1769480 | tf_op jit(solution)/shard_map/ppermute | solution.py:33
  54.3 27.7 %collective-permute-start.28 = (bf16[256,1152]{1,0:T(8,128)(2,1)S(1)}, bf16[256,1152]{1,0:T(8,128)(2,1)S(1)}, u32[]{:S(2)}, u32[]{:S(2)}) collective-permute-start(bf16[256,1152]{1,0:T(8,128)(2,1)S(1)} %get-tuple-element.61), channel_id=1, source_target_pairs={{32,0},{33,1},{34,2},{35,3},{36,4},{37,5},{38,6},{39,7},{40,8},{41... | collective-permute-start | bytes 1769480 | tf_op jit(solution)/shard_map/ppermute | solution.py:33
  55.2 4.3 %collective-permute-start.15 = (f32[16,8,128]{2,1,0:T(8,128)S(1)}, f32[16,8,128]{2,1,0:T(8,128)S(1)}, u32[]{:S(2)}, u32[]{:S(2)}) collective-permute-start(f32[16,8,128]{2,1,0:T(8,128)S(1)} %broadcast_in_dim.4), channel_id=1, source_target_pairs={{16,0},{17,1},{18,2},{19,3},{20,4},{21,5},{22,6},{23,7},{24,8},{25... | collective-permute-start | bytes 196616 | tf_op jit(solution)/shard_map/ppermute | solution.py:33
  57.9 16.2 %collective-permute-start.20 = (bf16[256,1152]{1,0:T(8,128)(2,1)S(1)}, bf16[256,1152]{1,0:T(8,128)(2,1)S(1)}, u32[]{:S(2)}, u32[]{:S(2)}) collective-permute-start(bf16[256,1152]{1,0:T(8,128)(2,1)S(1)} %get-tuple-element.74), channel_id=1, source_target_pairs={{3,0},{2,1},{1,2},{0,3},{7,4},{6,5},{5,6},{4,7},{11,8},{10,9},{9,1... | collective-permute-start | bytes 1769480 | tf_op jit(solution)/shard_map/ppermute | solution.py:33
  62.4 6.5 %collective-permute-start.21 = (f32[16,8,128]{2,1,0:T(8,128)S(1)}, f32[16,8,128]{2,1,0:T(8,128)S(1)}, u32[]{:S(2)}, u32[]{:S(2)}) collective-permute-start(f32[16,8,128]{2,1,0:T(8,128)S(1)} %broadcast_in_dim.5), channel_id=1, source_target_pairs={{20,0},{21,1},{22,2},{23,3},{16,4},{17,5},{18,6},{19,7},{28,8},{29... | collective-permute-start | bytes 196616 | tf_op jit(solution)/shard_map/ppermute | solution.py:33
  64.6 20.0 %collective-permute-start.18 = (bf16[256,1152]{1,0:T(8,128)(2,1)S(1)}, bf16[256,1152]{1,0:T(8,128)(2,1)S(1)}, u32[]{:S(2)}, u32[]{:S(2)}) collective-permute-start(bf16[256,1152]{1,0:T(8,128)(2,1)S(1)} %get-tuple-element.70), channel_id=1, source_target_pairs={{96,0},{97,1},{98,2},{99,3},{100,4},{101,5},{102,6},{103,7},{104,8... | collective-permute-start | bytes 1769480 | tf_op jit(solution)/shard_map/ppermute | solution.py:33
  68.9 3.7 %collective-permute-start.22 = (f32[8,128]{1,0:T(8,128)S(1)}, f32[8,128]{1,0:T(8,128)S(1)}, u32[]{:S(2)}, u32[]{:S(2)}) collective-permute-start(f32[8,128]{1,0:T(8,128)S(1)} %fusion), channel_id=1, source_target_pairs={{1,0},{0,1},{3,2},{2,3},{5,4},{4,5},{7,6},{6,7},{9,8},{8,9},{11,10... | collective-permute-start | bytes 12296 | tf_op jit(solution)/shard_map/ppermute | solution.py:33
  71.0 11.6 %collective-permute-start.31 = (bf16[128,1152]{1,0:T(8,128)(2,1)S(1)}, bf16[128,1152]{1,0:T(8,128)(2,1)S(1)}, u32[]{:S(2)}, u32[]{:S(2)}) collective-permute-start(bf16[128,1152]{1,0:T(8,128)(2,1)S(1)} %get-tuple-element.86), channel_id=1, source_target_pairs={{32,0},{33,1},{34,2},{35,3},{36,4},{37,5},{38,6},{39,7},{40,8},{41... | collective-permute-start | bytes 884744 | tf_op jit(solution)/shard_map/ppermute | solution.py:33
  74.5 12.6 %collective-permute-start.23 = (bf16[128,1152]{1,0:T(8,128)(2,1)S(1)}, bf16[128,1152]{1,0:T(8,128)(2,1)S(1)}, u32[]{:S(2)}, u32[]{:S(2)}) collective-permute-start(bf16[128,1152]{1,0:T(8,128)(2,1)S(1)} %get-tuple-element.78), channel_id=1, source_target_pairs={{96,0},{97,1},{98,2},{99,3},{100,4},{101,5},{102,6},{103,7},{104,8... | collective-permute-start | bytes 884744 | tf_op jit(solution)/shard_map/ppermute | solution.py:33
  77.1 3.6 %collective-permute-start.24 = (f32[8,128]{1,0:T(8,128)S(1)}, f32[8,128]{1,0:T(8,128)S(1)}, u32[]{:S(2)}, u32[]{:S(2)}) collective-permute-start(f32[8,128]{1,0:T(8,128)S(1)} %add.25), channel_id=1, source_target_pairs={{32,0},{33,1},{34,2},{35,3},{36,4},{37,5},{38,6},{39,7},{40,8},{41... | collective-permute-start | bytes 12296 | tf_op jit(solution)/shard_map/ppermute | solution.py:33
  80.7 6.4 %collective-permute-start.25 = (f32[8,128]{1,0:T(8,128)S(1)}, f32[8,128]{1,0:T(8,128)S(1)}, u32[]{:S(2)}, u32[]{:S(2)}) collective-permute-start(f32[8,128]{1,0:T(8,128)S(1)} %add.26), channel_id=1, source_target_pairs={{3,0},{2,1},{1,2},{0,3},{7,4},{6,5},{5,6},{4,7},{11,8},{10,9},{9,1... | collective-permute-start | bytes 12296 | tf_op jit(solution)/shard_map/ppermute | solution.py:33
  82.5 7.9 %collective-permute-start.29 = (bf16[128,1152]{1,0:T(8,128)(2,1)S(1)}, bf16[128,1152]{1,0:T(8,128)(2,1)S(1)}, u32[]{:S(2)}, u32[]{:S(2)}) collective-permute-start(bf16[128,1152]{1,0:T(8,128)(2,1)S(1)} %get-tuple-element.83), channel_id=1, source_target_pairs={{1,0},{0,1},{3,2},{2,3},{5,4},{4,5},{7,6},{6,7},{9,8},{8,9},{11,10... | collective-permute-start | bytes 884744 | tf_op jit(solution)/shard_map/ppermute | solution.py:33
  82.8 7.5 %copy-start = (bf16[128,1152]{1,0:T(8,128)(2,1)S(1)}, bf16[128,1152]{1,0:T(8,128)(2,1)}, u32[]{:S(2)}) copy-start(bf16[128,1152]{1,0:T(8,128)(2,1)} %raw_ref.3) | copy-start | bytes 884740
  82.8 7.5 %collective-permute-start.32 = (bf16[128,1152]{1,0:T(8,128)(2,1)S(1)}, bf16[128,1152]{1,0:T(8,128)(2,1)S(1)}, u32[]{:S(2)}, u32[]{:S(2)}) collective-permute-start(bf16[128,1152]{1,0:T(8,128)(2,1)S(1)} %add_codes.3), channel_id=1, source_target_pairs={{16,0},{17,1},{18,2},{19,3},{20,4},{21,5},{22,6},{23,7},{24,8},{25... | collective-permute-start | bytes 884744 | tf_op jit(solution)/shard_map/ppermute | solution.py:33
  85.0 9.4 %collective-permute-start.19 = (bf16[128,1152]{1,0:T(8,128)(2,1)S(1)}, bf16[128,1152]{1,0:T(8,128)(2,1)S(1)}, u32[]{:S(2)}, u32[]{:S(2)}) collective-permute-start(bf16[128,1152]{1,0:T(8,128)(2,1)S(1)} %get-tuple-element.72), channel_id=1, source_target_pairs={{3,0},{2,1},{1,2},{0,3},{7,4},{6,5},{5,6},{4,7},{11,8},{10,9},{9,1... | collective-permute-start | bytes 884744 | tf_op jit(solution)/shard_map/ppermute | solution.py:33
  87.1 8.3 %copy-start.1 = (bf16[128,1152]{1,0:T(8,128)(2,1)S(1)}, bf16[128,1152]{1,0:T(8,128)(2,1)}, u32[]{:S(2)}) copy-start(bf16[128,1152]{1,0:T(8,128)(2,1)} %raw_ref.2) | copy-start | bytes 884740
  87.4 8.0 %collective-permute-start.26 = (bf16[128,1152]{1,0:T(8,128)(2,1)S(1)}, bf16[128,1152]{1,0:T(8,128)(2,1)S(1)}, u32[]{:S(2)}, u32[]{:S(2)}) collective-permute-start(bf16[128,1152]{1,0:T(8,128)(2,1)S(1)} %add_codes.2), channel_id=1, source_target_pairs={{20,0},{21,1},{22,2},{23,3},{16,4},{17,5},{18,6},{19,7},{28,8},{29... | collective-permute-start | bytes 884744 | tf_op jit(solution)/shard_map/ppermute | solution.py:33
  89.6 4.8 %collective-permute-start.27 = (f32[8,128]{1,0:T(8,128)S(1)}, f32[8,128]{1,0:T(8,128)S(1)}, u32[]{:S(2)}, u32[]{:S(2)}) collective-permute-start(f32[8,128]{1,0:T(8,128)S(1)} %add.27.loss_ref.loss_in), channel_id=1, source_target_pairs={{96,0},{97,1},{98,2},{99,3},{100,4},{101,5},{102,6},{103,7},{104,8... | collective-permute-start | bytes 12296 | tf_op jit(solution)/shard_map/ppermute | solution.py:33
